TPU v7x, 512 devices: a whole 4x8x8 slice. The times are simulated.
512 devices in a mesh: pipe: 8 (over z_hi, x), expert: 64 (over y, z_lo, core).
Axes of the slice: x: 4, y: 8, z: 8 (z_hi: 2, z_lo: 4; z = z_hi * 4 + z_lo), core: 2. Of those that a mesh axis runs over, the one named last changes fastest.
Arguments:
- tokens: bfloat16 [8192, 3584], P('expert'), may hold values from -6 to 6
- expert_ids: int32 [8192, 8], P('expert'), may hold values from 0 to 63, all different within a row; in each aligned block of 128 rows (0 to 127, 128 to 255, ...) at most 17 rows name the same one
- gate_scale: float32 [8192, 8], P('expert'), may hold values from 0.1 to 0.6
- w_gate: bfloat16 [64, 3584, 1024], P('expert', None, 'pipe'), may hold values from -0.09375 to 0.09375
- w_up: bfloat16 [64, 3584, 1024], P('expert', None, 'pipe'), may hold values from -0.09375 to 0.09375
- w_down: bfloat16 [64, 1024, 3584], P('expert', 'pipe'), may hold values from -0.5 to 0.5
Outputs:
- mixed: bfloat16 [8192, 3584], P('expert', 'pipe')
Inputs may be any that keep to these rules, and one draw needn't show every extreme that they name: `expert_ids`: the 8 ids of a token differ. Among the 128 tokens held at one position of the expert axis no expert is named more than 17 times, a bound that some block reaches.
All inputs are finite; a program needn't handle non-finite values.
Results may differ from a plain program's by a relative error of at most 0.0057.
Values may be sent and summed in bfloat16 or wider, within the bound.
No kernel may reach another device: no remote copies, remote signals or barrier semaphores. Data moves between devices by JAX's collectives and lax.ppermute only.
A program may use at most 128 MiB of HBM per device.

v0:
```python
import jax
import jax.numpy as jnp
from jax import lax
from jax.sharding import PartitionSpec as P


def body(tokens, expert_ids, gate_scale, w_gate, w_up, w_down):
    tok_rows, width = tokens.shape
    topk = expert_ids.shape[1]
    groups = lax.axis_size("expert")
    pairs = tok_rows * topk
    capacity = pairs // groups + 1
    flat_ids = expert_ids.reshape(-1)
    onehot = (flat_ids[:, None] == jnp.arange(groups, dtype=jnp.int32)[None, :]).astype(jnp.int32)
    before = jnp.cumsum(onehot, axis=0) - onehot
    position = jnp.sum(before * onehot, axis=1)
    slot_index = flat_ids * capacity + position
    source_tok = jnp.arange(pairs, dtype=jnp.int32) // topk
    columns = tokens.shape[1]
    buffer = jnp.zeros((groups * capacity, columns), jnp.bfloat16)
    buffer = buffer.at[slot_index].set(tokens[source_tok])
    rows = lax.all_to_all(
        buffer.reshape(groups, capacity, columns), "expert", split_axis=0, concat_axis=0, tiled=True
    )
    senders, slots, full_width = rows.shape
    stacked = rows.reshape(senders * slots, full_width)
    gate_val = jnp.dot(stacked, w_gate[0], preferred_element_type=jnp.float32)
    up_val = jnp.dot(stacked, w_up[0], preferred_element_type=jnp.float32)
    hidden = (jax.nn.silu(gate_val) * up_val).astype(jnp.bfloat16)
    output = jnp.dot(hidden, w_down[0], preferred_element_type=jnp.float32).astype(jnp.bfloat16)
    output = output.reshape(senders, slots, full_width)
    returned = lax.all_to_all(output, "expert", split_axis=0, concat_axis=0, tiled=True)
    flat_back = returned.reshape(groups * capacity, width)
    picked = flat_back[slot_index].reshape(tok_rows, topk, width)
    accum = jnp.sum(picked.astype(jnp.float32) * gate_scale[:, :, None], axis=1)
    return lax.psum_scatter(accum, "pipe", scatter_dimension=1, tiled=True).astype(jnp.bfloat16)


def solution(mesh):
    placed = (
        P("expert", None),
        P("expert", None),
        P("expert", None),
        P("expert", None, "pipe"),
        P("expert", None, "pipe"),
        P("expert", "pipe", None),
    )
    return jax.shard_map(
        body, mesh=mesh, in_specs=placed, out_specs=P("expert", "pipe"), check_vma=False
    )
```

profile of v0, /device:TPU:1, one launch (start us, length us, event | category | flops | bytes accessed | tf_op | source)
XLA Modules:
  0.0 826.0 jit_solution(3050803669524750422)
XLA Ops:
  6.5 0.9 copy.29
  7.6 0.7 broadcast_multiply_fusion
  8.3 18.0 %reduce-window.6 = s32[64,8,128]{2,1,0:T(8,128)S(1)} reduce-window(s32[64,8,128]{2,1,0:T(8,128)S(1)} %fusion.19, s32[]{:T(128)} %constant.28.clone.1), window={size=1x1x128 pad=0_0x0_0x127_0}, to_apply=%region_0.0 | reduce-window | flops 8323072 | bytes 524292 | tf_op jit(solution)/shard_map/reduce-window
  26.3 0.1 slice.12
  26.5 0.1 copy.31
  26.7 0.1 broadcast_add_fusion
  26.9 0.1 copy.28
  27.0 0.1 mul.36
  27.2 44.0 %scatter_custom_fusion = bf16[1088,3584]{1,0:T(8,128)(2,1)} fusion(s32[1024]{0:T(1024)S(1)} %bitcast.43, bf16[128,3584]{1,0:T(8,128)(2,1)S(1)} %copy-done, s32[1024]{0:T(1024)S(1)} %broadcast_clamp_fusion.1, bf16[]{:T(256)} %constant.26.clone.1), kind=kCustom, calls=%fused_computation.6 | custom fusion | bytes 7798786 | tf_op jit(solution)/shard_map/scatter | solution.py:21
  71.2 10.2 %reshape.106 = bf16[64,17,3584]{2,1,0:T(8,128)(2,1)} reshape(bf16[1088,3584]{1,0:T(8,128)(2,1)} %scatter_custom_fusion) | data formatting | bytes 15597568 | tf_op jit(solution)/shard_map/reshape | solution.py:23
  81.3 256.8 %all_to_all.10 = bf16[64,17,3584]{2,1,0:T(8,128)(2,1)} all-to-all(bf16[64,17,3584]{2,1,0:T(8,128)(2,1)} %reshape.106), channel_id=1, replica_groups=mesh['pipe'=8,'expert'=64] {'expert'}, dimensions={0} | all-to-all | bytes 15597568 | tf_op jit(solution)/shard_map/all_to_all | solution.py:22
  338.1 10.5 %reshape.107 = bf16[1088,3584]{1,0:T(8,128)(2,1)} reshape(bf16[64,17,3584]{2,1,0:T(8,128)(2,1)} %all_to_all.10) | data formatting | bytes 15597568 | tf_op jit(solution)/shard_map/reshape | solution.py:26
  348.6 5.5 fusion.8
  354.2 12.3 %convolution_convert_fusion = bf16[1088,3584]{1,0:T(8,128)(2,1)} fusion(bf16[1088,3584]{1,0:T(8,128)(2,1)} %reshape.107, bf16[1,128,3584]{2,1,0:T(8,128)(2,1)S(1)} %copy-done.2, bf16[1,3584,128]{2,1,0:T(8,128)(2,1)S(1)} %copy-done.3, f32[1088,128]{1,0:T(8,128)S(1)} %fusion.8), kind=kOutput, calls=%fused_computation.3 | convolution fusion | flops 2001223680 | bytes 17989632 | tf_op jit(solution)/shard_map/dot_general | solution.py:30
  366.5 10.2 %reshape.108 = bf16[64,17,3584]{2,1,0:T(8,128)(2,1)} reshape(bf16[1088,3584]{1,0:T(8,128)(2,1)} %convolution_convert_fusion) | data formatting | bytes 15597568 | tf_op jit(solution)/shard_map/reshape | solution.py:31
  376.7 10.5 %all-to-all-start.1 = ((bf16[64,17,3584]{2,1,0:T(8,128)(2,1)}), bf16[64,17,3584]{2,1,0:T(8,128)(2,1)}, u32[]{:S(2)}, u32[]{:S(2)}) async-start(bf16[64,17,3584]{2,1,0:T(8,128)(2,1)} %reshape.108), calls=%async_computation.1 | async-start | bytes 22020096 | tf_op jit(solution)/shard_map/all_to_all | solution.py:32
  387.2 0.1 copy.33
  387.4 279.5 %all-to-all-done.1 = bf16[64,17,3584]{2,1,0:T(8,128)(2,1)} async-done(((bf16[64,17,3584]{2,1,0:T(8,128)(2,1)}), bf16[64,17,3584]{2,1,0:T(8,128)(2,1)}, u32[]{:S(2)}, u32[]{:S(2)}) %all-to-all-start.1) | async-done | bytes 7798816 | tf_op jit(solution)/shard_map/all_to_all | solution.py:32
  666.8 10.4 %reshape.109 = bf16[1088,3584]{1,0:T(8,128)(2,1)} reshape(bf16[64,17,3584]{2,1,0:T(8,128)(2,1)} %all-to-all-done.1) | data formatting | bytes 15597568 | tf_op jit(solution)/shard_map/reshape | solution.py:33
  677.2 18.1 %gather_fusion = bf16[1024,3584]{1,0:T(8,128)(2,1)} fusion(bf16[1088,3584]{1,0:T(8,128)(2,1)} %reshape.109, s32[1024]{0:T(1024)S(1)} %broadcast_clamp_fusion), kind=kCustom, calls=%fused_computation.1 | custom fusion | bytes 14684160 | tf_op jit(solution)/shard_map/gather | solution.py:34
  695.3 9.7 %fusion = f32[128,3584]{1,0:T(8,128)S(1)} fusion(bf16[1024,3584]{1,0:T(8,128)(2,1)} %gather_fusion, f32[128,8]{1,0:T(8,128)S(1)} %copy.33), kind=kLoop, calls=%fused_computation.5 | loop fusion | flops 10551296 | bytes 9179136 | tf_op jit(solution)/shard_map/reduce_sum | solution.py:35
  705.0 1.7 copy.35
  706.8 110.4 %reduce-scatter.4.cloned.1.call-done = f32[448,128]{1,0:T(8,128)} async-done(((f32[3584,128]{1,0:T(8,128)}), f32[448,128]{1,0:T(8,128)}) %reduce-scatter.4.cloned.1.call-update) | async-done | bytes 229392
  817.2 1.6 bitcast_convert_fusion
  (25 shorter events, 0.5 us)
Async XLA Ops:
  6.5 20.7 %copy-start = (bf16[128,3584]{1,0:T(8,128)(2,1)S(1)}, bf16[128,3584]{1,0:T(8,128)(2,1)}, u32[]{:S(2)}) copy-start(bf16[128,3584]{1,0:T(8,128)(2,1)} %param.6) | copy-start | bytes 2752516
  338.1 10.5 %copy-start.5 = (bf16[1,3584,128]{2,1,0:T(8,128)(2,1)S(1)}, bf16[1,3584,128]{2,1,0:T(8,128)(2,1)}, u32[]{:S(2)}) copy-start(bf16[1,3584,128]{2,1,0:T(8,128)(2,1)} %param.9) | copy-start | bytes 2752516
  348.6 5.6 copy-start.2
  348.6 5.6 copy-start.3
  376.7 10.6 %copy-start.4 = (f32[128,8]{0,1:T(8,128)S(1)}, f32[128,8]{0,1:T(8,128)}, u32[]{:S(2)}) copy-start(f32[128,8]{0,1:T(8,128)} %param.8) | copy-start | bytes 12292
  376.7 290.1 %all-to-all-start.1 = ((bf16[64,17,3584]{2,1,0:T(8,128)(2,1)}), bf16[64,17,3584]{2,1,0:T(8,128)(2,1)}, u32[]{:S(2)}, u32[]{:S(2)}) async-start(bf16[64,17,3584]{2,1,0:T(8,128)(2,1)} %reshape.108), calls=%async_computation.1 | async-start | bytes 22020096 | tf_op jit(solution)/shard_map/all_to_all | solution.py:32
  387.2 430.0 %reduce-scatter.4.cloned.1.call-start = ((), (), s32[]{:S(2)}) async-start(), calls=%async_computation.3 | async-start | bytes 2064384
  677.2 141.6 %copy-start.1 = (bf16[128,3584]{1,0:T(8,128)(2,1)S(1)}, bf16[128,3584]{1,0:T(8,128)(2,1)}, u32[]{:S(2)}) copy-start(bf16[128,3584]{1,0:T(8,128)(2,1)} %param.6) | copy-start | bytes 2752516
Sparse Core Ops, SparseCore 0:
  706.9 110.2 reduce-scatter.3
where the time goes:
time: 840 us; the launch traced here: 826 us
  waiting for transfers between devices  390 us (46%)
  blocking collectives  257 us (31%)
  local copies, waits for them, and re-layouts  107 us (13%)
  other arithmetic  30.3 us (4%)
  matrix products  17.9 us (2%)
  between operations  13.9 us (2%)
  starting transfers between devices  10.6 us (1%)
    all_to_all x1, waiting for transfers between devices, body(): lax.all_to_all(output, 'expert', split_axis=0, concat_axis=0, tiled=True)  279 us
    all_to_all x1, blocking collectives, body(): lax.all_to_all(buffer.reshape(groups, capacity, columns), 'expert', split...  257 us
    unnamed x2, waiting for transfers between devices  110 us
    scatter x1, local copies, waits for them, and re-layouts, body(): buffer = buffer.at[slot_index].set(tokens[source_tok])  44 us
    another operation x3, other arithmetic  18.2 us
    gather x1, local copies, waits for them, and re-layouts, body(): picked = flat_back[slot_index].reshape(tok_rows, topk, width)  18.1 us
  transfers between devices with their start and end apart: 2, of which 2 were waited for; matrix products, arithmetic and copies ran while one was open for 0% of the time, Pallas kernels for 0%

commit v1 on v0

v1 whole, which is shorter than its diff:
```python
import jax
import jax.numpy as jnp
from jax import lax
from jax.experimental import pallas as pl
from jax.experimental.pallas import tpu as pltpu
from jax.sharding import PartitionSpec as P

BF = jnp.bfloat16
F32 = jnp.float32
LANES = 128
X = 4
VMEM = 56 * 1024 * 1024


def params():
    return pltpu.CompilerParams(vmem_limit_bytes=VMEM)


def in_vmem():
    return pl.BlockSpec(memory_space=pltpu.VMEM)


def in_hbm():
    return pl.BlockSpec(memory_space=pl.ANY)


def slots(ids, experts):
    tokens, topk = ids.shape
    lane = lax.broadcasted_iota(jnp.int32, (tokens, experts), 1)
    named = jnp.zeros((tokens, experts), F32)
    for k in range(topk):
        named += (ids[:, k : k + 1] == lane).astype(F32)
    row = lax.broadcasted_iota(jnp.int32, (tokens, tokens), 0)
    col = lax.broadcasted_iota(jnp.int32, (tokens, tokens), 1)
    contract = (((0,), (0,)), ((), ()))
    named = named.astype(BF)
    chosen = lax.dot_general(named, (row == col).astype(BF), contract, preferred_element_type=F32)
    place = lax.dot_general(named, (row < col).astype(BF), contract, preferred_element_type=F32)
    return jnp.where(chosen > 0.5, place, -1.0)


def at_slot(place, first, count, value):
    experts, tokens = place.shape
    if first is None:
        hit = jnp.broadcast_to((place == 16.0)[:, None, :], (experts, count, tokens))
    else:
        slot = lax.broadcasted_iota(jnp.int32, (experts, count, tokens), 1).astype(F32) + first
        hit = place[:, None, :] == slot
    return jnp.where(hit, value, 0.0).reshape(experts * count, tokens)


def dispatch_kernel(x_ref, ids_ref, tok_ref, out_ref):
    experts = out_ref.shape[0]
    tok = tok_ref[...]
    tiles = tok.shape[1] // LANES
    place = slots(ids_ref[...], experts)
    pick = at_slot(place, 0.0, 16, 1.0).astype(BF)
    rows = jnp.dot(pick, tok, preferred_element_type=F32).astype(BF)
    for c in range(tiles):
        out_ref[:, c * 16 : (c + 1) * 16, :] = rows[:, c * LANES : (c + 1) * LANES].reshape(experts, 16, LANES)
    last = at_slot(place, None, 8, 1.0)
    sub = lax.broadcasted_iota(jnp.int32, (experts, 8, tok.shape[0]), 1).reshape(last.shape)
    tail = jnp.zeros((experts * 8, LANES), F32)
    for c in range(tiles):
        mine = jnp.where(sub == c, last, 0.0).astype(BF)
        tail += jnp.dot(mine, tok[:, c * LANES : (c + 1) * LANES], preferred_element_type=F32)
    out_ref[:, tiles * 16 : tiles * 16 + 8, :] = tail.astype(BF).reshape(experts, 8, LANES)


def dispatch(x, ids, tokens, experts):
    count, width = tokens.shape
    quarter = width // X
    depth = quarter // LANES * 16 + 8
    return pl.pallas_call(
        dispatch_kernel,
        out_shape=jax.ShapeDtypeStruct((experts, depth, LANES), BF),
        grid_spec=pltpu.PrefetchScalarGridSpec(
            num_scalar_prefetch=1,
            grid=(1,),
            in_specs=[
                pl.BlockSpec(ids.shape, lambda i, x: (0, 0)),
                pl.BlockSpec((count, quarter), lambda i, x: (0, x[0])),
            ],
            out_specs=pl.BlockSpec((experts, depth, LANES), lambda i, x: (0, 0, 0)),
        ),
        compiler_params=params(),
        name="dispatch",
    )(x, ids, tokens)


def pack_kernel(x_ref, gate_ref, up_ref, down_ref, *rest):
    outs, sems = rest[:-1], rest[-1]
    quarter = gate_ref.shape[0] // X
    depth = down_ref.shape[0]
    copies = []

    def copy(src, dst):
        one = pltpu.make_async_copy(src, dst, sems.at[len(copies)])
        one.start()
        copies.append(one)

    for d, out in enumerate(outs, 1):
        q = lax.rem(x_ref[0] + d, X)
        part = pl.ds(pl.multiple_of(q * quarter, quarter), quarter)
        copy(gate_ref.at[part, :], out.at[pl.ds(0, quarter), :])
        copy(up_ref.at[part, :], out.at[pl.ds(quarter, quarter), :])
        for c in range(quarter // LANES):
            cols = pl.ds(pl.multiple_of(q * quarter + c * LANES, LANES), LANES)
            copy(down_ref.at[:, cols], out.at[pl.ds(2 * quarter + c * depth, depth), :])
    for one in copies:
        one.wait()


def pack(x, w_gate, w_up, w_down):
    quarter = w_gate.shape[0] // X
    rows = 2 * quarter + quarter // LANES * w_down.shape[0]
    shape = jax.ShapeDtypeStruct((rows, LANES), BF)
    count = (X - 1) * (2 + quarter // LANES)
    return pl.pallas_call(
        pack_kernel,
        out_shape=[shape] * (X - 1),
        in_specs=[pl.BlockSpec(memory_space=pltpu.SMEM)] + [in_hbm()] * 3,
        out_specs=[in_hbm()] * (X - 1),
        scratch_shapes=[pltpu.SemaphoreType.DMA((count,))],
        compiler_params=params(),
        name="pack",
    )(x, w_gate, w_up, w_down)


def stacked(chunks_ref):
    sources, depth, _ = chunks_ref.shape
    tiles = depth // 16
    main = [chunks_ref[:, c * 16 : (c + 1) * 16, :].reshape(sources * 16, LANES) for c in range(tiles)]
    tail = chunks_ref[:, tiles * 16 : tiles * 16 + 8, :].reshape(sources * 8, LANES)
    row = lax.broadcasted_iota(jnp.int32, (sources, sources * 8), 0)
    col = lax.broadcasted_iota(jnp.int32, (sources, sources * 8), 1)
    last = [
        jnp.dot((col == row * 8 + c).astype(BF), tail, preferred_element_type=F32).astype(BF) for c in range(tiles)
    ]
    return jnp.concatenate(main, axis=1), jnp.concatenate(last, axis=1)


def project_kernel(chunks_ref, gate_ref, up_ref, out_ref):
    main, last = stacked(chunks_ref)
    weight = jnp.concatenate([gate_ref[...], up_ref[...]], axis=1)
    count = main.shape[0]
    out_ref[pl.ds(0, count), :] = jnp.dot(main, weight, preferred_element_type=F32).astype(out_ref.dtype)
    out_ref[pl.ds(count, last.shape[0]), :] = jnp.dot(last, weight, preferred_element_type=F32).astype(out_ref.dtype)


def project(chunks, block, gate, up, gate_at, up_at, dtype):
    sources, depth, _ = chunks.shape
    quarter = depth // 16 * LANES

    def kernel(block_ref, *refs):
        project_kernel(*refs)

    return pl.pallas_call(
        kernel,
        out_shape=jax.ShapeDtypeStruct((sources * 17, 2 * LANES), dtype),
        grid_spec=pltpu.PrefetchScalarGridSpec(
            num_scalar_prefetch=1,
            grid=(1,),
            in_specs=[
                pl.BlockSpec(chunks.shape, lambda i, b: (0, 0, 0)),
                pl.BlockSpec((quarter, LANES), lambda i, b: (gate_at(b), 0)),
                pl.BlockSpec((quarter, LANES), lambda i, b: (up_at(b), 0)),
            ],
            out_specs=pl.BlockSpec((sources * 17, 2 * LANES), lambda i, b: (0, 0)),
        ),
        compiler_params=params(),
        name="project",
    )(block, chunks, gate, up)


def down_kernel(x_ref, own_ref, h1, h2, h3, p1, p2, p3, down_ref, out_ref):
    experts = out_ref.shape[0]
    hidden = jnp.concatenate([own_ref[...], h1[...], h2[...], h3[...]], axis=1)
    tiles = out_ref.shape[1] // 16
    depth = down_ref.shape[0]
    base = 2 * tiles * LANES
    main = hidden[: experts * 16]
    last = hidden[experts * 16 :]
    row = lax.broadcasted_iota(jnp.int32, (experts * 8, experts), 0)
    col = lax.broadcasted_iota(jnp.int32, (experts * 8, experts), 1)
    tail = jnp.zeros((experts * 8, LANES), F32)
    for c in range(tiles):
        rows = pl.ds(base + c * depth, depth)
        weight = jnp.concatenate(
            [down_ref[:, c * LANES : (c + 1) * LANES], p1[rows, :], p2[rows, :], p3[rows, :]], axis=0
        )
        out = jnp.dot(main, weight, preferred_element_type=F32).astype(BF)
        out_ref[:, c * 16 : (c + 1) * 16, :] = out.reshape(experts, 16, LANES)
        end = jnp.dot(last, weight, preferred_element_type=F32).astype(BF)
        tail += jnp.dot((row == col * 8 + c).astype(BF), end, preferred_element_type=F32)
    out_ref[:, tiles * 16 : tiles * 16 + 8, :] = tail.astype(BF).reshape(experts, 8, LANES)


def down(x, hiddens, packs, w_down, experts):
    depth, width = w_down.shape
    quarter = width // X
    chunk = quarter // LANES * 16 + 8
    whole = lambda a: pl.BlockSpec(a.shape, lambda i, x: (0, 0))
    return pl.pallas_call(
        down_kernel,
        out_shape=jax.ShapeDtypeStruct((experts, chunk, LANES), BF),
        grid_spec=pltpu.PrefetchScalarGridSpec(
            num_scalar_prefetch=1,
            grid=(1,),
            in_specs=[whole(a) for a in (*hiddens, *packs)]
            + [pl.BlockSpec((depth, quarter), lambda i, x: (0, x[0]))],
            out_specs=pl.BlockSpec((experts, chunk, LANES), lambda i, x: (0, 0, 0)),
        ),
        compiler_params=params(),
        name="down",
    )(x, *hiddens, *packs, w_down)


def combine_kernel(ids_ref, scale_ref, chunks_ref, out_ref):
    experts, depth, _ = chunks_ref.shape
    tiles = depth // 16
    ids, scale = ids_ref[...], scale_ref[...]
    tokens, topk = ids.shape
    place = slots(ids, experts)
    lane = lax.broadcasted_iota(jnp.int32, (tokens, experts), 1)
    weight = jnp.zeros((tokens, experts), F32)
    for k in range(topk):
        weight += jnp.where(ids[:, k : k + 1] == lane, scale[:, k : k + 1], 0.0)
    high = weight.astype(BF)
    low = (weight - high.astype(F32)).astype(BF)
    row = lax.broadcasted_iota(jnp.int32, (tokens, tokens), 0)
    col = lax.broadcasted_iota(jnp.int32, (tokens, tokens), 1)
    same = (row == col).astype(BF)
    contract = (((0,), (0,)), ((), ()))
    tail = chunks_ref[:, tiles * 16 : tiles * 16 + 8, :].reshape(experts * 8, LANES)
    sub = lax.broadcasted_iota(jnp.int32, (experts, 8, tokens), 1).reshape(experts * 8, tokens)
    main = jnp.concatenate(
        [chunks_ref[:, c * 16 : (c + 1) * 16, :].reshape(experts * 16, LANES) for c in range(tiles)], axis=1
    )
    total = jnp.zeros((tokens, tiles * LANES), F32)
    ends = [jnp.zeros((tokens, LANES), F32) for _ in range(tiles)]
    for part in (high, low):
        turned = lax.dot_general(part, same, contract, preferred_element_type=F32)
        coef = at_slot(place, 0.0, 16, turned[:, None, :]).astype(BF)
        total += lax.dot_general(coef, main, contract, preferred_element_type=F32)
        last = at_slot(place, None, 8, turned[:, None, :])
        for c in range(tiles):
            mine = jnp.where(sub == c, last, 0.0).astype(BF)
            ends[c] += lax.dot_general(mine, tail, contract, preferred_element_type=F32)
    out_ref[...] = (total + jnp.concatenate(ends, axis=1)).astype(out_ref.dtype)


def combine(ids, scale, chunks):
    tiles = chunks.shape[1] // 16
    return pl.pallas_call(
        combine_kernel,
        out_shape=jax.ShapeDtypeStruct((ids.shape[0], tiles * LANES), F32),
        in_specs=[in_vmem()] * 3,
        out_specs=in_vmem(),
        compiler_params=params(),
        name="combine",
    )(ids, scale, chunks)


def turn(d):
    return [(z * X + x, z * X + (x + d) % X) for z in range(2) for x in range(X)]


def body(tokens, expert_ids, gate_scale, w_gate, w_up, w_down):
    groups = lax.axis_size("expert")
    x = lax.rem(lax.axis_index("pipe"), X)
    xs = x.reshape(1)
    w_gate, w_up, w_down = w_gate[0], w_up[0], w_down[0]
    packed = pack(xs, w_gate, w_up, w_down)
    packs = [lax.ppermute(packed[d - 1], "pipe", turn(d)) for d in range(1, X)]
    buffer = dispatch(xs, expert_ids, tokens, groups)
    chunks = lax.all_to_all(buffer, "expert", split_axis=0, concat_axis=0, tiled=True)
    arrived = {}
    for d in (2, 1, 3):
        pk = packs[d - 1]
        part = project(chunks, xs, pk, pk, lambda b: 0, lambda b: 1, BF)
        arrived[d] = lax.ppermute(part, "pipe", turn(-d))
    own = project(chunks, xs, w_gate, w_up, lambda b: b[0], lambda b: b[0], F32)
    summed = own + arrived[1].astype(F32) + arrived[2].astype(F32) + arrived[3].astype(F32)
    hidden = (jax.nn.silu(summed[:, :LANES]) * summed[:, LANES:]).astype(BF)
    hiddens = [hidden] + [lax.ppermute(hidden, "pipe", turn(d)) for d in (1, 2, 3)]
    output = down(xs, hiddens, packs, w_down, groups)
    returned = lax.all_to_all(output, "expert", split_axis=0, concat_axis=0, tiled=True)
    mixed = combine(expert_ids, gate_scale, returned)
    half = mixed.shape[1] // 2
    z = lax.axis_index("pipe") // X
    first = jnp.where(z == 0, mixed[:, :half], mixed[:, half:])
    second = jnp.where(z == 0, mixed[:, half:], mixed[:, :half])
    to_first = [(z * X + x, 2 * x + z) for z in range(2) for x in range(X)]
    to_second = [(z * X + x, 2 * x + 1 - z) for z in range(2) for x in range(X)]
    a = lax.ppermute(first.astype(BF), "pipe", to_first)
    b = lax.ppermute(second.astype(BF), "pipe", to_second)
    return (a.astype(F32) + b.astype(F32)).astype(BF)


def solution(mesh):
    placed = (
        P("expert", None),
        P("expert", None),
        P("expert", None),
        P("expert", None, "pipe"),
        P("expert", None, "pipe"),
        P("expert", "pipe", None),
    )
    return jax.shard_map(
        body, mesh=mesh, in_specs=placed, out_specs=P("expert", "pipe"), check_vma=False
    )
```

time: 840 us -> 271 us (0.32)
  the two profiles are of different devices: /device:TPU:1 before, /device:TPU:78 now
where the time goes in v1:
time: 271 us; the launch traced here: 270 us
  waiting for transfers between devices  101 us (37%)
  Pallas kernels  91.9 us (34%)
  starting transfers between devices  66.2 us (24%)
  local copies, waits for them, and re-layouts  7.92 us (3%)
  other arithmetic  2.79 us (1%)
    pallas_call x1, Pallas kernels, pack(): pl.pallas_call(pack_kernel, out_shape=[shape] * (X - 1), in_specs=[pl.Blo...  63.9 us
    all_to_all x1, waiting for transfers between devices, body(): lax.all_to_all(output, 'expert', split_axis=0, concat_axis=0, tiled=True)  46.9 us
    ppermute x3, waiting for transfers between devices, body(): arrived[d] = lax.ppermute(part, 'pipe', turn(-d))  15.1 us
    ppermute x3, starting transfers between devices, body(): arrived[d] = lax.ppermute(part, 'pipe', turn(-d))  13.9 us
    pallas_call x4, Pallas kernels, project(): pl.pallas_call(kernel, out_shape=jax.ShapeDtypeStruct((sources * 17, 2 *...  13.9 us
    ppermute x3, waiting for transfers between devices, body(): packs = [lax.ppermute(packed[d - 1], 'pipe', turn(d)) for d in range(1, X)]  13.4 us
    ppermute x3, waiting for transfers between devices, body(): lax.ppermute(hidden, 'pipe', turn(d))  13 us
    all_to_all x1, starting transfers between devices, body(): lax.all_to_all(buffer, 'expert', split_axis=0, concat_axis=0, tiled=True)  12.6 us
  transfers between devices with their start and end apart: 13, of which 10 were waited for; matrix products, arithmetic and copies ran while one was open for 0% of the time, Pallas kernels for 29%

profile of v1, /device:TPU:78, one launch (start us, length us, event | category | flops | bytes accessed | tf_op | source)
XLA Modules:
  0.0 270.5 jit_solution(175857967190531817)
XLA Ops:
  1.4 3.6 %dispatch.1 = bf16[64,120,128]{2,1,0:T(8,128)(2,1)} custom-call(s32[1]{0:T(128)} %bitcast.x_ref.block_ref, s32[128,8]{1,0:T(8,128)} %copy.8.ids_ref, bf16[128,3584]{1,0:T(8,128)(2,1)} %tok_ref.1), custom_call_target="tpu_custom_call" | custom-call | tf_op jit(solution)/shard_map/dispatch/pallas_call | solution.py:74
  5.0 12.6 %all-to-all-start = ((bf16[64,120,128]{2,1,0:T(8,128)(2,1)}), bf16[64,120,128]{2,1,0:T(8,128)(2,1)S(1)}, u32[]{:S(2)}, u32[]{:S(2)}) async-start(bf16[64,120,128]{2,1,0:T(8,128)(2,1)} %dispatch.1), calls=%async_computation | async-start | bytes 3932160 | tf_op jit(solution)/shard_map/all_to_all | solution.py:277
  17.6 63.9 %pack.1 = (bf16[2688,128]{1,0:T(8,128)(2,1)}, bf16[2688,128]{1,0:T(8,128)(2,1)}, bf16[2688,128]{1,0:T(8,128)(2,1)}) custom-call(s32[1]{0:T(128)} %bitcast.x_ref.block_ref, bf16[3584,128]{1,0:T(8,128)(2,1)} %bitcast.4, bf16[3584,128]{1,0:T(8,128)(2,1)} %bitcast.6, bf16[128,3584]{1,0:T(8,128)(2,1)} %bitcast.8), custom_call_target="tpu_custom_call" | custom-call | tf_op jit(solution)/shard_map/pack/pallas_call | solution.py:119
  83.9 4.3 %collective-permute-start.2 = (bf16[2688,128]{1,0:T(8,128)(2,1)}, bf16[2688,128]{1,0:T(8,128)(2,1)S(1)}, u32[]{:S(2)}, u32[]{:S(2)}) collective-permute-start(bf16[2688,128]{1,0:T(8,128)(2,1)} %get-tuple-element.9), channel_id=1, source_target_pairs={{0,128},{64,192},{128,0},{192,64},{256,384},{320,448},{384,256},{4... | collective-permute-start | bytes 2064392 | tf_op jit(solution)/shard_map/ppermute | solution.py:275
  90.2 11.7 %collective-permute-done.refs_1_.refs_2_.p1 = bf16[2688,128]{1,0:T(8,128)(2,1)S(1)} collective-permute-done((bf16[2688,128]{1,0:T(8,128)(2,1)}, bf16[2688,128]{1,0:T(8,128)(2,1)S(1)}, u32[]{:S(2)}, u32[]{:S(2)}) %collective-permute-start) | collective-permute-done | bytes 688160 | tf_op jit(solution)/shard_map/ppermute | solution.py:275
  104.1 3.4 %project.5 = bf16[1088,256]{1,0:T(8,128)(2,1)} custom-call(s32[1]{0:T(128)} %bitcast.x_ref.block_ref, bf16[64,120,128]{2,1,0:T(8,128)(2,1)} %copy-done, bf16[2688,128]{1,0:T(8,128)(2,1)} %copy-done.2, bf16[2688,128]{1,0:T(8,128)(2,1)} %copy-done.2), custom_call_target="tpu_custom_call" | custom-call | tf_op jit(solution)/shard_map/project/pallas_call | solution.py:158
  111.1 3.4 %project.6 = bf16[1088,256]{1,0:T(8,128)(2,1)} custom-call(s32[1]{0:T(128)} %bitcast.x_ref.block_ref, bf16[64,120,128]{2,1,0:T(8,128)(2,1)} %copy-done, bf16[2688,128]{1,0:T(8,128)(2,1)} %copy-done.3, bf16[2688,128]{1,0:T(8,128)(2,1)} %copy-done.3), custom_call_target="tpu_custom_call" | custom-call | tf_op jit(solution)/shard_map/project/pallas_call | solution.py:158
  114.6 3.4 %collective-permute-start.3 = (bf16[1088,256]{1,0:T(8,128)(2,1)}, bf16[1088,256]{1,0:T(8,128)(2,1)S(1)}, u32[]{:S(2)}, u32[]{:S(2)}) collective-permute-start(bf16[1088,256]{1,0:T(8,128)(2,1)} %project.6), channel_id=1, source_target_pairs={{0,128},{64,192},{128,0},{192,64},{256,384},{320,448},{384,256},{4... | collective-permute-start | bytes 1671176 | tf_op jit(solution)/shard_map/ppermute | solution.py:282
  119.7 3.4 %project.7 = bf16[1088,256]{1,0:T(8,128)(2,1)} custom-call(s32[1]{0:T(128)} %bitcast.x_ref.block_ref, bf16[64,120,128]{2,1,0:T(8,128)(2,1)} %copy-done, bf16[2688,128]{1,0:T(8,128)(2,1)} %collective-permute-done.4.refs_1_.refs_2_.p3, bf16[2688,128]{1,0:T(8,128)(2,1)} %collective-permute-done.4.refs_1_.refs_2_.p3), custom_call_target="tpu_custom_call" | custom-call | tf_op jit(solution)/shard_map/project/pallas_call | solution.py:158
  123.1 7.8 %collective-permute-start.5 = (bf16[1088,256]{1,0:T(8,128)(2,1)}, bf16[1088,256]{1,0:T(8,128)(2,1)S(1)}, u32[]{:S(2)}, u32[]{:S(2)}) collective-permute-start(bf16[1088,256]{1,0:T(8,128)(2,1)} %project.7), channel_id=1, source_target_pairs={{0,64},{64,128},{128,192},{192,0},{256,320},{320,384},{384,448},{4... | collective-permute-start | bytes 1671176 | tf_op jit(solution)/shard_map/ppermute | solution.py:282
  130.9 3.6 %project.4 = f32[1088,256]{1,0:T(8,128)} custom-call(s32[1]{0:T(128)} %bitcast.x_ref.block_ref, bf16[64,120,128]{2,1,0:T(8,128)(2,1)} %copy-done, bf16[3584,128]{1,0:T(8,128)(2,1)} %bitcast.5, bf16[3584,128]{1,0:T(8,128)(2,1)} %bitcast.7), custom_call_target="tpu_custom_call" | custom-call | tf_op jit(solution)/shard_map/project/pallas_call | solution.py:158
  134.5 8.9 %collective-permute-done.3 = bf16[1088,256]{1,0:T(8,128)(2,1)S(1)} collective-permute-done((bf16[1088,256]{1,0:T(8,128)(2,1)}, bf16[1088,256]{1,0:T(8,128)(2,1)S(1)}, u32[]{:S(2)}, u32[]{:S(2)}) %collective-permute-start.3) | collective-permute-done | bytes 557088 | tf_op jit(solution)/shard_map/ppermute | solution.py:282
  143.4 6.2 %collective-permute-done.5 = bf16[1088,256]{1,0:T(8,128)(2,1)S(1)} collective-permute-done((bf16[1088,256]{1,0:T(8,128)(2,1)}, bf16[1088,256]{1,0:T(8,128)(2,1)S(1)}, u32[]{:S(2)}, u32[]{:S(2)}) %collective-permute-start.5) | collective-permute-done | bytes 557088 | tf_op jit(solution)/shard_map/ppermute | solution.py:282
  151.2 4.5 %collective-permute-start.6 = (bf16[1088,128]{1,0:T(8,128)(2,1)S(1)}, bf16[1088,128]{1,0:T(8,128)(2,1)S(1)}, u32[]{:S(2)}, u32[]{:S(2)}) collective-permute-start(bf16[1088,128]{1,0:T(8,128)(2,1)S(1)} %fusion.own_ref), channel_id=1, source_target_pairs={{0,64},{64,128},{128,192},{192,0},{256,320},{320,384},{384,448},{4... | collective-permute-start | bytes 835592 | tf_op jit(solution)/shard_map/ppermute | solution.py:286
  160.5 7.3 %collective-permute-done.6.h1 = bf16[1088,128]{1,0:T(8,128)(2,1)S(1)} collective-permute-done((bf16[1088,128]{1,0:T(8,128)(2,1)S(1)}, bf16[1088,128]{1,0:T(8,128)(2,1)S(1)}, u32[]{:S(2)}, u32[]{:S(2)}) %collective-permute-start.6) | collective-permute-done | bytes 278560 | tf_op jit(solution)/shard_map/ppermute | solution.py:286
  168.8 4.7 %collective-permute-done.8.h3 = bf16[1088,128]{1,0:T(8,128)(2,1)S(1)} collective-permute-done((bf16[1088,128]{1,0:T(8,128)(2,1)S(1)}, bf16[1088,128]{1,0:T(8,128)(2,1)S(1)}, u32[]{:S(2)}, u32[]{:S(2)}) %collective-permute-start.8) | collective-permute-done | bytes 278560 | tf_op jit(solution)/shard_map/ppermute | solution.py:286
  174.1 6.1 %down.1 = bf16[64,120,128]{2,1,0:T(8,128)(2,1)} custom-call(s32[1]{0:T(128)} %bitcast.x_ref.block_ref, bf16[1088,128]{1,0:T(8,128)(2,1)} %copy-done.4, bf16[1088,128]{1,0:T(8,128)(2,1)} %copy-done.5, bf16[1088,128]{1,0:T(8,128)(2,1)} %copy-done.6, bf16[1088,128]{1,0:T(8,128)(2,1)} %copy-done.7, bf16[2688,128]{1,0:T(8,128)(2,1)} %copy-done.2, ...), custom_call_target="tpu_custom_call" | custom-call | tf_op jit(solution)/shard_map/down/pallas_call | solution.py:204
  180.3 10.7 %all-to-all-start.1 = ((bf16[64,120,128]{2,1,0:T(8,128)(2,1)}), bf16[64,120,128]{2,1,0:T(8,128)(2,1)S(1)}, u32[]{:S(2)}, u32[]{:S(2)}) async-start(bf16[64,120,128]{2,1,0:T(8,128)(2,1)} %down.1), calls=%async_computation.1 | async-start | bytes 3932160 | tf_op jit(solution)/shard_map/all_to_all | solution.py:288
  191.8 46.9 %all-to-all-done.1.chunks_ref = bf16[64,120,128]{2,1,0:T(8,128)(2,1)S(1)} async-done(((bf16[64,120,128]{2,1,0:T(8,128)(2,1)}), bf16[64,120,128]{2,1,0:T(8,128)(2,1)S(1)}, u32[]{:S(2)}, u32[]{:S(2)}) %all-to-all-start.1) | async-done | bytes 1966112 | tf_op jit(solution)/shard_map/all_to_all | solution.py:288
  239.9 4.4 %combine.1 = f32[128,896]{1,0:T(8,128)} custom-call(s32[128,8]{1,0:T(8,128)} %copy.8.ids_ref, f32[128,8]{1,0:T(8,128)} %copy.9.scale_ref, bf16[64,120,128]{2,1,0:T(8,128)(2,1)} %copy-done.1), custom_call_target="tpu_custom_call" | custom-call | tf_op jit(solution)/shard_map/combine/pallas_call | solution.py:255
  245.5 8.2 %collective-permute-start.10 = (bf16[128,448]{1,0:T(8,128)(2,1)S(1)}, bf16[128,448]{1,0:T(8,128)(2,1)S(1)}, u32[]{:S(2)}, u32[]{:S(2)}) collective-permute-start(bf16[128,448]{1,0:T(8,128)(2,1)S(1)} %get-tuple-element.12), channel_id=1, source_target_pairs={{0,64},{64,192},{128,320},{192,448},{256,0},{320,128},{384,256},{4... | collective-permute-start | bytes 344072 | tf_op jit(solution)/shard_map/ppermute | solution.py:297
  253.7 2.8 %collective-permute-start.9 = (bf16[128,448]{1,0:T(8,128)(2,1)S(1)}, bf16[128,448]{1,0:T(8,128)(2,1)S(1)}, u32[]{:S(2)}, u32[]{:S(2)}) collective-permute-start(bf16[128,448]{1,0:T(8,128)(2,1)S(1)} %get-tuple-element.11), channel_id=1, source_target_pairs={{0,0},{64,128},{128,256},{192,384},{256,64},{320,192},{384,320},{4... | collective-permute-start | bytes 344072 | tf_op jit(solution)/shard_map/ppermute | solution.py:296
  256.5 5.9 %collective-permute-done.10 = bf16[128,448]{1,0:T(8,128)(2,1)S(1)} collective-permute-done((bf16[128,448]{1,0:T(8,128)(2,1)S(1)}, bf16[128,448]{1,0:T(8,128)(2,1)S(1)}, u32[]{:S(2)}, u32[]{:S(2)}) %collective-permute-start.10) | collective-permute-done | bytes 114720 | tf_op jit(solution)/shard_map/ppermute | solution.py:297
  262.4 7.3 %collective-permute-done.9 = bf16[128,448]{1,0:T(8,128)(2,1)S(1)} collective-permute-done((bf16[128,448]{1,0:T(8,128)(2,1)S(1)}, bf16[128,448]{1,0:T(8,128)(2,1)S(1)}, u32[]{:S(2)}, u32[]{:S(2)}) %collective-permute-start.9) | collective-permute-done | bytes 114720 | tf_op jit(solution)/shard_map/ppermute | solution.py:296
  (35 shorter events, 25.1 us)
Async XLA Ops:
  5.0 96.9 %all-to-all-start = ((bf16[64,120,128]{2,1,0:T(8,128)(2,1)}), bf16[64,120,128]{2,1,0:T(8,128)(2,1)S(1)}, u32[]{:S(2)}, u32[]{:S(2)}) async-start(bf16[64,120,128]{2,1,0:T(8,128)(2,1)} %dispatch.1), calls=%async_computation | async-start | bytes 3932160 | tf_op jit(solution)/shard_map/all_to_all | solution.py:277
  81.5 20.4 %collective-permute-start = (bf16[2688,128]{1,0:T(8,128)(2,1)}, bf16[2688,128]{1,0:T(8,128)(2,1)S(1)}, u32[]{:S(2)}, u32[]{:S(2)}) collective-permute-start(bf16[2688,128]{1,0:T(8,128)(2,1)} %get-tuple-element.8), channel_id=1, source_target_pairs={{0,64},{64,128},{128,192},{192,0},{256,320},{320,384},{384,448},{4... | collective-permute-start | bytes 2064392 | tf_op jit(solution)/shard_map/ppermute | solution.py:275
  83.9 26.3 %collective-permute-start.2 = (bf16[2688,128]{1,0:T(8,128)(2,1)}, bf16[2688,128]{1,0:T(8,128)(2,1)S(1)}, u32[]{:S(2)}, u32[]{:S(2)}) collective-permute-start(bf16[2688,128]{1,0:T(8,128)(2,1)} %get-tuple-element.9), channel_id=1, source_target_pairs={{0,128},{64,192},{128,0},{192,64},{256,384},{320,448},{384,256},{4... | collective-permute-start | bytes 2064392 | tf_op jit(solution)/shard_map/ppermute | solution.py:275
  88.2 31.4 %collective-permute-start.4 = (bf16[2688,128]{1,0:T(8,128)(2,1)}, bf16[2688,128]{1,0:T(8,128)(2,1)}, u32[]{:S(2)}, u32[]{:S(2)}) collective-permute-start(bf16[2688,128]{1,0:T(8,128)(2,1)} %get-tuple-element.10), channel_id=1, source_target_pairs={{0,192},{64,0},{128,64},{192,128},{256,448},{320,256},{384,320},{4... | collective-permute-start | bytes 2064392 | tf_op jit(solution)/shard_map/ppermute | solution.py:275
  101.9 0.9 copy-start.2
  102.8 1.3 copy-start
  107.5 27.0 %collective-permute-start.1 = (bf16[1088,256]{1,0:T(8,128)(2,1)}, bf16[1088,256]{1,0:T(8,128)(2,1)S(1)}, u32[]{:S(2)}, u32[]{:S(2)}) collective-permute-start(bf16[1088,256]{1,0:T(8,128)(2,1)} %project.5), channel_id=1, source_target_pairs={{0,192},{64,0},{128,64},{192,128},{256,448},{320,256},{384,320},{4... | collective-permute-start | bytes 1671176 | tf_op jit(solution)/shard_map/ppermute | solution.py:282
  110.3 0.9 copy-start.3
  114.6 28.8 %collective-permute-start.3 = (bf16[1088,256]{1,0:T(8,128)(2,1)}, bf16[1088,256]{1,0:T(8,128)(2,1)S(1)}, u32[]{:S(2)}, u32[]{:S(2)}) collective-permute-start(bf16[1088,256]{1,0:T(8,128)(2,1)} %project.6), channel_id=1, source_target_pairs={{0,128},{64,192},{128,0},{192,64},{256,384},{320,448},{384,256},{4... | collective-permute-start | bytes 1671176 | tf_op jit(solution)/shard_map/ppermute | solution.py:282
  123.1 26.5 %collective-permute-start.5 = (bf16[1088,256]{1,0:T(8,128)(2,1)}, bf16[1088,256]{1,0:T(8,128)(2,1)S(1)}, u32[]{:S(2)}, u32[]{:S(2)}) collective-permute-start(bf16[1088,256]{1,0:T(8,128)(2,1)} %project.7), channel_id=1, source_target_pairs={{0,64},{64,128},{128,192},{192,0},{256,320},{320,384},{384,448},{4... | collective-permute-start | bytes 1671176 | tf_op jit(solution)/shard_map/ppermute | solution.py:282
  151.2 22.2 %copy-start.4 = (bf16[1088,128]{1,0:T(8,128)(2,1)}, bf16[1088,128]{1,0:T(8,128)(2,1)S(1)}, u32[]{:S(2)}) copy-start(bf16[1088,128]{1,0:T(8,128)(2,1)S(1)} %fusion.own_ref) | copy-start | bytes 835588
  151.2 16.6 %collective-permute-start.6 = (bf16[1088,128]{1,0:T(8,128)(2,1)S(1)}, bf16[1088,128]{1,0:T(8,128)(2,1)S(1)}, u32[]{:S(2)}, u32[]{:S(2)}) collective-permute-start(bf16[1088,128]{1,0:T(8,128)(2,1)S(1)} %fusion.own_ref), channel_id=1, source_target_pairs={{0,64},{64,128},{128,192},{192,0},{256,320},{320,384},{384,448},{4... | collective-permute-start | bytes 835592 | tf_op jit(solution)/shard_map/ppermute | solution.py:286
  155.8 13.0 %collective-permute-start.7 = (bf16[1088,128]{1,0:T(8,128)(2,1)S(1)}, bf16[1088,128]{1,0:T(8,128)(2,1)S(1)}, u32[]{:S(2)}, u32[]{:S(2)}) collective-permute-start(bf16[1088,128]{1,0:T(8,128)(2,1)S(1)} %fusion.own_ref), channel_id=1, source_target_pairs={{0,128},{64,192},{128,0},{192,64},{256,384},{320,448},{384,256},{4... | collective-permute-start | bytes 835592 | tf_op jit(solution)/shard_map/ppermute | solution.py:286
  157.9 15.6 %collective-permute-start.8 = (bf16[1088,128]{1,0:T(8,128)(2,1)S(1)}, bf16[1088,128]{1,0:T(8,128)(2,1)S(1)}, u32[]{:S(2)}, u32[]{:S(2)}) collective-permute-start(bf16[1088,128]{1,0:T(8,128)(2,1)S(1)} %fusion.own_ref), channel_id=1, source_target_pairs={{0,192},{64,0},{128,64},{192,128},{256,448},{320,256},{384,320},{4... | collective-permute-start | bytes 835592 | tf_op jit(solution)/shard_map/ppermute | solution.py:286
  167.8 5.6 %copy-start.5 = (bf16[1088,128]{1,0:T(8,128)(2,1)}, bf16[1088,128]{1,0:T(8,128)(2,1)S(1)}, u32[]{:S(2)}) copy-start(bf16[1088,128]{1,0:T(8,128)(2,1)S(1)} %collective-permute-done.6.h1) | copy-start | bytes 835588
  168.8 4.7 %copy-start.6 = (bf16[1088,128]{1,0:T(8,128)(2,1)}, bf16[1088,128]{1,0:T(8,128)(2,1)S(1)}, u32[]{:S(2)}) copy-start(bf16[1088,128]{1,0:T(8,128)(2,1)S(1)} %collective-permute-done.7.h2) | copy-start | bytes 835588
  173.4 0.7 copy-start.7
  180.3 10.8 %copy-start.8 = (f32[128,8]{0,1:T(8,128)S(1)}, f32[128,8]{0,1:T(8,128)}, u32[]{:S(2)}) copy-start(f32[128,8]{0,1:T(8,128)} %param.8) | copy-start | bytes 12292
  180.3 58.3 %all-to-all-start.1 = ((bf16[64,120,128]{2,1,0:T(8,128)(2,1)}), bf16[64,120,128]{2,1,0:T(8,128)(2,1)S(1)}, u32[]{:S(2)}, u32[]{:S(2)}) async-start(bf16[64,120,128]{2,1,0:T(8,128)(2,1)} %down.1), calls=%async_computation.1 | async-start | bytes 3932160 | tf_op jit(solution)/shard_map/all_to_all | solution.py:288
  238.6 1.3 copy-start.1
  245.5 16.9 %collective-permute-start.10 = (bf16[128,448]{1,0:T(8,128)(2,1)S(1)}, bf16[128,448]{1,0:T(8,128)(2,1)S(1)}, u32[]{:S(2)}, u32[]{:S(2)}) collective-permute-start(bf16[128,448]{1,0:T(8,128)(2,1)S(1)} %get-tuple-element.12), channel_id=1, source_target_pairs={{0,64},{64,192},{128,320},{192,448},{256,0},{320,128},{384,256},{4... | collective-permute-start | bytes 344072 | tf_op jit(solution)/shard_map/ppermute | solution.py:297
  253.7 16.0 %collective-permute-start.9 = (bf16[128,448]{1,0:T(8,128)(2,1)S(1)}, bf16[128,448]{1,0:T(8,128)(2,1)S(1)}, u32[]{:S(2)}, u32[]{:S(2)}) collective-permute-start(bf16[128,448]{1,0:T(8,128)(2,1)S(1)} %get-tuple-element.11), channel_id=1, source_target_pairs={{0,0},{64,128},{128,256},{192,384},{256,64},{320,192},{384,320},{4... | collective-permute-start | bytes 344072 | tf_op jit(solution)/shard_map/ppermute | solution.py:296

commit v2 on v0

v2 whole, which is shorter than its diff:
```python
import jax
import jax.numpy as jnp
from jax import lax
from jax.experimental import pallas as pl
from jax.experimental.pallas import tpu as pltpu
from jax.sharding import PartitionSpec as P

BF = jnp.bfloat16
F32 = jnp.float32
LANES = 128
X = 4
VMEM = 24 * 1024 * 1024


def call(kernel, name, out_shape, in_specs, out_specs=None):
    if out_specs is None:
        out_specs = jax.tree.map(lambda _: in_vmem(), out_shape)
    return pl.pallas_call(
        kernel,
        out_shape=out_shape,
        in_specs=in_specs,
        out_specs=out_specs,
        compiler_params=pltpu.CompilerParams(vmem_limit_bytes=VMEM),
        name=name,
    )


def in_vmem():
    return pl.BlockSpec(memory_space=pltpu.VMEM)


def in_smem():
    return pl.BlockSpec(memory_space=pltpu.SMEM)


def slots(ids, experts):
    topk, tokens = ids.shape
    lane = lax.broadcasted_iota(jnp.int32, (experts, tokens), 0)
    named = jnp.zeros((experts, tokens), F32)
    for k in range(topk):
        named += (ids[k : k + 1, :] == lane).astype(F32)
    row = lax.broadcasted_iota(jnp.int32, (tokens, tokens), 0)
    col = lax.broadcasted_iota(jnp.int32, (tokens, tokens), 1)
    place = jnp.dot(named.astype(BF), (row < col).astype(BF), preferred_element_type=F32)
    return jnp.where(named > 0.5, place, -1.0)


def spread(tiles, rows):
    count = tiles[0].shape[0]
    sub = lax.broadcasted_iota(jnp.int32, (count, rows, LANES), 1)
    out = jnp.zeros((count, rows, LANES), F32)
    for c, tile in enumerate(tiles):
        out += jnp.where(sub == c, tile[:, None, :], 0.0)
    return out


def dispatch_kernel(x_ref, ids_ref, tok_ref, out_ref):
    experts = out_ref.shape[0]
    tokens, width = tok_ref.shape
    tiles = width // X // LANES
    quarter = width // X
    tok = tok_ref[:, pl.ds(pl.multiple_of(x_ref[0] * quarter, LANES), quarter)]
    place = slots(ids_ref[...], experts)
    slot = lax.broadcasted_iota(jnp.int32, (experts, 16, tokens), 1).astype(F32)
    pick = jnp.where(place[:, None, :] == slot, 1.0, 0.0).reshape(experts * 16, tokens).astype(BF)
    rows = jnp.dot(pick, tok, preferred_element_type=F32).astype(BF)
    for c in range(tiles):
        out_ref[:, c * 16 : (c + 1) * 16, :] = rows[:, c * LANES : (c + 1) * LANES].reshape(experts, 16, LANES)
    last = jnp.dot((place == 16.0).astype(BF), tok, preferred_element_type=F32)
    tail = spread([last[:, c * LANES : (c + 1) * LANES] for c in range(tiles)], 8)
    out_ref[:, tiles * 16 : tiles * 16 + 8, :] = tail.astype(BF)


def dispatch(x, ids, tokens, experts):
    depth = tokens.shape[1] // X // LANES * 16 + 8
    shape = jax.ShapeDtypeStruct((experts, depth, LANES), BF)
    return call(dispatch_kernel, "dispatch", shape, [in_smem(), in_vmem(), in_vmem()])(x, ids, tokens)


def pack_kernel(x_ref, gate_ref, up_ref, down_ref, *outs):
    quarter = gate_ref.shape[0] // X
    depth = down_ref.shape[0]

    def put_down(out, base, q):
        for z in range(2):
            p = z * X + q
            pair, odd = p // 2, lax.rem(p, 2)
            first = pair * (quarter // LANES) + 4 * odd
            half = pair * (quarter // LANES) + 3
            for c in range(4):
                tile = half if c == 3 else first + c
                cols = pl.ds(pl.multiple_of(tile * LANES, LANES), LANES)
                out[pl.ds(base + (z * 4 + c) * depth, depth), :] = down_ref[:, cols]

    for d, out in enumerate(outs[1:], 1):
        q = lax.rem(x_ref[0] + d, X)
        part = pl.ds(pl.multiple_of(q * quarter, quarter), quarter)
        out[pl.ds(0, quarter), :] = gate_ref[part, :]
        out[pl.ds(quarter, quarter), :] = up_ref[part, :]
        put_down(out, 2 * quarter, q)
    put_down(outs[0], 0, x_ref[0])


def pack(x, w_gate, w_up, w_down):
    depth = w_down.shape[0]
    rows = 2 * (w_gate.shape[0] // X) + 8 * depth
    shapes = [jax.ShapeDtypeStruct((r, LANES), BF) for r in [8 * depth] + [rows] * (X - 1)]
    return call(pack_kernel, "pack", shapes, [in_smem()] + [in_vmem()] * 3)(x, w_gate, w_up, w_down)


def swap_kernel(z_ref, own_ref, p1, p2, p3, out_ref):
    rows = own_ref.shape[0] // 2
    start = (1 - z_ref[0]) * rows
    for d, ref in enumerate((own_ref, p1, p2, p3)):
        base = ref.shape[0] - 2 * rows
        out_ref[pl.ds(d * rows, rows), :] = ref[pl.ds(pl.multiple_of(base + start, LANES), rows), :]


def swap(z, own, packs):
    shape = jax.ShapeDtypeStruct((X * own.shape[0] // 2, LANES), BF)
    return call(swap_kernel, "swap", shape, [in_smem()] + [in_vmem()] * 4)(z, own, *packs)


def stacked(chunks_ref):
    sources, depth, _ = chunks_ref.shape
    tiles = depth // 16
    main = [chunks_ref[:, c * 16 : (c + 1) * 16, :].reshape(sources * 16, LANES) for c in range(tiles)]
    tail = chunks_ref[:, tiles * 16 : tiles * 16 + 8, :].reshape(sources * 8, LANES)
    row = lax.broadcasted_iota(jnp.int32, (sources, sources * 8), 0)
    col = lax.broadcasted_iota(jnp.int32, (sources, sources * 8), 1)
    last = [
        jnp.dot((col == row * 8 + c).astype(BF), tail, preferred_element_type=F32).astype(BF) for c in range(tiles)
    ]
    return jnp.concatenate(main, axis=1), jnp.concatenate(last, axis=1)


def project_into(out_ref, main, last, gate, up):
    weight = jnp.concatenate([gate, up], axis=1)
    count = main.shape[0]
    out_ref[pl.ds(0, count), :] = jnp.dot(main, weight, preferred_element_type=F32).astype(out_ref.dtype)
    out_ref[pl.ds(count, last.shape[0]), :] = jnp.dot(last, weight, preferred_element_type=F32).astype(out_ref.dtype)


def project_sent_kernel(chunks_ref, *refs):
    main, last = stacked(chunks_ref)
    quarter = main.shape[1]
    for pack_ref, out_ref in zip(refs[: X - 1], refs[X - 1 :]):
        project_into(out_ref, main, last, pack_ref[pl.ds(0, quarter), :], pack_ref[pl.ds(quarter, quarter), :])


def project_sent(chunks, packs):
    shapes = [jax.ShapeDtypeStruct((chunks.shape[0] * 17, 2 * LANES), BF)] * len(packs)
    return call(project_sent_kernel, "project_sent", shapes, [in_vmem()] * (1 + len(packs)))(chunks, *packs)


def project_own_kernel(x_ref, chunks_ref, gate_ref, up_ref, out_ref):
    main, last = stacked(chunks_ref)
    quarter = main.shape[1]
    part = pl.ds(pl.multiple_of(x_ref[0] * quarter, quarter), quarter)
    project_into(out_ref, main, last, gate_ref[part, :], up_ref[part, :])


def project_own(x, chunks, gate, up):
    shape = jax.ShapeDtypeStruct((chunks.shape[0] * 17, 2 * LANES), F32)
    return call(project_own_kernel, "project_own", shape, [in_smem()] + [in_vmem()] * 3)(x, chunks, gate, up)


def down_kernel(x_ref, z_ref, *refs):
    hiddens, (own_ref, p1, p2, p3, other_ref, out_ref) = refs[: 2 * X], refs[2 * X :]
    experts = out_ref.shape[0]
    rows = own_ref.shape[0] // 2
    depth = rows // 4
    hidden = jnp.concatenate([ref[...] for ref in hiddens], axis=1)
    blocks = []
    for ref in (own_ref, p1, p2, p3):
        base = ref.shape[0] - 2 * rows + z_ref[0] * rows
        tiles = [ref[pl.ds(pl.multiple_of(base + c * depth, LANES), depth), :] for c in range(4)]
        blocks.append(jnp.concatenate(tiles, axis=1))
    for d in range(X):
        tiles = [other_ref[pl.ds(d * rows + c * depth, depth), :] for c in range(4)]
        blocks.append(jnp.concatenate(tiles, axis=1))
    weight = jnp.concatenate(blocks, axis=0)
    count = experts * 16
    main = jnp.dot(hidden[:count], weight, preferred_element_type=F32)
    last = jnp.dot(hidden[count:], weight, preferred_element_type=F32)
    for c in range(3):
        out_ref[:, c * 16 : (c + 1) * 16, :] = (
            main[:, c * LANES : (c + 1) * LANES].astype(BF).reshape(experts, 16, LANES)
        )
    half = main[:, 3 * LANES :]
    turned = pltpu.roll(half, LANES // 2, 1)
    odd = lax.rem(x_ref[0], 2) == 1
    low = jnp.where(odd, turned, half).reshape(experts, 16, LANES)[:, :8]
    high = jnp.where(odd, half, turned).reshape(experts, 16, LANES)[:, 8:]
    lane = lax.broadcasted_iota(jnp.int32, low.shape, 2)
    halves = jnp.where(lane < LANES // 2, low, high)
    tail = spread([last[:, c * LANES : (c + 1) * LANES] for c in range(4)], 8)
    out_ref[:, 48:64, :] = jnp.concatenate([halves, tail], axis=1).astype(BF)


def down(x, z, hiddens, own, packs, other, experts):
    shape = jax.ShapeDtypeStruct((experts, 64, LANES), BF)
    specs = [in_smem()] * 2 + [in_vmem()] * (2 * X + X + 1)
    return call(down_kernel, "down", shape, specs)(x, z, *hiddens, own, *packs, other)


def combine_kernel(x_ref, ids_ref, scale_ref, chunks_ref, out_ref):
    experts = chunks_ref.shape[0]
    ids, scale = ids_ref[...], scale_ref[...]
    topk, tokens = ids.shape
    place = slots(ids, experts)
    lane = lax.broadcasted_iota(jnp.int32, (experts, tokens), 0)
    weight = jnp.zeros((experts, tokens), F32)
    for k in range(topk):
        weight += jnp.where(ids[k : k + 1, :] == lane, scale[k : k + 1, :], 0.0)
    upper = weight.astype(BF).astype(F32)
    lower = weight - upper
    sub = lax.broadcasted_iota(jnp.int32, (experts, 16, tokens), 1)
    slot = sub.astype(F32)
    place = place[:, None, :]
    contract = (((0,), (0,)), ((), ()))
    main = jnp.concatenate(
        [chunks_ref[:, c * 16 : (c + 1) * 16, :].reshape(experts * 16, LANES) for c in range(3)], axis=1
    )
    rest = chunks_ref[:, 48:64, :].reshape(experts * 16, LANES)
    whole = jnp.zeros((tokens, 3 * LANES), F32)
    low = jnp.zeros((tokens, LANES), F32)
    high = jnp.zeros((tokens, LANES), F32)
    ends = [jnp.zeros((tokens, LANES), F32) for _ in range(4)]

    def times(hit, part, rows):
        coef = jnp.where(hit, part[:, None, :], 0.0).reshape(experts * 16, tokens).astype(BF)
        return lax.dot_general(coef, rows, contract, preferred_element_type=F32)

    for part in (upper, lower):
        whole += times(place == slot, part, main)
        low += times((place == slot) & (sub < 8), part, rest)
        high += times((place == slot + 8.0) & (sub < 8), part, rest)
        for c in range(4):
            ends[c] += times((place == 16.0) & (sub == 8 + c), part, rest)
    odd = lax.rem(x_ref[0], 2) == 1
    even_half = low + pltpu.roll(high, LANES // 2, 1) + ends[3]
    odd_half = pltpu.roll(low, LANES // 2, 1) + high + ends[3]
    half = jnp.where(odd, odd_half, even_half)
    total = jnp.concatenate([whole + jnp.concatenate(ends[:3], axis=1), half], axis=1)
    total = jnp.where(odd, pltpu.roll(total, LANES // 2, 1), total)
    out_ref[...] = total[:, : out_ref.shape[1]].astype(BF)


def combine(x, ids, scale, chunks, columns):
    shape = jax.ShapeDtypeStruct((ids.shape[1], columns), BF)
    return call(combine_kernel, "combine", shape, [in_smem()] + [in_vmem()] * 3)(x, ids, scale, chunks)


def shift(value, d):
    pairs = [(z * X + x, z * X + (x + d) % X) for z in range(2) for x in range(X)]
    return lax.ppermute(value, "pipe", pairs)


def cross(value):
    return lax.ppermute(value, "pipe", [(p, (p + X) % (2 * X)) for p in range(2 * X)])


def body(tokens, expert_ids, gate_scale, w_gate, w_up, w_down):
    groups = lax.axis_size("expert")
    pipe = lax.axis_index("pipe")
    x = (pipe & (X - 1)).reshape(1)
    z = (pipe >> 2).reshape(1)
    ids, scale = expert_ids.T, gate_scale.T
    w_gate, w_up, w_down = w_gate[0], w_up[0], w_down[0]
    buffer = dispatch(x, ids, tokens, groups)
    chunks = lax.all_to_all(buffer, "expert", split_axis=0, concat_axis=0, tiled=True)
    own_down, *sent = pack(x, w_gate, w_up, w_down)
    packs = [shift(sent[d - 1], d) for d in range(1, X)]
    other_down = cross(swap(z, own_down, packs))
    parts = project_sent(chunks, packs)
    arrived = [shift(parts[d - 1], -d) for d in (2, 1, 3)]
    summed = project_own(x, chunks, w_gate, w_up)
    for part in arrived:
        summed = summed + part.astype(F32)
    hidden = (jax.nn.silu(summed[:, :LANES]) * summed[:, LANES:]).astype(BF)
    swapped = cross(hidden)
    hiddens = [hidden] + [shift(hidden, d) for d in range(1, X)]
    hiddens += [swapped] + [shift(swapped, d) for d in range(1, X)]
    output = down(x, z, hiddens, own_down, packs, other_down, groups)
    returned = lax.all_to_all(output, "expert", split_axis=0, concat_axis=0, tiled=True)
    return combine(x, ids, scale, returned, tokens.shape[1] // (2 * X))


def solution(mesh):
    placed = (
        P("expert", None),
        P("expert", None),
        P("expert", None),
        P("expert", None, "pipe"),
        P("expert", None, "pipe"),
        P("expert", "pipe", None),
    )
    return jax.shard_map(
        body, mesh=mesh, in_specs=placed, out_specs=P("expert", "pipe"), check_vma=False
    )
```

time: 840 us -> 193 us (0.23); the launches traced: 826 us -> 192 us
  waiting for transfers between devices: 390 us -> 66.3 us
  blocking collectives: 257 us -> 35.5 us
  local copies, waits for them, and re-layouts: 107 us -> 11 us
  starting transfers between devices: 10.6 us -> 68.9 us
  other arithmetic: 30.3 us -> 1.77 us
  matrix products: 17.9 us -> 0 us
  between operations: 13.9 us -> 0.31 us
  Pallas kernels: 0 us -> 8.56 us
    all_to_all x1, waiting for transfers between devices: 279 us -> 5.19 us  [body(): lax.all_to_all(buffer, 'expert', split_axis=0, concat_axis=0, tiled=True)]
    all_to_all x1, blocking collectives: 257 us -> 35.5 us  [body(): lax.all_to_all(output, 'expert', split_axis=0, concat_axis=0, tiled=True)]
    unnamed x2 -> x0, waiting for transfers between devices: 110 us -> none
    ppermute x0 -> x14, waiting for transfers between devices: none -> 61.2 us  [the longest x12 50.3 us: shift(): return lax.ppermute(value, 'pipe', pairs)]
    ppermute x0 -> x14, starting transfers between devices: none -> 54.1 us  [the longest x12 38 us: shift(): return lax.ppermute(value, 'pipe', pairs)]
    scatter x1 -> x0, local copies, waits for them, and re-layouts: 44 us -> none  [body(): buffer = buffer.at[slot_index].set(tokens[source_tok])]
    reshape x4 -> x0, local copies, waits for them, and re-layouts: 41.2 us -> none  [the longest x1 10.5 us: body(): stacked = rows.reshape(senders * slots, full_width)]
    another operation x3 -> x0, other arithmetic: 18.2 us -> none
  transfers between devices with their start and end apart: 2 -> 15, of which waited for: 2 -> 9; matrix products, arithmetic and copies ran while one was open for 0% -> 1% of each run, Pallas kernels for 0% -> 1%
where the time goes in v2:
time: 193 us; the launch traced here: 192 us
  starting transfers between devices  68.9 us (36%)
  waiting for transfers between devices  66.3 us (34%)
  blocking collectives  35.5 us (18%)
  local copies, waits for them, and re-layouts  11 us (6%)
  Pallas kernels  8.56 us (4%)
    ppermute x12, waiting for transfers between devices, shift(): return lax.ppermute(value, 'pipe', pairs)  50.3 us
    ppermute x12, starting transfers between devices, shift(): return lax.ppermute(value, 'pipe', pairs)  38 us
    all_to_all x1, blocking collectives, body(): lax.all_to_all(output, 'expert', split_axis=0, concat_axis=0, tiled=True)  35.5 us
    ppermute x2, starting transfers between devices, cross(): lax.ppermute(value, 'pipe', [(p, (p + X) % (2 * X)) for p in range(2 * X)])  16.1 us
    all_to_all x1, starting transfers between devices, body(): lax.all_to_all(buffer, 'expert', split_axis=0, concat_axis=0, tiled=True)  14.7 us
    ppermute x2, waiting for transfers between devices, cross(): lax.ppermute(value, 'pipe', [(p, (p + X) % (2 * X)) for p in range(2 * X)])  10.9 us
    unnamed x32, local copies, waits for them, and re-layouts  10.2 us
    all_to_all x1, waiting for transfers between devices, body(): lax.all_to_all(buffer, 'expert', split_axis=0, concat_axis=0, tiled=True)  5.19 us
  transfers between devices with their start and end apart: 15, of which 9 were waited for; matrix products, arithmetic and copies ran while one was open for 1% of the time, Pallas kernels for 1%

profile of v2, /device:TPU:1, one launch (start us, length us, event | category | flops | bytes accessed | tf_op | source)
XLA Modules:
  0.0 192.4 jit_solution(12156666758437569983)
XLA Ops:
  4.2 14.7 %all-to-all-start = ((bf16[64,120,128]{2,1,0:T(8,128)(2,1)}), bf16[64,120,128]{2,1,0:T(8,128)(2,1)S(1)}, u32[]{:S(2)}, u32[]{:S(2)}) async-start(bf16[64,120,128]{2,1,0:T(8,128)(2,1)} %copy-done), calls=%async_computation | async-start | bytes 3932160 | tf_op jit(solution)/shard_map/all_to_all | solution.py:272
  22.3 3.1 %collective-permute-start = (bf16[2816,128]{1,0:T(8,128)(2,1)S(1)}, bf16[2816,128]{1,0:T(8,128)(2,1)S(1)}, u32[]{:S(2)}, u32[]{:S(2)}) collective-permute-start(bf16[2816,128]{1,0:T(8,128)(2,1)S(1)} %get-tuple-element.12), channel_id=1, source_target_pairs={{0,64},{64,128},{128,192},{192,0},{256,320},{320,384},{384,448},{4... | collective-permute-start | bytes 2162696 | tf_op jit(solution)/shard_map/ppermute | solution.py:257
  25.4 4.4 %collective-permute-start.1 = (bf16[2816,128]{1,0:T(8,128)(2,1)S(1)}, bf16[2816,128]{1,0:T(8,128)(2,1)S(1)}, u32[]{:S(2)}, u32[]{:S(2)}) collective-permute-start(bf16[2816,128]{1,0:T(8,128)(2,1)S(1)} %get-tuple-element.13), channel_id=1, source_target_pairs={{0,128},{64,192},{128,0},{192,64},{256,384},{320,448},{384,256},{4... | collective-permute-start | bytes 2162696 | tf_op jit(solution)/shard_map/ppermute | solution.py:257
  29.7 3.1 %collective-permute-start.2 = (bf16[2816,128]{1,0:T(8,128)(2,1)S(1)}, bf16[2816,128]{1,0:T(8,128)(2,1)S(1)}, u32[]{:S(2)}, u32[]{:S(2)}) collective-permute-start(bf16[2816,128]{1,0:T(8,128)(2,1)S(1)} %get-tuple-element.14), channel_id=1, source_target_pairs={{0,192},{64,0},{128,64},{192,128},{256,448},{320,256},{384,320},{4... | collective-permute-start | bytes 2162696 | tf_op jit(solution)/shard_map/ppermute | solution.py:257
  32.8 9.8 %collective-permute-done.refs_0_.p1.refs_9_ = bf16[2816,128]{1,0:T(8,128)(2,1)S(1)} collective-permute-done((bf16[2816,128]{1,0:T(8,128)(2,1)S(1)}, bf16[2816,128]{1,0:T(8,128)(2,1)S(1)}, u32[]{:S(2)}, u32[]{:S(2)}) %collective-permute-start) | collective-permute-done | bytes 720928 | tf_op jit(solution)/shard_map/ppermute | solution.py:257
  42.6 16.4 %collective-permute-done.1.refs_1_.p2.refs_10_ = bf16[2816,128]{1,0:T(8,128)(2,1)S(1)} collective-permute-done((bf16[2816,128]{1,0:T(8,128)(2,1)S(1)}, bf16[2816,128]{1,0:T(8,128)(2,1)S(1)}, u32[]{:S(2)}, u32[]{:S(2)}) %collective-permute-start.1) | collective-permute-done | bytes 720928 | tf_op jit(solution)/shard_map/ppermute | solution.py:257
  61.2 5.2 %all-to-all-done.chunks_ref = bf16[64,120,128]{2,1,0:T(8,128)(2,1)S(1)} async-done(((bf16[64,120,128]{2,1,0:T(8,128)(2,1)}), bf16[64,120,128]{2,1,0:T(8,128)(2,1)S(1)}, u32[]{:S(2)}, u32[]{:S(2)}) %all-to-all-start) | async-done | bytes 1966112 | tf_op jit(solution)/shard_map/all_to_all | solution.py:272
  67.5 3.1 %project_sent.1 = (bf16[1088,256]{1,0:T(8,128)(2,1)}, bf16[1088,256]{1,0:T(8,128)(2,1)}, bf16[1088,256]{1,0:T(8,128)(2,1)}) custom-call(bf16[64,120,128]{2,1,0:T(8,128)(2,1)S(1)} %all-to-all-done.chunks_ref, bf16[2816,128]{1,0:T(8,128)(2,1)S(1)} %collective-permute-done.refs_0_.p1.refs_9_, bf16[2816,128]{1,0:T(8,128)(2,1)S(1)} %collective-permute-done.1.refs_1_.p2.refs_10_, ...), custom_call_target="tpu_custom_call" | custom-call | tf_op jit(solution)/shard_map/project_sent/pallas_call | solution.py:153
  70.6 4.6 %collective-permute-start.3 = (bf16[1088,256]{1,0:T(8,128)(2,1)}, bf16[1088,256]{1,0:T(8,128)(2,1)}, u32[]{:S(2)}, u32[]{:S(2)}) collective-permute-start(bf16[1088,256]{1,0:T(8,128)(2,1)} %get-tuple-element.15), channel_id=1, source_target_pairs={{0,128},{64,192},{128,0},{192,64},{256,384},{320,448},{384,256},{4... | collective-permute-start | bytes 1671176 | tf_op jit(solution)/shard_map/ppermute | solution.py:257
  75.2 2.8 %collective-permute-start.4 = (bf16[1088,256]{1,0:T(8,128)(2,1)}, bf16[1088,256]{1,0:T(8,128)(2,1)}, u32[]{:S(2)}, u32[]{:S(2)}) collective-permute-start(bf16[1088,256]{1,0:T(8,128)(2,1)} %get-tuple-element.16), channel_id=1, source_target_pairs={{0,192},{64,0},{128,64},{192,128},{256,448},{320,256},{384,320},{4... | collective-permute-start | bytes 1671176 | tf_op jit(solution)/shard_map/ppermute | solution.py:257
  78.0 2.5 %collective-permute-start.5 = (bf16[1088,256]{1,0:T(8,128)(2,1)}, bf16[1088,256]{1,0:T(8,128)(2,1)}, u32[]{:S(2)}, u32[]{:S(2)}) collective-permute-start(bf16[1088,256]{1,0:T(8,128)(2,1)} %get-tuple-element.17), channel_id=1, source_target_pairs={{0,64},{64,128},{128,192},{192,0},{256,320},{320,384},{384,448},{4... | collective-permute-start | bytes 1671176 | tf_op jit(solution)/shard_map/ppermute | solution.py:257
  82.6 8.1 %collective-permute-start.13 = (bf16[2048,128]{1,0:T(8,128)(2,1)S(1)}, bf16[2048,128]{1,0:T(8,128)(2,1)S(1)}, u32[]{:S(2)}, u32[]{:S(2)}) collective-permute-start(bf16[2048,128]{1,0:T(8,128)(2,1)S(1)} %swap.1), channel_id=1, source_target_pairs={{0,256},{64,320},{128,384},{192,448},{256,0},{320,64},{384,128},{4... | collective-permute-start | bytes 1572872 | tf_op jit(solution)/shard_map/ppermute | solution.py:261
  91.7 9.3 %collective-permute-done.4 = bf16[1088,256]{1,0:T(8,128)(2,1)} collective-permute-done((bf16[1088,256]{1,0:T(8,128)(2,1)}, bf16[1088,256]{1,0:T(8,128)(2,1)}, u32[]{:S(2)}, u32[]{:S(2)}) %collective-permute-start.4) | collective-permute-done | bytes 557088 | tf_op jit(solution)/shard_map/ppermute | solution.py:257
  102.8 8.1 %collective-permute-start.9 = (bf16[1088,128]{1,0:T(8,128)(2,1)S(1)}, bf16[1088,128]{1,0:T(8,128)(2,1)S(1)}, u32[]{:S(2)}, u32[]{:S(2)}) collective-permute-start(bf16[1088,128]{1,0:T(8,128)(2,1)S(1)} %fusion.refs_0_), channel_id=1, source_target_pairs={{0,256},{64,320},{128,384},{192,448},{256,0},{320,64},{384,128},{4... | collective-permute-start | bytes 835592 | tf_op jit(solution)/shard_map/ppermute | solution.py:261
  110.8 4.3 %collective-permute-start.8 = (bf16[1088,128]{1,0:T(8,128)(2,1)S(1)}, bf16[1088,128]{1,0:T(8,128)(2,1)S(1)}, u32[]{:S(2)}, u32[]{:S(2)}) collective-permute-start(bf16[1088,128]{1,0:T(8,128)(2,1)S(1)} %fusion.refs_0_), channel_id=1, source_target_pairs={{0,192},{64,0},{128,64},{192,128},{256,448},{320,256},{384,320},{4... | collective-permute-start | bytes 835592 | tf_op jit(solution)/shard_map/ppermute | solution.py:257
  115.1 2.5 %collective-permute-start.7 = (bf16[1088,128]{1,0:T(8,128)(2,1)S(1)}, bf16[1088,128]{1,0:T(8,128)(2,1)S(1)}, u32[]{:S(2)}, u32[]{:S(2)}) collective-permute-start(bf16[1088,128]{1,0:T(8,128)(2,1)S(1)} %fusion.refs_0_), channel_id=1, source_target_pairs={{0,128},{64,192},{128,0},{192,64},{256,384},{320,448},{384,256},{4... | collective-permute-start | bytes 835592 | tf_op jit(solution)/shard_map/ppermute | solution.py:257
  117.6 2.4 %collective-permute-start.6 = (bf16[1088,128]{1,0:T(8,128)(2,1)S(1)}, bf16[1088,128]{1,0:T(8,128)(2,1)S(1)}, u32[]{:S(2)}, u32[]{:S(2)}) collective-permute-start(bf16[1088,128]{1,0:T(8,128)(2,1)S(1)} %fusion.refs_0_), channel_id=1, source_target_pairs={{0,64},{64,128},{128,192},{192,0},{256,320},{320,384},{384,448},{4... | collective-permute-start | bytes 835592 | tf_op jit(solution)/shard_map/ppermute | solution.py:257
  120.0 10.9 %collective-permute-done.9.refs_4_ = bf16[1088,128]{1,0:T(8,128)(2,1)S(1)} collective-permute-done((bf16[1088,128]{1,0:T(8,128)(2,1)S(1)}, bf16[1088,128]{1,0:T(8,128)(2,1)S(1)}, u32[]{:S(2)}, u32[]{:S(2)}) %collective-permute-start.9) | collective-permute-done | bytes 278560 | tf_op jit(solution)/shard_map/ppermute | solution.py:261
  130.9 4.0 %collective-permute-start.12 = (bf16[1088,128]{1,0:T(8,128)(2,1)S(1)}, bf16[1088,128]{1,0:T(8,128)(2,1)S(1)}, u32[]{:S(2)}, u32[]{:S(2)}) collective-permute-start(bf16[1088,128]{1,0:T(8,128)(2,1)S(1)} %collective-permute-done.9.refs_4_), channel_id=1, source_target_pairs={{0,192},{64,0},{128,64},{192,128},{256,448},{320,256},{384,320},{4... | collective-permute-start | bytes 835592 | tf_op jit(solution)/shard_map/ppermute | solution.py:257
  134.9 1.9 %collective-permute-start.11 = (bf16[1088,128]{1,0:T(8,128)(2,1)S(1)}, bf16[1088,128]{1,0:T(8,128)(2,1)S(1)}, u32[]{:S(2)}, u32[]{:S(2)}) collective-permute-start(bf16[1088,128]{1,0:T(8,128)(2,1)S(1)} %collective-permute-done.9.refs_4_), channel_id=1, source_target_pairs={{0,128},{64,192},{128,0},{192,64},{256,384},{320,448},{384,256},{4... | collective-permute-start | bytes 835592 | tf_op jit(solution)/shard_map/ppermute | solution.py:257
  136.8 2.5 %collective-permute-start.10 = (bf16[1088,128]{1,0:T(8,128)(2,1)S(1)}, bf16[1088,128]{1,0:T(8,128)(2,1)S(1)}, u32[]{:S(2)}, u32[]{:S(2)}) collective-permute-start(bf16[1088,128]{1,0:T(8,128)(2,1)S(1)} %collective-permute-done.9.refs_4_), channel_id=1, source_target_pairs={{0,64},{64,128},{128,192},{192,0},{256,320},{320,384},{384,448},{4... | collective-permute-start | bytes 835592 | tf_op jit(solution)/shard_map/ppermute | solution.py:257
  140.8 5.0 %collective-permute-done.11.refs_6_ = bf16[1088,128]{1,0:T(8,128)(2,1)S(1)} collective-permute-done((bf16[1088,128]{1,0:T(8,128)(2,1)S(1)}, bf16[1088,128]{1,0:T(8,128)(2,1)S(1)}, u32[]{:S(2)}, u32[]{:S(2)}) %collective-permute-start.11) | collective-permute-done | bytes 278560 | tf_op jit(solution)/shard_map/ppermute | solution.py:257
  145.8 7.0 %collective-permute-done.10.refs_5_ = bf16[1088,128]{1,0:T(8,128)(2,1)S(1)} collective-permute-done((bf16[1088,128]{1,0:T(8,128)(2,1)S(1)}, bf16[1088,128]{1,0:T(8,128)(2,1)S(1)}, u32[]{:S(2)}, u32[]{:S(2)}) %collective-permute-start.10) | collective-permute-done | bytes 278560 | tf_op jit(solution)/shard_map/ppermute | solution.py:257
  154.4 35.5 %all_to_all.10.chunks_ref = bf16[64,64,128]{2,1,0:T(8,128)(2,1)S(1)} all-to-all(bf16[64,64,128]{2,1,0:T(8,128)(2,1)S(1)} %down.1), channel_id=1, replica_groups=mesh['pipe'=8,'expert'=64] {'expert'}, dimensions={0} | all-to-all | bytes 2097152 | tf_op jit(solution)/shard_map/all_to_all | solution.py:286
  (49 shorter events, 21.0 us)
Async XLA Ops:
  0.0 1.2 copy-start.11
  2.9 1.3 copy-start
  4.2 14.7 %copy-start.5 = (bf16[1,3584,128]{2,1,0:T(8,128)(2,1)S(1)}, bf16[1,3584,128]{2,1,0:T(8,128)(2,1)}, u32[]{:S(2)}) copy-start(bf16[1,3584,128]{2,1,0:T(8,128)(2,1)} %param.9) | copy-start | bytes 2752516
  4.2 62.2 %all-to-all-start = ((bf16[64,120,128]{2,1,0:T(8,128)(2,1)}), bf16[64,120,128]{2,1,0:T(8,128)(2,1)S(1)}, u32[]{:S(2)}, u32[]{:S(2)}) async-start(bf16[64,120,128]{2,1,0:T(8,128)(2,1)} %copy-done), calls=%async_computation | async-start | bytes 3932160 | tf_op jit(solution)/shard_map/all_to_all | solution.py:272
  18.9 1.2 copy-start.7
  22.3 20.3 %collective-permute-start = (bf16[2816,128]{1,0:T(8,128)(2,1)S(1)}, bf16[2816,128]{1,0:T(8,128)(2,1)S(1)}, u32[]{:S(2)}, u32[]{:S(2)}) collective-permute-start(bf16[2816,128]{1,0:T(8,128)(2,1)S(1)} %get-tuple-element.12), channel_id=1, source_target_pairs={{0,64},{64,128},{128,192},{192,0},{256,320},{320,384},{384,448},{4... | collective-permute-start | bytes 2162696 | tf_op jit(solution)/shard_map/ppermute | solution.py:257
  25.4 33.7 %collective-permute-start.1 = (bf16[2816,128]{1,0:T(8,128)(2,1)S(1)}, bf16[2816,128]{1,0:T(8,128)(2,1)S(1)}, u32[]{:S(2)}, u32[]{:S(2)}) collective-permute-start(bf16[2816,128]{1,0:T(8,128)(2,1)S(1)} %get-tuple-element.13), channel_id=1, source_target_pairs={{0,128},{64,192},{128,0},{192,64},{256,384},{320,448},{384,256},{4... | collective-permute-start | bytes 2162696 | tf_op jit(solution)/shard_map/ppermute | solution.py:257
  29.7 30.6 %collective-permute-start.2 = (bf16[2816,128]{1,0:T(8,128)(2,1)S(1)}, bf16[2816,128]{1,0:T(8,128)(2,1)S(1)}, u32[]{:S(2)}, u32[]{:S(2)}) collective-permute-start(bf16[2816,128]{1,0:T(8,128)(2,1)S(1)} %get-tuple-element.14), channel_id=1, source_target_pairs={{0,192},{64,0},{128,64},{192,128},{256,448},{320,256},{384,320},{4... | collective-permute-start | bytes 2162696 | tf_op jit(solution)/shard_map/ppermute | solution.py:257
  70.6 21.1 %collective-permute-start.3 = (bf16[1088,256]{1,0:T(8,128)(2,1)}, bf16[1088,256]{1,0:T(8,128)(2,1)}, u32[]{:S(2)}, u32[]{:S(2)}) collective-permute-start(bf16[1088,256]{1,0:T(8,128)(2,1)} %get-tuple-element.15), channel_id=1, source_target_pairs={{0,128},{64,192},{128,0},{192,64},{256,384},{320,448},{384,256},{4... | collective-permute-start | bytes 1671176 | tf_op jit(solution)/shard_map/ppermute | solution.py:257
  75.2 25.7 %collective-permute-start.4 = (bf16[1088,256]{1,0:T(8,128)(2,1)}, bf16[1088,256]{1,0:T(8,128)(2,1)}, u32[]{:S(2)}, u32[]{:S(2)}) collective-permute-start(bf16[1088,256]{1,0:T(8,128)(2,1)} %get-tuple-element.16), channel_id=1, source_target_pairs={{0,192},{64,0},{128,64},{192,128},{256,448},{320,256},{384,320},{4... | collective-permute-start | bytes 1671176 | tf_op jit(solution)/shard_map/ppermute | solution.py:257
  78.0 23.0 %collective-permute-start.5 = (bf16[1088,256]{1,0:T(8,128)(2,1)}, bf16[1088,256]{1,0:T(8,128)(2,1)}, u32[]{:S(2)}, u32[]{:S(2)}) collective-permute-start(bf16[1088,256]{1,0:T(8,128)(2,1)} %get-tuple-element.17), channel_id=1, source_target_pairs={{0,64},{64,128},{128,192},{192,0},{256,320},{320,384},{384,448},{4... | collective-permute-start | bytes 1671176 | tf_op jit(solution)/shard_map/ppermute | solution.py:257
  82.6 8.1 %copy-start.6 = (bf16[1,3584,128]{2,1,0:T(8,128)(2,1)S(1)}, bf16[1,3584,128]{2,1,0:T(8,128)(2,1)}, u32[]{:S(2)}) copy-start(bf16[1,3584,128]{2,1,0:T(8,128)(2,1)} %param.9) | copy-start | bytes 2752516
  82.6 8.1 %copy-start.8 = (bf16[1,3584,128]{2,1,0:T(8,128)(2,1)S(1)}, bf16[1,3584,128]{2,1,0:T(8,128)(2,1)}, u32[]{:S(2)}) copy-start(bf16[1,3584,128]{2,1,0:T(8,128)(2,1)} %param.10) | copy-start | bytes 2752516
  82.6 52.2 %collective-permute-start.13 = (bf16[2048,128]{1,0:T(8,128)(2,1)S(1)}, bf16[2048,128]{1,0:T(8,128)(2,1)S(1)}, u32[]{:S(2)}, u32[]{:S(2)}) collective-permute-start(bf16[2048,128]{1,0:T(8,128)(2,1)S(1)} %swap.1), channel_id=1, source_target_pairs={{0,256},{64,320},{128,384},{192,448},{256,0},{320,64},{384,128},{4... | collective-permute-start | bytes 1572872 | tf_op jit(solution)/shard_map/ppermute | solution.py:261
  102.6 50.2 %copy-start.4 = (bf16[2816,128]{1,0:T(8,128)(2,1)S(1)}, bf16[2816,128]{1,0:T(8,128)(2,1)}, u32[]{:S(2)}) copy-start(bf16[2816,128]{1,0:T(8,128)(2,1)} %copy-done.1) | copy-start | bytes 2162692
  102.8 28.1 %collective-permute-start.9 = (bf16[1088,128]{1,0:T(8,128)(2,1)S(1)}, bf16[1088,128]{1,0:T(8,128)(2,1)S(1)}, u32[]{:S(2)}, u32[]{:S(2)}) collective-permute-start(bf16[1088,128]{1,0:T(8,128)(2,1)S(1)} %fusion.refs_0_), channel_id=1, source_target_pairs={{0,256},{64,320},{128,384},{192,448},{256,0},{320,64},{384,128},{4... | collective-permute-start | bytes 835592 | tf_op jit(solution)/shard_map/ppermute | solution.py:261
  110.8 26.0 %collective-permute-start.8 = (bf16[1088,128]{1,0:T(8,128)(2,1)S(1)}, bf16[1088,128]{1,0:T(8,128)(2,1)S(1)}, u32[]{:S(2)}, u32[]{:S(2)}) collective-permute-start(bf16[1088,128]{1,0:T(8,128)(2,1)S(1)} %fusion.refs_0_), channel_id=1, source_target_pairs={{0,192},{64,0},{128,64},{192,128},{256,448},{320,256},{384,320},{4... | collective-permute-start | bytes 835592 | tf_op jit(solution)/shard_map/ppermute | solution.py:257
  115.1 24.2 %collective-permute-start.7 = (bf16[1088,128]{1,0:T(8,128)(2,1)S(1)}, bf16[1088,128]{1,0:T(8,128)(2,1)S(1)}, u32[]{:S(2)}, u32[]{:S(2)}) collective-permute-start(bf16[1088,128]{1,0:T(8,128)(2,1)S(1)} %fusion.refs_0_), channel_id=1, source_target_pairs={{0,128},{64,192},{128,0},{192,64},{256,384},{320,448},{384,256},{4... | collective-permute-start | bytes 835592 | tf_op jit(solution)/shard_map/ppermute | solution.py:257
  117.6 21.7 %collective-permute-start.6 = (bf16[1088,128]{1,0:T(8,128)(2,1)S(1)}, bf16[1088,128]{1,0:T(8,128)(2,1)S(1)}, u32[]{:S(2)}, u32[]{:S(2)}) collective-permute-start(bf16[1088,128]{1,0:T(8,128)(2,1)S(1)} %fusion.refs_0_), channel_id=1, source_target_pairs={{0,64},{64,128},{128,192},{192,0},{256,320},{320,384},{384,448},{4... | collective-permute-start | bytes 835592 | tf_op jit(solution)/shard_map/ppermute | solution.py:257
  130.9 9.9 %collective-permute-start.12 = (bf16[1088,128]{1,0:T(8,128)(2,1)S(1)}, bf16[1088,128]{1,0:T(8,128)(2,1)S(1)}, u32[]{:S(2)}, u32[]{:S(2)}) collective-permute-start(bf16[1088,128]{1,0:T(8,128)(2,1)S(1)} %collective-permute-done.9.refs_4_), channel_id=1, source_target_pairs={{0,192},{64,0},{128,64},{192,128},{256,448},{320,256},{384,320},{4... | collective-permute-start | bytes 835592 | tf_op jit(solution)/shard_map/ppermute | solution.py:257
  134.9 10.9 %collective-permute-start.11 = (bf16[1088,128]{1,0:T(8,128)(2,1)S(1)}, bf16[1088,128]{1,0:T(8,128)(2,1)S(1)}, u32[]{:S(2)}, u32[]{:S(2)}) collective-permute-start(bf16[1088,128]{1,0:T(8,128)(2,1)S(1)} %collective-permute-done.9.refs_4_), channel_id=1, source_target_pairs={{0,128},{64,192},{128,0},{192,64},{256,384},{320,448},{384,256},{4... | collective-permute-start | bytes 835592 | tf_op jit(solution)/shard_map/ppermute | solution.py:257
  136.8 16.0 %collective-permute-start.10 = (bf16[1088,128]{1,0:T(8,128)(2,1)S(1)}, bf16[1088,128]{1,0:T(8,128)(2,1)S(1)}, u32[]{:S(2)}, u32[]{:S(2)}) collective-permute-start(bf16[1088,128]{1,0:T(8,128)(2,1)S(1)} %collective-permute-done.9.refs_4_), channel_id=1, source_target_pairs={{0,64},{64,128},{128,192},{192,0},{256,320},{320,384},{384,448},{4... | collective-permute-start | bytes 835592 | tf_op jit(solution)/shard_map/ppermute | solution.py:257
  154.3 35.5 %copy-start.14 = (s32[128,8]{0,1:T(8,128)S(1)}, s32[128,8]{0,1:T(8,128)}, u32[]{:S(2)}) copy-start(s32[128,8]{0,1:T(8,128)} %param.7) | copy-start | bytes 12292
  154.4 35.5 %copy-start.15 = (f32[128,8]{0,1:T(8,128)S(1)}, f32[128,8]{0,1:T(8,128)}, u32[]{:S(2)}) copy-start(f32[128,8]{0,1:T(8,128)} %param.8) | copy-start | bytes 12292
  (7 other events, 6.6 us)

commit v3 on v2

--- a/solution.py
+++ b/solution.py
@@ -141,36 +141,45 @@
     out_ref[pl.ds(count, last.shape[0]), :] = jnp.dot(last, weight, preferred_element_type=F32).astype(out_ref.dtype)
 
 
-def project_sent_kernel(chunks_ref, *refs):
+def project_kernel(x_ref, chunks_ref, gate_ref, up_ref, *refs):
+    packs, out_ref = refs[:-1], refs[-1]
     main, last = stacked(chunks_ref)
     quarter = main.shape[1]
-    for pack_ref, out_ref in zip(refs[: X - 1], refs[X - 1 :]):
-        project_into(out_ref, main, last, pack_ref[pl.ds(0, quarter), :], pack_ref[pl.ds(quarter, quarter), :])
-
-
-def project_sent(chunks, packs):
-    shapes = [jax.ShapeDtypeStruct((chunks.shape[0] * 17, 2 * LANES), BF)] * len(packs)
-    return call(project_sent_kernel, "project_sent", shapes, [in_vmem()] * (1 + len(packs)))(chunks, *packs)
-
-
-def project_own_kernel(x_ref, chunks_ref, gate_ref, up_ref, out_ref):
-    main, last = stacked(chunks_ref)
-    quarter = main.shape[1]
-    part = pl.ds(pl.multiple_of(x_ref[0] * quarter, quarter), quarter)
-    project_into(out_ref, main, last, gate_ref[part, :], up_ref[part, :])
-
-
-def project_own(x, chunks, gate, up):
-    shape = jax.ShapeDtypeStruct((chunks.shape[0] * 17, 2 * LANES), F32)
-    return call(project_own_kernel, "project_own", shape, [in_smem()] + [in_vmem()] * 3)(x, chunks, gate, up)
+    x = x_ref[0]
+    for d, pack_ref in enumerate(packs, 1):
+        gate, up = pack_ref[pl.ds(0, quarter), :], pack_ref[pl.ds(quarter, quarter), :]
+        project_into(out_ref.at[lax.rem(x + X - d, X)], main, last, gate, up)
+    part = pl.ds(pl.multiple_of(x * quarter, quarter), quarter)
+    project_into(out_ref.at[x], main, last, gate_ref[part, :], up_ref[part, :])
+
+
+def project(x, chunks, gate, up, packs):
+    shape = jax.ShapeDtypeStruct((X, chunks.shape[0] * 17, 2 * LANES), BF)
+    return call(project_kernel, "project", shape, [in_smem()] + [in_vmem()] * (3 + len(packs)))(
+        x, chunks, gate, up, *packs
+    )
+
+
+def activate_kernel(parts_ref, out_ref):
+    total = parts_ref[0].astype(F32)
+    for d in range(1, X):
+        total += parts_ref[d].astype(F32)
+    gate, up = total[:, :LANES], total[:, LANES:]
+    out_ref[...] = (gate / (1.0 + jnp.exp(-gate)) * up).astype(BF)
+
+
+def activate(parts):
+    shape = jax.ShapeDtypeStruct((parts.shape[1], LANES), BF)
+    return call(activate_kernel, "activate", shape, [in_vmem()])(parts)
 
 
 def down_kernel(x_ref, z_ref, *refs):
-    hiddens, (own_ref, p1, p2, p3, other_ref, out_ref) = refs[: 2 * X], refs[2 * X :]
+    near_ref, far_ref, own_ref, p1, p2, p3, other_ref, out_ref = refs
     experts = out_ref.shape[0]
     rows = own_ref.shape[0] // 2
     depth = rows // 4
-    hidden = jnp.concatenate([ref[...] for ref in hiddens], axis=1)
+    source = [lax.rem(x_ref[0] + X - d, X) for d in range(X)]
+    hidden = jnp.concatenate([ref[s] for ref in (near_ref, far_ref) for s in source], axis=1)
     blocks = []
     for ref in (own_ref, p1, p2, p3):
         base = ref.shape[0] - 2 * rows + z_ref[0] * rows
@@ -198,10 +207,10 @@
     out_ref[:, 48:64, :] = jnp.concatenate([halves, tail], axis=1).astype(BF)
 
 
-def down(x, z, hiddens, own, packs, other, experts):
+def down(x, z, near, far, own, packs, other, experts):
     shape = jax.ShapeDtypeStruct((experts, 64, LANES), BF)
-    specs = [in_smem()] * 2 + [in_vmem()] * (2 * X + X + 1)
-    return call(down_kernel, "down", shape, specs)(x, z, *hiddens, own, *packs, other)
+    specs = [in_smem()] * 2 + [in_vmem()] * (X + 3)
+    return call(down_kernel, "down", shape, specs)(x, z, near, far, own, *packs, other)
 
 
 def combine_kernel(x_ref, ids_ref, scale_ref, chunks_ref, out_ref):
@@ -261,6 +270,11 @@
     return lax.ppermute(value, "pipe", [(p, (p + X) % (2 * X)) for p in range(2 * X)])
 
 
+def across(value):
+    groups = [[z * X + x for x in range(X)] for z in range(2)]
+    return lax.all_to_all(value, "pipe", split_axis=0, concat_axis=0, axis_index_groups=groups, tiled=True)
+
+
 def body(tokens, expert_ids, gate_scale, w_gate, w_up, w_down):
     groups = lax.axis_size("expert")
     pipe = lax.axis_index("pipe")
@@ -273,16 +287,12 @@
     own_down, *sent = pack(x, w_gate, w_up, w_down)
     packs = [shift(sent[d - 1], d) for d in range(1, X)]
     other_down = cross(swap(z, own_down, packs))
-    parts = project_sent(chunks, packs)
-    arrived = [shift(parts[d - 1], -d) for d in (2, 1, 3)]
-    summed = project_own(x, chunks, w_gate, w_up)
-    for part in arrived:
-        summed = summed + part.astype(F32)
-    hidden = (jax.nn.silu(summed[:, :LANES]) * summed[:, LANES:]).astype(BF)
+    arrived = across(project(x, chunks, w_gate, w_up, packs))
+    hidden = activate(arrived)
     swapped = cross(hidden)
-    hiddens = [hidden] + [shift(hidden, d) for d in range(1, X)]
-    hiddens += [swapped] + [shift(swapped, d) for d in range(1, X)]
-    output = down(x, z, hiddens, own_down, packs, other_down, groups)
+    near = across(jnp.broadcast_to(hidden[None], (X, *hidden.shape)))
+    far = across(jnp.broadcast_to(swapped[None], (X, *swapped.shape)))
+    output = down(x, z, near, far, own_down, packs, other_down, groups)
     returned = lax.all_to_all(output, "expert", split_axis=0, concat_axis=0, tiled=True)
     return combine(x, ids, scale, returned, tokens.shape[1] // (2 * X))
 

time: 193 us -> 207 us (1.073)
  blocking collectives: 35.5 us -> 67.2 us
  starting transfers between devices: 68.9 us -> 45.3 us
  local copies, waits for them, and re-layouts: 11 us -> 16.1 us
    all_to_all x0 -> x1, blocking collectives: none -> 31.8 us  [across(): lax.all_to_all(value, 'pipe', split_axis=0, concat_axis=0, axis_index_gro...]
    ppermute x12 -> x3, starting transfers between devices: 38 us -> 10.5 us  [shift(): return lax.ppermute(value, 'pipe', pairs)]
    ppermute x2, waiting for transfers between devices: 10.9 us -> 33.9 us  [cross(): lax.ppermute(value, 'pipe', [(p, (p + X) % (2 * X)) for p in range(2 * X)])]
    ppermute x12 -> x3, waiting for transfers between devices: 50.3 us -> 27.5 us  [shift(): return lax.ppermute(value, 'pipe', pairs)]
    all_to_all x0 -> x2, starting transfers between devices: none -> 7.9 us  [across(): lax.all_to_all(value, 'pipe', split_axis=0, concat_axis=0, axis_index_gro...]
    ppermute x2, starting transfers between devices: 16.1 us -> 12.1 us  [cross(): lax.ppermute(value, 'pipe', [(p, (p + X) % (2 * X)) for p in range(2 * X)])]
    broadcast_in_dim x0 -> x2, local copies, waits for them, and re-layouts: none -> 3.25 us  [the longest x1 2.1 us: body(): far = across(jnp.broadcast_to(swapped[None], (X, *swapped.shape)))]
    unnamed x32 -> x34, local copies, waits for them, and re-layouts: 10.2 us -> 12.1 us
  transfers between devices with their start and end apart: 15 -> 8, of which waited for: 9 -> 6; matrix products, arithmetic and copies ran while one was open for 1% -> 0% of each run, Pallas kernels for 1% -> 0%
where the time goes in v3:
time: 207 us; the launch traced here: 205 us
  blocking collectives  67.2 us (32%)
  waiting for transfers between devices  66.7 us (32%)
  starting transfers between devices  45.3 us (22%)
  local copies, waits for them, and re-layouts  16.1 us (8%)
  Pallas kernels  10.1 us (5%)
    all_to_all x1, blocking collectives, body(): lax.all_to_all(output, 'expert', split_axis=0, concat_axis=0, tiled=True)  35.4 us
    ppermute x2, waiting for transfers between devices, cross(): lax.ppermute(value, 'pipe', [(p, (p + X) % (2 * X)) for p in range(2 * X)])  33.9 us
    all_to_all x1, blocking collectives, across(): lax.all_to_all(value, 'pipe', split_axis=0, concat_axis=0, axis_index_gro...  31.8 us
    ppermute x3, waiting for transfers between devices, shift(): return lax.ppermute(value, 'pipe', pairs)  27.5 us
    all_to_all x1, starting transfers between devices, body(): lax.all_to_all(buffer, 'expert', split_axis=0, concat_axis=0, tiled=True)  14.7 us
    ppermute x2, starting transfers between devices, cross(): lax.ppermute(value, 'pipe', [(p, (p + X) % (2 * X)) for p in range(2 * X)])  12.1 us
    unnamed x34, local copies, waits for them, and re-layouts  12.1 us
    ppermute x3, starting transfers between devices, shift(): return lax.ppermute(value, 'pipe', pairs)  10.5 us
  transfers between devices with their start and end apart: 8, of which 6 were waited for; matrix products, arithmetic and copies ran while one was open for 0% of the time, Pallas kernels for 0%

profile of v3, /device:TPU:1, one launch (start us, length us, event | category | flops | bytes accessed | tf_op | source)
XLA Modules:
  0.0 205.5 jit_solution(12374908305255405178)
XLA Ops:
  0.0 1.2 copy-done.10
  1.9 2.3 %dispatch.1 = bf16[64,120,128]{2,1,0:T(8,128)(2,1)} custom-call(s32[1]{0:T(128)} %bitcast.x_ref, s32[8,128]{1,0:T(8,128)S(1)} %bitcast.12, bf16[128,3584]{1,0:T(8,128)(2,1)S(1)} %copy-done.10), custom_call_target="tpu_custom_call" | custom-call | tf_op jit(solution)/shard_map/dispatch/pallas_call | solution.py:77
  4.1 14.7 %all-to-all-start = ((bf16[64,120,128]{2,1,0:T(8,128)(2,1)}), bf16[64,120,128]{2,1,0:T(8,128)(2,1)S(1)}, u32[]{:S(2)}, u32[]{:S(2)}) async-start(bf16[64,120,128]{2,1,0:T(8,128)(2,1)} %dispatch.1), calls=%async_computation | async-start | bytes 3932160 | tf_op jit(solution)/shard_map/all_to_all | solution.py:286
  20.1 1.2 copy-done.11
  22.2 3.1 %collective-permute-start = (bf16[2816,128]{1,0:T(8,128)(2,1)S(1)}, bf16[2816,128]{1,0:T(8,128)(2,1)S(1)}, u32[]{:S(2)}, u32[]{:S(2)}) collective-permute-start(bf16[2816,128]{1,0:T(8,128)(2,1)S(1)} %get-tuple-element.9), channel_id=1, source_target_pairs={{0,64},{64,128},{128,192},{192,0},{256,320},{320,384},{384,448},{4... | collective-permute-start | bytes 2162696 | tf_op jit(solution)/shard_map/ppermute | solution.py:266
  25.4 4.4 %collective-permute-start.1 = (bf16[2816,128]{1,0:T(8,128)(2,1)S(1)}, bf16[2816,128]{1,0:T(8,128)(2,1)S(1)}, u32[]{:S(2)}, u32[]{:S(2)}) collective-permute-start(bf16[2816,128]{1,0:T(8,128)(2,1)S(1)} %get-tuple-element.10), channel_id=1, source_target_pairs={{0,128},{64,192},{128,0},{192,64},{256,384},{320,448},{384,256},{4... | collective-permute-start | bytes 2162696 | tf_op jit(solution)/shard_map/ppermute | solution.py:266
  29.7 3.1 %collective-permute-start.2 = (bf16[2816,128]{1,0:T(8,128)(2,1)S(1)}, bf16[2816,128]{1,0:T(8,128)(2,1)S(1)}, u32[]{:S(2)}, u32[]{:S(2)}) collective-permute-start(bf16[2816,128]{1,0:T(8,128)(2,1)S(1)} %get-tuple-element.11), channel_id=1, source_target_pairs={{0,192},{64,0},{128,64},{192,128},{256,448},{320,256},{384,320},{4... | collective-permute-start | bytes 2162696 | tf_op jit(solution)/shard_map/ppermute | solution.py:266
  32.8 9.8 %collective-permute-done.refs_0_.p1.refs_3_ = bf16[2816,128]{1,0:T(8,128)(2,1)S(1)} collective-permute-done((bf16[2816,128]{1,0:T(8,128)(2,1)S(1)}, bf16[2816,128]{1,0:T(8,128)(2,1)S(1)}, u32[]{:S(2)}, u32[]{:S(2)}) %collective-permute-start) | collective-permute-done | bytes 720928 | tf_op jit(solution)/shard_map/ppermute | solution.py:266
  42.6 16.4 %collective-permute-done.1.refs_1_.p2.refs_4_ = bf16[2816,128]{1,0:T(8,128)(2,1)S(1)} collective-permute-done((bf16[2816,128]{1,0:T(8,128)(2,1)S(1)}, bf16[2816,128]{1,0:T(8,128)(2,1)S(1)}, u32[]{:S(2)}, u32[]{:S(2)}) %collective-permute-start.1) | collective-permute-done | bytes 720928 | tf_op jit(solution)/shard_map/ppermute | solution.py:266
  59.0 1.3 collective-permute-done.2.refs_2_.p3.refs_5_
  61.2 5.2 %all-to-all-done.chunks_ref = bf16[64,120,128]{2,1,0:T(8,128)(2,1)S(1)} async-done(((bf16[64,120,128]{2,1,0:T(8,128)(2,1)}), bf16[64,120,128]{2,1,0:T(8,128)(2,1)S(1)}, u32[]{:S(2)}, u32[]{:S(2)}) %all-to-all-start) | async-done | bytes 1966112 | tf_op jit(solution)/shard_map/all_to_all | solution.py:286
  67.5 1.2 copy-done.4
  69.9 2.8 %project.1 = bf16[4,1088,256]{2,1,0:T(8,128)(2,1)S(1)} custom-call(s32[1]{0:T(128)} %bitcast.x_ref, bf16[64,120,128]{2,1,0:T(8,128)(2,1)S(1)} %all-to-all-done.chunks_ref, bf16[3584,128]{1,0:T(8,128)(2,1)S(1)} %bitcast.8, bf16[3584,128]{1,0:T(8,128)(2,1)S(1)} %bitcast.10, bf16[2816,128]{1,0:T(8,128)(2,1)S(1)} %collective-permute-done.refs_0_.p1.refs_3_, ...), custom_call_target="tpu_custom_call" | custom-call | tf_op jit(solution)/shard_map/project/pallas_call | solution.py:158
  72.6 31.8 %all_to_all.25.parts_ref = bf16[4,1088,256]{2,1,0:T(8,128)(2,1)S(1)} all-to-all(bf16[4,1088,256]{2,1,0:T(8,128)(2,1)S(1)} %project.1), channel_id=1, replica_groups={{0,64,128,192},{256,320,384,448},{1,65,129,193},{257,321,385,449},{2,66..., dimensions={0} | all-to-all | bytes 4456448 | tf_op jit(solution)/shard_map/all_to_all | solution.py:275
  106.0 3.5 %all-to-all-start.2 = ((bf16[4,1088,128]{2,1,0:T(8,128)(2,1)}), bf16[4,1088,128]{2,1,0:T(8,128)(2,1)S(1)}, u32[]{:S(2)}, u32[]{:S(2)}) async-start(bf16[4,1088,128]{2,1,0:T(8,128)(2,1)} %broadcast_in_dim.4), calls=%async_computation.2 | async-start | bytes 2228224 | tf_op jit(solution)/shard_map/all_to_all | solution.py:275
  109.6 8.1 %collective-permute-start.3 = (bf16[1088,128]{1,0:T(8,128)(2,1)S(1)}, bf16[1088,128]{1,0:T(8,128)(2,1)}, u32[]{:S(2)}, u32[]{:S(2)}) collective-permute-start(bf16[1088,128]{1,0:T(8,128)(2,1)S(1)} %activate.1), channel_id=1, source_target_pairs={{0,256},{64,320},{128,384},{192,448},{256,0},{320,64},{384,128},{4... | collective-permute-start | bytes 835592 | tf_op jit(solution)/shard_map/ppermute | solution.py:270
  117.6 12.4 %collective-permute-done.3 = bf16[1088,128]{1,0:T(8,128)(2,1)} collective-permute-done((bf16[1088,128]{1,0:T(8,128)(2,1)S(1)}, bf16[1088,128]{1,0:T(8,128)(2,1)}, u32[]{:S(2)}, u32[]{:S(2)}) %collective-permute-start.3) | collective-permute-done | bytes 278560 | tf_op jit(solution)/shard_map/ppermute | solution.py:270
  130.1 2.1 %broadcast_in_dim.5 = bf16[4,1088,128]{2,1,0:T(8,128)(2,1)} broadcast(bf16[1088,128]{1,0:T(8,128)(2,1)} %collective-permute-done.3), dimensions={1,2} | broadcast | bytes 1392640 | tf_op jit(solution)/shard_map/broadcast_in_dim | solution.py:294
  132.2 4.4 %all-to-all-start.3 = ((bf16[4,1088,128]{2,1,0:T(8,128)(2,1)}), bf16[4,1088,128]{2,1,0:T(8,128)(2,1)}, u32[]{:S(2)}, u32[]{:S(2)}) async-start(bf16[4,1088,128]{2,1,0:T(8,128)(2,1)} %broadcast_in_dim.5), calls=%async_computation.3 | async-start | bytes 2228224 | tf_op jit(solution)/shard_map/all_to_all | solution.py:275
  137.6 4.1 %collective-permute-start.4 = (bf16[2048,128]{1,0:T(8,128)(2,1)S(1)}, bf16[2048,128]{1,0:T(8,128)(2,1)S(1)}, u32[]{:S(2)}, u32[]{:S(2)}) collective-permute-start(bf16[2048,128]{1,0:T(8,128)(2,1)S(1)} %swap.1), channel_id=1, source_target_pairs={{0,256},{64,320},{128,384},{192,448},{256,0},{320,64},{384,128},{4... | collective-permute-start | bytes 1572872 | tf_op jit(solution)/shard_map/ppermute | solution.py:270
  141.6 21.5 %collective-permute-done.4.refs_6_ = bf16[2048,128]{1,0:T(8,128)(2,1)S(1)} collective-permute-done((bf16[2048,128]{1,0:T(8,128)(2,1)S(1)}, bf16[2048,128]{1,0:T(8,128)(2,1)S(1)}, u32[]{:S(2)}, u32[]{:S(2)}) %collective-permute-start.4) | collective-permute-done | bytes 524320 | tf_op jit(solution)/shard_map/ppermute | solution.py:270
  165.0 2.8 %down.1 = bf16[64,64,128]{2,1,0:T(8,128)(2,1)S(1)} custom-call(s32[1]{0:T(128)} %bitcast.x_ref, s32[1]{0:T(128)} %bitcast.3.z_ref, bf16[4,1088,128]{2,1,0:T(8,128)(2,1)S(1)} %all-to-all-done.2.refs_0_, bf16[4,1088,128]{2,1,0:T(8,128)(2,1)} %all-to-all-done.3.refs_1_, bf16[1024,128]{1,0:T(8,128)(2,1)S(1)} %copy-done.9, ...), custom_call_target="tpu_custom_call" | custom-call | tf_op jit(solution)/shard_map/down/pallas_call | solution.py:213
  167.8 35.4 %all_to_all.26.chunks_ref = bf16[64,64,128]{2,1,0:T(8,128)(2,1)S(1)} all-to-all(bf16[64,64,128]{2,1,0:T(8,128)(2,1)S(1)} %down.1), channel_id=1, replica_groups=mesh['pipe'=8,'expert'=64] {'expert'}, dimensions={0} | all-to-all | bytes 2097152 | tf_op jit(solution)/shard_map/all_to_all | solution.py:296
  203.2 1.6 combine.1
  (38 shorter events, 11.2 us)
Async XLA Ops:
  0.0 1.2 copy-start.10
  4.1 14.7 %copy-start.3 = (bf16[1,3584,128]{2,1,0:T(8,128)(2,1)S(1)}, bf16[1,3584,128]{2,1,0:T(8,128)(2,1)}, u32[]{:S(2)}) copy-start(bf16[1,3584,128]{2,1,0:T(8,128)(2,1)} %param.9) | copy-start | bytes 2752516
  4.1 62.2 %all-to-all-start = ((bf16[64,120,128]{2,1,0:T(8,128)(2,1)}), bf16[64,120,128]{2,1,0:T(8,128)(2,1)S(1)}, u32[]{:S(2)}, u32[]{:S(2)}) async-start(bf16[64,120,128]{2,1,0:T(8,128)(2,1)} %dispatch.1), calls=%async_computation | async-start | bytes 3932160 | tf_op jit(solution)/shard_map/all_to_all | solution.py:286
  18.9 1.2 copy-start.5
  20.1 1.2 copy-start.11
  21.5 0.7 copy-start.7
  22.2 20.3 %collective-permute-start = (bf16[2816,128]{1,0:T(8,128)(2,1)S(1)}, bf16[2816,128]{1,0:T(8,128)(2,1)S(1)}, u32[]{:S(2)}, u32[]{:S(2)}) collective-permute-start(bf16[2816,128]{1,0:T(8,128)(2,1)S(1)} %get-tuple-element.9), channel_id=1, source_target_pairs={{0,64},{64,128},{128,192},{192,0},{256,320},{320,384},{384,448},{4... | collective-permute-start | bytes 2162696 | tf_op jit(solution)/shard_map/ppermute | solution.py:266
  25.4 33.7 %collective-permute-start.1 = (bf16[2816,128]{1,0:T(8,128)(2,1)S(1)}, bf16[2816,128]{1,0:T(8,128)(2,1)S(1)}, u32[]{:S(2)}, u32[]{:S(2)}) collective-permute-start(bf16[2816,128]{1,0:T(8,128)(2,1)S(1)} %get-tuple-element.10), channel_id=1, source_target_pairs={{0,128},{64,192},{128,0},{192,64},{256,384},{320,448},{384,256},{4... | collective-permute-start | bytes 2162696 | tf_op jit(solution)/shard_map/ppermute | solution.py:266
  29.7 30.6 %collective-permute-start.2 = (bf16[2816,128]{1,0:T(8,128)(2,1)S(1)}, bf16[2816,128]{1,0:T(8,128)(2,1)S(1)}, u32[]{:S(2)}, u32[]{:S(2)}) collective-permute-start(bf16[2816,128]{1,0:T(8,128)(2,1)S(1)} %get-tuple-element.11), channel_id=1, source_target_pairs={{0,192},{64,0},{128,64},{192,128},{256,448},{320,256},{384,320},{4... | collective-permute-start | bytes 2162696 | tf_op jit(solution)/shard_map/ppermute | solution.py:266
  60.3 0.9 copy-start
  66.4 1.1 copy-start.1
  67.5 1.2 copy-start.4
  68.7 1.2 copy-start.6
  106.0 24.1 %all-to-all-start.2 = ((bf16[4,1088,128]{2,1,0:T(8,128)(2,1)}), bf16[4,1088,128]{2,1,0:T(8,128)(2,1)S(1)}, u32[]{:S(2)}, u32[]{:S(2)}) async-start(bf16[4,1088,128]{2,1,0:T(8,128)(2,1)} %broadcast_in_dim.4), calls=%async_computation.2 | async-start | bytes 2228224 | tf_op jit(solution)/shard_map/all_to_all | solution.py:275
  109.5 27.0 %copy-start.2 = (bf16[2816,128]{1,0:T(8,128)(2,1)S(1)}, bf16[2816,128]{1,0:T(8,128)(2,1)}, u32[]{:S(2)}) copy-start(bf16[2816,128]{1,0:T(8,128)(2,1)} %copy-done) | copy-start | bytes 2162692
  109.6 20.5 %collective-permute-start.3 = (bf16[1088,128]{1,0:T(8,128)(2,1)S(1)}, bf16[1088,128]{1,0:T(8,128)(2,1)}, u32[]{:S(2)}, u32[]{:S(2)}) collective-permute-start(bf16[1088,128]{1,0:T(8,128)(2,1)S(1)} %activate.1), channel_id=1, source_target_pairs={{0,256},{64,320},{128,384},{192,448},{256,0},{320,64},{384,128},{4... | collective-permute-start | bytes 835592 | tf_op jit(solution)/shard_map/ppermute | solution.py:270
  132.2 31.8 %copy-start.9 = (bf16[1024,128]{1,0:T(8,128)(2,1)S(1)}, bf16[1024,128]{1,0:T(8,128)(2,1)}, u32[]{:S(2)}) copy-start(bf16[1024,128]{1,0:T(8,128)(2,1)} %copy-done.7) | copy-start | bytes 786436
  132.2 31.8 %all-to-all-start.3 = ((bf16[4,1088,128]{2,1,0:T(8,128)(2,1)}), bf16[4,1088,128]{2,1,0:T(8,128)(2,1)}, u32[]{:S(2)}, u32[]{:S(2)}) async-start(bf16[4,1088,128]{2,1,0:T(8,128)(2,1)} %broadcast_in_dim.5), calls=%async_computation.3 | async-start | bytes 2228224 | tf_op jit(solution)/shard_map/all_to_all | solution.py:275
  136.6 1.0 copy-start.8
  137.6 25.6 %collective-permute-start.4 = (bf16[2048,128]{1,0:T(8,128)(2,1)S(1)}, bf16[2048,128]{1,0:T(8,128)(2,1)S(1)}, u32[]{:S(2)}, u32[]{:S(2)}) collective-permute-start(bf16[2048,128]{1,0:T(8,128)(2,1)S(1)} %swap.1), channel_id=1, source_target_pairs={{0,256},{64,320},{128,384},{192,448},{256,0},{320,64},{384,128},{4... | collective-permute-start | bytes 1572872 | tf_op jit(solution)/shard_map/ppermute | solution.py:270
  163.1 0.8 copy-start.12
  163.9 1.0 copy-start.13
  167.8 35.4 %copy-start.15 = (s32[128,8]{0,1:T(8,128)S(1)}, s32[128,8]{0,1:T(8,128)}, u32[]{:S(2)}) copy-start(s32[128,8]{0,1:T(8,128)} %param.7) | copy-start | bytes 12292
  167.8 35.4 %copy-start.16 = (f32[128,8]{0,1:T(8,128)S(1)}, f32[128,8]{0,1:T(8,128)}, u32[]{:S(2)}) copy-start(f32[128,8]{0,1:T(8,128)} %param.8) | copy-start | bytes 12292
  (1 other events, 0.7 us)

commit v4 on v2

--- a/solution.py
+++ b/solution.py
@@ -275,6 +275,7 @@
     other_down = cross(swap(z, own_down, packs))
     parts = project_sent(chunks, packs)
     arrived = [shift(parts[d - 1], -d) for d in (2, 1, 3)]
+    chunks, other_down = lax.optimization_barrier((chunks, other_down))
     summed = project_own(x, chunks, w_gate, w_up)
     for part in arrived:
         summed = summed + part.astype(F32)

time: 193 us -> 198 us (1.026)
  blocking collectives: 35.5 us -> 49.1 us
  waiting for transfers between devices: 66.3 us -> 57.6 us
    all_to_all x1, blocking collectives: 35.5 us -> 49.1 us  [body(): lax.all_to_all(output, 'expert', split_axis=0, concat_axis=0, tiled=True)]
    ppermute x12, waiting for transfers between devices: 50.3 us -> 39.3 us  [shift(): return lax.ppermute(value, 'pipe', pairs)]
    ppermute x2, waiting for transfers between devices: 10.9 us -> 13.2 us  [cross(): lax.ppermute(value, 'pipe', [(p, (p + X) % (2 * X)) for p in range(2 * X)])]
  transfers between devices with their start and end apart: 15 -> 15, of which waited for: 9 -> 7; matrix products, arithmetic and copies ran while one was open for 1% -> 0% of each run, Pallas kernels for 1% -> 1%
where the time goes in v4:
time: 198 us; the launch traced here: 197 us
  starting transfers between devices  68.4 us (35%)
  waiting for transfers between devices  57.6 us (29%)
  blocking collectives  49.1 us (25%)
  local copies, waits for them, and re-layouts  11 us (6%)
  Pallas kernels  8.56 us (4%)
    all_to_all x1, blocking collectives, body(): lax.all_to_all(output, 'expert', split_axis=0, concat_axis=0, tiled=True)  49.1 us
    ppermute x12, waiting for transfers between devices, shift(): return lax.ppermute(value, 'pipe', pairs)  39.3 us
    ppermute x12, starting transfers between devices, shift(): return lax.ppermute(value, 'pipe', pairs)  38.4 us
    ppermute x2, starting transfers between devices, cross(): lax.ppermute(value, 'pipe', [(p, (p + X) % (2 * X)) for p in range(2 * X)])  15.2 us
    all_to_all x1, starting transfers between devices, body(): lax.all_to_all(buffer, 'expert', split_axis=0, concat_axis=0, tiled=True)  14.7 us
    ppermute x2, waiting for transfers between devices, cross(): lax.ppermute(value, 'pipe', [(p, (p + X) % (2 * X)) for p in range(2 * X)])  13.2 us
    unnamed x32, local copies, waits for them, and re-layouts  10.2 us
    all_to_all x1, waiting for transfers between devices, body(): lax.all_to_all(buffer, 'expert', split_axis=0, concat_axis=0, tiled=True)  5.19 us
  transfers between devices with their start and end apart: 15, of which 7 were waited for; matrix products, arithmetic and copies ran while one was open for 0% of the time, Pallas kernels for 1%

profile of v4, /device:TPU:1, one launch (start us, length us, event | category | flops | bytes accessed | tf_op | source)
XLA Modules:
  0.0 196.7 jit_solution(6218712293335462715)
XLA Ops:
  4.2 14.7 %all-to-all-start = ((bf16[64,120,128]{2,1,0:T(8,128)(2,1)}), bf16[64,120,128]{2,1,0:T(8,128)(2,1)S(1)}, u32[]{:S(2)}, u32[]{:S(2)}) async-start(bf16[64,120,128]{2,1,0:T(8,128)(2,1)} %copy-done), calls=%async_computation | async-start | bytes 3932160 | tf_op jit(solution)/shard_map/all_to_all | solution.py:272
  22.3 3.1 %collective-permute-start = (bf16[2816,128]{1,0:T(8,128)(2,1)S(1)}, bf16[2816,128]{1,0:T(8,128)(2,1)S(1)}, u32[]{:S(2)}, u32[]{:S(2)}) collective-permute-start(bf16[2816,128]{1,0:T(8,128)(2,1)S(1)} %get-tuple-element.15), channel_id=1, source_target_pairs={{0,64},{64,128},{128,192},{192,0},{256,320},{320,384},{384,448},{4... | collective-permute-start | bytes 2162696 | tf_op jit(solution)/shard_map/ppermute | solution.py:257
  25.4 4.4 %collective-permute-start.1 = (bf16[2816,128]{1,0:T(8,128)(2,1)S(1)}, bf16[2816,128]{1,0:T(8,128)(2,1)S(1)}, u32[]{:S(2)}, u32[]{:S(2)}) collective-permute-start(bf16[2816,128]{1,0:T(8,128)(2,1)S(1)} %get-tuple-element.16), channel_id=1, source_target_pairs={{0,128},{64,192},{128,0},{192,64},{256,384},{320,448},{384,256},{4... | collective-permute-start | bytes 2162696 | tf_op jit(solution)/shard_map/ppermute | solution.py:257
  29.7 3.1 %collective-permute-start.2 = (bf16[2816,128]{1,0:T(8,128)(2,1)S(1)}, bf16[2816,128]{1,0:T(8,128)(2,1)S(1)}, u32[]{:S(2)}, u32[]{:S(2)}) collective-permute-start(bf16[2816,128]{1,0:T(8,128)(2,1)S(1)} %get-tuple-element.17), channel_id=1, source_target_pairs={{0,192},{64,0},{128,64},{192,128},{256,448},{320,256},{384,320},{4... | collective-permute-start | bytes 2162696 | tf_op jit(solution)/shard_map/ppermute | solution.py:257
  32.8 9.8 %collective-permute-done.p1.refs_0_.refs_9_ = bf16[2816,128]{1,0:T(8,128)(2,1)S(1)} collective-permute-done((bf16[2816,128]{1,0:T(8,128)(2,1)S(1)}, bf16[2816,128]{1,0:T(8,128)(2,1)S(1)}, u32[]{:S(2)}, u32[]{:S(2)}) %collective-permute-start) | collective-permute-done | bytes 720928 | tf_op jit(solution)/shard_map/ppermute | solution.py:257
  42.6 16.4 %collective-permute-done.1.p2.refs_1_.refs_10_ = bf16[2816,128]{1,0:T(8,128)(2,1)S(1)} collective-permute-done((bf16[2816,128]{1,0:T(8,128)(2,1)S(1)}, bf16[2816,128]{1,0:T(8,128)(2,1)S(1)}, u32[]{:S(2)}, u32[]{:S(2)}) %collective-permute-start.1) | collective-permute-done | bytes 720928 | tf_op jit(solution)/shard_map/ppermute | solution.py:257
  61.2 5.2 %all-to-all-done.chunks_ref = bf16[64,120,128]{2,1,0:T(8,128)(2,1)S(1)} async-done(((bf16[64,120,128]{2,1,0:T(8,128)(2,1)}), bf16[64,120,128]{2,1,0:T(8,128)(2,1)S(1)}, u32[]{:S(2)}, u32[]{:S(2)}) %all-to-all-start) | async-done | bytes 1966112 | tf_op jit(solution)/shard_map/all_to_all | solution.py:272
  67.5 3.1 %project_sent.1 = (bf16[1088,256]{1,0:T(8,128)(2,1)}, bf16[1088,256]{1,0:T(8,128)(2,1)}, bf16[1088,256]{1,0:T(8,128)(2,1)}) custom-call(bf16[64,120,128]{2,1,0:T(8,128)(2,1)S(1)} %all-to-all-done.chunks_ref, bf16[2816,128]{1,0:T(8,128)(2,1)S(1)} %collective-permute-done.p1.refs_0_.refs_9_, bf16[2816,128]{1,0:T(8,128)(2,1)S(1)} %collective-permute-done.1.p2.refs_1_.refs_10_, ...), custom_call_target="tpu_custom_call" | custom-call | tf_op jit(solution)/shard_map/project_sent/pallas_call | solution.py:153
  70.6 4.6 %collective-permute-start.4 = (bf16[1088,256]{1,0:T(8,128)(2,1)}, bf16[1088,256]{1,0:T(8,128)(2,1)}, u32[]{:S(2)}, u32[]{:S(2)}) collective-permute-start(bf16[1088,256]{1,0:T(8,128)(2,1)} %get-tuple-element.19), channel_id=1, source_target_pairs={{0,128},{64,192},{128,0},{192,64},{256,384},{320,448},{384,256},{4... | collective-permute-start | bytes 1671176 | tf_op jit(solution)/shard_map/ppermute | solution.py:257
  75.2 2.8 %collective-permute-start.5 = (bf16[1088,256]{1,0:T(8,128)(2,1)}, bf16[1088,256]{1,0:T(8,128)(2,1)}, u32[]{:S(2)}, u32[]{:S(2)}) collective-permute-start(bf16[1088,256]{1,0:T(8,128)(2,1)} %get-tuple-element.20), channel_id=1, source_target_pairs={{0,192},{64,0},{128,64},{192,128},{256,448},{320,256},{384,320},{4... | collective-permute-start | bytes 1671176 | tf_op jit(solution)/shard_map/ppermute | solution.py:257
  78.0 2.5 %collective-permute-start.6 = (bf16[1088,256]{1,0:T(8,128)(2,1)}, bf16[1088,256]{1,0:T(8,128)(2,1)}, u32[]{:S(2)}, u32[]{:S(2)}) collective-permute-start(bf16[1088,256]{1,0:T(8,128)(2,1)} %get-tuple-element.21), channel_id=1, source_target_pairs={{0,64},{64,128},{128,192},{192,0},{256,320},{320,384},{384,448},{4... | collective-permute-start | bytes 1671176 | tf_op jit(solution)/shard_map/ppermute | solution.py:257
  82.6 8.1 %collective-permute-start.3 = (bf16[2048,128]{1,0:T(8,128)(2,1)S(1)}, bf16[2048,128]{1,0:T(8,128)(2,1)S(1)}, u32[]{:S(2)}, u32[]{:S(2)}) collective-permute-start(bf16[2048,128]{1,0:T(8,128)(2,1)S(1)} %swap.1), channel_id=1, source_target_pairs={{0,256},{64,320},{128,384},{192,448},{256,0},{320,64},{384,128},{4... | collective-permute-start | bytes 1572872 | tf_op jit(solution)/shard_map/ppermute | solution.py:261
  90.7 13.2 %collective-permute-done.3.refs_12_ = bf16[2048,128]{1,0:T(8,128)(2,1)S(1)} collective-permute-done((bf16[2048,128]{1,0:T(8,128)(2,1)S(1)}, bf16[2048,128]{1,0:T(8,128)(2,1)S(1)}, u32[]{:S(2)}, u32[]{:S(2)}) %collective-permute-start.3) | collective-permute-done | bytes 524320 | tf_op jit(solution)/shard_map/ppermute | solution.py:261
  106.6 7.2 %collective-permute-start.10 = (bf16[1088,128]{1,0:T(8,128)(2,1)S(1)}, bf16[1088,128]{1,0:T(8,128)(2,1)S(1)}, u32[]{:S(2)}, u32[]{:S(2)}) collective-permute-start(bf16[1088,128]{1,0:T(8,128)(2,1)S(1)} %fusion.refs_0_), channel_id=1, source_target_pairs={{0,256},{64,320},{128,384},{192,448},{256,0},{320,64},{384,128},{4... | collective-permute-start | bytes 835592 | tf_op jit(solution)/shard_map/ppermute | solution.py:261
  113.8 4.0 %collective-permute-start.9 = (bf16[1088,128]{1,0:T(8,128)(2,1)S(1)}, bf16[1088,128]{1,0:T(8,128)(2,1)S(1)}, u32[]{:S(2)}, u32[]{:S(2)}) collective-permute-start(bf16[1088,128]{1,0:T(8,128)(2,1)S(1)} %fusion.refs_0_), channel_id=1, source_target_pairs={{0,192},{64,0},{128,64},{192,128},{256,448},{320,256},{384,320},{4... | collective-permute-start | bytes 835592 | tf_op jit(solution)/shard_map/ppermute | solution.py:257
  117.8 1.9 collective-permute-start.8
  119.7 2.5 %collective-permute-start.7 = (bf16[1088,128]{1,0:T(8,128)(2,1)S(1)}, bf16[1088,128]{1,0:T(8,128)(2,1)S(1)}, u32[]{:S(2)}, u32[]{:S(2)}) collective-permute-start(bf16[1088,128]{1,0:T(8,128)(2,1)S(1)} %fusion.refs_0_), channel_id=1, source_target_pairs={{0,64},{64,128},{128,192},{192,0},{256,320},{320,384},{384,448},{4... | collective-permute-start | bytes 835592 | tf_op jit(solution)/shard_map/ppermute | solution.py:257
  122.2 4.0 %collective-permute-start.13 = (bf16[1088,128]{1,0:T(8,128)(2,1)S(1)}, bf16[1088,128]{1,0:T(8,128)(2,1)S(1)}, u32[]{:S(2)}, u32[]{:S(2)}) collective-permute-start(bf16[1088,128]{1,0:T(8,128)(2,1)S(1)} %collective-permute-done.10.refs_4_), channel_id=1, source_target_pairs={{0,192},{64,0},{128,64},{192,128},{256,448},{320,256},{384,320},{4... | collective-permute-start | bytes 835592 | tf_op jit(solution)/shard_map/ppermute | solution.py:257
  126.3 3.6 %collective-permute-start.12 = (bf16[1088,128]{1,0:T(8,128)(2,1)S(1)}, bf16[1088,128]{1,0:T(8,128)(2,1)S(1)}, u32[]{:S(2)}, u32[]{:S(2)}) collective-permute-start(bf16[1088,128]{1,0:T(8,128)(2,1)S(1)} %collective-permute-done.10.refs_4_), channel_id=1, source_target_pairs={{0,128},{64,192},{128,0},{192,64},{256,384},{320,448},{384,256},{4... | collective-permute-start | bytes 835592 | tf_op jit(solution)/shard_map/ppermute | solution.py:257
  129.9 1.9 collective-permute-start.11
  131.9 3.2 %collective-permute-done.12.refs_6_ = bf16[1088,128]{1,0:T(8,128)(2,1)S(1)} collective-permute-done((bf16[1088,128]{1,0:T(8,128)(2,1)S(1)}, bf16[1088,128]{1,0:T(8,128)(2,1)S(1)}, u32[]{:S(2)}, u32[]{:S(2)}) %collective-permute-start.12) | collective-permute-done | bytes 278560 | tf_op jit(solution)/shard_map/ppermute | solution.py:257
  135.1 8.5 %collective-permute-done.11.refs_5_ = bf16[1088,128]{1,0:T(8,128)(2,1)S(1)} collective-permute-done((bf16[1088,128]{1,0:T(8,128)(2,1)S(1)}, bf16[1088,128]{1,0:T(8,128)(2,1)S(1)}, u32[]{:S(2)}, u32[]{:S(2)}) %collective-permute-start.11) | collective-permute-done | bytes 278560 | tf_op jit(solution)/shard_map/ppermute | solution.py:257
  145.2 49.1 %all_to_all.10.chunks_ref = bf16[64,64,128]{2,1,0:T(8,128)(2,1)S(1)} all-to-all(bf16[64,64,128]{2,1,0:T(8,128)(2,1)S(1)} %down.1), channel_id=1, replica_groups=mesh['pipe'=8,'expert'=64] {'expert'}, dimensions={0} | all-to-all | bytes 2097152 | tf_op jit(solution)/shard_map/all_to_all | solution.py:287
  194.3 1.7 combine.1
  (49 shorter events, 17.9 us)
Async XLA Ops:
  0.0 1.2 copy-start.11
  2.9 1.3 copy-start
  4.2 14.7 %copy-start.5 = (bf16[1,3584,128]{2,1,0:T(8,128)(2,1)S(1)}, bf16[1,3584,128]{2,1,0:T(8,128)(2,1)}, u32[]{:S(2)}) copy-start(bf16[1,3584,128]{2,1,0:T(8,128)(2,1)} %param.9) | copy-start | bytes 2752516
  4.2 62.2 %all-to-all-start = ((bf16[64,120,128]{2,1,0:T(8,128)(2,1)}), bf16[64,120,128]{2,1,0:T(8,128)(2,1)S(1)}, u32[]{:S(2)}, u32[]{:S(2)}) async-start(bf16[64,120,128]{2,1,0:T(8,128)(2,1)} %copy-done), calls=%async_computation | async-start | bytes 3932160 | tf_op jit(solution)/shard_map/all_to_all | solution.py:272
  18.9 1.2 copy-start.7
  22.3 20.3 %collective-permute-start = (bf16[2816,128]{1,0:T(8,128)(2,1)S(1)}, bf16[2816,128]{1,0:T(8,128)(2,1)S(1)}, u32[]{:S(2)}, u32[]{:S(2)}) collective-permute-start(bf16[2816,128]{1,0:T(8,128)(2,1)S(1)} %get-tuple-element.15), channel_id=1, source_target_pairs={{0,64},{64,128},{128,192},{192,0},{256,320},{320,384},{384,448},{4... | collective-permute-start | bytes 2162696 | tf_op jit(solution)/shard_map/ppermute | solution.py:257
  25.4 33.7 %collective-permute-start.1 = (bf16[2816,128]{1,0:T(8,128)(2,1)S(1)}, bf16[2816,128]{1,0:T(8,128)(2,1)S(1)}, u32[]{:S(2)}, u32[]{:S(2)}) collective-permute-start(bf16[2816,128]{1,0:T(8,128)(2,1)S(1)} %get-tuple-element.16), channel_id=1, source_target_pairs={{0,128},{64,192},{128,0},{192,64},{256,384},{320,448},{384,256},{4... | collective-permute-start | bytes 2162696 | tf_op jit(solution)/shard_map/ppermute | solution.py:257
  29.7 30.6 %collective-permute-start.2 = (bf16[2816,128]{1,0:T(8,128)(2,1)S(1)}, bf16[2816,128]{1,0:T(8,128)(2,1)S(1)}, u32[]{:S(2)}, u32[]{:S(2)}) collective-permute-start(bf16[2816,128]{1,0:T(8,128)(2,1)S(1)} %get-tuple-element.17), channel_id=1, source_target_pairs={{0,192},{64,0},{128,64},{192,128},{256,448},{320,256},{384,320},{4... | collective-permute-start | bytes 2162696 | tf_op jit(solution)/shard_map/ppermute | solution.py:257
  70.6 34.2 %collective-permute-start.4 = (bf16[1088,256]{1,0:T(8,128)(2,1)}, bf16[1088,256]{1,0:T(8,128)(2,1)}, u32[]{:S(2)}, u32[]{:S(2)}) collective-permute-start(bf16[1088,256]{1,0:T(8,128)(2,1)} %get-tuple-element.19), channel_id=1, source_target_pairs={{0,128},{64,192},{128,0},{192,64},{256,384},{320,448},{384,256},{4... | collective-permute-start | bytes 1671176 | tf_op jit(solution)/shard_map/ppermute | solution.py:257
  75.2 29.6 %collective-permute-start.5 = (bf16[1088,256]{1,0:T(8,128)(2,1)}, bf16[1088,256]{1,0:T(8,128)(2,1)}, u32[]{:S(2)}, u32[]{:S(2)}) collective-permute-start(bf16[1088,256]{1,0:T(8,128)(2,1)} %get-tuple-element.20), channel_id=1, source_target_pairs={{0,192},{64,0},{128,64},{192,128},{256,448},{320,256},{384,320},{4... | collective-permute-start | bytes 1671176 | tf_op jit(solution)/shard_map/ppermute | solution.py:257
  78.0 26.8 %collective-permute-start.6 = (bf16[1088,256]{1,0:T(8,128)(2,1)}, bf16[1088,256]{1,0:T(8,128)(2,1)}, u32[]{:S(2)}, u32[]{:S(2)}) collective-permute-start(bf16[1088,256]{1,0:T(8,128)(2,1)} %get-tuple-element.21), channel_id=1, source_target_pairs={{0,64},{64,128},{128,192},{192,0},{256,320},{320,384},{384,448},{4... | collective-permute-start | bytes 1671176 | tf_op jit(solution)/shard_map/ppermute | solution.py:257
  82.6 21.3 %copy-start.6 = (bf16[1,3584,128]{2,1,0:T(8,128)(2,1)S(1)}, bf16[1,3584,128]{2,1,0:T(8,128)(2,1)}, u32[]{:S(2)}) copy-start(bf16[1,3584,128]{2,1,0:T(8,128)(2,1)} %param.9) | copy-start | bytes 2752516
  82.6 21.3 %copy-start.8 = (bf16[1,3584,128]{2,1,0:T(8,128)(2,1)S(1)}, bf16[1,3584,128]{2,1,0:T(8,128)(2,1)}, u32[]{:S(2)}) copy-start(bf16[1,3584,128]{2,1,0:T(8,128)(2,1)} %param.10) | copy-start | bytes 2752516
  82.6 21.2 %collective-permute-start.3 = (bf16[2048,128]{1,0:T(8,128)(2,1)S(1)}, bf16[2048,128]{1,0:T(8,128)(2,1)S(1)}, u32[]{:S(2)}, u32[]{:S(2)}) collective-permute-start(bf16[2048,128]{1,0:T(8,128)(2,1)S(1)} %swap.1), channel_id=1, source_target_pairs={{0,256},{64,320},{128,384},{192,448},{256,0},{320,64},{384,128},{4... | collective-permute-start | bytes 1572872 | tf_op jit(solution)/shard_map/ppermute | solution.py:261
  106.5 37.1 %copy-start.4 = (bf16[2816,128]{1,0:T(8,128)(2,1)S(1)}, bf16[2816,128]{1,0:T(8,128)(2,1)}, u32[]{:S(2)}) copy-start(bf16[2816,128]{1,0:T(8,128)(2,1)} %copy-done.1) | copy-start | bytes 2162692
  106.6 15.6 %collective-permute-start.10 = (bf16[1088,128]{1,0:T(8,128)(2,1)S(1)}, bf16[1088,128]{1,0:T(8,128)(2,1)S(1)}, u32[]{:S(2)}, u32[]{:S(2)}) collective-permute-start(bf16[1088,128]{1,0:T(8,128)(2,1)S(1)} %fusion.refs_0_), channel_id=1, source_target_pairs={{0,256},{64,320},{128,384},{192,448},{256,0},{320,64},{384,128},{4... | collective-permute-start | bytes 835592 | tf_op jit(solution)/shard_map/ppermute | solution.py:261
  113.8 16.1 %collective-permute-start.9 = (bf16[1088,128]{1,0:T(8,128)(2,1)S(1)}, bf16[1088,128]{1,0:T(8,128)(2,1)S(1)}, u32[]{:S(2)}, u32[]{:S(2)}) collective-permute-start(bf16[1088,128]{1,0:T(8,128)(2,1)S(1)} %fusion.refs_0_), channel_id=1, source_target_pairs={{0,192},{64,0},{128,64},{192,128},{256,448},{320,256},{384,320},{4... | collective-permute-start | bytes 835592 | tf_op jit(solution)/shard_map/ppermute | solution.py:257
  117.8 14.1 %collective-permute-start.8 = (bf16[1088,128]{1,0:T(8,128)(2,1)S(1)}, bf16[1088,128]{1,0:T(8,128)(2,1)S(1)}, u32[]{:S(2)}, u32[]{:S(2)}) collective-permute-start(bf16[1088,128]{1,0:T(8,128)(2,1)S(1)} %fusion.refs_0_), channel_id=1, source_target_pairs={{0,128},{64,192},{128,0},{192,64},{256,384},{320,448},{384,256},{4... | collective-permute-start | bytes 835592 | tf_op jit(solution)/shard_map/ppermute | solution.py:257
  119.7 12.1 %collective-permute-start.7 = (bf16[1088,128]{1,0:T(8,128)(2,1)S(1)}, bf16[1088,128]{1,0:T(8,128)(2,1)S(1)}, u32[]{:S(2)}, u32[]{:S(2)}) collective-permute-start(bf16[1088,128]{1,0:T(8,128)(2,1)S(1)} %fusion.refs_0_), channel_id=1, source_target_pairs={{0,64},{64,128},{128,192},{192,0},{256,320},{320,384},{384,448},{4... | collective-permute-start | bytes 835592 | tf_op jit(solution)/shard_map/ppermute | solution.py:257
  122.2 9.6 %collective-permute-start.13 = (bf16[1088,128]{1,0:T(8,128)(2,1)S(1)}, bf16[1088,128]{1,0:T(8,128)(2,1)S(1)}, u32[]{:S(2)}, u32[]{:S(2)}) collective-permute-start(bf16[1088,128]{1,0:T(8,128)(2,1)S(1)} %collective-permute-done.10.refs_4_), channel_id=1, source_target_pairs={{0,192},{64,0},{128,64},{192,128},{256,448},{320,256},{384,320},{4... | collective-permute-start | bytes 835592 | tf_op jit(solution)/shard_map/ppermute | solution.py:257
  126.3 8.8 %collective-permute-start.12 = (bf16[1088,128]{1,0:T(8,128)(2,1)S(1)}, bf16[1088,128]{1,0:T(8,128)(2,1)S(1)}, u32[]{:S(2)}, u32[]{:S(2)}) collective-permute-start(bf16[1088,128]{1,0:T(8,128)(2,1)S(1)} %collective-permute-done.10.refs_4_), channel_id=1, source_target_pairs={{0,128},{64,192},{128,0},{192,64},{256,384},{320,448},{384,256},{4... | collective-permute-start | bytes 835592 | tf_op jit(solution)/shard_map/ppermute | solution.py:257
  129.9 13.7 %collective-permute-start.11 = (bf16[1088,128]{1,0:T(8,128)(2,1)S(1)}, bf16[1088,128]{1,0:T(8,128)(2,1)S(1)}, u32[]{:S(2)}, u32[]{:S(2)}) collective-permute-start(bf16[1088,128]{1,0:T(8,128)(2,1)S(1)} %collective-permute-done.10.refs_4_), channel_id=1, source_target_pairs={{0,64},{64,128},{128,192},{192,0},{256,320},{320,384},{384,448},{4... | collective-permute-start | bytes 835592 | tf_op jit(solution)/shard_map/ppermute | solution.py:257
  145.1 49.1 %copy-start.14 = (s32[128,8]{0,1:T(8,128)S(1)}, s32[128,8]{0,1:T(8,128)}, u32[]{:S(2)}) copy-start(s32[128,8]{0,1:T(8,128)} %param.7) | copy-start | bytes 12292
  145.2 49.1 %copy-start.15 = (f32[128,8]{0,1:T(8,128)S(1)}, f32[128,8]{0,1:T(8,128)}, u32[]{:S(2)}) copy-start(f32[128,8]{0,1:T(8,128)} %param.8) | copy-start | bytes 12292
  (7 other events, 6.6 us)

commit v5 on v3

--- a/solution.py
+++ b/solution.py
@@ -174,12 +174,11 @@
 
 
 def down_kernel(x_ref, z_ref, *refs):
-    near_ref, far_ref, own_ref, p1, p2, p3, other_ref, out_ref = refs
+    hiddens, (own_ref, p1, p2, p3, other_ref, out_ref) = refs[: 2 * X], refs[2 * X :]
     experts = out_ref.shape[0]
     rows = own_ref.shape[0] // 2
     depth = rows // 4
-    source = [lax.rem(x_ref[0] + X - d, X) for d in range(X)]
-    hidden = jnp.concatenate([ref[s] for ref in (near_ref, far_ref) for s in source], axis=1)
+    hidden = jnp.concatenate([ref[...] for ref in hiddens], axis=1)
     blocks = []
     for ref in (own_ref, p1, p2, p3):
         base = ref.shape[0] - 2 * rows + z_ref[0] * rows
@@ -207,10 +206,10 @@
     out_ref[:, 48:64, :] = jnp.concatenate([halves, tail], axis=1).astype(BF)
 
 
-def down(x, z, near, far, own, packs, other, experts):
+def down(x, z, hiddens, own, packs, other, experts):
     shape = jax.ShapeDtypeStruct((experts, 64, LANES), BF)
-    specs = [in_smem()] * 2 + [in_vmem()] * (X + 3)
-    return call(down_kernel, "down", shape, specs)(x, z, near, far, own, *packs, other)
+    specs = [in_smem()] * 2 + [in_vmem()] * (2 * X + X + 1)
+    return call(down_kernel, "down", shape, specs)(x, z, *hiddens, own, *packs, other)
 
 
 def combine_kernel(x_ref, ids_ref, scale_ref, chunks_ref, out_ref):
@@ -288,11 +287,12 @@
     packs = [shift(sent[d - 1], d) for d in range(1, X)]
     other_down = cross(swap(z, own_down, packs))
     arrived = across(project(x, chunks, w_gate, w_up, packs))
+    arrived, other_down = lax.optimization_barrier((arrived, other_down))
     hidden = activate(arrived)
     swapped = cross(hidden)
-    near = across(jnp.broadcast_to(hidden[None], (X, *hidden.shape)))
-    far = across(jnp.broadcast_to(swapped[None], (X, *swapped.shape)))
-    output = down(x, z, near, far, own_down, packs, other_down, groups)
+    hiddens = [hidden] + [shift(hidden, d) for d in range(1, X)]
+    hiddens += [swapped] + [shift(swapped, d) for d in range(1, X)]
+    output = down(x, z, hiddens, own_down, packs, other_down, groups)
     returned = lax.all_to_all(output, "expert", split_axis=0, concat_axis=0, tiled=True)
     return combine(x, ids, scale, returned, tokens.shape[1] // (2 * X))
 

time: 207 us -> 196 us (0.947)
  blocking collectives: 67.2 us -> 44.6 us
  starting transfers between devices: 45.3 us -> 62.6 us
  waiting for transfers between devices: 66.7 us -> 62.5 us
    all_to_all x1 -> x0, blocking collectives: 31.8 us -> none  [across(): lax.all_to_all(value, 'pipe', split_axis=0, concat_axis=0, axis_index_gro...]
    ppermute x2, waiting for transfers between devices: 33.9 us -> 13.3 us  [cross(): lax.ppermute(value, 'pipe', [(p, (p + X) % (2 * X)) for p in range(2 * X)])]
    ppermute x3 -> x9, starting transfers between devices: 10.5 us -> 27.9 us  [shift(): return lax.ppermute(value, 'pipe', pairs)]
    ppermute x3 -> x9, waiting for transfers between devices: 27.5 us -> 39.6 us  [shift(): return lax.ppermute(value, 'pipe', pairs)]
    all_to_all x1, blocking collectives: 35.4 us -> 44.6 us  [body(): lax.all_to_all(output, 'expert', split_axis=0, concat_axis=0, tiled=True)]
    all_to_all x2 -> x1, starting transfers between devices: 7.9 us -> 4.01 us  [across(): lax.all_to_all(value, 'pipe', split_axis=0, concat_axis=0, axis_index_gro...]
    ppermute x2, starting transfers between devices: 12.1 us -> 16 us  [cross(): lax.ppermute(value, 'pipe', [(p, (p + X) % (2 * X)) for p in range(2 * X)])]
    all_to_all x2 -> x1, waiting for transfers between devices: 0.01 us -> 3.68 us  [across(): lax.all_to_all(value, 'pipe', split_axis=0, concat_axis=0, axis_index_gro...]
  transfers between devices with their start and end apart: 8 -> 13, of which waited for: 6 -> 8; matrix products, arithmetic and copies ran while one was open for 0% -> 0% of each run, Pallas kernels for 0% -> 0%
where the time goes in v5:
time: 196 us; the launch traced here: 195 us
  starting transfers between devices  62.6 us (32%)
  waiting for transfers between devices  62.5 us (32%)
  blocking collectives  44.6 us (23%)
  local copies, waits for them, and re-layouts  15.8 us (8%)
  Pallas kernels  9.05 us (5%)
    all_to_all x1, blocking collectives, body(): lax.all_to_all(output, 'expert', split_axis=0, concat_axis=0, tiled=True)  44.6 us
    ppermute x9, waiting for transfers between devices, shift(): return lax.ppermute(value, 'pipe', pairs)  39.6 us
    ppermute x9, starting transfers between devices, shift(): return lax.ppermute(value, 'pipe', pairs)  27.9 us
    ppermute x2, starting transfers between devices, cross(): lax.ppermute(value, 'pipe', [(p, (p + X) % (2 * X)) for p in range(2 * X)])  16 us
    unnamed x40, local copies, waits for them, and re-layouts  15 us
    all_to_all x1, starting transfers between devices, body(): lax.all_to_all(buffer, 'expert', split_axis=0, concat_axis=0, tiled=True)  14.7 us
    ppermute x2, waiting for transfers between devices, cross(): lax.ppermute(value, 'pipe', [(p, (p + X) % (2 * X)) for p in range(2 * X)])  13.3 us
    all_to_all x1, waiting for transfers between devices, body(): lax.all_to_all(buffer, 'expert', split_axis=0, concat_axis=0, tiled=True)  5.9 us
  transfers between devices with their start and end apart: 13, of which 8 were waited for; matrix products, arithmetic and copies ran while one was open for 0% of the time, Pallas kernels for 0%

profile of v5, /device:TPU:1, one launch (start us, length us, event | category | flops | bytes accessed | tf_op | source)
XLA Modules:
  0.0 194.7 jit_solution(4591132658730144901)
XLA Ops:
  1.9 2.3 %dispatch.1 = bf16[64,120,128]{2,1,0:T(8,128)(2,1)} custom-call(s32[1]{0:T(128)} %bitcast.x_ref, s32[8,128]{1,0:T(8,128)S(1)} %bitcast.12, bf16[128,3584]{1,0:T(8,128)(2,1)S(1)} %copy-done.13), custom_call_target="tpu_custom_call" | custom-call | tf_op jit(solution)/shard_map/dispatch/pallas_call | solution.py:77
  4.2 14.7 %all-to-all-start = ((bf16[64,120,128]{2,1,0:T(8,128)(2,1)}), bf16[64,120,128]{2,1,0:T(8,128)(2,1)S(1)}, u32[]{:S(2)}, u32[]{:S(2)}) async-start(bf16[64,120,128]{2,1,0:T(8,128)(2,1)} %dispatch.1), calls=%async_computation | async-start | bytes 3932160 | tf_op jit(solution)/shard_map/all_to_all | solution.py:285
  21.6 3.1 %collective-permute-start = (bf16[2816,128]{1,0:T(8,128)(2,1)S(1)}, bf16[2816,128]{1,0:T(8,128)(2,1)S(1)}, u32[]{:S(2)}, u32[]{:S(2)}) collective-permute-start(bf16[2816,128]{1,0:T(8,128)(2,1)S(1)} %get-tuple-element.11), channel_id=1, source_target_pairs={{0,64},{64,128},{128,192},{192,0},{256,320},{320,384},{384,448},{4... | collective-permute-start | bytes 2162696 | tf_op jit(solution)/shard_map/ppermute | solution.py:265
  24.7 4.4 %collective-permute-start.1 = (bf16[2816,128]{1,0:T(8,128)(2,1)S(1)}, bf16[2816,128]{1,0:T(8,128)(2,1)S(1)}, u32[]{:S(2)}, u32[]{:S(2)}) collective-permute-start(bf16[2816,128]{1,0:T(8,128)(2,1)S(1)} %get-tuple-element.12), channel_id=1, source_target_pairs={{0,128},{64,192},{128,0},{192,64},{256,384},{320,448},{384,256},{4... | collective-permute-start | bytes 2162696 | tf_op jit(solution)/shard_map/ppermute | solution.py:265
  29.1 3.1 %collective-permute-start.2 = (bf16[2816,128]{1,0:T(8,128)(2,1)S(1)}, bf16[2816,128]{1,0:T(8,128)(2,1)S(1)}, u32[]{:S(2)}, u32[]{:S(2)}) collective-permute-start(bf16[2816,128]{1,0:T(8,128)(2,1)S(1)} %get-tuple-element.13), channel_id=1, source_target_pairs={{0,192},{64,0},{128,64},{192,128},{256,448},{320,256},{384,320},{4... | collective-permute-start | bytes 2162696 | tf_op jit(solution)/shard_map/ppermute | solution.py:265
  32.1 9.8 %collective-permute-done.refs_0_.p1.refs_9_ = bf16[2816,128]{1,0:T(8,128)(2,1)S(1)} collective-permute-done((bf16[2816,128]{1,0:T(8,128)(2,1)S(1)}, bf16[2816,128]{1,0:T(8,128)(2,1)S(1)}, u32[]{:S(2)}, u32[]{:S(2)}) %collective-permute-start) | collective-permute-done | bytes 720928 | tf_op jit(solution)/shard_map/ppermute | solution.py:265
  41.9 16.4 %collective-permute-done.1.refs_1_.p2.refs_10_ = bf16[2816,128]{1,0:T(8,128)(2,1)S(1)} collective-permute-done((bf16[2816,128]{1,0:T(8,128)(2,1)S(1)}, bf16[2816,128]{1,0:T(8,128)(2,1)S(1)}, u32[]{:S(2)}, u32[]{:S(2)}) %collective-permute-start.1) | collective-permute-done | bytes 720928 | tf_op jit(solution)/shard_map/ppermute | solution.py:265
  60.5 5.9 %all-to-all-done.chunks_ref = bf16[64,120,128]{2,1,0:T(8,128)(2,1)S(1)} async-done(((bf16[64,120,128]{2,1,0:T(8,128)(2,1)}), bf16[64,120,128]{2,1,0:T(8,128)(2,1)S(1)}, u32[]{:S(2)}, u32[]{:S(2)}) %all-to-all-start) | async-done | bytes 1966112 | tf_op jit(solution)/shard_map/all_to_all | solution.py:285
  71.0 2.8 %project.1 = bf16[4,1088,256]{2,1,0:T(8,128)(2,1)S(1)} custom-call(s32[1]{0:T(128)} %bitcast.x_ref, bf16[64,120,128]{2,1,0:T(8,128)(2,1)S(1)} %all-to-all-done.chunks_ref, bf16[3584,128]{1,0:T(8,128)(2,1)S(1)} %bitcast.8, bf16[3584,128]{1,0:T(8,128)(2,1)S(1)} %bitcast.10, bf16[2816,128]{1,0:T(8,128)(2,1)S(1)} %collective-permute-done.refs_0_.p1.refs_9_, ...), custom_call_target="tpu_custom_call" | custom-call | tf_op jit(solution)/shard_map/project/pallas_call | solution.py:158
  75.2 4.0 %all-to-all-start.1 = ((bf16[4,1088,256]{2,1,0:T(8,128)(2,1)}), bf16[4,1088,256]{2,1,0:T(8,128)(2,1)S(1)}, u32[]{:S(2)}, u32[]{:S(2)}) async-start(bf16[4,1088,256]{2,1,0:T(8,128)(2,1)} %copy-done), calls=%async_computation.1 | async-start | bytes 4456448 | tf_op jit(solution)/shard_map/all_to_all | solution.py:274
  81.5 7.9 %collective-permute-start.3 = (bf16[2048,128]{1,0:T(8,128)(2,1)S(1)}, bf16[2048,128]{1,0:T(8,128)(2,1)S(1)}, u32[]{:S(2)}, u32[]{:S(2)}) collective-permute-start(bf16[2048,128]{1,0:T(8,128)(2,1)S(1)} %swap.1), channel_id=1, source_target_pairs={{0,256},{64,320},{128,384},{192,448},{256,0},{320,64},{384,128},{4... | collective-permute-start | bytes 1572872 | tf_op jit(solution)/shard_map/ppermute | solution.py:269
  89.4 13.3 %collective-permute-done.3.refs_12_ = bf16[2048,128]{1,0:T(8,128)(2,1)S(1)} collective-permute-done((bf16[2048,128]{1,0:T(8,128)(2,1)S(1)}, bf16[2048,128]{1,0:T(8,128)(2,1)S(1)}, u32[]{:S(2)}, u32[]{:S(2)}) %collective-permute-start.3) | collective-permute-done | bytes 524320 | tf_op jit(solution)/shard_map/ppermute | solution.py:269
  103.5 3.7 %all-to-all-done.1.parts_ref = bf16[4,1088,256]{2,1,0:T(8,128)(2,1)S(1)} async-done(((bf16[4,1088,256]{2,1,0:T(8,128)(2,1)}), bf16[4,1088,256]{2,1,0:T(8,128)(2,1)S(1)}, u32[]{:S(2)}, u32[]{:S(2)}) %all-to-all-start.1) | async-done | bytes 2228256 | tf_op jit(solution)/shard_map/all_to_all | solution.py:274
  107.6 8.1 %collective-permute-start.7 = (bf16[1088,128]{1,0:T(8,128)(2,1)S(1)}, bf16[1088,128]{1,0:T(8,128)(2,1)S(1)}, u32[]{:S(2)}, u32[]{:S(2)}) collective-permute-start(bf16[1088,128]{1,0:T(8,128)(2,1)S(1)} %activate.1.refs_0_), channel_id=1, source_target_pairs={{0,256},{64,320},{128,384},{192,448},{256,0},{320,64},{384,128},{4... | collective-permute-start | bytes 835592 | tf_op jit(solution)/shard_map/ppermute | solution.py:269
  115.7 2.8 %collective-permute-start.6 = (bf16[1088,128]{1,0:T(8,128)(2,1)S(1)}, bf16[1088,128]{1,0:T(8,128)(2,1)S(1)}, u32[]{:S(2)}, u32[]{:S(2)}) collective-permute-start(bf16[1088,128]{1,0:T(8,128)(2,1)S(1)} %activate.1.refs_0_), channel_id=1, source_target_pairs={{0,192},{64,0},{128,64},{192,128},{256,448},{320,256},{384,320},{4... | collective-permute-start | bytes 835592 | tf_op jit(solution)/shard_map/ppermute | solution.py:265
  118.5 3.1 %collective-permute-start.5 = (bf16[1088,128]{1,0:T(8,128)(2,1)S(1)}, bf16[1088,128]{1,0:T(8,128)(2,1)S(1)}, u32[]{:S(2)}, u32[]{:S(2)}) collective-permute-start(bf16[1088,128]{1,0:T(8,128)(2,1)S(1)} %activate.1.refs_0_), channel_id=1, source_target_pairs={{0,128},{64,192},{128,0},{192,64},{256,384},{320,448},{384,256},{4... | collective-permute-start | bytes 835592 | tf_op jit(solution)/shard_map/ppermute | solution.py:265
  121.6 1.9 collective-permute-start.4
  123.6 4.6 %collective-permute-start.10 = (bf16[1088,128]{1,0:T(8,128)(2,1)S(1)}, bf16[1088,128]{1,0:T(8,128)(2,1)S(1)}, u32[]{:S(2)}, u32[]{:S(2)}) collective-permute-start(bf16[1088,128]{1,0:T(8,128)(2,1)S(1)} %collective-permute-done.7.refs_4_), channel_id=1, source_target_pairs={{0,192},{64,0},{128,64},{192,128},{256,448},{320,256},{384,320},{4... | collective-permute-start | bytes 835592 | tf_op jit(solution)/shard_map/ppermute | solution.py:265
  128.2 2.5 %collective-permute-start.9 = (bf16[1088,128]{1,0:T(8,128)(2,1)S(1)}, bf16[1088,128]{1,0:T(8,128)(2,1)S(1)}, u32[]{:S(2)}, u32[]{:S(2)}) collective-permute-start(bf16[1088,128]{1,0:T(8,128)(2,1)S(1)} %collective-permute-done.7.refs_4_), channel_id=1, source_target_pairs={{0,128},{64,192},{128,0},{192,64},{256,384},{320,448},{384,256},{4... | collective-permute-start | bytes 835592 | tf_op jit(solution)/shard_map/ppermute | solution.py:265
  130.7 2.5 %collective-permute-start.8 = (bf16[1088,128]{1,0:T(8,128)(2,1)S(1)}, bf16[1088,128]{1,0:T(8,128)(2,1)S(1)}, u32[]{:S(2)}, u32[]{:S(2)}) collective-permute-start(bf16[1088,128]{1,0:T(8,128)(2,1)S(1)} %collective-permute-done.7.refs_4_), channel_id=1, source_target_pairs={{0,64},{64,128},{128,192},{192,0},{256,320},{320,384},{384,448},{4... | collective-permute-start | bytes 835592 | tf_op jit(solution)/shard_map/ppermute | solution.py:265
  133.2 7.4 %collective-permute-done.10.refs_7_ = bf16[1088,128]{1,0:T(8,128)(2,1)S(1)} collective-permute-done((bf16[1088,128]{1,0:T(8,128)(2,1)S(1)}, bf16[1088,128]{1,0:T(8,128)(2,1)S(1)}, u32[]{:S(2)}, u32[]{:S(2)}) %collective-permute-start.10) | collective-permute-done | bytes 278560 | tf_op jit(solution)/shard_map/ppermute | solution.py:265
  140.6 5.5 %collective-permute-done.8.refs_5_ = bf16[1088,128]{1,0:T(8,128)(2,1)S(1)} collective-permute-done((bf16[1088,128]{1,0:T(8,128)(2,1)S(1)}, bf16[1088,128]{1,0:T(8,128)(2,1)S(1)}, u32[]{:S(2)}, u32[]{:S(2)}) %collective-permute-start.8) | collective-permute-done | bytes 278560 | tf_op jit(solution)/shard_map/ppermute | solution.py:265
  147.7 44.6 %all_to_all.15.chunks_ref = bf16[64,64,128]{2,1,0:T(8,128)(2,1)S(1)} all-to-all(bf16[64,64,128]{2,1,0:T(8,128)(2,1)S(1)} %down.1), channel_id=1, replica_groups=mesh['pipe'=8,'expert'=64] {'expert'}, dimensions={0} | all-to-all | bytes 2097152 | tf_op jit(solution)/shard_map/all_to_all | solution.py:296
  192.2 1.7 combine.1
  (51 shorter events, 18.4 us)
Async XLA Ops:
  0.0 1.2 copy-start.13
  4.2 14.7 %copy-start.9 = (bf16[1,3584,128]{2,1,0:T(8,128)(2,1)S(1)}, bf16[1,3584,128]{2,1,0:T(8,128)(2,1)}, u32[]{:S(2)}) copy-start(bf16[1,3584,128]{2,1,0:T(8,128)(2,1)} %param.9) | copy-start | bytes 2752516
  4.2 62.2 %all-to-all-start = ((bf16[64,120,128]{2,1,0:T(8,128)(2,1)}), bf16[64,120,128]{2,1,0:T(8,128)(2,1)S(1)}, u32[]{:S(2)}, u32[]{:S(2)}) async-start(bf16[64,120,128]{2,1,0:T(8,128)(2,1)} %dispatch.1), calls=%async_computation | async-start | bytes 3932160 | tf_op jit(solution)/shard_map/all_to_all | solution.py:285
  18.9 1.2 copy-start.11
  20.1 1.2 copy-start.14
  21.6 20.4 %collective-permute-start = (bf16[2816,128]{1,0:T(8,128)(2,1)S(1)}, bf16[2816,128]{1,0:T(8,128)(2,1)S(1)}, u32[]{:S(2)}, u32[]{:S(2)}) collective-permute-start(bf16[2816,128]{1,0:T(8,128)(2,1)S(1)} %get-tuple-element.11), channel_id=1, source_target_pairs={{0,64},{64,128},{128,192},{192,0},{256,320},{320,384},{384,448},{4... | collective-permute-start | bytes 2162696 | tf_op jit(solution)/shard_map/ppermute | solution.py:265
  24.7 33.7 %collective-permute-start.1 = (bf16[2816,128]{1,0:T(8,128)(2,1)S(1)}, bf16[2816,128]{1,0:T(8,128)(2,1)S(1)}, u32[]{:S(2)}, u32[]{:S(2)}) collective-permute-start(bf16[2816,128]{1,0:T(8,128)(2,1)S(1)} %get-tuple-element.12), channel_id=1, source_target_pairs={{0,128},{64,192},{128,0},{192,64},{256,384},{320,448},{384,256},{4... | collective-permute-start | bytes 2162696 | tf_op jit(solution)/shard_map/ppermute | solution.py:265
  29.1 30.6 %collective-permute-start.2 = (bf16[2816,128]{1,0:T(8,128)(2,1)S(1)}, bf16[2816,128]{1,0:T(8,128)(2,1)S(1)}, u32[]{:S(2)}, u32[]{:S(2)}) collective-permute-start(bf16[2816,128]{1,0:T(8,128)(2,1)S(1)} %get-tuple-element.13), channel_id=1, source_target_pairs={{0,192},{64,0},{128,64},{192,128},{256,448},{320,256},{384,320},{4... | collective-permute-start | bytes 2162696 | tf_op jit(solution)/shard_map/ppermute | solution.py:265
  68.6 1.2 copy-start.10
  73.8 1.4 copy-start
  75.2 32.0 %all-to-all-start.1 = ((bf16[4,1088,256]{2,1,0:T(8,128)(2,1)}), bf16[4,1088,256]{2,1,0:T(8,128)(2,1)S(1)}, u32[]{:S(2)}, u32[]{:S(2)}) async-start(bf16[4,1088,256]{2,1,0:T(8,128)(2,1)} %copy-done), calls=%async_computation.1 | async-start | bytes 4456448 | tf_op jit(solution)/shard_map/all_to_all | solution.py:274
  81.5 21.3 %collective-permute-start.3 = (bf16[2048,128]{1,0:T(8,128)(2,1)S(1)}, bf16[2048,128]{1,0:T(8,128)(2,1)S(1)}, u32[]{:S(2)}, u32[]{:S(2)}) collective-permute-start(bf16[2048,128]{1,0:T(8,128)(2,1)S(1)} %swap.1), channel_id=1, source_target_pairs={{0,256},{64,320},{128,384},{192,448},{256,0},{320,64},{384,128},{4... | collective-permute-start | bytes 1572872 | tf_op jit(solution)/shard_map/ppermute | solution.py:269
  107.2 38.9 %copy-start.4 = (bf16[2816,128]{1,0:T(8,128)(2,1)S(1)}, bf16[2816,128]{1,0:T(8,128)(2,1)}, u32[]{:S(2)}) copy-start(bf16[2816,128]{1,0:T(8,128)(2,1)} %copy-done.1) | copy-start | bytes 2162692
  107.2 38.9 %copy-start.8 = (bf16[2816,128]{1,0:T(8,128)(2,1)S(1)}, bf16[2816,128]{1,0:T(8,128)(2,1)}, u32[]{:S(2)}) copy-start(bf16[2816,128]{1,0:T(8,128)(2,1)} %copy-done.5) | copy-start | bytes 2162692
  107.2 38.9 %copy-start.16 = (bf16[2048,128]{1,0:T(8,128)(2,1)S(1)}, bf16[2048,128]{1,0:T(8,128)(2,1)}, u32[]{:S(2)}) copy-start(bf16[2048,128]{1,0:T(8,128)(2,1)} %copy-done.15) | copy-start | bytes 1572868
  107.6 84.6 %copy-start.18 = (s32[128,8]{0,1:T(8,128)S(1)}, s32[128,8]{0,1:T(8,128)}, u32[]{:S(2)}) copy-start(s32[128,8]{0,1:T(8,128)} %param.7) | copy-start | bytes 12292
  107.6 84.6 %copy-start.19 = (f32[128,8]{0,1:T(8,128)S(1)}, f32[128,8]{0,1:T(8,128)}, u32[]{:S(2)}) copy-start(f32[128,8]{0,1:T(8,128)} %param.8) | copy-start | bytes 12292
  107.6 15.9 %collective-permute-start.7 = (bf16[1088,128]{1,0:T(8,128)(2,1)S(1)}, bf16[1088,128]{1,0:T(8,128)(2,1)S(1)}, u32[]{:S(2)}, u32[]{:S(2)}) collective-permute-start(bf16[1088,128]{1,0:T(8,128)(2,1)S(1)} %activate.1.refs_0_), channel_id=1, source_target_pairs={{0,256},{64,320},{128,384},{192,448},{256,0},{320,64},{384,128},{4... | collective-permute-start | bytes 835592 | tf_op jit(solution)/shard_map/ppermute | solution.py:269
  115.7 14.9 %collective-permute-start.6 = (bf16[1088,128]{1,0:T(8,128)(2,1)S(1)}, bf16[1088,128]{1,0:T(8,128)(2,1)S(1)}, u32[]{:S(2)}, u32[]{:S(2)}) collective-permute-start(bf16[1088,128]{1,0:T(8,128)(2,1)S(1)} %activate.1.refs_0_), channel_id=1, source_target_pairs={{0,192},{64,0},{128,64},{192,128},{256,448},{320,256},{384,320},{4... | collective-permute-start | bytes 835592 | tf_op jit(solution)/shard_map/ppermute | solution.py:265
  118.5 14.6 %collective-permute-start.5 = (bf16[1088,128]{1,0:T(8,128)(2,1)S(1)}, bf16[1088,128]{1,0:T(8,128)(2,1)S(1)}, u32[]{:S(2)}, u32[]{:S(2)}) collective-permute-start(bf16[1088,128]{1,0:T(8,128)(2,1)S(1)} %activate.1.refs_0_), channel_id=1, source_target_pairs={{0,128},{64,192},{128,0},{192,64},{256,384},{320,448},{384,256},{4... | collective-permute-start | bytes 835592 | tf_op jit(solution)/shard_map/ppermute | solution.py:265
  121.6 11.5 %collective-permute-start.4 = (bf16[1088,128]{1,0:T(8,128)(2,1)S(1)}, bf16[1088,128]{1,0:T(8,128)(2,1)S(1)}, u32[]{:S(2)}, u32[]{:S(2)}) collective-permute-start(bf16[1088,128]{1,0:T(8,128)(2,1)S(1)} %activate.1.refs_0_), channel_id=1, source_target_pairs={{0,64},{64,128},{128,192},{192,0},{256,320},{320,384},{384,448},{4... | collective-permute-start | bytes 835592 | tf_op jit(solution)/shard_map/ppermute | solution.py:265
  123.6 17.0 %collective-permute-start.10 = (bf16[1088,128]{1,0:T(8,128)(2,1)S(1)}, bf16[1088,128]{1,0:T(8,128)(2,1)S(1)}, u32[]{:S(2)}, u32[]{:S(2)}) collective-permute-start(bf16[1088,128]{1,0:T(8,128)(2,1)S(1)} %collective-permute-done.7.refs_4_), channel_id=1, source_target_pairs={{0,192},{64,0},{128,64},{192,128},{256,448},{320,256},{384,320},{4... | collective-permute-start | bytes 835592 | tf_op jit(solution)/shard_map/ppermute | solution.py:265
  128.2 12.4 %collective-permute-start.9 = (bf16[1088,128]{1,0:T(8,128)(2,1)S(1)}, bf16[1088,128]{1,0:T(8,128)(2,1)S(1)}, u32[]{:S(2)}, u32[]{:S(2)}) collective-permute-start(bf16[1088,128]{1,0:T(8,128)(2,1)S(1)} %collective-permute-done.7.refs_4_), channel_id=1, source_target_pairs={{0,128},{64,192},{128,0},{192,64},{256,384},{320,448},{384,256},{4... | collective-permute-start | bytes 835592 | tf_op jit(solution)/shard_map/ppermute | solution.py:265
  130.7 15.5 %collective-permute-start.8 = (bf16[1088,128]{1,0:T(8,128)(2,1)S(1)}, bf16[1088,128]{1,0:T(8,128)(2,1)S(1)}, u32[]{:S(2)}, u32[]{:S(2)}) collective-permute-start(bf16[1088,128]{1,0:T(8,128)(2,1)S(1)} %collective-permute-done.7.refs_4_), channel_id=1, source_target_pairs={{0,64},{64,128},{128,192},{192,0},{256,320},{320,384},{384,448},{4... | collective-permute-start | bytes 835592 | tf_op jit(solution)/shard_map/ppermute | solution.py:265
  (9 other events, 8.8 us)

commit v6 on v5

--- a/solution.py
+++ b/solution.py
@@ -9,7 +9,7 @@
 F32 = jnp.float32
 LANES = 128
 X = 4
-VMEM = 24 * 1024 * 1024
+VMEM = 12 * 1024 * 1024
 
 
 def call(kernel, name, out_shape, in_specs, out_specs=None):
@@ -92,24 +92,23 @@
                 cols = pl.ds(pl.multiple_of(tile * LANES, LANES), LANES)
                 out[pl.ds(base + (z * 4 + c) * depth, depth), :] = down_ref[:, cols]
 
-    for d, out in enumerate(outs[1:], 1):
+    for d, out in enumerate(outs):
         q = lax.rem(x_ref[0] + d, X)
         part = pl.ds(pl.multiple_of(q * quarter, quarter), quarter)
         out[pl.ds(0, quarter), :] = gate_ref[part, :]
         out[pl.ds(quarter, quarter), :] = up_ref[part, :]
         put_down(out, 2 * quarter, q)
-    put_down(outs[0], 0, x_ref[0])
 
 
 def pack(x, w_gate, w_up, w_down):
     depth = w_down.shape[0]
     rows = 2 * (w_gate.shape[0] // X) + 8 * depth
-    shapes = [jax.ShapeDtypeStruct((r, LANES), BF) for r in [8 * depth] + [rows] * (X - 1)]
+    shapes = [jax.ShapeDtypeStruct((r, LANES), BF) for r in [rows] * X]
     return call(pack_kernel, "pack", shapes, [in_smem()] + [in_vmem()] * 3)(x, w_gate, w_up, w_down)
 
 
 def swap_kernel(z_ref, own_ref, p1, p2, p3, out_ref):
-    rows = own_ref.shape[0] // 2
+    rows = out_ref.shape[0] // X
     start = (1 - z_ref[0]) * rows
     for d, ref in enumerate((own_ref, p1, p2, p3)):
         base = ref.shape[0] - 2 * rows
@@ -117,7 +116,7 @@
 
 
 def swap(z, own, packs):
-    shape = jax.ShapeDtypeStruct((X * own.shape[0] // 2, LANES), BF)
+    shape = jax.ShapeDtypeStruct((X * 4 * LANES, LANES), BF)
     return call(swap_kernel, "swap", shape, [in_smem()] + [in_vmem()] * 4)(z, own, *packs)
 
 
@@ -141,23 +140,31 @@
     out_ref[pl.ds(count, last.shape[0]), :] = jnp.dot(last, weight, preferred_element_type=F32).astype(out_ref.dtype)
 
 
-def project_kernel(x_ref, chunks_ref, gate_ref, up_ref, *refs):
-    packs, out_ref = refs[:-1], refs[-1]
+def project_kernel(x_ref, chunks_ref, *refs):
+    packs, (out_ref, rows_ref, sems) = refs[:X], refs[X:]
     main, last = stacked(chunks_ref)
     quarter = main.shape[1]
-    x = x_ref[0]
-    for d, pack_ref in enumerate(packs, 1):
+    copies = []
+    for d, pack_ref in enumerate(packs):
         gate, up = pack_ref[pl.ds(0, quarter), :], pack_ref[pl.ds(quarter, quarter), :]
-        project_into(out_ref.at[lax.rem(x + X - d, X)], main, last, gate, up)
-    part = pl.ds(pl.multiple_of(x * quarter, quarter), quarter)
-    project_into(out_ref.at[x], main, last, gate_ref[part, :], up_ref[part, :])
-
-
-def project(x, chunks, gate, up, packs):
-    shape = jax.ShapeDtypeStruct((X, chunks.shape[0] * 17, 2 * LANES), BF)
-    return call(project_kernel, "project", shape, [in_smem()] + [in_vmem()] * (3 + len(packs)))(
-        x, chunks, gate, up, *packs
-    )
+        project_into(rows_ref.at[d], main, last, gate, up)
+        copies.append(pltpu.make_async_copy(rows_ref.at[d], out_ref.at[lax.rem(x_ref[0] + X - d, X)], sems.at[d]))
+        copies[d].start()
+    for copy in copies:
+        copy.wait()
+
+
+def project(x, chunks, packs):
+    shape = (X, chunks.shape[0] * 17, 2 * LANES)
+    return pl.pallas_call(
+        project_kernel,
+        out_shape=jax.ShapeDtypeStruct(shape, BF),
+        in_specs=[in_smem()] + [in_vmem()] * (1 + len(packs)),
+        out_specs=pl.BlockSpec(memory_space=pltpu.HBM),
+        scratch_shapes=[pltpu.VMEM(shape, BF), pltpu.SemaphoreType.DMA((X,))],
+        compiler_params=pltpu.CompilerParams(vmem_limit_bytes=VMEM),
+        name="project",
+    )(x, chunks, *packs)
 
 
 def activate_kernel(parts_ref, out_ref):
@@ -176,7 +183,7 @@
 def down_kernel(x_ref, z_ref, *refs):
     hiddens, (own_ref, p1, p2, p3, other_ref, out_ref) = refs[: 2 * X], refs[2 * X :]
     experts = out_ref.shape[0]
-    rows = own_ref.shape[0] // 2
+    rows = other_ref.shape[0] // X
     depth = rows // 4
     hidden = jnp.concatenate([ref[...] for ref in hiddens], axis=1)
     blocks = []
@@ -283,16 +290,18 @@
     w_gate, w_up, w_down = w_gate[0], w_up[0], w_down[0]
     buffer = dispatch(x, ids, tokens, groups)
     chunks = lax.all_to_all(buffer, "expert", split_axis=0, concat_axis=0, tiled=True)
-    own_down, *sent = pack(x, w_gate, w_up, w_down)
+    own, *sent = pack(x, w_gate, w_up, w_down)
     packs = [shift(sent[d - 1], d) for d in range(1, X)]
-    other_down = cross(swap(z, own_down, packs))
-    arrived = across(project(x, chunks, w_gate, w_up, packs))
+    to_swap = swap(z, own, packs)
+    chunks, to_swap = lax.optimization_barrier((chunks, to_swap))
+    other_down = cross(to_swap)
+    arrived = across(project(x, chunks, [own] + packs))
     arrived, other_down = lax.optimization_barrier((arrived, other_down))
     hidden = activate(arrived)
     swapped = cross(hidden)
     hiddens = [hidden] + [shift(hidden, d) for d in range(1, X)]
     hiddens += [swapped] + [shift(swapped, d) for d in range(1, X)]
-    output = down(x, z, hiddens, own_down, packs, other_down, groups)
+    output = down(x, z, hiddens, own, packs, other_down, groups)
     returned = lax.all_to_all(output, "expert", split_axis=0, concat_axis=0, tiled=True)
     return combine(x, ids, scale, returned, tokens.shape[1] // (2 * X))
 

time: 196 us -> 196 us (level)
  Pallas kernels: 9.05 us -> 16.2 us
  local copies, waits for them, and re-layouts: 15.8 us -> 9.58 us
    unnamed x40 -> x22, local copies, waits for them, and re-layouts: 15 us -> 8.82 us
    pallas_call x1, Pallas kernels: 2.78 us -> 7 us  [project(): pl.pallas_call(project_kernel, out_shape=jax.ShapeDtypeStruct(shape, BF),...]
    all_to_all x1, waiting for transfers between devices: 5.9 us -> 2.42 us  [body(): lax.all_to_all(buffer, 'expert', split_axis=0, concat_axis=0, tiled=True)]
    all_to_all x1, waiting for transfers between devices: 3.68 us -> 5.96 us  [across(): lax.all_to_all(value, 'pipe', split_axis=0, concat_axis=0, axis_index_gro...]
  transfers between devices with their start and end apart: 13 -> 13, of which waited for: 8 -> 9; matrix products, arithmetic and copies ran while one was open for 0% -> 0% of each run, Pallas kernels for 0% -> 2%
where the time goes in v6:
time: 196 us; the launch traced here: 195 us
  waiting for transfers between devices  63 us (32%)
  starting transfers between devices  62.3 us (32%)
  blocking collectives  43.5 us (22%)
  Pallas kernels  16.2 us (8%)
  local copies, waits for them, and re-layouts  9.58 us (5%)
    all_to_all x1, blocking collectives, body(): lax.all_to_all(output, 'expert', split_axis=0, concat_axis=0, tiled=True)  43.5 us
    ppermute x9, waiting for transfers between devices, shift(): return lax.ppermute(value, 'pipe', pairs)  41.3 us
    ppermute x9, starting transfers between devices, shift(): return lax.ppermute(value, 'pipe', pairs)  27.9 us
    ppermute x2, starting transfers between devices, cross(): lax.ppermute(value, 'pipe', [(p, (p + X) % (2 * X)) for p in range(2 * X)])  15.9 us
    all_to_all x1, starting transfers between devices, body(): lax.all_to_all(buffer, 'expert', split_axis=0, concat_axis=0, tiled=True)  14.6 us
    ppermute x2, waiting for transfers between devices, cross(): lax.ppermute(value, 'pipe', [(p, (p + X) % (2 * X)) for p in range(2 * X)])  13.3 us
    unnamed x22, local copies, waits for them, and re-layouts  8.82 us
    pallas_call x1, Pallas kernels, project(): pl.pallas_call(project_kernel, out_shape=jax.ShapeDtypeStruct(shape, BF),...  7 us
  transfers between devices with their start and end apart: 13, of which 9 were waited for; matrix products, arithmetic and copies ran while one was open for 0% of the time, Pallas kernels for 2%

profile of v6, /device:TPU:1, one launch (start us, length us, event | category | flops | bytes accessed | tf_op | source)
XLA Modules:
  0.0 194.9 jit_solution(4759761922909678761)
XLA Ops:
  4.1 14.6 %all-to-all-start = ((bf16[64,120,128]{2,1,0:T(8,128)(2,1)}), bf16[64,120,128]{2,1,0:T(8,128)(2,1)S(1)}, u32[]{:S(2)}, u32[]{:S(2)}) async-start(bf16[64,120,128]{2,1,0:T(8,128)(2,1)} %copy-done.1), calls=%async_computation | async-start | bytes 3932160 | tf_op jit(solution)/shard_map/all_to_all | solution.py:292
  23.9 3.1 %collective-permute-start = (bf16[2816,128]{1,0:T(8,128)(2,1)}, bf16[2816,128]{1,0:T(8,128)(2,1)}, u32[]{:S(2)}, u32[]{:S(2)}) collective-permute-start(bf16[2816,128]{1,0:T(8,128)(2,1)} %get-tuple-element.14), channel_id=1, source_target_pairs={{0,64},{64,128},{128,192},{192,0},{256,320},{320,384},{384,448},{4... | collective-permute-start | bytes 2162696 | tf_op jit(solution)/shard_map/ppermute | solution.py:272
  27.0 4.4 %collective-permute-start.1 = (bf16[2816,128]{1,0:T(8,128)(2,1)}, bf16[2816,128]{1,0:T(8,128)(2,1)}, u32[]{:S(2)}, u32[]{:S(2)}) collective-permute-start(bf16[2816,128]{1,0:T(8,128)(2,1)} %get-tuple-element.15), channel_id=1, source_target_pairs={{0,128},{64,192},{128,0},{192,64},{256,384},{320,448},{384,256},{4... | collective-permute-start | bytes 2162696 | tf_op jit(solution)/shard_map/ppermute | solution.py:272
  31.3 3.1 %collective-permute-start.2 = (bf16[2816,128]{1,0:T(8,128)(2,1)}, bf16[2816,128]{1,0:T(8,128)(2,1)}, u32[]{:S(2)}, u32[]{:S(2)}) collective-permute-start(bf16[2816,128]{1,0:T(8,128)(2,1)} %get-tuple-element.16), channel_id=1, source_target_pairs={{0,192},{64,0},{128,64},{192,128},{256,448},{320,256},{384,320},{4... | collective-permute-start | bytes 2162696 | tf_op jit(solution)/shard_map/ppermute | solution.py:272
  34.4 10.1 %collective-permute-done.p1.refs_1_.refs_9_ = bf16[2816,128]{1,0:T(8,128)(2,1)} collective-permute-done((bf16[2816,128]{1,0:T(8,128)(2,1)}, bf16[2816,128]{1,0:T(8,128)(2,1)}, u32[]{:S(2)}, u32[]{:S(2)}) %collective-permute-start) | collective-permute-done | bytes 720928 | tf_op jit(solution)/shard_map/ppermute | solution.py:272
  44.5 16.4 %collective-permute-done.1.p2.refs_2_.refs_10_ = bf16[2816,128]{1,0:T(8,128)(2,1)} collective-permute-done((bf16[2816,128]{1,0:T(8,128)(2,1)}, bf16[2816,128]{1,0:T(8,128)(2,1)}, u32[]{:S(2)}, u32[]{:S(2)}) %collective-permute-start.1) | collective-permute-done | bytes 720928 | tf_op jit(solution)/shard_map/ppermute | solution.py:272
  63.8 2.4 %all-to-all-done.chunks_ref = bf16[64,120,128]{2,1,0:T(8,128)(2,1)S(1)} async-done(((bf16[64,120,128]{2,1,0:T(8,128)(2,1)}), bf16[64,120,128]{2,1,0:T(8,128)(2,1)S(1)}, u32[]{:S(2)}, u32[]{:S(2)}) %all-to-all-start) | async-done | bytes 1966112 | tf_op jit(solution)/shard_map/all_to_all | solution.py:292
  66.2 7.0 %project.1 = bf16[4,1088,256]{2,1,0:T(8,128)(2,1)S(1)} custom-call(s32[1]{0:T(128)} %bitcast.x_ref, bf16[64,120,128]{2,1,0:T(8,128)(2,1)S(1)} %all-to-all-done.chunks_ref, bf16[2816,128]{1,0:T(8,128)(2,1)S(1)} %get-tuple-element.13.own_ref.refs_0_.refs_8_, bf16[2816,128]{1,0:T(8,128)(2,1)} %collective-permute-done.p1.refs_1_.refs_9_, ...), custom_call_target="tpu_custom_call" | custom-call | tf_op jit(solution)/shard_map/project/pallas_call | solution.py:159
  74.6 4.0 %all-to-all-start.1 = ((bf16[4,1088,256]{2,1,0:T(8,128)(2,1)}), bf16[4,1088,256]{2,1,0:T(8,128)(2,1)S(1)}, u32[]{:S(2)}, u32[]{:S(2)}) async-start(bf16[4,1088,256]{2,1,0:T(8,128)(2,1)} %copy-done), calls=%async_computation.1 | async-start | bytes 4456448 | tf_op jit(solution)/shard_map/all_to_all | solution.py:281
  78.6 7.9 %collective-permute-start.3 = (bf16[2048,128]{1,0:T(8,128)(2,1)S(1)}, bf16[2048,128]{1,0:T(8,128)(2,1)S(1)}, u32[]{:S(2)}, u32[]{:S(2)}) collective-permute-start(bf16[2048,128]{1,0:T(8,128)(2,1)S(1)} %swap.1), channel_id=1, source_target_pairs={{0,256},{64,320},{128,384},{192,448},{256,0},{320,64},{384,128},{4... | collective-permute-start | bytes 1572872 | tf_op jit(solution)/shard_map/ppermute | solution.py:276
  86.6 13.3 %collective-permute-done.3.refs_12_ = bf16[2048,128]{1,0:T(8,128)(2,1)S(1)} collective-permute-done((bf16[2048,128]{1,0:T(8,128)(2,1)S(1)}, bf16[2048,128]{1,0:T(8,128)(2,1)S(1)}, u32[]{:S(2)}, u32[]{:S(2)}) %collective-permute-start.3) | collective-permute-done | bytes 524320 | tf_op jit(solution)/shard_map/ppermute | solution.py:276
  100.7 6.0 %all-to-all-done.1.parts_ref = bf16[4,1088,256]{2,1,0:T(8,128)(2,1)S(1)} async-done(((bf16[4,1088,256]{2,1,0:T(8,128)(2,1)}), bf16[4,1088,256]{2,1,0:T(8,128)(2,1)S(1)}, u32[]{:S(2)}, u32[]{:S(2)}) %all-to-all-start.1) | async-done | bytes 2228256 | tf_op jit(solution)/shard_map/all_to_all | solution.py:281
  107.1 7.9 %collective-permute-start.7 = (bf16[1088,128]{1,0:T(8,128)(2,1)S(1)}, bf16[1088,128]{1,0:T(8,128)(2,1)S(1)}, u32[]{:S(2)}, u32[]{:S(2)}) collective-permute-start(bf16[1088,128]{1,0:T(8,128)(2,1)S(1)} %activate.1.refs_0_), channel_id=1, source_target_pairs={{0,256},{64,320},{128,384},{192,448},{256,0},{320,64},{384,128},{4... | collective-permute-start | bytes 835592 | tf_op jit(solution)/shard_map/ppermute | solution.py:276
  115.0 2.8 %collective-permute-start.6 = (bf16[1088,128]{1,0:T(8,128)(2,1)S(1)}, bf16[1088,128]{1,0:T(8,128)(2,1)S(1)}, u32[]{:S(2)}, u32[]{:S(2)}) collective-permute-start(bf16[1088,128]{1,0:T(8,128)(2,1)S(1)} %activate.1.refs_0_), channel_id=1, source_target_pairs={{0,192},{64,0},{128,64},{192,128},{256,448},{320,256},{384,320},{4... | collective-permute-start | bytes 835592 | tf_op jit(solution)/shard_map/ppermute | solution.py:272
  117.8 3.1 %collective-permute-start.5 = (bf16[1088,128]{1,0:T(8,128)(2,1)S(1)}, bf16[1088,128]{1,0:T(8,128)(2,1)S(1)}, u32[]{:S(2)}, u32[]{:S(2)}) collective-permute-start(bf16[1088,128]{1,0:T(8,128)(2,1)S(1)} %activate.1.refs_0_), channel_id=1, source_target_pairs={{0,128},{64,192},{128,0},{192,64},{256,384},{320,448},{384,256},{4... | collective-permute-start | bytes 835592 | tf_op jit(solution)/shard_map/ppermute | solution.py:272
  120.9 1.9 collective-permute-start.4
  122.9 4.6 %collective-permute-start.10 = (bf16[1088,128]{1,0:T(8,128)(2,1)S(1)}, bf16[1088,128]{1,0:T(8,128)(2,1)S(1)}, u32[]{:S(2)}, u32[]{:S(2)}) collective-permute-start(bf16[1088,128]{1,0:T(8,128)(2,1)S(1)} %collective-permute-done.7.refs_4_), channel_id=1, source_target_pairs={{0,192},{64,0},{128,64},{192,128},{256,448},{320,256},{384,320},{4... | collective-permute-start | bytes 835592 | tf_op jit(solution)/shard_map/ppermute | solution.py:272
  127.5 2.5 %collective-permute-start.9 = (bf16[1088,128]{1,0:T(8,128)(2,1)S(1)}, bf16[1088,128]{1,0:T(8,128)(2,1)S(1)}, u32[]{:S(2)}, u32[]{:S(2)}) collective-permute-start(bf16[1088,128]{1,0:T(8,128)(2,1)S(1)} %collective-permute-done.7.refs_4_), channel_id=1, source_target_pairs={{0,128},{64,192},{128,0},{192,64},{256,384},{320,448},{384,256},{4... | collective-permute-start | bytes 835592 | tf_op jit(solution)/shard_map/ppermute | solution.py:272
  130.0 2.5 %collective-permute-start.8 = (bf16[1088,128]{1,0:T(8,128)(2,1)S(1)}, bf16[1088,128]{1,0:T(8,128)(2,1)S(1)}, u32[]{:S(2)}, u32[]{:S(2)}) collective-permute-start(bf16[1088,128]{1,0:T(8,128)(2,1)S(1)} %collective-permute-done.7.refs_4_), channel_id=1, source_target_pairs={{0,64},{64,128},{128,192},{192,0},{256,320},{320,384},{384,448},{4... | collective-permute-start | bytes 835592 | tf_op jit(solution)/shard_map/ppermute | solution.py:272
  132.5 4.2 %collective-permute-done.10.refs_7_ = bf16[1088,128]{1,0:T(8,128)(2,1)S(1)} collective-permute-done((bf16[1088,128]{1,0:T(8,128)(2,1)S(1)}, bf16[1088,128]{1,0:T(8,128)(2,1)S(1)}, u32[]{:S(2)}, u32[]{:S(2)}) %collective-permute-start.10) | collective-permute-done | bytes 278560 | tf_op jit(solution)/shard_map/ppermute | solution.py:272
  136.7 2.5 %collective-permute-done.9.refs_6_ = bf16[1088,128]{1,0:T(8,128)(2,1)S(1)} collective-permute-done((bf16[1088,128]{1,0:T(8,128)(2,1)S(1)}, bf16[1088,128]{1,0:T(8,128)(2,1)S(1)}, u32[]{:S(2)}, u32[]{:S(2)}) %collective-permute-start.9) | collective-permute-done | bytes 278560 | tf_op jit(solution)/shard_map/ppermute | solution.py:272
  139.2 6.7 %collective-permute-done.8.refs_5_ = bf16[1088,128]{1,0:T(8,128)(2,1)S(1)} collective-permute-done((bf16[1088,128]{1,0:T(8,128)(2,1)S(1)}, bf16[1088,128]{1,0:T(8,128)(2,1)S(1)}, u32[]{:S(2)}, u32[]{:S(2)}) %collective-permute-start.8) | collective-permute-done | bytes 278560 | tf_op jit(solution)/shard_map/ppermute | solution.py:272
  145.9 3.1 %down.1 = bf16[64,64,128]{2,1,0:T(8,128)(2,1)S(1)} custom-call(s32[1]{0:T(128)} %bitcast.x_ref, s32[1]{0:T(128)} %bitcast.3.z_ref, bf16[1088,128]{1,0:T(8,128)(2,1)S(1)} %activate.1.refs_0_, bf16[1088,128]{1,0:T(8,128)(2,1)S(1)} %collective-permute-done.4.refs_1_, bf16[1088,128]{1,0:T(8,128)(2,1)S(1)} %collective-permute-done.5.refs_2_, ...), custom_call_target="tpu_custom_call" | custom-call | tf_op jit(solution)/shard_map/down/pallas_call | solution.py:219
  149.0 43.5 %all_to_all.15.chunks_ref = bf16[64,64,128]{2,1,0:T(8,128)(2,1)S(1)} all-to-all(bf16[64,64,128]{2,1,0:T(8,128)(2,1)S(1)} %down.1), channel_id=1, replica_groups=mesh['pipe'=8,'expert'=64] {'expert'}, dimensions={0} | all-to-all | bytes 2097152 | tf_op jit(solution)/shard_map/all_to_all | solution.py:305
  (33 shorter events, 17.0 us)
Async XLA Ops:
  0.0 1.2 copy-start.2
  1.2 0.7 copy-start.8
  2.9 1.3 copy-start.1
  4.1 62.1 %all-to-all-start = ((bf16[64,120,128]{2,1,0:T(8,128)(2,1)}), bf16[64,120,128]{2,1,0:T(8,128)(2,1)S(1)}, u32[]{:S(2)}, u32[]{:S(2)}) async-start(bf16[64,120,128]{2,1,0:T(8,128)(2,1)} %copy-done.1), calls=%async_computation | async-start | bytes 3932160 | tf_op jit(solution)/shard_map/all_to_all | solution.py:292
  18.7 1.2 copy-start.3
  19.9 1.2 copy-start.4
  21.1 1.2 copy-start.5
  23.9 20.7 %collective-permute-start = (bf16[2816,128]{1,0:T(8,128)(2,1)}, bf16[2816,128]{1,0:T(8,128)(2,1)}, u32[]{:S(2)}, u32[]{:S(2)}) collective-permute-start(bf16[2816,128]{1,0:T(8,128)(2,1)} %get-tuple-element.14), channel_id=1, source_target_pairs={{0,64},{64,128},{128,192},{192,0},{256,320},{320,384},{384,448},{4... | collective-permute-start | bytes 2162696 | tf_op jit(solution)/shard_map/ppermute | solution.py:272
  27.0 34.0 %collective-permute-start.1 = (bf16[2816,128]{1,0:T(8,128)(2,1)}, bf16[2816,128]{1,0:T(8,128)(2,1)}, u32[]{:S(2)}, u32[]{:S(2)}) collective-permute-start(bf16[2816,128]{1,0:T(8,128)(2,1)} %get-tuple-element.15), channel_id=1, source_target_pairs={{0,128},{64,192},{128,0},{192,64},{256,384},{320,448},{384,256},{4... | collective-permute-start | bytes 2162696 | tf_op jit(solution)/shard_map/ppermute | solution.py:272
  31.3 30.9 %collective-permute-start.2 = (bf16[2816,128]{1,0:T(8,128)(2,1)}, bf16[2816,128]{1,0:T(8,128)(2,1)}, u32[]{:S(2)}, u32[]{:S(2)}) collective-permute-start(bf16[2816,128]{1,0:T(8,128)(2,1)} %get-tuple-element.16), channel_id=1, source_target_pairs={{0,192},{64,0},{128,64},{192,128},{256,448},{320,256},{384,320},{4... | collective-permute-start | bytes 2162696 | tf_op jit(solution)/shard_map/ppermute | solution.py:272
  73.3 1.4 copy-start
  74.6 32.0 %all-to-all-start.1 = ((bf16[4,1088,256]{2,1,0:T(8,128)(2,1)}), bf16[4,1088,256]{2,1,0:T(8,128)(2,1)S(1)}, u32[]{:S(2)}, u32[]{:S(2)}) async-start(bf16[4,1088,256]{2,1,0:T(8,128)(2,1)} %copy-done), calls=%async_computation.1 | async-start | bytes 4456448 | tf_op jit(solution)/shard_map/all_to_all | solution.py:281
  78.6 21.3 %collective-permute-start.3 = (bf16[2048,128]{1,0:T(8,128)(2,1)S(1)}, bf16[2048,128]{1,0:T(8,128)(2,1)S(1)}, u32[]{:S(2)}, u32[]{:S(2)}) collective-permute-start(bf16[2048,128]{1,0:T(8,128)(2,1)S(1)} %swap.1), channel_id=1, source_target_pairs={{0,256},{64,320},{128,384},{192,448},{256,0},{320,64},{384,128},{4... | collective-permute-start | bytes 1572872 | tf_op jit(solution)/shard_map/ppermute | solution.py:276
  99.9 0.8 copy-start.6
  106.7 39.2 %copy-start.7 = (bf16[2048,128]{1,0:T(8,128)(2,1)S(1)}, bf16[2048,128]{1,0:T(8,128)(2,1)}, u32[]{:S(2)}) copy-start(bf16[2048,128]{1,0:T(8,128)(2,1)} %copy-done.6) | copy-start | bytes 1572868
  107.1 85.5 %copy-start.9 = (s32[128,8]{0,1:T(8,128)S(1)}, s32[128,8]{0,1:T(8,128)}, u32[]{:S(2)}) copy-start(s32[128,8]{0,1:T(8,128)} %param.7) | copy-start | bytes 12292
  107.1 85.4 %copy-start.10 = (f32[128,8]{0,1:T(8,128)S(1)}, f32[128,8]{0,1:T(8,128)}, u32[]{:S(2)}) copy-start(f32[128,8]{0,1:T(8,128)} %param.8) | copy-start | bytes 12292
  107.1 15.8 %collective-permute-start.7 = (bf16[1088,128]{1,0:T(8,128)(2,1)S(1)}, bf16[1088,128]{1,0:T(8,128)(2,1)S(1)}, u32[]{:S(2)}, u32[]{:S(2)}) collective-permute-start(bf16[1088,128]{1,0:T(8,128)(2,1)S(1)} %activate.1.refs_0_), channel_id=1, source_target_pairs={{0,256},{64,320},{128,384},{192,448},{256,0},{320,64},{384,128},{4... | collective-permute-start | bytes 835592 | tf_op jit(solution)/shard_map/ppermute | solution.py:276
  115.0 14.9 %collective-permute-start.6 = (bf16[1088,128]{1,0:T(8,128)(2,1)S(1)}, bf16[1088,128]{1,0:T(8,128)(2,1)S(1)}, u32[]{:S(2)}, u32[]{:S(2)}) collective-permute-start(bf16[1088,128]{1,0:T(8,128)(2,1)S(1)} %activate.1.refs_0_), channel_id=1, source_target_pairs={{0,192},{64,0},{128,64},{192,128},{256,448},{320,256},{384,320},{4... | collective-permute-start | bytes 835592 | tf_op jit(solution)/shard_map/ppermute | solution.py:272
  117.8 14.6 %collective-permute-start.5 = (bf16[1088,128]{1,0:T(8,128)(2,1)S(1)}, bf16[1088,128]{1,0:T(8,128)(2,1)S(1)}, u32[]{:S(2)}, u32[]{:S(2)}) collective-permute-start(bf16[1088,128]{1,0:T(8,128)(2,1)S(1)} %activate.1.refs_0_), channel_id=1, source_target_pairs={{0,128},{64,192},{128,0},{192,64},{256,384},{320,448},{384,256},{4... | collective-permute-start | bytes 835592 | tf_op jit(solution)/shard_map/ppermute | solution.py:272
  120.9 11.5 %collective-permute-start.4 = (bf16[1088,128]{1,0:T(8,128)(2,1)S(1)}, bf16[1088,128]{1,0:T(8,128)(2,1)S(1)}, u32[]{:S(2)}, u32[]{:S(2)}) collective-permute-start(bf16[1088,128]{1,0:T(8,128)(2,1)S(1)} %activate.1.refs_0_), channel_id=1, source_target_pairs={{0,64},{64,128},{128,192},{192,0},{256,320},{320,384},{384,448},{4... | collective-permute-start | bytes 835592 | tf_op jit(solution)/shard_map/ppermute | solution.py:272
  122.9 13.8 %collective-permute-start.10 = (bf16[1088,128]{1,0:T(8,128)(2,1)S(1)}, bf16[1088,128]{1,0:T(8,128)(2,1)S(1)}, u32[]{:S(2)}, u32[]{:S(2)}) collective-permute-start(bf16[1088,128]{1,0:T(8,128)(2,1)S(1)} %collective-permute-done.7.refs_4_), channel_id=1, source_target_pairs={{0,192},{64,0},{128,64},{192,128},{256,448},{320,256},{384,320},{4... | collective-permute-start | bytes 835592 | tf_op jit(solution)/shard_map/ppermute | solution.py:272
  127.5 11.7 %collective-permute-start.9 = (bf16[1088,128]{1,0:T(8,128)(2,1)S(1)}, bf16[1088,128]{1,0:T(8,128)(2,1)S(1)}, u32[]{:S(2)}, u32[]{:S(2)}) collective-permute-start(bf16[1088,128]{1,0:T(8,128)(2,1)S(1)} %collective-permute-done.7.refs_4_), channel_id=1, source_target_pairs={{0,128},{64,192},{128,0},{192,64},{256,384},{320,448},{384,256},{4... | collective-permute-start | bytes 835592 | tf_op jit(solution)/shard_map/ppermute | solution.py:272
  130.0 15.9 %collective-permute-start.8 = (bf16[1088,128]{1,0:T(8,128)(2,1)S(1)}, bf16[1088,128]{1,0:T(8,128)(2,1)S(1)}, u32[]{:S(2)}, u32[]{:S(2)}) collective-permute-start(bf16[1088,128]{1,0:T(8,128)(2,1)S(1)} %collective-permute-done.7.refs_4_), channel_id=1, source_target_pairs={{0,64},{64,128},{128,192},{192,0},{256,320},{320,384},{384,448},{4... | collective-permute-start | bytes 835592 | tf_op jit(solution)/shard_map/ppermute | solution.py:272

commit v7 on v2

--- a/solution.py
+++ b/solution.py
@@ -9,10 +9,13 @@
 F32 = jnp.float32
 LANES = 128
 X = 4
-VMEM = 24 * 1024 * 1024
-
-
-def call(kernel, name, out_shape, in_specs, out_specs=None):
+PARTS = 4
+HOLD = 50_000_000_000
+FULL = 60 * 1024 * 1024
+VMEM = 16 * 1024 * 1024
+
+
+def call(kernel, name, out_shape, in_specs, out_specs=None, scratch=(), vmem=VMEM, cost=None):
     if out_specs is None:
         out_specs = jax.tree.map(lambda _: in_vmem(), out_shape)
     return pl.pallas_call(
@@ -20,13 +23,19 @@
         out_shape=out_shape,
         in_specs=in_specs,
         out_specs=out_specs,
-        compiler_params=pltpu.CompilerParams(vmem_limit_bytes=VMEM),
+        scratch_shapes=scratch,
+        compiler_params=pltpu.CompilerParams(vmem_limit_bytes=vmem),
+        cost_estimate=cost,
         name=name,
     )
 
 
 def in_vmem():
     return pl.BlockSpec(memory_space=pltpu.VMEM)
+
+
+def anywhere():
+    return pl.BlockSpec(memory_space=pl.ANY)
 
 
 def in_smem():
@@ -54,27 +63,48 @@
     return out
 
 
-def dispatch_kernel(x_ref, ids_ref, tok_ref, out_ref):
+def dispatch_kernel(x_ref, ids_ref, tok_ref, out_ref, own_ref, rows_ref, sem, sems):
     experts = out_ref.shape[0]
-    tokens, width = tok_ref.shape
-    tiles = width // X // LANES
-    quarter = width // X
-    tok = tok_ref[:, pl.ds(pl.multiple_of(x_ref[0] * quarter, LANES), quarter)]
+    tokens, quarter = own_ref.shape
+    tiles = quarter // LANES
+    part = pl.ds(pl.multiple_of(x_ref[0] * quarter, LANES), quarter)
+    fetch = pltpu.make_async_copy(tok_ref.at[:, part], own_ref, sem)
+    fetch.start()
     place = slots(ids_ref[...], experts)
-    slot = lax.broadcasted_iota(jnp.int32, (experts, 16, tokens), 1).astype(F32)
-    pick = jnp.where(place[:, None, :] == slot, 1.0, 0.0).reshape(experts * 16, tokens).astype(BF)
-    rows = jnp.dot(pick, tok, preferred_element_type=F32).astype(BF)
-    for c in range(tiles):
-        out_ref[:, c * 16 : (c + 1) * 16, :] = rows[:, c * LANES : (c + 1) * LANES].reshape(experts, 16, LANES)
+    fetch.wait()
+    tok = own_ref[...]
     last = jnp.dot((place == 16.0).astype(BF), tok, preferred_element_type=F32)
     tail = spread([last[:, c * LANES : (c + 1) * LANES] for c in range(tiles)], 8)
-    out_ref[:, tiles * 16 : tiles * 16 + 8, :] = tail.astype(BF)
+    rows_ref[:, tiles * 16 : tiles * 16 + 8, :] = tail.astype(BF)
+    count = experts // PARTS
+    slot = lax.broadcasted_iota(jnp.int32, (count, 16, tokens), 1).astype(F32)
+    copies = []
+    for g in range(PARTS):
+        group = slice(g * count, (g + 1) * count)
+        pick = jnp.where(place[group][:, None, :] == slot, 1.0, 0.0).reshape(count * 16, tokens).astype(BF)
+        rows = jnp.dot(pick, tok, preferred_element_type=F32).astype(BF)
+        for c in range(tiles):
+            rows_ref[group, c * 16 : (c + 1) * 16, :] = rows[:, c * LANES : (c + 1) * LANES].reshape(count, 16, LANES)
+        some = pl.ds(g * count, count)
+        copies.append(pltpu.make_async_copy(rows_ref.at[some], out_ref.at[some], sems.at[g]))
+        copies[g].start()
+    for copy in copies:
+        copy.wait()
 
 
 def dispatch(x, ids, tokens, experts):
-    depth = tokens.shape[1] // X // LANES * 16 + 8
-    shape = jax.ShapeDtypeStruct((experts, depth, LANES), BF)
-    return call(dispatch_kernel, "dispatch", shape, [in_smem(), in_vmem(), in_vmem()])(x, ids, tokens)
+    count, width = tokens.shape
+    quarter = width // X
+    shape = (experts, quarter // LANES * 16 + 8, LANES)
+    scratch = [
+        pltpu.VMEM((count, quarter), BF),
+        pltpu.VMEM(shape, BF),
+        pltpu.SemaphoreType.DMA,
+        pltpu.SemaphoreType.DMA((PARTS,)),
+    ]
+    specs = [in_smem(), in_vmem(), anywhere()]
+    out = jax.ShapeDtypeStruct(shape, BF)
+    return call(dispatch_kernel, "dispatch", out, specs, anywhere(), scratch, FULL)(x, ids, tokens)
 
 
 def pack_kernel(x_ref, gate_ref, up_ref, down_ref, *outs):
@@ -92,33 +122,58 @@
                 cols = pl.ds(pl.multiple_of(tile * LANES, LANES), LANES)
                 out[pl.ds(base + (z * 4 + c) * depth, depth), :] = down_ref[:, cols]
 
-    for d, out in enumerate(outs[1:], 1):
+    for d, out in enumerate(outs):
         q = lax.rem(x_ref[0] + d, X)
         part = pl.ds(pl.multiple_of(q * quarter, quarter), quarter)
         out[pl.ds(0, quarter), :] = gate_ref[part, :]
         out[pl.ds(quarter, quarter), :] = up_ref[part, :]
         put_down(out, 2 * quarter, q)
-    put_down(outs[0], 0, x_ref[0])
 
 
 def pack(x, w_gate, w_up, w_down):
     depth = w_down.shape[0]
     rows = 2 * (w_gate.shape[0] // X) + 8 * depth
-    shapes = [jax.ShapeDtypeStruct((r, LANES), BF) for r in [8 * depth] + [rows] * (X - 1)]
+    shapes = [jax.ShapeDtypeStruct((r, LANES), BF) for r in [rows] * X]
     return call(pack_kernel, "pack", shapes, [in_smem()] + [in_vmem()] * 3)(x, w_gate, w_up, w_down)
 
 
-def swap_kernel(z_ref, own_ref, p1, p2, p3, out_ref):
-    rows = own_ref.shape[0] // 2
-    start = (1 - z_ref[0]) * rows
-    for d, ref in enumerate((own_ref, p1, p2, p3)):
-        base = ref.shape[0] - 2 * rows
-        out_ref[pl.ds(d * rows, rows), :] = ref[pl.ds(pl.multiple_of(base + start, LANES), rows), :]
-
-
-def swap(z, own, packs):
-    shape = jax.ShapeDtypeStruct((X * own.shape[0] // 2, LANES), BF)
-    return call(swap_kernel, "swap", shape, [in_smem()] + [in_vmem()] * 4)(z, own, *packs)
+def unpack_kernel(z_ref, *refs):
+    packs, (weight_ref, out_ref) = refs[:X], refs[X:]
+    quarter = weight_ref.shape[1]
+    rows = out_ref.shape[0] // X
+    start = pl.multiple_of(2 * quarter + (1 - z_ref[0]) * rows, LANES)
+    for d, ref in enumerate(packs):
+        weight_ref[d, :, pl.ds(0, LANES)] = ref[pl.ds(0, quarter), :]
+        weight_ref[d, :, pl.ds(LANES, LANES)] = ref[pl.ds(quarter, quarter), :]
+        out_ref[pl.ds(d * rows, rows), :] = ref[pl.ds(start, rows), :]
+
+
+def unpack(z, packs, quarter):
+    rows = (packs[0].shape[0] - 2 * quarter) // 2
+    shapes = [
+        jax.ShapeDtypeStruct((X, quarter, 2 * LANES), BF),
+        jax.ShapeDtypeStruct((X * rows, LANES), BF),
+    ]
+    return call(unpack_kernel, "unpack", shapes, [in_smem()] + [in_vmem()] * X)(z, *packs)
+
+
+def assemble_kernel(z_ref, *refs):
+    packs, (other_ref, out_ref) = refs[:X], refs[X:]
+    rows = other_ref.shape[0] // X
+    depth = rows // 4
+    for d, ref in enumerate(packs):
+        base = ref.shape[0] - 2 * rows + z_ref[0] * rows
+        for c in range(4):
+            cols = pl.ds(c * LANES, LANES)
+            out_ref[pl.ds(d * depth, depth), cols] = ref[pl.ds(pl.multiple_of(base + c * depth, LANES), depth), :]
+            out_ref[pl.ds((X + d) * depth, depth), cols] = other_ref[pl.ds(d * rows + c * depth, depth), :]
+
+
+def assemble(z, packs, other):
+    shape = jax.ShapeDtypeStruct((other.shape[0] // 2, 4 * LANES), BF)
+    specs = [in_smem()] + [in_vmem()] * (X + 1)
+    cost = pl.CostEstimate(flops=HOLD, bytes_accessed=4 * other.size, transcendentals=0)
+    return call(assemble_kernel, "assemble", shape, specs, cost=cost)(z, *packs, other)
 
 
 def stacked(chunks_ref):
@@ -134,52 +189,41 @@
     return jnp.concatenate(main, axis=1), jnp.concatenate(last, axis=1)
 
 
-def project_into(out_ref, main, last, gate, up):
-    weight = jnp.concatenate([gate, up], axis=1)
+def project_into(out_ref, main, last, weight):
     count = main.shape[0]
     out_ref[pl.ds(0, count), :] = jnp.dot(main, weight, preferred_element_type=F32).astype(out_ref.dtype)
     out_ref[pl.ds(count, last.shape[0]), :] = jnp.dot(last, weight, preferred_element_type=F32).astype(out_ref.dtype)
 
 
-def project_sent_kernel(chunks_ref, *refs):
-    main, last = stacked(chunks_ref)
-    quarter = main.shape[1]
-    for pack_ref, out_ref in zip(refs[: X - 1], refs[X - 1 :]):
-        project_into(out_ref, main, last, pack_ref[pl.ds(0, quarter), :], pack_ref[pl.ds(quarter, quarter), :])
-
-
-def project_sent(chunks, packs):
-    shapes = [jax.ShapeDtypeStruct((chunks.shape[0] * 17, 2 * LANES), BF)] * len(packs)
-    return call(project_sent_kernel, "project_sent", shapes, [in_vmem()] * (1 + len(packs)))(chunks, *packs)
-
-
-def project_own_kernel(x_ref, chunks_ref, gate_ref, up_ref, out_ref):
-    main, last = stacked(chunks_ref)
-    quarter = main.shape[1]
-    part = pl.ds(pl.multiple_of(x_ref[0] * quarter, quarter), quarter)
-    project_into(out_ref, main, last, gate_ref[part, :], up_ref[part, :])
-
-
-def project_own(x, chunks, gate, up):
-    shape = jax.ShapeDtypeStruct((chunks.shape[0] * 17, 2 * LANES), F32)
-    return call(project_own_kernel, "project_own", shape, [in_smem()] + [in_vmem()] * 3)(x, chunks, gate, up)
-
-
-def down_kernel(x_ref, z_ref, *refs):
-    hiddens, (own_ref, p1, p2, p3, other_ref, out_ref) = refs[: 2 * X], refs[2 * X :]
+def project(chunks, weight, blocks, dtype, name):
+    def kernel(chunks_ref, weight_ref, *outs):
+        main, last = stacked(chunks_ref)
+        for d, out_ref in zip(blocks, outs):
+            project_into(out_ref, main, last, weight_ref[d])
+
+    shapes = [jax.ShapeDtypeStruct((chunks.shape[0] * 17, 2 * LANES), dtype)] * len(blocks)
+    return call(kernel, name, shapes, [in_vmem()] * 2)(chunks, weight)
+
+
+def activate_kernel(own_ref, *refs):
+    parts, out_ref = refs[:-1], refs[-1]
+    total = own_ref[...]
+    for ref in parts:
+        total += ref[...].astype(F32)
+    gate, up = total[:, :LANES], total[:, LANES:]
+    out_ref[...] = (gate / (1.0 + jnp.exp(-gate)) * up).astype(BF)
+
+
+def activate(own, parts):
+    shape = jax.ShapeDtypeStruct((own.shape[0], LANES), BF)
+    return call(activate_kernel, "activate", shape, [in_vmem()] * (1 + len(parts)))(own, *parts)
+
+
+def down_kernel(x_ref, weight_ref, *refs):
+    hiddens, out_ref = refs[:-1], refs[-1]
     experts = out_ref.shape[0]
-    rows = own_ref.shape[0] // 2
-    depth = rows // 4
     hidden = jnp.concatenate([ref[...] for ref in hiddens], axis=1)
-    blocks = []
-    for ref in (own_ref, p1, p2, p3):
-        base = ref.shape[0] - 2 * rows + z_ref[0] * rows
-        tiles = [ref[pl.ds(pl.multiple_of(base + c * depth, LANES), depth), :] for c in range(4)]
-        blocks.append(jnp.concatenate(tiles, axis=1))
-    for d in range(X):
-        tiles = [other_ref[pl.ds(d * rows + c * depth, depth), :] for c in range(4)]
-        blocks.append(jnp.concatenate(tiles, axis=1))
-    weight = jnp.concatenate(blocks, axis=0)
+    weight = weight_ref[...]
     count = experts * 16
     main = jnp.dot(hidden[:count], weight, preferred_element_type=F32)
     last = jnp.dot(hidden[count:], weight, preferred_element_type=F32)
@@ -198,10 +242,10 @@
     out_ref[:, 48:64, :] = jnp.concatenate([halves, tail], axis=1).astype(BF)
 
 
-def down(x, z, hiddens, own, packs, other, experts):
+def down(x, weight, hiddens, experts):
     shape = jax.ShapeDtypeStruct((experts, 64, LANES), BF)
-    specs = [in_smem()] * 2 + [in_vmem()] * (2 * X + X + 1)
-    return call(down_kernel, "down", shape, specs)(x, z, *hiddens, own, *packs, other)
+    specs = [in_smem()] + [in_vmem()] * (1 + len(hiddens))
+    return call(down_kernel, "down", shape, specs)(x, weight, *hiddens)
 
 
 def combine_kernel(x_ref, ids_ref, scale_ref, chunks_ref, out_ref):
@@ -270,19 +314,19 @@
     w_gate, w_up, w_down = w_gate[0], w_up[0], w_down[0]
     buffer = dispatch(x, ids, tokens, groups)
     chunks = lax.all_to_all(buffer, "expert", split_axis=0, concat_axis=0, tiled=True)
-    own_down, *sent = pack(x, w_gate, w_up, w_down)
-    packs = [shift(sent[d - 1], d) for d in range(1, X)]
-    other_down = cross(swap(z, own_down, packs))
-    parts = project_sent(chunks, packs)
-    arrived = [shift(parts[d - 1], -d) for d in (2, 1, 3)]
-    summed = project_own(x, chunks, w_gate, w_up)
-    for part in arrived:
-        summed = summed + part.astype(F32)
-    hidden = (jax.nn.silu(summed[:, :LANES]) * summed[:, LANES:]).astype(BF)
+    own, *sent = pack(x, w_gate, w_up, w_down)
+    packs = [own] + [shift(sent[d - 1], d) for d in range(1, X)]
+    projection, to_swap = unpack(z, packs, tokens.shape[1] // X)
+    parts = project(chunks, projection, (2, 1, 3), BF, "project_sent")
+    arrived = [shift(part, -d) for d, part in zip((2, 1, 3), parts)]
+    weight = assemble(z, packs, cross(to_swap))
+    chunks, weight = lax.optimization_barrier((chunks, weight))
+    (mine,) = project(chunks, projection, (0,), F32, "project_own")
+    hidden = activate(mine, arrived)
     swapped = cross(hidden)
     hiddens = [hidden] + [shift(hidden, d) for d in range(1, X)]
     hiddens += [swapped] + [shift(swapped, d) for d in range(1, X)]
-    output = down(x, z, hiddens, own_down, packs, other_down, groups)
+    output = down(x, weight, hiddens, groups)
     returned = lax.all_to_all(output, "expert", split_axis=0, concat_axis=0, tiled=True)
     return combine(x, ids, scale, returned, tokens.shape[1] // (2 * X))
 

time: 193 us -> 193 us (level)
  waiting for transfers between devices: 66.3 us -> 47.7 us
  blocking collectives: 35.5 us -> 49.5 us
  Pallas kernels: 8.56 us -> 15.4 us
    all_to_all x1, blocking collectives: 35.5 us -> 49.5 us  [body(): lax.all_to_all(output, 'expert', split_axis=0, concat_axis=0, tiled=True)]
    ppermute x2, waiting for transfers between devices: 10.9 us -> 0.01 us  [cross(): lax.ppermute(value, 'pipe', [(p, (p + X) % (2 * X)) for p in range(2 * X)])]
    ppermute x12, starting transfers between devices: 38 us -> 44.8 us  [shift(): return lax.ppermute(value, 'pipe', pairs)]
    ppermute x2, starting transfers between devices: 16.1 us -> 10.1 us  [cross(): lax.ppermute(value, 'pipe', [(p, (p + X) % (2 * X)) for p in range(2 * X)])]
    pallas_call x5 -> x7, Pallas kernels: 6.57 us -> 12.3 us  [the longest x1 3.54 us: dispatch(): call(dispatch_kernel, 'dispatch', out, specs, anywhere(), scratch, FULL)]
    all_to_all x1, waiting for transfers between devices: 5.19 us -> 0.01 us  [body(): lax.all_to_all(buffer, 'expert', split_axis=0, concat_axis=0, tiled=True)]
    ppermute x12, waiting for transfers between devices: 50.3 us -> 47.6 us  [shift(): return lax.ppermute(value, 'pipe', pairs)]
    unnamed x32 -> x28, local copies, waits for them, and re-layouts: 10.2 us -> 9.05 us
  transfers between devices with their start and end apart: 15 -> 15, of which waited for: 9 -> 7; matrix products, arithmetic and copies ran while one was open for 1% -> 0% of each run, Pallas kernels for 1% -> 4%
where the time goes in v7:
time: 193 us; the launch traced here: 192 us
  starting transfers between devices  69.6 us (36%)
  blocking collectives  49.5 us (26%)
  waiting for transfers between devices  47.7 us (25%)
  Pallas kernels  15.4 us (8%)
  local copies, waits for them, and re-layouts  9.81 us (5%)
    all_to_all x1, blocking collectives, body(): lax.all_to_all(output, 'expert', split_axis=0, concat_axis=0, tiled=True)  49.5 us
    ppermute x12, waiting for transfers between devices, shift(): return lax.ppermute(value, 'pipe', pairs)  47.6 us
    ppermute x12, starting transfers between devices, shift(): return lax.ppermute(value, 'pipe', pairs)  44.8 us
    all_to_all x1, starting transfers between devices, body(): lax.all_to_all(buffer, 'expert', split_axis=0, concat_axis=0, tiled=True)  14.7 us
    ppermute x2, starting transfers between devices, cross(): lax.ppermute(value, 'pipe', [(p, (p + X) % (2 * X)) for p in range(2 * X)])  10.1 us
    unnamed x28, local copies, waits for them, and re-layouts  9.05 us
  transfers between devices with their start and end apart: 15, of which 7 were waited for; matrix products, arithmetic and copies ran while one was open for 0% of the time, Pallas kernels for 4%

profile of v7, /device:TPU:1, one launch (start us, length us, event | category | flops | bytes accessed | tf_op | source)
XLA Modules:
  0.0 192.3 jit_solution(9945167294082514977)
XLA Ops:
  0.0 3.5 %dispatch.1 = bf16[64,120,128]{2,1,0:T(8,128)(2,1)} custom-call(s32[1]{0:T(128)} %bitcast.x_ref, s32[8,128]{1,0:T(8,128)} %bitcast.10, bf16[128,3584]{1,0:T(8,128)(2,1)} %tok_ref.1), custom_call_target="tpu_custom_call" | custom-call | tf_op jit(solution)/shard_map/dispatch/pallas_call | solution.py:107
  3.6 14.7 %all-to-all-start = ((bf16[64,120,128]{2,1,0:T(8,128)(2,1)}), bf16[64,120,128]{2,1,0:T(8,128)(2,1)S(1)}, u32[]{:S(2)}, u32[]{:S(2)}) async-start(bf16[64,120,128]{2,1,0:T(8,128)(2,1)} %dispatch.1), calls=%async_computation | async-start | bytes 3932160 | tf_op jit(solution)/shard_map/all_to_all | solution.py:316
  23.1 3.1 %collective-permute-start = (bf16[2816,128]{1,0:T(8,128)(2,1)}, bf16[2816,128]{1,0:T(8,128)(2,1)S(1)}, u32[]{:S(2)}, u32[]{:S(2)}) collective-permute-start(bf16[2816,128]{1,0:T(8,128)(2,1)} %get-tuple-element.17), channel_id=1, source_target_pairs={{0,64},{64,128},{128,192},{192,0},{256,320},{320,384},{384,448},{4... | collective-permute-start | bytes 2162696 | tf_op jit(solution)/shard_map/ppermute | solution.py:301
  26.2 4.4 %collective-permute-start.1 = (bf16[2816,128]{1,0:T(8,128)(2,1)}, bf16[2816,128]{1,0:T(8,128)(2,1)S(1)}, u32[]{:S(2)}, u32[]{:S(2)}) collective-permute-start(bf16[2816,128]{1,0:T(8,128)(2,1)} %get-tuple-element.18), channel_id=1, source_target_pairs={{0,128},{64,192},{128,0},{192,64},{256,384},{320,448},{384,256},{4... | collective-permute-start | bytes 2162696 | tf_op jit(solution)/shard_map/ppermute | solution.py:301
  30.6 3.1 %collective-permute-start.2 = (bf16[2816,128]{1,0:T(8,128)(2,1)}, bf16[2816,128]{1,0:T(8,128)(2,1)}, u32[]{:S(2)}, u32[]{:S(2)}) collective-permute-start(bf16[2816,128]{1,0:T(8,128)(2,1)} %get-tuple-element.19), channel_id=1, source_target_pairs={{0,192},{64,0},{128,64},{192,128},{256,448},{320,256},{384,320},{4... | collective-permute-start | bytes 2162696 | tf_op jit(solution)/shard_map/ppermute | solution.py:301
  33.7 10.0 %collective-permute-done.refs_1_ = bf16[2816,128]{1,0:T(8,128)(2,1)S(1)} collective-permute-done((bf16[2816,128]{1,0:T(8,128)(2,1)}, bf16[2816,128]{1,0:T(8,128)(2,1)S(1)}, u32[]{:S(2)}, u32[]{:S(2)}) %collective-permute-start) | collective-permute-done | bytes 720928 | tf_op jit(solution)/shard_map/ppermute | solution.py:301
  43.7 16.4 %collective-permute-done.1.refs_2_ = bf16[2816,128]{1,0:T(8,128)(2,1)S(1)} collective-permute-done((bf16[2816,128]{1,0:T(8,128)(2,1)}, bf16[2816,128]{1,0:T(8,128)(2,1)S(1)}, u32[]{:S(2)}, u32[]{:S(2)}) %collective-permute-start.1) | collective-permute-done | bytes 720928 | tf_op jit(solution)/shard_map/ppermute | solution.py:301
  63.7 2.3 %unpack.1 = (bf16[4,896,256]{2,1,0:T(8,128)(2,1)S(1)}, bf16[2048,128]{1,0:T(8,128)(2,1)}) custom-call(s32[1]{0:T(128)} %bitcast.3.z_ref, bf16[2816,128]{1,0:T(8,128)(2,1)S(1)} %copy-done.7, bf16[2816,128]{1,0:T(8,128)(2,1)S(1)} %collective-permute-done.refs_1_, bf16[2816,128]{1,0:T(8,128)(2,1)S(1)} %copy-done.10, ...), custom_call_target="tpu_custom_call" | custom-call | tf_op jit(solution)/shard_map/unpack/pallas_call | solution.py:157
  67.3 7.9 %collective-permute-start.3 = (bf16[2048,128]{1,0:T(8,128)(2,1)}, bf16[2048,128]{1,0:T(8,128)(2,1)}, u32[]{:S(2)}, u32[]{:S(2)}) collective-permute-start(bf16[2048,128]{1,0:T(8,128)(2,1)} %get-tuple-element.20), channel_id=1, source_target_pairs={{0,256},{64,320},{128,384},{192,448},{256,0},{320,64},{384,128},{4... | collective-permute-start | bytes 1572872 | tf_op jit(solution)/shard_map/ppermute | solution.py:305
  76.7 2.2 %project_sent.1 = (bf16[1088,256]{1,0:T(8,128)(2,1)S(1)}, bf16[1088,256]{1,0:T(8,128)(2,1)S(1)}, bf16[1088,256]{1,0:T(8,128)(2,1)S(1)}) custom-call(bf16[64,120,128]{2,1,0:T(8,128)(2,1)S(1)} %all-to-all-done.chunks_ref, bf16[4,896,256]{2,1,0:T(8,128)(2,1)S(1)} %copy-done.1), custom_call_target="tpu_custom_call" | custom-call | tf_op jit(solution)/shard_map/project_sent/pallas_call | solution.py:205
  78.9 4.7 %collective-permute-start.4 = (bf16[1088,256]{1,0:T(8,128)(2,1)S(1)}, bf16[1088,256]{1,0:T(8,128)(2,1)S(1)}, u32[]{:S(2)}, u32[]{:S(2)}) collective-permute-start(bf16[1088,256]{1,0:T(8,128)(2,1)S(1)} %get-tuple-element.24), channel_id=1, source_target_pairs={{0,128},{64,192},{128,0},{192,64},{256,384},{320,448},{384,256},{4... | collective-permute-start | bytes 1671176 | tf_op jit(solution)/shard_map/ppermute | solution.py:301
  83.5 4.7 %collective-permute-start.5 = (bf16[1088,256]{1,0:T(8,128)(2,1)S(1)}, bf16[1088,256]{1,0:T(8,128)(2,1)S(1)}, u32[]{:S(2)}, u32[]{:S(2)}) collective-permute-start(bf16[1088,256]{1,0:T(8,128)(2,1)S(1)} %get-tuple-element.25), channel_id=1, source_target_pairs={{0,192},{64,0},{128,64},{192,128},{256,448},{320,256},{384,320},{4... | collective-permute-start | bytes 1671176 | tf_op jit(solution)/shard_map/ppermute | solution.py:301
  88.3 2.1 %collective-permute-start.6 = (bf16[1088,256]{1,0:T(8,128)(2,1)S(1)}, bf16[1088,256]{1,0:T(8,128)(2,1)S(1)}, u32[]{:S(2)}, u32[]{:S(2)}) collective-permute-start(bf16[1088,256]{1,0:T(8,128)(2,1)S(1)} %get-tuple-element.26), channel_id=1, source_target_pairs={{0,64},{64,128},{128,192},{192,0},{256,320},{320,384},{384,448},{4... | collective-permute-start | bytes 1671176 | tf_op jit(solution)/shard_map/ppermute | solution.py:301
  94.6 14.2 %collective-permute-done.5.refs_1_ = bf16[1088,256]{1,0:T(8,128)(2,1)S(1)} collective-permute-done((bf16[1088,256]{1,0:T(8,128)(2,1)S(1)}, bf16[1088,256]{1,0:T(8,128)(2,1)S(1)}, u32[]{:S(2)}, u32[]{:S(2)}) %collective-permute-start.5) | collective-permute-done | bytes 557088 | tf_op jit(solution)/shard_map/ppermute | solution.py:301
  109.1 2.1 %collective-permute-start.10 = (bf16[1088,128]{1,0:T(8,128)(2,1)S(1)}, bf16[1088,128]{1,0:T(8,128)(2,1)S(1)}, u32[]{:S(2)}, u32[]{:S(2)}) collective-permute-start(bf16[1088,128]{1,0:T(8,128)(2,1)S(1)} %activate.1.refs_0_), channel_id=1, source_target_pairs={{0,256},{64,320},{128,384},{192,448},{256,0},{320,64},{384,128},{4... | collective-permute-start | bytes 835592 | tf_op jit(solution)/shard_map/ppermute | solution.py:305
  111.3 4.9 %collective-permute-start.7 = (bf16[1088,128]{1,0:T(8,128)(2,1)S(1)}, bf16[1088,128]{1,0:T(8,128)(2,1)S(1)}, u32[]{:S(2)}, u32[]{:S(2)}) collective-permute-start(bf16[1088,128]{1,0:T(8,128)(2,1)S(1)} %activate.1.refs_0_), channel_id=1, source_target_pairs={{0,64},{64,128},{128,192},{192,0},{256,320},{320,384},{384,448},{4... | collective-permute-start | bytes 835592 | tf_op jit(solution)/shard_map/ppermute | solution.py:301
  116.1 3.3 %collective-permute-start.8 = (bf16[1088,128]{1,0:T(8,128)(2,1)S(1)}, bf16[1088,128]{1,0:T(8,128)(2,1)S(1)}, u32[]{:S(2)}, u32[]{:S(2)}) collective-permute-start(bf16[1088,128]{1,0:T(8,128)(2,1)S(1)} %activate.1.refs_0_), channel_id=1, source_target_pairs={{0,128},{64,192},{128,0},{192,64},{256,384},{320,448},{384,256},{4... | collective-permute-start | bytes 835592 | tf_op jit(solution)/shard_map/ppermute | solution.py:301
  119.5 2.9 %collective-permute-start.9 = (bf16[1088,128]{1,0:T(8,128)(2,1)S(1)}, bf16[1088,128]{1,0:T(8,128)(2,1)S(1)}, u32[]{:S(2)}, u32[]{:S(2)}) collective-permute-start(bf16[1088,128]{1,0:T(8,128)(2,1)S(1)} %activate.1.refs_0_), channel_id=1, source_target_pairs={{0,192},{64,0},{128,64},{192,128},{256,448},{320,256},{384,320},{4... | collective-permute-start | bytes 835592 | tf_op jit(solution)/shard_map/ppermute | solution.py:301
  122.4 5.5 %collective-permute-start.11 = (bf16[1088,128]{1,0:T(8,128)(2,1)S(1)}, bf16[1088,128]{1,0:T(8,128)(2,1)S(1)}, u32[]{:S(2)}, u32[]{:S(2)}) collective-permute-start(bf16[1088,128]{1,0:T(8,128)(2,1)S(1)} %collective-permute-done.10.refs_4_), channel_id=1, source_target_pairs={{0,64},{64,128},{128,192},{192,0},{256,320},{320,384},{384,448},{4... | collective-permute-start | bytes 835592 | tf_op jit(solution)/shard_map/ppermute | solution.py:301
  127.9 3.3 %collective-permute-start.12 = (bf16[1088,128]{1,0:T(8,128)(2,1)S(1)}, bf16[1088,128]{1,0:T(8,128)(2,1)S(1)}, u32[]{:S(2)}, u32[]{:S(2)}) collective-permute-start(bf16[1088,128]{1,0:T(8,128)(2,1)S(1)} %collective-permute-done.10.refs_4_), channel_id=1, source_target_pairs={{0,128},{64,192},{128,0},{192,64},{256,384},{320,448},{384,256},{4... | collective-permute-start | bytes 835592 | tf_op jit(solution)/shard_map/ppermute | solution.py:301
  131.3 2.9 %collective-permute-start.13 = (bf16[1088,128]{1,0:T(8,128)(2,1)S(1)}, bf16[1088,128]{1,0:T(8,128)(2,1)S(1)}, u32[]{:S(2)}, u32[]{:S(2)}) collective-permute-start(bf16[1088,128]{1,0:T(8,128)(2,1)S(1)} %collective-permute-done.10.refs_4_), channel_id=1, source_target_pairs={{0,192},{64,0},{128,64},{192,128},{256,448},{320,256},{384,320},{4... | collective-permute-start | bytes 835592 | tf_op jit(solution)/shard_map/ppermute | solution.py:301
  134.2 2.5 %collective-permute-done.12.refs_6_ = bf16[1088,128]{1,0:T(8,128)(2,1)S(1)} collective-permute-done((bf16[1088,128]{1,0:T(8,128)(2,1)S(1)}, bf16[1088,128]{1,0:T(8,128)(2,1)S(1)}, u32[]{:S(2)}, u32[]{:S(2)}) %collective-permute-start.12) | collective-permute-done | bytes 278560 | tf_op jit(solution)/shard_map/ppermute | solution.py:301
  136.7 2.1 %collective-permute-done.13.refs_7_ = bf16[1088,128]{1,0:T(8,128)(2,1)S(1)} collective-permute-done((bf16[1088,128]{1,0:T(8,128)(2,1)S(1)}, bf16[1088,128]{1,0:T(8,128)(2,1)S(1)}, u32[]{:S(2)}, u32[]{:S(2)}) %collective-permute-start.13) | collective-permute-done | bytes 278560 | tf_op jit(solution)/shard_map/ppermute | solution.py:301
  140.4 49.5 %all_to_all.10.chunks_ref = bf16[64,64,128]{2,1,0:T(8,128)(2,1)S(1)} all-to-all(bf16[64,64,128]{2,1,0:T(8,128)(2,1)S(1)} %down.1), channel_id=1, replica_groups=mesh['pipe'=8,'expert'=64] {'expert'}, dimensions={0} | all-to-all | bytes 2097152 | tf_op jit(solution)/shard_map/all_to_all | solution.py:330
  (45 shorter events, 19.6 us)
Async XLA Ops:
  3.5 14.8 %copy-start.3 = (bf16[1,3584,128]{2,1,0:T(8,128)(2,1)S(1)}, bf16[1,3584,128]{2,1,0:T(8,128)(2,1)}, u32[]{:S(2)}) copy-start(bf16[1,3584,128]{2,1,0:T(8,128)(2,1)} %param.9) | copy-start | bytes 2752516
  3.6 71.6 %all-to-all-start = ((bf16[64,120,128]{2,1,0:T(8,128)(2,1)}), bf16[64,120,128]{2,1,0:T(8,128)(2,1)S(1)}, u32[]{:S(2)}, u32[]{:S(2)}) async-start(bf16[64,120,128]{2,1,0:T(8,128)(2,1)} %dispatch.1), calls=%async_computation | async-start | bytes 3932160 | tf_op jit(solution)/shard_map/all_to_all | solution.py:316
  18.3 1.2 copy-start.4
  23.1 20.6 %collective-permute-start = (bf16[2816,128]{1,0:T(8,128)(2,1)}, bf16[2816,128]{1,0:T(8,128)(2,1)S(1)}, u32[]{:S(2)}, u32[]{:S(2)}) collective-permute-start(bf16[2816,128]{1,0:T(8,128)(2,1)} %get-tuple-element.17), channel_id=1, source_target_pairs={{0,64},{64,128},{128,192},{192,0},{256,320},{320,384},{384,448},{4... | collective-permute-start | bytes 2162696 | tf_op jit(solution)/shard_map/ppermute | solution.py:301
  26.2 33.9 %collective-permute-start.1 = (bf16[2816,128]{1,0:T(8,128)(2,1)}, bf16[2816,128]{1,0:T(8,128)(2,1)S(1)}, u32[]{:S(2)}, u32[]{:S(2)}) collective-permute-start(bf16[2816,128]{1,0:T(8,128)(2,1)} %get-tuple-element.18), channel_id=1, source_target_pairs={{0,128},{64,192},{128,0},{192,64},{256,384},{320,448},{384,256},{4... | collective-permute-start | bytes 2162696 | tf_op jit(solution)/shard_map/ppermute | solution.py:301
  30.6 30.9 %collective-permute-start.2 = (bf16[2816,128]{1,0:T(8,128)(2,1)}, bf16[2816,128]{1,0:T(8,128)(2,1)}, u32[]{:S(2)}, u32[]{:S(2)}) collective-permute-start(bf16[2816,128]{1,0:T(8,128)(2,1)} %get-tuple-element.19), channel_id=1, source_target_pairs={{0,192},{64,0},{128,64},{192,128},{256,448},{320,256},{384,320},{4... | collective-permute-start | bytes 2162696 | tf_op jit(solution)/shard_map/ppermute | solution.py:301
  63.7 26.6 %copy-start.8 = (bf16[2816,128]{1,0:T(8,128)(2,1)S(1)}, bf16[2816,128]{1,0:T(8,128)(2,1)}, u32[]{:S(2)}) copy-start(bf16[2816,128]{1,0:T(8,128)(2,1)} %copy-done.6) | copy-start | bytes 2162692
  66.1 1.2 copy-start
  67.3 23.1 %collective-permute-start.3 = (bf16[2048,128]{1,0:T(8,128)(2,1)}, bf16[2048,128]{1,0:T(8,128)(2,1)}, u32[]{:S(2)}, u32[]{:S(2)}) collective-permute-start(bf16[2048,128]{1,0:T(8,128)(2,1)} %get-tuple-element.20), channel_id=1, source_target_pairs={{0,256},{64,320},{128,384},{192,448},{256,0},{320,64},{384,128},{4... | collective-permute-start | bytes 1572872 | tf_op jit(solution)/shard_map/ppermute | solution.py:305
  75.2 1.5 copy-start.1
  76.7 13.6 %copy-start.11 = (bf16[2816,128]{1,0:T(8,128)(2,1)S(1)}, bf16[2816,128]{1,0:T(8,128)(2,1)}, u32[]{:S(2)}) copy-start(bf16[2816,128]{1,0:T(8,128)(2,1)} %copy-done.9) | copy-start | bytes 2162692
  78.9 15.7 %collective-permute-start.4 = (bf16[1088,256]{1,0:T(8,128)(2,1)S(1)}, bf16[1088,256]{1,0:T(8,128)(2,1)S(1)}, u32[]{:S(2)}, u32[]{:S(2)}) collective-permute-start(bf16[1088,256]{1,0:T(8,128)(2,1)S(1)} %get-tuple-element.24), channel_id=1, source_target_pairs={{0,128},{64,192},{128,0},{192,64},{256,384},{320,448},{384,256},{4... | collective-permute-start | bytes 1671176 | tf_op jit(solution)/shard_map/ppermute | solution.py:301
  83.5 25.2 %collective-permute-start.5 = (bf16[1088,256]{1,0:T(8,128)(2,1)S(1)}, bf16[1088,256]{1,0:T(8,128)(2,1)S(1)}, u32[]{:S(2)}, u32[]{:S(2)}) collective-permute-start(bf16[1088,256]{1,0:T(8,128)(2,1)S(1)} %get-tuple-element.25), channel_id=1, source_target_pairs={{0,192},{64,0},{128,64},{192,128},{256,448},{320,256},{384,320},{4... | collective-permute-start | bytes 1671176 | tf_op jit(solution)/shard_map/ppermute | solution.py:301
  88.3 3.5 %copy-start.2 = (bf16[4,896,256]{2,1,0:T(8,128)(2,1)S(1)}, bf16[4,896,256]{2,1,0:T(8,128)(2,1)}, u32[]{:S(2)}) copy-start(bf16[4,896,256]{2,1,0:T(8,128)(2,1)} %copy-done) | copy-start | bytes 5505028
  88.3 20.5 %collective-permute-start.6 = (bf16[1088,256]{1,0:T(8,128)(2,1)S(1)}, bf16[1088,256]{1,0:T(8,128)(2,1)S(1)}, u32[]{:S(2)}, u32[]{:S(2)}) collective-permute-start(bf16[1088,256]{1,0:T(8,128)(2,1)S(1)} %get-tuple-element.26), channel_id=1, source_target_pairs={{0,64},{64,128},{128,192},{192,0},{256,320},{320,384},{384,448},{4... | collective-permute-start | bytes 1671176 | tf_op jit(solution)/shard_map/ppermute | solution.py:301
  109.1 13.2 %collective-permute-start.10 = (bf16[1088,128]{1,0:T(8,128)(2,1)S(1)}, bf16[1088,128]{1,0:T(8,128)(2,1)S(1)}, u32[]{:S(2)}, u32[]{:S(2)}) collective-permute-start(bf16[1088,128]{1,0:T(8,128)(2,1)S(1)} %activate.1.refs_0_), channel_id=1, source_target_pairs={{0,256},{64,320},{128,384},{192,448},{256,0},{320,64},{384,128},{4... | collective-permute-start | bytes 835592 | tf_op jit(solution)/shard_map/ppermute | solution.py:305
  111.3 20.0 %collective-permute-start.7 = (bf16[1088,128]{1,0:T(8,128)(2,1)S(1)}, bf16[1088,128]{1,0:T(8,128)(2,1)S(1)}, u32[]{:S(2)}, u32[]{:S(2)}) collective-permute-start(bf16[1088,128]{1,0:T(8,128)(2,1)S(1)} %activate.1.refs_0_), channel_id=1, source_target_pairs={{0,64},{64,128},{128,192},{192,0},{256,320},{320,384},{384,448},{4... | collective-permute-start | bytes 835592 | tf_op jit(solution)/shard_map/ppermute | solution.py:301
  116.1 18.0 %collective-permute-start.8 = (bf16[1088,128]{1,0:T(8,128)(2,1)S(1)}, bf16[1088,128]{1,0:T(8,128)(2,1)S(1)}, u32[]{:S(2)}, u32[]{:S(2)}) collective-permute-start(bf16[1088,128]{1,0:T(8,128)(2,1)S(1)} %activate.1.refs_0_), channel_id=1, source_target_pairs={{0,128},{64,192},{128,0},{192,64},{256,384},{320,448},{384,256},{4... | collective-permute-start | bytes 835592 | tf_op jit(solution)/shard_map/ppermute | solution.py:301
  119.5 14.7 %collective-permute-start.9 = (bf16[1088,128]{1,0:T(8,128)(2,1)S(1)}, bf16[1088,128]{1,0:T(8,128)(2,1)S(1)}, u32[]{:S(2)}, u32[]{:S(2)}) collective-permute-start(bf16[1088,128]{1,0:T(8,128)(2,1)S(1)} %activate.1.refs_0_), channel_id=1, source_target_pairs={{0,192},{64,0},{128,64},{192,128},{256,448},{320,256},{384,320},{4... | collective-permute-start | bytes 835592 | tf_op jit(solution)/shard_map/ppermute | solution.py:301
  122.4 11.8 %collective-permute-start.11 = (bf16[1088,128]{1,0:T(8,128)(2,1)S(1)}, bf16[1088,128]{1,0:T(8,128)(2,1)S(1)}, u32[]{:S(2)}, u32[]{:S(2)}) collective-permute-start(bf16[1088,128]{1,0:T(8,128)(2,1)S(1)} %collective-permute-done.10.refs_4_), channel_id=1, source_target_pairs={{0,64},{64,128},{128,192},{192,0},{256,320},{320,384},{384,448},{4... | collective-permute-start | bytes 835592 | tf_op jit(solution)/shard_map/ppermute | solution.py:301
  127.9 8.8 %collective-permute-start.12 = (bf16[1088,128]{1,0:T(8,128)(2,1)S(1)}, bf16[1088,128]{1,0:T(8,128)(2,1)S(1)}, u32[]{:S(2)}, u32[]{:S(2)}) collective-permute-start(bf16[1088,128]{1,0:T(8,128)(2,1)S(1)} %collective-permute-done.10.refs_4_), channel_id=1, source_target_pairs={{0,128},{64,192},{128,0},{192,64},{256,384},{320,448},{384,256},{4... | collective-permute-start | bytes 835592 | tf_op jit(solution)/shard_map/ppermute | solution.py:301
  131.3 7.6 %collective-permute-start.13 = (bf16[1088,128]{1,0:T(8,128)(2,1)S(1)}, bf16[1088,128]{1,0:T(8,128)(2,1)S(1)}, u32[]{:S(2)}, u32[]{:S(2)}) collective-permute-start(bf16[1088,128]{1,0:T(8,128)(2,1)S(1)} %collective-permute-done.10.refs_4_), channel_id=1, source_target_pairs={{0,192},{64,0},{128,64},{192,128},{256,448},{320,256},{384,320},{4... | collective-permute-start | bytes 835592 | tf_op jit(solution)/shard_map/ppermute | solution.py:301
  140.4 49.5 %copy-start.12 = (s32[128,8]{0,1:T(8,128)S(1)}, s32[128,8]{0,1:T(8,128)}, u32[]{:S(2)}) copy-start(s32[128,8]{0,1:T(8,128)} %param.7) | copy-start | bytes 12292
  140.4 49.5 %copy-start.13 = (f32[128,8]{0,1:T(8,128)S(1)}, f32[128,8]{0,1:T(8,128)}, u32[]{:S(2)}) copy-start(f32[128,8]{0,1:T(8,128)} %param.8) | copy-start | bytes 12292
  (5 other events, 5.1 us)

commit v8 on v7

--- a/solution.py
+++ b/solution.py
@@ -10,7 +10,6 @@
 LANES = 128
 X = 4
 PARTS = 4
-HOLD = 50_000_000_000
 FULL = 60 * 1024 * 1024
 VMEM = 16 * 1024 * 1024
 
@@ -107,73 +106,50 @@
     return call(dispatch_kernel, "dispatch", out, specs, anywhere(), scratch, FULL)(x, ids, tokens)
 
 
-def pack_kernel(x_ref, gate_ref, up_ref, down_ref, *outs):
+def pack_kernel(x_ref, z_ref, gate_ref, up_ref, down_ref, *outs):
+    near, far = outs[:X], outs[X:]
     quarter = gate_ref.shape[0] // X
     depth = down_ref.shape[0]
 
-    def put_down(out, base, q):
-        for z in range(2):
-            p = z * X + q
-            pair, odd = p // 2, lax.rem(p, 2)
-            first = pair * (quarter // LANES) + 4 * odd
-            half = pair * (quarter // LANES) + 3
-            for c in range(4):
-                tile = half if c == 3 else first + c
-                cols = pl.ds(pl.multiple_of(tile * LANES, LANES), LANES)
-                out[pl.ds(base + (z * 4 + c) * depth, depth), :] = down_ref[:, cols]
-
-    for d, out in enumerate(outs):
+    def put_down(out, base, z, q):
+        p = z * X + q
+        first = p // 2 * (quarter // LANES)
+        for c in range(4):
+            tile = first + 3 if c == 3 else first + c + 4 * lax.rem(p, 2)
+            cols = pl.ds(pl.multiple_of(tile * LANES, LANES), LANES)
+            out[pl.ds(base + c * depth, depth), :] = down_ref[:, cols]
+
+    for d in range(X):
         q = lax.rem(x_ref[0] + d, X)
         part = pl.ds(pl.multiple_of(q * quarter, quarter), quarter)
-        out[pl.ds(0, quarter), :] = gate_ref[part, :]
-        out[pl.ds(quarter, quarter), :] = up_ref[part, :]
-        put_down(out, 2 * quarter, q)
-
-
-def pack(x, w_gate, w_up, w_down):
-    depth = w_down.shape[0]
-    rows = 2 * (w_gate.shape[0] // X) + 8 * depth
-    shapes = [jax.ShapeDtypeStruct((r, LANES), BF) for r in [rows] * X]
-    return call(pack_kernel, "pack", shapes, [in_smem()] + [in_vmem()] * 3)(x, w_gate, w_up, w_down)
-
-
-def unpack_kernel(z_ref, *refs):
-    packs, (weight_ref, out_ref) = refs[:X], refs[X:]
-    quarter = weight_ref.shape[1]
-    rows = out_ref.shape[0] // X
-    start = pl.multiple_of(2 * quarter + (1 - z_ref[0]) * rows, LANES)
-    for d, ref in enumerate(packs):
-        weight_ref[d, :, pl.ds(0, LANES)] = ref[pl.ds(0, quarter), :]
-        weight_ref[d, :, pl.ds(LANES, LANES)] = ref[pl.ds(quarter, quarter), :]
-        out_ref[pl.ds(d * rows, rows), :] = ref[pl.ds(start, rows), :]
-
-
-def unpack(z, packs, quarter):
-    rows = (packs[0].shape[0] - 2 * quarter) // 2
-    shapes = [
-        jax.ShapeDtypeStruct((X, quarter, 2 * LANES), BF),
-        jax.ShapeDtypeStruct((X * rows, LANES), BF),
-    ]
-    return call(unpack_kernel, "unpack", shapes, [in_smem()] + [in_vmem()] * X)(z, *packs)
-
-
-def assemble_kernel(z_ref, *refs):
-    packs, (other_ref, out_ref) = refs[:X], refs[X:]
-    rows = other_ref.shape[0] // X
+        near[d][pl.ds(0, quarter), :] = gate_ref[part, :]
+        near[d][pl.ds(quarter, quarter), :] = up_ref[part, :]
+        put_down(near[d], 2 * quarter, z_ref[0], q)
+        put_down(far[d], 0, 1 - z_ref[0], q)
+
+
+def pack(x, z, w_gate, w_up, w_down):
+    rows = 2 * (w_gate.shape[0] // X) + 4 * w_down.shape[0]
+    shapes = [jax.ShapeDtypeStruct((r, LANES), BF) for r in [rows] * X + [4 * w_down.shape[0]] * X]
+    outs = call(pack_kernel, "pack", shapes, [in_smem()] * 2 + [in_vmem()] * 3)(x, z, w_gate, w_up, w_down)
+    return outs[:X], outs[X:]
+
+
+def assemble_kernel(*refs):
+    near, far, out_ref = refs[:X], refs[X : 2 * X], refs[2 * X]
+    rows = far[0].shape[0]
     depth = rows // 4
-    for d, ref in enumerate(packs):
-        base = ref.shape[0] - 2 * rows + z_ref[0] * rows
+    for d in range(X):
+        base = near[d].shape[0] - rows
         for c in range(4):
             cols = pl.ds(c * LANES, LANES)
-            out_ref[pl.ds(d * depth, depth), cols] = ref[pl.ds(pl.multiple_of(base + c * depth, LANES), depth), :]
-            out_ref[pl.ds((X + d) * depth, depth), cols] = other_ref[pl.ds(d * rows + c * depth, depth), :]
-
-
-def assemble(z, packs, other):
-    shape = jax.ShapeDtypeStruct((other.shape[0] // 2, 4 * LANES), BF)
-    specs = [in_smem()] + [in_vmem()] * (X + 1)
-    cost = pl.CostEstimate(flops=HOLD, bytes_accessed=4 * other.size, transcendentals=0)
-    return call(assemble_kernel, "assemble", shape, specs, cost=cost)(z, *packs, other)
+            out_ref[pl.ds(d * depth, depth), cols] = near[d][pl.ds(base + c * depth, depth), :]
+            out_ref[pl.ds((X + d) * depth, depth), cols] = far[d][pl.ds(c * depth, depth), :]
+
+
+def assemble(near, far):
+    shape = jax.ShapeDtypeStruct((2 * far[0].shape[0], 4 * LANES), BF)
+    return call(assemble_kernel, "assemble", shape, [in_vmem()] * (2 * X))(*near, *far)
 
 
 def stacked(chunks_ref):
@@ -189,20 +165,32 @@
     return jnp.concatenate(main, axis=1), jnp.concatenate(last, axis=1)
 
 
-def project_into(out_ref, main, last, weight):
-    count = main.shape[0]
-    out_ref[pl.ds(0, count), :] = jnp.dot(main, weight, preferred_element_type=F32).astype(out_ref.dtype)
-    out_ref[pl.ds(count, last.shape[0]), :] = jnp.dot(last, weight, preferred_element_type=F32).astype(out_ref.dtype)
-
-
-def project(chunks, weight, blocks, dtype, name):
-    def kernel(chunks_ref, weight_ref, *outs):
+def project(chunks, packs, dtype, name):
+    sources, depth, _ = chunks.shape
+    quarter = depth // 16 * LANES
+
+    def kernel(chunks_ref, *refs):
+        count = len(packs)
+        sent, outs, (weight_ref, sems) = refs[:count], refs[count : 2 * count], refs[2 * count :]
+        copies = []
+        for d in range(count):
+            for half in range(2):
+                rows, cols = pl.ds(half * quarter, quarter), pl.ds(half * LANES, LANES)
+                copy = pltpu.make_async_copy(sent[d].at[rows, :], weight_ref.at[d, :, cols], sems.at[d, half])
+                copy.start()
+                copies.append(copy)
         main, last = stacked(chunks_ref)
-        for d, out_ref in zip(blocks, outs):
-            project_into(out_ref, main, last, weight_ref[d])
-
-    shapes = [jax.ShapeDtypeStruct((chunks.shape[0] * 17, 2 * LANES), dtype)] * len(blocks)
-    return call(kernel, name, shapes, [in_vmem()] * 2)(chunks, weight)
+        for d in range(count):
+            copies[2 * d].wait()
+            copies[2 * d + 1].wait()
+            weight = weight_ref[d]
+            outs[d][pl.ds(0, sources * 16), :] = jnp.dot(main, weight, preferred_element_type=F32).astype(dtype)
+            outs[d][pl.ds(sources * 16, sources), :] = jnp.dot(last, weight, preferred_element_type=F32).astype(dtype)
+
+    shapes = [jax.ShapeDtypeStruct((sources * 17, 2 * LANES), dtype)] * len(packs)
+    scratch = [pltpu.VMEM((len(packs), quarter, 2 * LANES), BF), pltpu.SemaphoreType.DMA((len(packs), 2))]
+    specs = [in_vmem()] + [anywhere()] * len(packs)
+    return call(kernel, name, shapes, specs, scratch=scratch)(chunks, *packs)
 
 
 def activate_kernel(own_ref, *refs):
@@ -301,8 +289,9 @@
     return lax.ppermute(value, "pipe", pairs)
 
 
-def cross(value):
-    return lax.ppermute(value, "pipe", [(p, (p + X) % (2 * X)) for p in range(2 * X)])
+def cross(value, d=0):
+    pairs = [(z * X + x, (1 - z) * X + (x + d) % X) for z in range(2) for x in range(X)]
+    return lax.ppermute(value, "pipe", pairs)
 
 
 def body(tokens, expert_ids, gate_scale, w_gate, w_up, w_down):
@@ -314,14 +303,14 @@
     w_gate, w_up, w_down = w_gate[0], w_up[0], w_down[0]
     buffer = dispatch(x, ids, tokens, groups)
     chunks = lax.all_to_all(buffer, "expert", split_axis=0, concat_axis=0, tiled=True)
-    own, *sent = pack(x, w_gate, w_up, w_down)
-    packs = [own] + [shift(sent[d - 1], d) for d in range(1, X)]
-    projection, to_swap = unpack(z, packs, tokens.shape[1] // X)
-    parts = project(chunks, projection, (2, 1, 3), BF, "project_sent")
+    near, far = pack(x, z, w_gate, w_up, w_down)
+    near = [near[0]] + [shift(near[d], d) for d in range(1, X)]
+    far = [cross(far[d], d) for d in range(X)]
+    chunks, *far = lax.optimization_barrier((chunks, *far))
+    parts = project(chunks, [near[d] for d in (2, 1, 3)], BF, "project_sent")
     arrived = [shift(part, -d) for d, part in zip((2, 1, 3), parts)]
-    weight = assemble(z, packs, cross(to_swap))
-    chunks, weight = lax.optimization_barrier((chunks, weight))
-    (mine,) = project(chunks, projection, (0,), F32, "project_own")
+    (mine,) = project(chunks, near[:1], F32, "project_own")
+    weight = assemble(near, far)
     hidden = activate(mine, arrived)
     swapped = cross(hidden)
     hiddens = [hidden] + [shift(hidden, d) for d in range(1, X)]

time: 193 us -> 216 us (1.12)
  waiting for transfers between devices: 47.7 us -> 73.7 us
  starting transfers between devices: 69.6 us -> 81.9 us
  blocking collectives: 49.5 us -> 40.3 us
  local copies, waits for them, and re-layouts: 9.81 us -> 3.79 us
    ppermute x2 -> x5, waiting for transfers between devices: 0.01 us -> 40 us  [cross(): return lax.ppermute(value, 'pipe', pairs)]
    ppermute x2 -> x5, starting transfers between devices: 10.1 us -> 28.9 us  [cross(): return lax.ppermute(value, 'pipe', pairs)]
    ppermute x12, waiting for transfers between devices: 47.6 us -> 33.7 us  [shift(): return lax.ppermute(value, 'pipe', pairs)]
    all_to_all x1, blocking collectives: 49.5 us -> 40.3 us  [body(): lax.all_to_all(output, 'expert', split_axis=0, concat_axis=0, tiled=True)]
    ppermute x12, starting transfers between devices: 44.8 us -> 38.2 us  [shift(): return lax.ppermute(value, 'pipe', pairs)]
    unnamed x28 -> x14, local copies, waits for them, and re-layouts: 9.05 us -> 3.03 us
    pallas_call x5 -> x4, Pallas kernels: 8.41 us -> 8.35 us  [the longest x2 5.56 us: project(): return call(kernel, name, shapes, specs, scratch=scratch)(chunks, *packs)]
  transfers between devices with their start and end apart: 15 -> 18, of which waited for: 7 -> 8; matrix products, arithmetic and copies ran while one was open for 0% -> 0% of each run, Pallas kernels for 4% -> 2%
where the time goes in v8:
time: 216 us; the launch traced here: 215 us
  starting transfers between devices  81.9 us (38%)
  waiting for transfers between devices  73.7 us (34%)
  blocking collectives  40.3 us (19%)
  Pallas kernels  15.5 us (7%)
  local copies, waits for them, and re-layouts  3.79 us (2%)
    all_to_all x1, blocking collectives, body(): lax.all_to_all(output, 'expert', split_axis=0, concat_axis=0, tiled=True)  40.3 us
    ppermute x5, waiting for transfers between devices, cross(): return lax.ppermute(value, 'pipe', pairs)  40 us
    ppermute x12, starting transfers between devices, shift(): return lax.ppermute(value, 'pipe', pairs)  38.2 us
    ppermute x12, waiting for transfers between devices, shift(): return lax.ppermute(value, 'pipe', pairs)  33.7 us
    ppermute x5, starting transfers between devices, cross(): return lax.ppermute(value, 'pipe', pairs)  28.9 us
    all_to_all x1, starting transfers between devices, body(): lax.all_to_all(buffer, 'expert', split_axis=0, concat_axis=0, tiled=True)  14.7 us
    pallas_call x2, Pallas kernels, project(): return call(kernel, name, shapes, specs, scratch=scratch)(chunks, *packs)  5.56 us
  transfers between devices with their start and end apart: 18, of which 8 were waited for; matrix products, arithmetic and copies ran while one was open for 0% of the time, Pallas kernels for 2%

profile of v8, /device:TPU:1, one launch (start us, length us, event | category | flops | bytes accessed | tf_op | source)
XLA Modules:
  0.0 215.5 jit_solution(9767013973187977371)
XLA Ops:
  0.0 3.5 %dispatch.1 = bf16[64,120,128]{2,1,0:T(8,128)(2,1)} custom-call(s32[1]{0:T(128)} %bitcast.x_ref, s32[8,128]{1,0:T(8,128)} %bitcast.10, bf16[128,3584]{1,0:T(8,128)(2,1)} %tok_ref.1), custom_call_target="tpu_custom_call" | custom-call | tf_op jit(solution)/shard_map/dispatch/pallas_call | solution.py:106
  3.6 14.7 %all-to-all-start = ((bf16[64,120,128]{2,1,0:T(8,128)(2,1)}), bf16[64,120,128]{2,1,0:T(8,128)(2,1)S(1)}, u32[]{:S(2)}, u32[]{:S(2)}) async-start(bf16[64,120,128]{2,1,0:T(8,128)(2,1)} %dispatch.1), calls=%async_computation | async-start | bytes 3932160 | tf_op jit(solution)/shard_map/all_to_all | solution.py:305
  22.0 3.1 %collective-permute-start = (bf16[2304,128]{1,0:T(8,128)(2,1)}, bf16[2304,128]{1,0:T(8,128)(2,1)S(1)}, u32[]{:S(2)}, u32[]{:S(2)}) collective-permute-start(bf16[2304,128]{1,0:T(8,128)(2,1)} %get-tuple-element.22), channel_id=1, source_target_pairs={{0,64},{64,128},{128,192},{192,0},{256,320},{320,384},{384,448},{4... | collective-permute-start | bytes 1769480 | tf_op jit(solution)/shard_map/ppermute | solution.py:289
  25.1 4.4 %collective-permute-start.1 = (bf16[2304,128]{1,0:T(8,128)(2,1)}, bf16[2304,128]{1,0:T(8,128)(2,1)}, u32[]{:S(2)}, u32[]{:S(2)}) collective-permute-start(bf16[2304,128]{1,0:T(8,128)(2,1)} %get-tuple-element.23), channel_id=1, source_target_pairs={{0,128},{64,192},{128,0},{192,64},{256,384},{320,448},{384,256},{4... | collective-permute-start | bytes 1769480 | tf_op jit(solution)/shard_map/ppermute | solution.py:289
  29.5 3.1 %collective-permute-start.2 = (bf16[2304,128]{1,0:T(8,128)(2,1)}, bf16[2304,128]{1,0:T(8,128)(2,1)}, u32[]{:S(2)}, u32[]{:S(2)}) collective-permute-start(bf16[2304,128]{1,0:T(8,128)(2,1)} %get-tuple-element.24), channel_id=1, source_target_pairs={{0,192},{64,0},{128,64},{192,128},{256,448},{320,256},{384,320},{4... | collective-permute-start | bytes 1769480 | tf_op jit(solution)/shard_map/ppermute | solution.py:289
  32.6 7.9 %collective-permute-start.3 = (bf16[512,128]{1,0:T(8,128)(2,1)S(1)}, bf16[512,128]{1,0:T(8,128)(2,1)S(1)}, u32[]{:S(2)}, u32[]{:S(2)}) collective-permute-start(bf16[512,128]{1,0:T(8,128)(2,1)S(1)} %get-tuple-element.25), channel_id=1, source_target_pairs={{0,256},{64,320},{128,384},{192,448},{256,0},{320,64},{384,128},{4... | collective-permute-start | bytes 393224 | tf_op jit(solution)/shard_map/ppermute | solution.py:294
  42.5 36.2 %collective-permute-done.3.refs_4_ = bf16[512,128]{1,0:T(8,128)(2,1)S(1)} collective-permute-done((bf16[512,128]{1,0:T(8,128)(2,1)S(1)}, bf16[512,128]{1,0:T(8,128)(2,1)S(1)}, u32[]{:S(2)}, u32[]{:S(2)}) %collective-permute-start.3) | collective-permute-done | bytes 131104 | tf_op jit(solution)/shard_map/ppermute | solution.py:294
  78.7 6.5 %collective-permute-start.5 = (bf16[512,128]{1,0:T(8,128)(2,1)S(1)}, bf16[512,128]{1,0:T(8,128)(2,1)S(1)}, u32[]{:S(2)}, u32[]{:S(2)}) collective-permute-start(bf16[512,128]{1,0:T(8,128)(2,1)S(1)} %get-tuple-element.27), channel_id=1, source_target_pairs={{0,384},{64,448},{128,256},{192,320},{256,128},{320,192},{384,0},{... | collective-permute-start | bytes 393224 | tf_op jit(solution)/shard_map/ppermute | solution.py:294
  85.3 6.8 %collective-permute-start.6 = (bf16[512,128]{1,0:T(8,128)(2,1)S(1)}, bf16[512,128]{1,0:T(8,128)(2,1)S(1)}, u32[]{:S(2)}, u32[]{:S(2)}) collective-permute-start(bf16[512,128]{1,0:T(8,128)(2,1)S(1)} %get-tuple-element.28), channel_id=1, source_target_pairs={{0,448},{64,256},{128,320},{192,384},{256,192},{320,0},{384,64},{4... | collective-permute-start | bytes 393224 | tf_op jit(solution)/shard_map/ppermute | solution.py:294
  92.1 3.7 %collective-permute-done.6.refs_7_ = bf16[512,128]{1,0:T(8,128)(2,1)S(1)} collective-permute-done((bf16[512,128]{1,0:T(8,128)(2,1)S(1)}, bf16[512,128]{1,0:T(8,128)(2,1)S(1)}, u32[]{:S(2)}, u32[]{:S(2)}) %collective-permute-start.6) | collective-permute-done | bytes 131104 | tf_op jit(solution)/shard_map/ppermute | solution.py:294
  96.5 4.4 %project_sent.1 = (bf16[1088,256]{1,0:T(8,128)(2,1)S(1)}, bf16[1088,256]{1,0:T(8,128)(2,1)S(1)}, bf16[1088,256]{1,0:T(8,128)(2,1)S(1)}) custom-call(bf16[64,120,128]{2,1,0:T(8,128)(2,1)S(1)} %all-to-all-done.chunks_ref, bf16[2304,128]{1,0:T(8,128)(2,1)} %collective-permute-done.1.refs_2_.refs_0_, bf16[2304,128]{1,0:T(8,128)(2,1)S(1)} %collective-permute-done.refs_1_, ...), custom_call_target="tpu_custom_call" | custom-call | tf_op jit(solution)/shard_map/project_sent/pallas_call | solution.py:193
  100.9 3.8 %collective-permute-start.7 = (bf16[1088,256]{1,0:T(8,128)(2,1)S(1)}, bf16[1088,256]{1,0:T(8,128)(2,1)S(1)}, u32[]{:S(2)}, u32[]{:S(2)}) collective-permute-start(bf16[1088,256]{1,0:T(8,128)(2,1)S(1)} %get-tuple-element.34), channel_id=1, source_target_pairs={{0,128},{64,192},{128,0},{192,64},{256,384},{320,448},{384,256},{4... | collective-permute-start | bytes 1671176 | tf_op jit(solution)/shard_map/ppermute | solution.py:289
  104.7 3.0 %collective-permute-start.8 = (bf16[1088,256]{1,0:T(8,128)(2,1)S(1)}, bf16[1088,256]{1,0:T(8,128)(2,1)S(1)}, u32[]{:S(2)}, u32[]{:S(2)}) collective-permute-start(bf16[1088,256]{1,0:T(8,128)(2,1)S(1)} %get-tuple-element.35), channel_id=1, source_target_pairs={{0,192},{64,0},{128,64},{192,128},{256,448},{320,256},{384,320},{4... | collective-permute-start | bytes 1671176 | tf_op jit(solution)/shard_map/ppermute | solution.py:289
  111.2 5.1 %collective-permute-done.7.refs_0_ = bf16[1088,256]{1,0:T(8,128)(2,1)S(1)} collective-permute-done((bf16[1088,256]{1,0:T(8,128)(2,1)S(1)}, bf16[1088,256]{1,0:T(8,128)(2,1)S(1)}, u32[]{:S(2)}, u32[]{:S(2)}) %collective-permute-start.7) | collective-permute-done | bytes 557088 | tf_op jit(solution)/shard_map/ppermute | solution.py:289
  116.3 13.2 %collective-permute-done.8.refs_1_ = bf16[1088,256]{1,0:T(8,128)(2,1)S(1)} collective-permute-done((bf16[1088,256]{1,0:T(8,128)(2,1)S(1)}, bf16[1088,256]{1,0:T(8,128)(2,1)S(1)}, u32[]{:S(2)}, u32[]{:S(2)}) %collective-permute-start.8) | collective-permute-done | bytes 557088 | tf_op jit(solution)/shard_map/ppermute | solution.py:289
  131.0 5.7 %collective-permute-start.13 = (bf16[1088,128]{1,0:T(8,128)(2,1)S(1)}, bf16[1088,128]{1,0:T(8,128)(2,1)S(1)}, u32[]{:S(2)}, u32[]{:S(2)}) collective-permute-start(bf16[1088,128]{1,0:T(8,128)(2,1)S(1)} %activate.1.refs_0_), channel_id=1, source_target_pairs={{0,256},{64,320},{128,384},{192,448},{256,0},{320,64},{384,128},{4... | collective-permute-start | bytes 835592 | tf_op jit(solution)/shard_map/ppermute | solution.py:294
  136.7 4.6 %collective-permute-start.12 = (bf16[1088,128]{1,0:T(8,128)(2,1)S(1)}, bf16[1088,128]{1,0:T(8,128)(2,1)S(1)}, u32[]{:S(2)}, u32[]{:S(2)}) collective-permute-start(bf16[1088,128]{1,0:T(8,128)(2,1)S(1)} %activate.1.refs_0_), channel_id=1, source_target_pairs={{0,192},{64,0},{128,64},{192,128},{256,448},{320,256},{384,320},{4... | collective-permute-start | bytes 835592 | tf_op jit(solution)/shard_map/ppermute | solution.py:289
  143.3 2.5 %collective-permute-start.10 = (bf16[1088,128]{1,0:T(8,128)(2,1)S(1)}, bf16[1088,128]{1,0:T(8,128)(2,1)S(1)}, u32[]{:S(2)}, u32[]{:S(2)}) collective-permute-start(bf16[1088,128]{1,0:T(8,128)(2,1)S(1)} %activate.1.refs_0_), channel_id=1, source_target_pairs={{0,64},{64,128},{128,192},{192,0},{256,320},{320,384},{384,448},{4... | collective-permute-start | bytes 835592 | tf_op jit(solution)/shard_map/ppermute | solution.py:289
  145.7 4.0 %collective-permute-start.16 = (bf16[1088,128]{1,0:T(8,128)(2,1)S(1)}, bf16[1088,128]{1,0:T(8,128)(2,1)S(1)}, u32[]{:S(2)}, u32[]{:S(2)}) collective-permute-start(bf16[1088,128]{1,0:T(8,128)(2,1)S(1)} %collective-permute-done.13.refs_4_), channel_id=1, source_target_pairs={{0,192},{64,0},{128,64},{192,128},{256,448},{320,256},{384,320},{4... | collective-permute-start | bytes 835592 | tf_op jit(solution)/shard_map/ppermute | solution.py:289
  149.8 3.6 %collective-permute-start.15 = (bf16[1088,128]{1,0:T(8,128)(2,1)S(1)}, bf16[1088,128]{1,0:T(8,128)(2,1)S(1)}, u32[]{:S(2)}, u32[]{:S(2)}) collective-permute-start(bf16[1088,128]{1,0:T(8,128)(2,1)S(1)} %collective-permute-done.13.refs_4_), channel_id=1, source_target_pairs={{0,128},{64,192},{128,0},{192,64},{256,384},{320,448},{384,256},{4... | collective-permute-start | bytes 835592 | tf_op jit(solution)/shard_map/ppermute | solution.py:289
  156.8 3.9 %collective-permute-done.10.refs_1_ = bf16[1088,128]{1,0:T(8,128)(2,1)S(1)} collective-permute-done((bf16[1088,128]{1,0:T(8,128)(2,1)S(1)}, bf16[1088,128]{1,0:T(8,128)(2,1)S(1)}, u32[]{:S(2)}, u32[]{:S(2)}) %collective-permute-start.10) | collective-permute-done | bytes 278560 | tf_op jit(solution)/shard_map/ppermute | solution.py:289
  160.7 3.1 %collective-permute-done.15.refs_6_ = bf16[1088,128]{1,0:T(8,128)(2,1)S(1)} collective-permute-done((bf16[1088,128]{1,0:T(8,128)(2,1)S(1)}, bf16[1088,128]{1,0:T(8,128)(2,1)S(1)}, u32[]{:S(2)}, u32[]{:S(2)}) %collective-permute-start.15) | collective-permute-done | bytes 278560 | tf_op jit(solution)/shard_map/ppermute | solution.py:289
  163.8 7.3 %collective-permute-done.14.refs_5_ = bf16[1088,128]{1,0:T(8,128)(2,1)S(1)} collective-permute-done((bf16[1088,128]{1,0:T(8,128)(2,1)S(1)}, bf16[1088,128]{1,0:T(8,128)(2,1)S(1)}, u32[]{:S(2)}, u32[]{:S(2)}) %collective-permute-start.14) | collective-permute-done | bytes 278560 | tf_op jit(solution)/shard_map/ppermute | solution.py:289
  172.6 40.3 %all_to_all.10.chunks_ref = bf16[64,64,128]{2,1,0:T(8,128)(2,1)S(1)} all-to-all(bf16[64,64,128]{2,1,0:T(8,128)(2,1)S(1)} %down.1), channel_id=1, replica_groups=mesh['pipe'=8,'expert'=64] {'expert'}, dimensions={0} | all-to-all | bytes 2097152 | tf_op jit(solution)/shard_map/all_to_all | solution.py:319
  (36 shorter events, 20.6 us)
Async XLA Ops:
  3.5 14.8 %copy-start = (bf16[1,3584,128]{2,1,0:T(8,128)(2,1)S(1)}, bf16[1,3584,128]{2,1,0:T(8,128)(2,1)}, u32[]{:S(2)}) copy-start(bf16[1,3584,128]{2,1,0:T(8,128)(2,1)} %param.9) | copy-start | bytes 2752516
  3.6 92.9 %all-to-all-start = ((bf16[64,120,128]{2,1,0:T(8,128)(2,1)}), bf16[64,120,128]{2,1,0:T(8,128)(2,1)S(1)}, u32[]{:S(2)}, u32[]{:S(2)}) async-start(bf16[64,120,128]{2,1,0:T(8,128)(2,1)} %dispatch.1), calls=%async_computation | async-start | bytes 3932160 | tf_op jit(solution)/shard_map/all_to_all | solution.py:305
  18.3 1.2 copy-start.1
  19.5 1.2 copy-start.2
  22.0 74.4 %collective-permute-start = (bf16[2304,128]{1,0:T(8,128)(2,1)}, bf16[2304,128]{1,0:T(8,128)(2,1)S(1)}, u32[]{:S(2)}, u32[]{:S(2)}) collective-permute-start(bf16[2304,128]{1,0:T(8,128)(2,1)} %get-tuple-element.22), channel_id=1, source_target_pairs={{0,64},{64,128},{128,192},{192,0},{256,320},{320,384},{384,448},{4... | collective-permute-start | bytes 1769480 | tf_op jit(solution)/shard_map/ppermute | solution.py:289
  25.1 71.3 %collective-permute-start.1 = (bf16[2304,128]{1,0:T(8,128)(2,1)}, bf16[2304,128]{1,0:T(8,128)(2,1)}, u32[]{:S(2)}, u32[]{:S(2)}) collective-permute-start(bf16[2304,128]{1,0:T(8,128)(2,1)} %get-tuple-element.23), channel_id=1, source_target_pairs={{0,128},{64,192},{128,0},{192,64},{256,384},{320,448},{384,256},{4... | collective-permute-start | bytes 1769480 | tf_op jit(solution)/shard_map/ppermute | solution.py:289
  29.5 67.0 %collective-permute-start.2 = (bf16[2304,128]{1,0:T(8,128)(2,1)}, bf16[2304,128]{1,0:T(8,128)(2,1)}, u32[]{:S(2)}, u32[]{:S(2)}) collective-permute-start(bf16[2304,128]{1,0:T(8,128)(2,1)} %get-tuple-element.24), channel_id=1, source_target_pairs={{0,192},{64,0},{128,64},{192,128},{256,448},{320,256},{384,320},{4... | collective-permute-start | bytes 1769480 | tf_op jit(solution)/shard_map/ppermute | solution.py:289
  32.6 46.2 %collective-permute-start.3 = (bf16[512,128]{1,0:T(8,128)(2,1)S(1)}, bf16[512,128]{1,0:T(8,128)(2,1)S(1)}, u32[]{:S(2)}, u32[]{:S(2)}) collective-permute-start(bf16[512,128]{1,0:T(8,128)(2,1)S(1)} %get-tuple-element.25), channel_id=1, source_target_pairs={{0,256},{64,320},{128,384},{192,448},{256,0},{320,64},{384,128},{4... | collective-permute-start | bytes 393224 | tf_op jit(solution)/shard_map/ppermute | solution.py:294
  40.5 44.8 %collective-permute-start.4 = (bf16[512,128]{1,0:T(8,128)(2,1)S(1)}, bf16[512,128]{1,0:T(8,128)(2,1)S(1)}, u32[]{:S(2)}, u32[]{:S(2)}) collective-permute-start(bf16[512,128]{1,0:T(8,128)(2,1)S(1)} %get-tuple-element.26), channel_id=1, source_target_pairs={{0,320},{64,384},{128,448},{192,256},{256,64},{320,128},{384,192},... | collective-permute-start | bytes 393224 | tf_op jit(solution)/shard_map/ppermute | solution.py:294
  78.7 13.3 %collective-permute-start.5 = (bf16[512,128]{1,0:T(8,128)(2,1)S(1)}, bf16[512,128]{1,0:T(8,128)(2,1)S(1)}, u32[]{:S(2)}, u32[]{:S(2)}) collective-permute-start(bf16[512,128]{1,0:T(8,128)(2,1)S(1)} %get-tuple-element.27), channel_id=1, source_target_pairs={{0,384},{64,448},{128,256},{192,320},{256,128},{320,192},{384,0},{... | collective-permute-start | bytes 393224 | tf_op jit(solution)/shard_map/ppermute | solution.py:294
  85.3 10.5 %collective-permute-start.6 = (bf16[512,128]{1,0:T(8,128)(2,1)S(1)}, bf16[512,128]{1,0:T(8,128)(2,1)S(1)}, u32[]{:S(2)}, u32[]{:S(2)}) collective-permute-start(bf16[512,128]{1,0:T(8,128)(2,1)S(1)} %get-tuple-element.28), channel_id=1, source_target_pairs={{0,448},{64,256},{128,320},{192,384},{256,192},{320,0},{384,64},{4... | collective-permute-start | bytes 393224 | tf_op jit(solution)/shard_map/ppermute | solution.py:294
  100.9 15.5 %collective-permute-start.7 = (bf16[1088,256]{1,0:T(8,128)(2,1)S(1)}, bf16[1088,256]{1,0:T(8,128)(2,1)S(1)}, u32[]{:S(2)}, u32[]{:S(2)}) collective-permute-start(bf16[1088,256]{1,0:T(8,128)(2,1)S(1)} %get-tuple-element.34), channel_id=1, source_target_pairs={{0,128},{64,192},{128,0},{192,64},{256,384},{320,448},{384,256},{4... | collective-permute-start | bytes 1671176 | tf_op jit(solution)/shard_map/ppermute | solution.py:289
  104.7 24.8 %collective-permute-start.8 = (bf16[1088,256]{1,0:T(8,128)(2,1)S(1)}, bf16[1088,256]{1,0:T(8,128)(2,1)S(1)}, u32[]{:S(2)}, u32[]{:S(2)}) collective-permute-start(bf16[1088,256]{1,0:T(8,128)(2,1)S(1)} %get-tuple-element.35), channel_id=1, source_target_pairs={{0,192},{64,0},{128,64},{192,128},{256,448},{320,256},{384,320},{4... | collective-permute-start | bytes 1671176 | tf_op jit(solution)/shard_map/ppermute | solution.py:289
  107.8 22.9 %collective-permute-start.9 = (bf16[1088,256]{1,0:T(8,128)(2,1)S(1)}, bf16[1088,256]{1,0:T(8,128)(2,1)S(1)}, u32[]{:S(2)}, u32[]{:S(2)}) collective-permute-start(bf16[1088,256]{1,0:T(8,128)(2,1)S(1)} %get-tuple-element.36), channel_id=1, source_target_pairs={{0,64},{64,128},{128,192},{192,0},{256,320},{320,384},{384,448},{4... | collective-permute-start | bytes 1671176 | tf_op jit(solution)/shard_map/ppermute | solution.py:289
  111.2 44.1 %copy-start.4 = (bf16[512,128]{1,0:T(8,128)(2,1)S(1)}, bf16[512,128]{1,0:T(8,128)(2,1)}, u32[]{:S(2)}) copy-start(bf16[512,128]{1,0:T(8,128)(2,1)} %copy-done.3) | copy-start | bytes 393220
  131.0 14.7 %collective-permute-start.13 = (bf16[1088,128]{1,0:T(8,128)(2,1)S(1)}, bf16[1088,128]{1,0:T(8,128)(2,1)S(1)}, u32[]{:S(2)}, u32[]{:S(2)}) collective-permute-start(bf16[1088,128]{1,0:T(8,128)(2,1)S(1)} %activate.1.refs_0_), channel_id=1, source_target_pairs={{0,256},{64,320},{128,384},{192,448},{256,0},{320,64},{384,128},{4... | collective-permute-start | bytes 835592 | tf_op jit(solution)/shard_map/ppermute | solution.py:294
  136.7 16.7 %collective-permute-start.12 = (bf16[1088,128]{1,0:T(8,128)(2,1)S(1)}, bf16[1088,128]{1,0:T(8,128)(2,1)S(1)}, u32[]{:S(2)}, u32[]{:S(2)}) collective-permute-start(bf16[1088,128]{1,0:T(8,128)(2,1)S(1)} %activate.1.refs_0_), channel_id=1, source_target_pairs={{0,192},{64,0},{128,64},{192,128},{256,448},{320,256},{384,320},{4... | collective-permute-start | bytes 835592 | tf_op jit(solution)/shard_map/ppermute | solution.py:289
  141.3 15.5 %collective-permute-start.11 = (bf16[1088,128]{1,0:T(8,128)(2,1)S(1)}, bf16[1088,128]{1,0:T(8,128)(2,1)S(1)}, u32[]{:S(2)}, u32[]{:S(2)}) collective-permute-start(bf16[1088,128]{1,0:T(8,128)(2,1)S(1)} %activate.1.refs_0_), channel_id=1, source_target_pairs={{0,128},{64,192},{128,0},{192,64},{256,384},{320,448},{384,256},{4... | collective-permute-start | bytes 835592 | tf_op jit(solution)/shard_map/ppermute | solution.py:289
  143.3 17.4 %collective-permute-start.10 = (bf16[1088,128]{1,0:T(8,128)(2,1)S(1)}, bf16[1088,128]{1,0:T(8,128)(2,1)S(1)}, u32[]{:S(2)}, u32[]{:S(2)}) collective-permute-start(bf16[1088,128]{1,0:T(8,128)(2,1)S(1)} %activate.1.refs_0_), channel_id=1, source_target_pairs={{0,64},{64,128},{128,192},{192,0},{256,320},{320,384},{384,448},{4... | collective-permute-start | bytes 835592 | tf_op jit(solution)/shard_map/ppermute | solution.py:289
  145.7 14.9 %collective-permute-start.16 = (bf16[1088,128]{1,0:T(8,128)(2,1)S(1)}, bf16[1088,128]{1,0:T(8,128)(2,1)S(1)}, u32[]{:S(2)}, u32[]{:S(2)}) collective-permute-start(bf16[1088,128]{1,0:T(8,128)(2,1)S(1)} %collective-permute-done.13.refs_4_), channel_id=1, source_target_pairs={{0,192},{64,0},{128,64},{192,128},{256,448},{320,256},{384,320},{4... | collective-permute-start | bytes 835592 | tf_op jit(solution)/shard_map/ppermute | solution.py:289
  149.8 14.1 %collective-permute-start.15 = (bf16[1088,128]{1,0:T(8,128)(2,1)S(1)}, bf16[1088,128]{1,0:T(8,128)(2,1)S(1)}, u32[]{:S(2)}, u32[]{:S(2)}) collective-permute-start(bf16[1088,128]{1,0:T(8,128)(2,1)S(1)} %collective-permute-done.13.refs_4_), channel_id=1, source_target_pairs={{0,128},{64,192},{128,0},{192,64},{256,384},{320,448},{384,256},{4... | collective-permute-start | bytes 835592 | tf_op jit(solution)/shard_map/ppermute | solution.py:289
  153.4 17.7 %collective-permute-start.14 = (bf16[1088,128]{1,0:T(8,128)(2,1)S(1)}, bf16[1088,128]{1,0:T(8,128)(2,1)S(1)}, u32[]{:S(2)}, u32[]{:S(2)}) collective-permute-start(bf16[1088,128]{1,0:T(8,128)(2,1)S(1)} %collective-permute-done.13.refs_4_), channel_id=1, source_target_pairs={{0,64},{64,128},{128,192},{192,0},{256,320},{320,384},{384,448},{4... | collective-permute-start | bytes 835592 | tf_op jit(solution)/shard_map/ppermute | solution.py:289
  172.6 40.3 %copy-start.5 = (s32[128,8]{0,1:T(8,128)S(1)}, s32[128,8]{0,1:T(8,128)}, u32[]{:S(2)}) copy-start(s32[128,8]{0,1:T(8,128)} %param.7) | copy-start | bytes 12292
  172.6 40.3 %copy-start.6 = (f32[128,8]{0,1:T(8,128)S(1)}, f32[128,8]{0,1:T(8,128)}, u32[]{:S(2)}) copy-start(f32[128,8]{0,1:T(8,128)} %param.8) | copy-start | bytes 12292
  (1 other events, 0.7 us)

commit v9 on v8

--- a/solution.py
+++ b/solution.py
@@ -10,6 +10,7 @@
 LANES = 128
 X = 4
 PARTS = 4
+HOLD = 50_000_000_000
 FULL = 60 * 1024 * 1024
 VMEM = 16 * 1024 * 1024
 
@@ -107,7 +108,7 @@
 
 
 def pack_kernel(x_ref, z_ref, gate_ref, up_ref, down_ref, *outs):
-    near, far = outs[:X], outs[X:]
+    near, far = outs[:X], outs[X]
     quarter = gate_ref.shape[0] // X
     depth = down_ref.shape[0]
 
@@ -125,14 +126,26 @@
         near[d][pl.ds(0, quarter), :] = gate_ref[part, :]
         near[d][pl.ds(quarter, quarter), :] = up_ref[part, :]
         put_down(near[d], 2 * quarter, z_ref[0], q)
-        put_down(far[d], 0, 1 - z_ref[0], q)
+        put_down(far, 4 * d * depth, 1 - z_ref[0], q)
 
 
 def pack(x, z, w_gate, w_up, w_down):
     rows = 2 * (w_gate.shape[0] // X) + 4 * w_down.shape[0]
-    shapes = [jax.ShapeDtypeStruct((r, LANES), BF) for r in [rows] * X + [4 * w_down.shape[0]] * X]
+    shapes = [jax.ShapeDtypeStruct((r, LANES), BF) for r in [rows] * X + [4 * X * w_down.shape[0]]]
     outs = call(pack_kernel, "pack", shapes, [in_smem()] * 2 + [in_vmem()] * 3)(x, z, w_gate, w_up, w_down)
-    return outs[:X], outs[X:]
+    return outs[:X], outs[X]
+
+
+def split_kernel(rows_ref, *outs):
+    count = outs[0].shape[0]
+    for d, out_ref in enumerate(outs):
+        out_ref[...] = rows_ref[pl.ds(d * count, count), :]
+
+
+def split(rows):
+    shapes = [jax.ShapeDtypeStruct((rows.shape[0] // X, LANES), BF)] * X
+    cost = pl.CostEstimate(flops=HOLD, bytes_accessed=4 * rows.size, transcendentals=0)
+    return call(split_kernel, "split", shapes, [in_vmem()], cost=cost)(rows)
 
 
 def assemble_kernel(*refs):
@@ -289,9 +302,8 @@
     return lax.ppermute(value, "pipe", pairs)
 
 
-def cross(value, d=0):
-    pairs = [(z * X + x, (1 - z) * X + (x + d) % X) for z in range(2) for x in range(X)]
-    return lax.ppermute(value, "pipe", pairs)
+def cross(value):
+    return lax.ppermute(value, "pipe", [(p, (p + X) % (2 * X)) for p in range(2 * X)])
 
 
 def body(tokens, expert_ids, gate_scale, w_gate, w_up, w_down):
@@ -305,12 +317,13 @@
     chunks = lax.all_to_all(buffer, "expert", split_axis=0, concat_axis=0, tiled=True)
     near, far = pack(x, z, w_gate, w_up, w_down)
     near = [near[0]] + [shift(near[d], d) for d in range(1, X)]
-    far = [cross(far[d], d) for d in range(X)]
-    chunks, *far = lax.optimization_barrier((chunks, *far))
+    far = split(cross(far))
     parts = project(chunks, [near[d] for d in (2, 1, 3)], BF, "project_sent")
     arrived = [shift(part, -d) for d, part in zip((2, 1, 3), parts)]
+    chunks, *far = lax.optimization_barrier((chunks, *far))
     (mine,) = project(chunks, near[:1], F32, "project_own")
-    weight = assemble(near, far)
+    far = [far[0]] + [shift(far[d], d) for d in range(1, X)]
+    mine, weight = lax.optimization_barrier((mine, assemble(near, far)))
     hidden = activate(mine, arrived)
     swapped = cross(hidden)
     hiddens = [hidden] + [shift(hidden, d) for d in range(1, X)]

time: 216 us -> 215 us (level)
  waiting for transfers between devices: 73.7 us -> 62.9 us
  blocking collectives: 40.3 us -> 46 us
  local copies, waits for them, and re-layouts: 3.79 us -> 6.93 us
    ppermute x5 -> x2, waiting for transfers between devices: 40 us -> 3.26 us  [cross(): lax.ppermute(value, 'pipe', [(p, (p + X) % (2 * X)) for p in range(2 * X)])]
    all_to_all x1, waiting for transfers between devices: 0.01 us -> 18 us  [body(): lax.all_to_all(buffer, 'expert', split_axis=0, concat_axis=0, tiled=True)]
    ppermute x12 -> x15, starting transfers between devices: 38.2 us -> 50.2 us  [shift(): return lax.ppermute(value, 'pipe', pairs)]
    ppermute x5 -> x2, starting transfers between devices: 28.9 us -> 18.4 us  [cross(): lax.ppermute(value, 'pipe', [(p, (p + X) % (2 * X)) for p in range(2 * X)])]
    ppermute x12 -> x15, waiting for transfers between devices: 33.7 us -> 41.7 us  [shift(): return lax.ppermute(value, 'pipe', pairs)]
    all_to_all x1, blocking collectives: 40.3 us -> 46 us  [body(): lax.all_to_all(output, 'expert', split_axis=0, concat_axis=0, tiled=True)]
    unnamed x14 -> x22, local copies, waits for them, and re-layouts: 3.03 us -> 6.16 us
  transfers between devices with their start and end apart: 18 -> 18, of which waited for: 8 -> 9; matrix products, arithmetic and copies ran while one was open for 0% -> 0% of each run, Pallas kernels for 2% -> 3%
where the time goes in v9:
time: 215 us; the launch traced here: 214 us
  starting transfers between devices  83.4 us (39%)
  waiting for transfers between devices  62.9 us (29%)
  blocking collectives  46 us (21%)
  Pallas kernels  14.4 us (7%)
  local copies, waits for them, and re-layouts  6.93 us (3%)
    ppermute x15, starting transfers between devices, shift(): return lax.ppermute(value, 'pipe', pairs)  50.2 us
    all_to_all x1, blocking collectives, body(): lax.all_to_all(output, 'expert', split_axis=0, concat_axis=0, tiled=True)  46 us
    ppermute x15, waiting for transfers between devices, shift(): return lax.ppermute(value, 'pipe', pairs)  41.7 us
    ppermute x2, starting transfers between devices, cross(): lax.ppermute(value, 'pipe', [(p, (p + X) % (2 * X)) for p in range(2 * X)])  18.4 us
    all_to_all x1, waiting for transfers between devices, body(): lax.all_to_all(buffer, 'expert', split_axis=0, concat_axis=0, tiled=True)  18 us
    all_to_all x1, starting transfers between devices, body(): lax.all_to_all(buffer, 'expert', split_axis=0, concat_axis=0, tiled=True)  14.7 us
    unnamed x22, local copies, waits for them, and re-layouts  6.16 us
    pallas_call x2, Pallas kernels, project(): return call(kernel, name, shapes, specs, scratch=scratch)(chunks, *packs)  5.08 us
  transfers between devices with their start and end apart: 18, of which 9 were waited for; matrix products, arithmetic and copies ran while one was open for 0% of the time, Pallas kernels for 3%

profile of v9, /device:TPU:1, one launch (start us, length us, event | category | flops | bytes accessed | tf_op | source)
XLA Modules:
  0.0 214.0 jit_solution(11413681075334577621)
XLA Ops:
  0.0 3.5 %dispatch.1 = bf16[64,120,128]{2,1,0:T(8,128)(2,1)} custom-call(s32[1]{0:T(128)} %bitcast.x_ref, s32[8,128]{1,0:T(8,128)} %bitcast.10, bf16[128,3584]{1,0:T(8,128)(2,1)} %tok_ref.1), custom_call_target="tpu_custom_call" | custom-call | tf_op jit(solution)/shard_map/dispatch/pallas_call | solution.py:107
  3.6 14.7 %all-to-all-start = ((bf16[64,120,128]{2,1,0:T(8,128)(2,1)}), bf16[64,120,128]{2,1,0:T(8,128)(2,1)S(1)}, u32[]{:S(2)}, u32[]{:S(2)}) async-start(bf16[64,120,128]{2,1,0:T(8,128)(2,1)} %dispatch.1), calls=%async_computation | async-start | bytes 3932160 | tf_op jit(solution)/shard_map/all_to_all | solution.py:317
  21.8 3.1 %collective-permute-start.1 = (bf16[2304,128]{1,0:T(8,128)(2,1)S(1)}, bf16[2304,128]{1,0:T(8,128)(2,1)S(1)}, u32[]{:S(2)}, u32[]{:S(2)}) collective-permute-start(bf16[2304,128]{1,0:T(8,128)(2,1)S(1)} %get-tuple-element.31), channel_id=1, source_target_pairs={{0,64},{64,128},{128,192},{192,0},{256,320},{320,384},{384,448},{4... | collective-permute-start | bytes 1769480 | tf_op jit(solution)/shard_map/ppermute | solution.py:302
  24.9 4.4 %collective-permute-start.2 = (bf16[2304,128]{1,0:T(8,128)(2,1)S(1)}, bf16[2304,128]{1,0:T(8,128)(2,1)S(1)}, u32[]{:S(2)}, u32[]{:S(2)}) collective-permute-start(bf16[2304,128]{1,0:T(8,128)(2,1)S(1)} %get-tuple-element.32), channel_id=1, source_target_pairs={{0,128},{64,192},{128,0},{192,64},{256,384},{320,448},{384,256},{4... | collective-permute-start | bytes 1769480 | tf_op jit(solution)/shard_map/ppermute | solution.py:302
  29.3 3.1 %collective-permute-start.3 = (bf16[2304,128]{1,0:T(8,128)(2,1)S(1)}, bf16[2304,128]{1,0:T(8,128)(2,1)S(1)}, u32[]{:S(2)}, u32[]{:S(2)}) collective-permute-start(bf16[2304,128]{1,0:T(8,128)(2,1)S(1)} %get-tuple-element.33), channel_id=1, source_target_pairs={{0,192},{64,0},{128,64},{192,128},{256,448},{320,256},{384,320},{4... | collective-permute-start | bytes 1769480 | tf_op jit(solution)/shard_map/ppermute | solution.py:302
  32.3 7.9 %collective-permute-start = (bf16[2048,128]{1,0:T(8,128)(2,1)}, bf16[2048,128]{1,0:T(8,128)(2,1)}, u32[]{:S(2)}, u32[]{:S(2)}) collective-permute-start(bf16[2048,128]{1,0:T(8,128)(2,1)} %get-tuple-element.24), channel_id=1, source_target_pairs={{0,256},{64,320},{128,384},{192,448},{256,0},{320,64},{384,128},{4... | collective-permute-start | bytes 1572872 | tf_op jit(solution)/shard_map/ppermute | solution.py:306
  40.3 12.7 %collective-permute-done.2.refs_2_.refs_0_ = bf16[2304,128]{1,0:T(8,128)(2,1)S(1)} collective-permute-done((bf16[2304,128]{1,0:T(8,128)(2,1)S(1)}, bf16[2304,128]{1,0:T(8,128)(2,1)S(1)}, u32[]{:S(2)}, u32[]{:S(2)}) %collective-permute-start.2) | collective-permute-done | bytes 589856 | tf_op jit(solution)/shard_map/ppermute | solution.py:302
  55.1 18.0 %all-to-all-done.chunks_ref = bf16[64,120,128]{2,1,0:T(8,128)(2,1)S(1)} async-done(((bf16[64,120,128]{2,1,0:T(8,128)(2,1)}), bf16[64,120,128]{2,1,0:T(8,128)(2,1)S(1)}, u32[]{:S(2)}, u32[]{:S(2)}) %all-to-all-start) | async-done | bytes 1966112 | tf_op jit(solution)/shard_map/all_to_all | solution.py:317
  75.2 3.9 %project_sent.1 = (bf16[1088,256]{1,0:T(8,128)(2,1)S(1)}, bf16[1088,256]{1,0:T(8,128)(2,1)S(1)}, bf16[1088,256]{1,0:T(8,128)(2,1)S(1)}) custom-call(bf16[64,120,128]{2,1,0:T(8,128)(2,1)S(1)} %all-to-all-done.chunks_ref, bf16[2304,128]{1,0:T(8,128)(2,1)S(1)} %copy-done.1, bf16[2304,128]{1,0:T(8,128)(2,1)S(1)} %collective-permute-done.1.refs_1_, ...), custom_call_target="tpu_custom_call" | custom-call | tf_op jit(solution)/shard_map/project_sent/pallas_call | solution.py:206
  79.1 7.3 %collective-permute-start.7 = (bf16[1088,256]{1,0:T(8,128)(2,1)S(1)}, bf16[1088,256]{1,0:T(8,128)(2,1)S(1)}, u32[]{:S(2)}, u32[]{:S(2)}) collective-permute-start(bf16[1088,256]{1,0:T(8,128)(2,1)S(1)} %get-tuple-element.40), channel_id=1, source_target_pairs={{0,128},{64,192},{128,0},{192,64},{256,384},{320,448},{384,256},{4... | collective-permute-start | bytes 1671176 | tf_op jit(solution)/shard_map/ppermute | solution.py:302
  88.3 3.4 %collective-permute-start.9 = (bf16[1088,256]{1,0:T(8,128)(2,1)S(1)}, bf16[1088,256]{1,0:T(8,128)(2,1)S(1)}, u32[]{:S(2)}, u32[]{:S(2)}) collective-permute-start(bf16[1088,256]{1,0:T(8,128)(2,1)S(1)} %get-tuple-element.42), channel_id=1, source_target_pairs={{0,64},{64,128},{128,192},{192,0},{256,320},{320,384},{384,448},{4... | collective-permute-start | bytes 1671176 | tf_op jit(solution)/shard_map/ppermute | solution.py:302
  94.9 4.2 %collective-permute-start.5 = (bf16[512,128]{1,0:T(8,128)(2,1)S(1)}, bf16[512,128]{1,0:T(8,128)(2,1)S(1)}, u32[]{:S(2)}, u32[]{:S(2)}) collective-permute-start(bf16[512,128]{1,0:T(8,128)(2,1)S(1)} %get-tuple-element.36), channel_id=1, source_target_pairs={{0,128},{64,192},{128,0},{192,64},{256,384},{320,448},{384,256},{4... | collective-permute-start | bytes 393224 | tf_op jit(solution)/shard_map/ppermute | solution.py:302
  99.1 15.0 %collective-permute-done.4.refs_5_ = bf16[512,128]{1,0:T(8,128)(2,1)S(1)} collective-permute-done((bf16[512,128]{1,0:T(8,128)(2,1)S(1)}, bf16[512,128]{1,0:T(8,128)(2,1)S(1)}, u32[]{:S(2)}, u32[]{:S(2)}) %collective-permute-start.4) | collective-permute-done | bytes 131104 | tf_op jit(solution)/shard_map/ppermute | solution.py:302
  114.1 2.3 %collective-permute-start.6 = (bf16[512,128]{1,0:T(8,128)(2,1)S(1)}, bf16[512,128]{1,0:T(8,128)(2,1)S(1)}, u32[]{:S(2)}, u32[]{:S(2)}) collective-permute-start(bf16[512,128]{1,0:T(8,128)(2,1)S(1)} %get-tuple-element.37), channel_id=1, source_target_pairs={{0,192},{64,0},{128,64},{192,128},{256,448},{320,256},{384,320},{4... | collective-permute-start | bytes 393224 | tf_op jit(solution)/shard_map/ppermute | solution.py:302
  117.6 3.0 %collective-permute-done.6.refs_7_ = bf16[512,128]{1,0:T(8,128)(2,1)S(1)} collective-permute-done((bf16[512,128]{1,0:T(8,128)(2,1)S(1)}, bf16[512,128]{1,0:T(8,128)(2,1)S(1)}, u32[]{:S(2)}, u32[]{:S(2)}) %collective-permute-start.6) | collective-permute-done | bytes 131104 | tf_op jit(solution)/shard_map/ppermute | solution.py:302
  121.2 10.5 %collective-permute-start.13 = (bf16[1088,128]{1,0:T(8,128)(2,1)S(1)}, bf16[1088,128]{1,0:T(8,128)(2,1)S(1)}, u32[]{:S(2)}, u32[]{:S(2)}) collective-permute-start(bf16[1088,128]{1,0:T(8,128)(2,1)S(1)} %activate.1.refs_0_), channel_id=1, source_target_pairs={{0,256},{64,320},{128,384},{192,448},{256,0},{320,64},{384,128},{4... | collective-permute-start | bytes 835592 | tf_op jit(solution)/shard_map/ppermute | solution.py:306
  131.7 3.4 %collective-permute-start.12 = (bf16[1088,128]{1,0:T(8,128)(2,1)S(1)}, bf16[1088,128]{1,0:T(8,128)(2,1)S(1)}, u32[]{:S(2)}, u32[]{:S(2)}) collective-permute-start(bf16[1088,128]{1,0:T(8,128)(2,1)S(1)} %activate.1.refs_0_), channel_id=1, source_target_pairs={{0,192},{64,0},{128,64},{192,128},{256,448},{320,256},{384,320},{4... | collective-permute-start | bytes 835592 | tf_op jit(solution)/shard_map/ppermute | solution.py:302
  135.1 4.0 %collective-permute-start.11 = (bf16[1088,128]{1,0:T(8,128)(2,1)S(1)}, bf16[1088,128]{1,0:T(8,128)(2,1)S(1)}, u32[]{:S(2)}, u32[]{:S(2)}) collective-permute-start(bf16[1088,128]{1,0:T(8,128)(2,1)S(1)} %activate.1.refs_0_), channel_id=1, source_target_pairs={{0,128},{64,192},{128,0},{192,64},{256,384},{320,448},{384,256},{4... | collective-permute-start | bytes 835592 | tf_op jit(solution)/shard_map/ppermute | solution.py:302
  141.3 3.3 %collective-permute-done.13.refs_4_ = bf16[1088,128]{1,0:T(8,128)(2,1)S(1)} collective-permute-done((bf16[1088,128]{1,0:T(8,128)(2,1)S(1)}, bf16[1088,128]{1,0:T(8,128)(2,1)S(1)}, u32[]{:S(2)}, u32[]{:S(2)}) %collective-permute-start.13) | collective-permute-done | bytes 278560 | tf_op jit(solution)/shard_map/ppermute | solution.py:306
  144.6 2.7 %collective-permute-start.16 = (bf16[1088,128]{1,0:T(8,128)(2,1)S(1)}, bf16[1088,128]{1,0:T(8,128)(2,1)S(1)}, u32[]{:S(2)}, u32[]{:S(2)}) collective-permute-start(bf16[1088,128]{1,0:T(8,128)(2,1)S(1)} %collective-permute-done.13.refs_4_), channel_id=1, source_target_pairs={{0,192},{64,0},{128,64},{192,128},{256,448},{320,256},{384,320},{4... | collective-permute-start | bytes 835592 | tf_op jit(solution)/shard_map/ppermute | solution.py:302
  147.3 4.0 %collective-permute-start.15 = (bf16[1088,128]{1,0:T(8,128)(2,1)S(1)}, bf16[1088,128]{1,0:T(8,128)(2,1)S(1)}, u32[]{:S(2)}, u32[]{:S(2)}) collective-permute-start(bf16[1088,128]{1,0:T(8,128)(2,1)S(1)} %collective-permute-done.13.refs_4_), channel_id=1, source_target_pairs={{0,128},{64,192},{128,0},{192,64},{256,384},{320,448},{384,256},{4... | collective-permute-start | bytes 835592 | tf_op jit(solution)/shard_map/ppermute | solution.py:302
  153.7 3.4 %collective-permute-done.15.refs_6_ = bf16[1088,128]{1,0:T(8,128)(2,1)S(1)} collective-permute-done((bf16[1088,128]{1,0:T(8,128)(2,1)S(1)}, bf16[1088,128]{1,0:T(8,128)(2,1)S(1)}, u32[]{:S(2)}, u32[]{:S(2)}) %collective-permute-start.15) | collective-permute-done | bytes 278560 | tf_op jit(solution)/shard_map/ppermute | solution.py:302
  157.1 7.0 %collective-permute-done.14.refs_5_ = bf16[1088,128]{1,0:T(8,128)(2,1)S(1)} collective-permute-done((bf16[1088,128]{1,0:T(8,128)(2,1)S(1)}, bf16[1088,128]{1,0:T(8,128)(2,1)S(1)}, u32[]{:S(2)}, u32[]{:S(2)}) %collective-permute-start.14) | collective-permute-done | bytes 278560 | tf_op jit(solution)/shard_map/ppermute | solution.py:302
  165.7 46.0 %all_to_all.10.chunks_ref = bf16[64,64,128]{2,1,0:T(8,128)(2,1)S(1)} all-to-all(bf16[64,64,128]{2,1,0:T(8,128)(2,1)S(1)} %down.1), channel_id=1, replica_groups=mesh['pipe'=8,'expert'=64] {'expert'}, dimensions={0} | all-to-all | bytes 2097152 | tf_op jit(solution)/shard_map/all_to_all | solution.py:332
  (45 shorter events, 23.0 us)
Async XLA Ops:
  3.5 14.8 %copy-start.6 = (bf16[1,3584,128]{2,1,0:T(8,128)(2,1)S(1)}, bf16[1,3584,128]{2,1,0:T(8,128)(2,1)}, u32[]{:S(2)}) copy-start(bf16[1,3584,128]{2,1,0:T(8,128)(2,1)} %param.9) | copy-start | bytes 2752516
  3.6 69.5 %all-to-all-start = ((bf16[64,120,128]{2,1,0:T(8,128)(2,1)}), bf16[64,120,128]{2,1,0:T(8,128)(2,1)S(1)}, u32[]{:S(2)}, u32[]{:S(2)}) async-start(bf16[64,120,128]{2,1,0:T(8,128)(2,1)} %dispatch.1), calls=%async_computation | async-start | bytes 3932160 | tf_op jit(solution)/shard_map/all_to_all | solution.py:317
  18.3 1.2 copy-start.7
  21.8 18.5 %collective-permute-start.1 = (bf16[2304,128]{1,0:T(8,128)(2,1)S(1)}, bf16[2304,128]{1,0:T(8,128)(2,1)S(1)}, u32[]{:S(2)}, u32[]{:S(2)}) collective-permute-start(bf16[2304,128]{1,0:T(8,128)(2,1)S(1)} %get-tuple-element.31), channel_id=1, source_target_pairs={{0,64},{64,128},{128,192},{192,0},{256,320},{320,384},{384,448},{4... | collective-permute-start | bytes 1769480 | tf_op jit(solution)/shard_map/ppermute | solution.py:302
  24.9 28.0 %collective-permute-start.2 = (bf16[2304,128]{1,0:T(8,128)(2,1)S(1)}, bf16[2304,128]{1,0:T(8,128)(2,1)S(1)}, u32[]{:S(2)}, u32[]{:S(2)}) collective-permute-start(bf16[2304,128]{1,0:T(8,128)(2,1)S(1)} %get-tuple-element.32), channel_id=1, source_target_pairs={{0,128},{64,192},{128,0},{192,64},{256,384},{320,448},{384,256},{4... | collective-permute-start | bytes 1769480 | tf_op jit(solution)/shard_map/ppermute | solution.py:302
  29.3 25.0 %collective-permute-start.3 = (bf16[2304,128]{1,0:T(8,128)(2,1)S(1)}, bf16[2304,128]{1,0:T(8,128)(2,1)S(1)}, u32[]{:S(2)}, u32[]{:S(2)}) collective-permute-start(bf16[2304,128]{1,0:T(8,128)(2,1)S(1)} %get-tuple-element.33), channel_id=1, source_target_pairs={{0,192},{64,0},{128,64},{192,128},{256,448},{320,256},{384,320},{4... | collective-permute-start | bytes 1769480 | tf_op jit(solution)/shard_map/ppermute | solution.py:302
  32.3 59.3 %collective-permute-start = (bf16[2048,128]{1,0:T(8,128)(2,1)}, bf16[2048,128]{1,0:T(8,128)(2,1)}, u32[]{:S(2)}, u32[]{:S(2)}) collective-permute-start(bf16[2048,128]{1,0:T(8,128)(2,1)} %get-tuple-element.24), channel_id=1, source_target_pairs={{0,256},{64,320},{128,384},{192,448},{256,0},{320,64},{384,128},{4... | collective-permute-start | bytes 1572872 | tf_op jit(solution)/shard_map/ppermute | solution.py:306
  79.1 41.8 %collective-permute-start.7 = (bf16[1088,256]{1,0:T(8,128)(2,1)S(1)}, bf16[1088,256]{1,0:T(8,128)(2,1)S(1)}, u32[]{:S(2)}, u32[]{:S(2)}) collective-permute-start(bf16[1088,256]{1,0:T(8,128)(2,1)S(1)} %get-tuple-element.40), channel_id=1, source_target_pairs={{0,128},{64,192},{128,0},{192,64},{256,384},{320,448},{384,256},{4... | collective-permute-start | bytes 1671176 | tf_op jit(solution)/shard_map/ppermute | solution.py:302
  86.3 34.5 %collective-permute-start.8 = (bf16[1088,256]{1,0:T(8,128)(2,1)S(1)}, bf16[1088,256]{1,0:T(8,128)(2,1)S(1)}, u32[]{:S(2)}, u32[]{:S(2)}) collective-permute-start(bf16[1088,256]{1,0:T(8,128)(2,1)S(1)} %get-tuple-element.41), channel_id=1, source_target_pairs={{0,192},{64,0},{128,64},{192,128},{256,448},{320,256},{384,320},{4... | collective-permute-start | bytes 1671176 | tf_op jit(solution)/shard_map/ppermute | solution.py:302
  88.3 32.6 %collective-permute-start.9 = (bf16[1088,256]{1,0:T(8,128)(2,1)S(1)}, bf16[1088,256]{1,0:T(8,128)(2,1)S(1)}, u32[]{:S(2)}, u32[]{:S(2)}) collective-permute-start(bf16[1088,256]{1,0:T(8,128)(2,1)S(1)} %get-tuple-element.42), channel_id=1, source_target_pairs={{0,64},{64,128},{128,192},{192,0},{256,320},{320,384},{384,448},{4... | collective-permute-start | bytes 1671176 | tf_op jit(solution)/shard_map/ppermute | solution.py:302
  92.7 27.9 %copy-start.2 = (bf16[2304,128]{1,0:T(8,128)(2,1)S(1)}, bf16[2304,128]{1,0:T(8,128)(2,1)}, u32[]{:S(2)}) copy-start(bf16[2304,128]{1,0:T(8,128)(2,1)} %copy-done) | copy-start | bytes 1769476
  92.7 27.9 %copy-start.5 = (bf16[2304,128]{1,0:T(8,128)(2,1)S(1)}, bf16[2304,128]{1,0:T(8,128)(2,1)}, u32[]{:S(2)}) copy-start(bf16[2304,128]{1,0:T(8,128)(2,1)} %copy-done.3) | copy-start | bytes 1769476
  92.7 21.4 %collective-permute-start.4 = (bf16[512,128]{1,0:T(8,128)(2,1)S(1)}, bf16[512,128]{1,0:T(8,128)(2,1)S(1)}, u32[]{:S(2)}, u32[]{:S(2)}) collective-permute-start(bf16[512,128]{1,0:T(8,128)(2,1)S(1)} %get-tuple-element.35), channel_id=1, source_target_pairs={{0,64},{64,128},{128,192},{192,0},{256,320},{320,384},{384,448},{4... | collective-permute-start | bytes 393224 | tf_op jit(solution)/shard_map/ppermute | solution.py:302
  94.9 22.7 %collective-permute-start.5 = (bf16[512,128]{1,0:T(8,128)(2,1)S(1)}, bf16[512,128]{1,0:T(8,128)(2,1)S(1)}, u32[]{:S(2)}, u32[]{:S(2)}) collective-permute-start(bf16[512,128]{1,0:T(8,128)(2,1)S(1)} %get-tuple-element.36), channel_id=1, source_target_pairs={{0,128},{64,192},{128,0},{192,64},{256,384},{320,448},{384,256},{4... | collective-permute-start | bytes 393224 | tf_op jit(solution)/shard_map/ppermute | solution.py:302
  114.1 6.5 %collective-permute-start.6 = (bf16[512,128]{1,0:T(8,128)(2,1)S(1)}, bf16[512,128]{1,0:T(8,128)(2,1)S(1)}, u32[]{:S(2)}, u32[]{:S(2)}) collective-permute-start(bf16[512,128]{1,0:T(8,128)(2,1)S(1)} %get-tuple-element.37), channel_id=1, source_target_pairs={{0,192},{64,0},{128,64},{192,128},{256,448},{320,256},{384,320},{4... | collective-permute-start | bytes 393224 | tf_op jit(solution)/shard_map/ppermute | solution.py:302
  121.2 23.3 %collective-permute-start.13 = (bf16[1088,128]{1,0:T(8,128)(2,1)S(1)}, bf16[1088,128]{1,0:T(8,128)(2,1)S(1)}, u32[]{:S(2)}, u32[]{:S(2)}) collective-permute-start(bf16[1088,128]{1,0:T(8,128)(2,1)S(1)} %activate.1.refs_0_), channel_id=1, source_target_pairs={{0,256},{64,320},{128,384},{192,448},{256,0},{320,64},{384,128},{4... | collective-permute-start | bytes 835592 | tf_op jit(solution)/shard_map/ppermute | solution.py:306
  131.7 19.6 %collective-permute-start.12 = (bf16[1088,128]{1,0:T(8,128)(2,1)S(1)}, bf16[1088,128]{1,0:T(8,128)(2,1)S(1)}, u32[]{:S(2)}, u32[]{:S(2)}) collective-permute-start(bf16[1088,128]{1,0:T(8,128)(2,1)S(1)} %activate.1.refs_0_), channel_id=1, source_target_pairs={{0,192},{64,0},{128,64},{192,128},{256,448},{320,256},{384,320},{4... | collective-permute-start | bytes 835592 | tf_op jit(solution)/shard_map/ppermute | solution.py:302
  135.1 18.4 %collective-permute-start.11 = (bf16[1088,128]{1,0:T(8,128)(2,1)S(1)}, bf16[1088,128]{1,0:T(8,128)(2,1)S(1)}, u32[]{:S(2)}, u32[]{:S(2)}) collective-permute-start(bf16[1088,128]{1,0:T(8,128)(2,1)S(1)} %activate.1.refs_0_), channel_id=1, source_target_pairs={{0,128},{64,192},{128,0},{192,64},{256,384},{320,448},{384,256},{4... | collective-permute-start | bytes 835592 | tf_op jit(solution)/shard_map/ppermute | solution.py:302
  139.1 14.4 %collective-permute-start.10 = (bf16[1088,128]{1,0:T(8,128)(2,1)S(1)}, bf16[1088,128]{1,0:T(8,128)(2,1)S(1)}, u32[]{:S(2)}, u32[]{:S(2)}) collective-permute-start(bf16[1088,128]{1,0:T(8,128)(2,1)S(1)} %activate.1.refs_0_), channel_id=1, source_target_pairs={{0,64},{64,128},{128,192},{192,0},{256,320},{320,384},{384,448},{4... | collective-permute-start | bytes 835592 | tf_op jit(solution)/shard_map/ppermute | solution.py:302
  144.6 9.1 %collective-permute-start.16 = (bf16[1088,128]{1,0:T(8,128)(2,1)S(1)}, bf16[1088,128]{1,0:T(8,128)(2,1)S(1)}, u32[]{:S(2)}, u32[]{:S(2)}) collective-permute-start(bf16[1088,128]{1,0:T(8,128)(2,1)S(1)} %collective-permute-done.13.refs_4_), channel_id=1, source_target_pairs={{0,192},{64,0},{128,64},{192,128},{256,448},{320,256},{384,320},{4... | collective-permute-start | bytes 835592 | tf_op jit(solution)/shard_map/ppermute | solution.py:302
  147.3 9.8 %collective-permute-start.15 = (bf16[1088,128]{1,0:T(8,128)(2,1)S(1)}, bf16[1088,128]{1,0:T(8,128)(2,1)S(1)}, u32[]{:S(2)}, u32[]{:S(2)}) collective-permute-start(bf16[1088,128]{1,0:T(8,128)(2,1)S(1)} %collective-permute-done.13.refs_4_), channel_id=1, source_target_pairs={{0,128},{64,192},{128,0},{192,64},{256,384},{320,448},{384,256},{4... | collective-permute-start | bytes 835592 | tf_op jit(solution)/shard_map/ppermute | solution.py:302
  151.4 12.7 %collective-permute-start.14 = (bf16[1088,128]{1,0:T(8,128)(2,1)S(1)}, bf16[1088,128]{1,0:T(8,128)(2,1)S(1)}, u32[]{:S(2)}, u32[]{:S(2)}) collective-permute-start(bf16[1088,128]{1,0:T(8,128)(2,1)S(1)} %collective-permute-done.13.refs_4_), channel_id=1, source_target_pairs={{0,64},{64,128},{128,192},{192,0},{256,320},{320,384},{384,448},{4... | collective-permute-start | bytes 835592 | tf_op jit(solution)/shard_map/ppermute | solution.py:302
  165.6 46.0 %copy-start.9 = (s32[128,8]{0,1:T(8,128)S(1)}, s32[128,8]{0,1:T(8,128)}, u32[]{:S(2)}) copy-start(s32[128,8]{0,1:T(8,128)} %param.7) | copy-start | bytes 12292
  165.7 46.0 %copy-start.10 = (f32[128,8]{0,1:T(8,128)S(1)}, f32[128,8]{0,1:T(8,128)}, u32[]{:S(2)}) copy-start(f32[128,8]{0,1:T(8,128)} %param.8) | copy-start | bytes 12292
  (5 other events, 5.0 us)

commit v10 on v8

--- a/solution.py
+++ b/solution.py
@@ -10,6 +10,7 @@
 LANES = 128
 X = 4
 PARTS = 4
+HOLD = 50_000_000_000
 FULL = 60 * 1024 * 1024
 VMEM = 16 * 1024 * 1024
 
@@ -106,50 +107,78 @@
     return call(dispatch_kernel, "dispatch", out, specs, anywhere(), scratch, FULL)(x, ids, tokens)
 
 
-def pack_kernel(x_ref, z_ref, gate_ref, up_ref, down_ref, *outs):
-    near, far = outs[:X], outs[X:]
+def pack_kernel(x_ref, gate_ref, up_ref, down_ref, *refs):
+    both, downs, (rows_ref, sems) = refs[:X], refs[X : 2 * X], refs[2 * X :]
     quarter = gate_ref.shape[0] // X
     depth = down_ref.shape[0]
-
-    def put_down(out, base, z, q):
-        p = z * X + q
-        first = p // 2 * (quarter // LANES)
-        for c in range(4):
-            tile = first + 3 if c == 3 else first + c + 4 * lax.rem(p, 2)
-            cols = pl.ds(pl.multiple_of(tile * LANES, LANES), LANES)
-            out[pl.ds(base + c * depth, depth), :] = down_ref[:, cols]
-
+    fetch = pltpu.make_async_copy(down_ref, rows_ref, sems.at[0])
+    fetch.start()
+    copies = []
+    for d in (2, 1, 3, 0):
+        q = lax.rem(x_ref[0] + d, X)
+        part = pl.ds(pl.multiple_of(q * quarter, quarter), quarter)
+        for half, ref in enumerate((gate_ref, up_ref)):
+            rows = pl.ds(half * quarter, quarter)
+            copies.append(pltpu.make_async_copy(ref.at[part, :], both[d].at[rows, :], sems.at[1 + len(copies)]))
+            copies[-1].start()
+    fetch.wait()
     for d in range(X):
         q = lax.rem(x_ref[0] + d, X)
-        part = pl.ds(pl.multiple_of(q * quarter, quarter), quarter)
-        near[d][pl.ds(0, quarter), :] = gate_ref[part, :]
-        near[d][pl.ds(quarter, quarter), :] = up_ref[part, :]
-        put_down(near[d], 2 * quarter, z_ref[0], q)
-        put_down(far[d], 0, 1 - z_ref[0], q)
-
-
-def pack(x, z, w_gate, w_up, w_down):
-    rows = 2 * (w_gate.shape[0] // X) + 4 * w_down.shape[0]
-    shapes = [jax.ShapeDtypeStruct((r, LANES), BF) for r in [rows] * X + [4 * w_down.shape[0]] * X]
-    outs = call(pack_kernel, "pack", shapes, [in_smem()] * 2 + [in_vmem()] * 3)(x, z, w_gate, w_up, w_down)
+        for z in range(2):
+            p = z * X + q
+            first = p // 2 * (quarter // LANES)
+            for c in range(4):
+                tile = first + 3 if c == 3 else first + c + 4 * lax.rem(p, 2)
+                cols = pl.ds(pl.multiple_of(tile * LANES, LANES), LANES)
+                downs[d][pl.ds((z * 4 + c) * depth, depth), :] = rows_ref[:, cols]
+    for copy in copies:
+        copy.wait()
+
+
+def pack(x, w_gate, w_up, w_down):
+    depth = w_down.shape[0]
+    both = jax.ShapeDtypeStruct((2 * (w_gate.shape[0] // X), LANES), BF)
+    downs = jax.ShapeDtypeStruct((8 * depth, LANES), BF)
+    scratch = [pltpu.VMEM(w_down.shape, BF), pltpu.SemaphoreType.DMA((1 + 2 * X,))]
+    specs = [in_smem()] + [anywhere()] * 3
+    outs = call(pack_kernel, "pack", [both] * X + [downs] * X, specs, scratch=scratch, vmem=FULL)(x, w_gate, w_up, w_down)
     return outs[:X], outs[X:]
 
 
-def assemble_kernel(*refs):
-    near, far, out_ref = refs[:X], refs[X : 2 * X], refs[2 * X]
-    rows = far[0].shape[0]
+def swap_kernel(z_ref, *refs):
+    downs, (out_ref, sems) = refs[:X], refs[X:]
+    rows = out_ref.shape[0] // X
+    start = pl.multiple_of((1 - z_ref[0]) * rows, rows)
+    copies = []
+    for d, ref in enumerate(downs):
+        copies.append(pltpu.make_async_copy(ref.at[pl.ds(start, rows), :], out_ref.at[pl.ds(d * rows, rows), :], sems.at[d]))
+        copies[d].start()
+    for copy in copies:
+        copy.wait()
+
+
+def swap(z, downs):
+    shape = jax.ShapeDtypeStruct((X * downs[0].shape[0] // 2, LANES), BF)
+    scratch = [pltpu.SemaphoreType.DMA((X,))]
+    return call(swap_kernel, "swap", shape, [in_smem()] + [anywhere()] * X, scratch=scratch, vmem=FULL)(z, *downs)
+
+
+def assemble_kernel(z_ref, *refs):
+    downs, (other_ref, out_ref) = refs[:X], refs[X:]
+    rows = other_ref.shape[0] // X
     depth = rows // 4
-    for d in range(X):
-        base = near[d].shape[0] - rows
+    start = z_ref[0] * rows
+    for d, ref in enumerate(downs):
         for c in range(4):
             cols = pl.ds(c * LANES, LANES)
-            out_ref[pl.ds(d * depth, depth), cols] = near[d][pl.ds(base + c * depth, depth), :]
-            out_ref[pl.ds((X + d) * depth, depth), cols] = far[d][pl.ds(c * depth, depth), :]
-
-
-def assemble(near, far):
-    shape = jax.ShapeDtypeStruct((2 * far[0].shape[0], 4 * LANES), BF)
-    return call(assemble_kernel, "assemble", shape, [in_vmem()] * (2 * X))(*near, *far)
+            out_ref[pl.ds(d * depth, depth), cols] = ref[pl.ds(pl.multiple_of(start + c * depth, LANES), depth), :]
+            out_ref[pl.ds((X + d) * depth, depth), cols] = other_ref[pl.ds(d * rows + c * depth, depth), :]
+
+
+def assemble(z, downs, other):
+    shape = jax.ShapeDtypeStruct((other.shape[0] // 2, 4 * LANES), BF)
+    cost = pl.CostEstimate(flops=HOLD, bytes_accessed=4 * other.size, transcendentals=0)
+    return call(assemble_kernel, "assemble", shape, [in_smem()] + [in_vmem()] * (X + 1), cost=cost)(z, *downs, other)
 
 
 def stacked(chunks_ref):
@@ -289,9 +318,8 @@
     return lax.ppermute(value, "pipe", pairs)
 
 
-def cross(value, d=0):
-    pairs = [(z * X + x, (1 - z) * X + (x + d) % X) for z in range(2) for x in range(X)]
-    return lax.ppermute(value, "pipe", pairs)
+def cross(value):
+    return lax.ppermute(value, "pipe", [(p, (p + X) % (2 * X)) for p in range(2 * X)])
 
 
 def body(tokens, expert_ids, gate_scale, w_gate, w_up, w_down):
@@ -303,14 +331,16 @@
     w_gate, w_up, w_down = w_gate[0], w_up[0], w_down[0]
     buffer = dispatch(x, ids, tokens, groups)
     chunks = lax.all_to_all(buffer, "expert", split_axis=0, concat_axis=0, tiled=True)
-    near, far = pack(x, z, w_gate, w_up, w_down)
-    near = [near[0]] + [shift(near[d], d) for d in range(1, X)]
-    far = [cross(far[d], d) for d in range(X)]
-    chunks, *far = lax.optimization_barrier((chunks, *far))
-    parts = project(chunks, [near[d] for d in (2, 1, 3)], BF, "project_sent")
+    both, downs = pack(x, w_gate, w_up, w_down)
+    both = [both[0]] + [shift(both[d], d) for d in range(1, X)]
+    downs = [downs[0]] + [shift(downs[d], d) for d in range(1, X)]
+    held = lax.optimization_barrier((*both, *downs))
+    both, downs = held[:X], held[X:]
+    other = cross(swap(z, downs))
+    parts = project(chunks, [both[d] for d in (2, 1, 3)], BF, "project_sent")
     arrived = [shift(part, -d) for d, part in zip((2, 1, 3), parts)]
-    (mine,) = project(chunks, near[:1], F32, "project_own")
-    weight = assemble(near, far)
+    chunks, weight = lax.optimization_barrier((chunks, assemble(z, downs, other)))
+    (mine,) = project(chunks, both[:1], F32, "project_own")
     hidden = activate(mine, arrived)
     swapped = cross(hidden)
     hiddens = [hidden] + [shift(hidden, d) for d in range(1, X)]

time: 216 us -> 191 us (0.88)
  waiting for transfers between devices: 73.7 us -> 43.3 us
  blocking collectives: 40.3 us -> 49.5 us
  starting transfers between devices: 81.9 us -> 77.5 us
  Pallas kernels: 15.5 us -> 18.9 us
  local copies, waits for them, and re-layouts: 3.79 us -> 0.79 us
    ppermute x5 -> x2, waiting for transfers between devices: 40 us -> 0.01 us  [cross(): lax.ppermute(value, 'pipe', [(p, (p + X) % (2 * X)) for p in range(2 * X)])]
    ppermute x5 -> x2, starting transfers between devices: 28.9 us -> 10.1 us  [cross(): lax.ppermute(value, 'pipe', [(p, (p + X) % (2 * X)) for p in range(2 * X)])]
    ppermute x12 -> x15, starting transfers between devices: 38.2 us -> 52.8 us  [shift(): return lax.ppermute(value, 'pipe', pairs)]
    ppermute x12 -> x15, waiting for transfers between devices: 33.7 us -> 43.3 us  [shift(): return lax.ppermute(value, 'pipe', pairs)]
    all_to_all x1, blocking collectives: 40.3 us -> 49.5 us  [body(): lax.all_to_all(output, 'expert', split_axis=0, concat_axis=0, tiled=True)]
    pallas_call x2 -> x3, Pallas kernels: 2.79 us -> 6.79 us  [the longest x1 3.4 us: pack(): call(pack_kernel, 'pack', [both] * X + [downs] * X, specs, scratch=scratc...]
    unnamed x14 -> x8, local copies, waits for them, and re-layouts: 3.03 us -> 0.02 us
  transfers between devices with their start and end apart: 18 -> 18, of which waited for: 8 -> 6; matrix products, arithmetic and copies ran while one was open for 0% -> 0% of each run, Pallas kernels for 2% -> 6%
where the time goes in v10:
time: 191 us; the launch traced here: 190 us
  starting transfers between devices  77.5 us (41%)
  blocking collectives  49.5 us (26%)
  waiting for transfers between devices  43.3 us (23%)
  Pallas kernels  18.9 us (10%)
    ppermute x15, starting transfers between devices, shift(): return lax.ppermute(value, 'pipe', pairs)  52.8 us
    all_to_all x1, blocking collectives, body(): lax.all_to_all(output, 'expert', split_axis=0, concat_axis=0, tiled=True)  49.5 us
    ppermute x15, waiting for transfers between devices, shift(): return lax.ppermute(value, 'pipe', pairs)  43.3 us
    all_to_all x1, starting transfers between devices, body(): lax.all_to_all(buffer, 'expert', split_axis=0, concat_axis=0, tiled=True)  14.6 us
    ppermute x2, starting transfers between devices, cross(): lax.ppermute(value, 'pipe', [(p, (p + X) % (2 * X)) for p in range(2 * X)])  10.1 us
    pallas_call x2, Pallas kernels, project(): return call(kernel, name, shapes, specs, scratch=scratch)(chunks, *packs)  5.08 us
  transfers between devices with their start and end apart: 18, of which 6 were waited for; matrix products, arithmetic and copies ran while one was open for 0% of the time, Pallas kernels for 6%

profile of v10, /device:TPU:1, one launch (start us, length us, event | category | flops | bytes accessed | tf_op | source)
XLA Modules:
  0.0 190.3 jit_solution(15927356306455425483)
XLA Ops:
  0.0 3.5 %dispatch.1 = bf16[64,120,128]{2,1,0:T(8,128)(2,1)} custom-call(s32[1]{0:T(128)} %bitcast.x_ref, s32[8,128]{1,0:T(8,128)} %bitcast.7, bf16[128,3584]{1,0:T(8,128)(2,1)} %tok_ref.1), custom_call_target="tpu_custom_call" | custom-call | tf_op jit(solution)/shard_map/dispatch/pallas_call | solution.py:107
  3.5 14.6 %all-to-all-start = ((bf16[64,120,128]{2,1,0:T(8,128)(2,1)}), bf16[64,120,128]{2,1,0:T(8,128)(2,1)S(1)}, u32[]{:S(2)}, u32[]{:S(2)}) async-start(bf16[64,120,128]{2,1,0:T(8,128)(2,1)} %dispatch.1), calls=%async_computation | async-start | bytes 3932160 | tf_op jit(solution)/shard_map/all_to_all | solution.py:333
  18.2 3.4 %pack.1 = (bf16[1792,128]{1,0:T(8,128)(2,1)}, bf16[1792,128]{1,0:T(8,128)(2,1)}, bf16[1792,128]{1,0:T(8,128)(2,1)}, bf16[1792,128]{1,0:T(8,128)(2,1)}, bf16[1024...) custom-call(s32[1]{0:T(128)} %bitcast.x_ref, ...), custom_call_target="tpu_custom_call" | custom-call | tf_op jit(solution)/shard_map/pack/pallas_call | solution.py:144
  21.6 3.1 %collective-permute-start.3 = (bf16[1024,128]{1,0:T(8,128)(2,1)}, bf16[1024,128]{1,0:T(8,128)(2,1)}, u32[]{:S(2)}, u32[]{:S(2)}) collective-permute-start(bf16[1024,128]{1,0:T(8,128)(2,1)} %get-tuple-element.31), channel_id=1, source_target_pairs={{0,64},{64,128},{128,192},{192,0},{256,320},{320,384},{384,448},{4... | collective-permute-start | bytes 786440 | tf_op jit(solution)/shard_map/ppermute | solution.py:318
  24.7 3.1 %collective-permute-start = (bf16[1792,128]{1,0:T(8,128)(2,1)}, bf16[1792,128]{1,0:T(8,128)(2,1)S(1)}, u32[]{:S(2)}, u32[]{:S(2)}) collective-permute-start(bf16[1792,128]{1,0:T(8,128)(2,1)} %get-tuple-element.27), channel_id=1, source_target_pairs={{0,64},{64,128},{128,192},{192,0},{256,320},{320,384},{384,448},{4... | collective-permute-start | bytes 1376264 | tf_op jit(solution)/shard_map/ppermute | solution.py:318
  27.8 3.3 %collective-permute-start.1 = (bf16[1792,128]{1,0:T(8,128)(2,1)}, bf16[1792,128]{1,0:T(8,128)(2,1)S(1)}, u32[]{:S(2)}, u32[]{:S(2)}) collective-permute-start(bf16[1792,128]{1,0:T(8,128)(2,1)} %get-tuple-element.28), channel_id=1, source_target_pairs={{0,128},{64,192},{128,0},{192,64},{256,384},{320,448},{384,256},{4... | collective-permute-start | bytes 1376264 | tf_op jit(solution)/shard_map/ppermute | solution.py:318
  31.2 3.8 %collective-permute-start.2 = (bf16[1792,128]{1,0:T(8,128)(2,1)}, bf16[1792,128]{1,0:T(8,128)(2,1)S(1)}, u32[]{:S(2)}, u32[]{:S(2)}) collective-permute-start(bf16[1792,128]{1,0:T(8,128)(2,1)} %get-tuple-element.29), channel_id=1, source_target_pairs={{0,192},{64,0},{128,64},{192,128},{256,448},{320,256},{384,320},{4... | collective-permute-start | bytes 1376264 | tf_op jit(solution)/shard_map/ppermute | solution.py:318
  37.4 3.4 %collective-permute-start.5 = (bf16[1024,128]{1,0:T(8,128)(2,1)}, bf16[1024,128]{1,0:T(8,128)(2,1)}, u32[]{:S(2)}, u32[]{:S(2)}) collective-permute-start(bf16[1024,128]{1,0:T(8,128)(2,1)} %get-tuple-element.33), channel_id=1, source_target_pairs={{0,192},{64,0},{128,64},{192,128},{256,448},{320,256},{384,320},{4... | collective-permute-start | bytes 786440 | tf_op jit(solution)/shard_map/ppermute | solution.py:318
  40.8 17.9 %collective-permute-done.4.refs_2_ = bf16[1024,128]{1,0:T(8,128)(2,1)} collective-permute-done((bf16[1024,128]{1,0:T(8,128)(2,1)}, bf16[1024,128]{1,0:T(8,128)(2,1)}, u32[]{:S(2)}, u32[]{:S(2)}) %collective-permute-start.4) | collective-permute-done | bytes 262176 | tf_op jit(solution)/shard_map/ppermute | solution.py:318
  58.7 4.4 %collective-permute-done.5.refs_3_ = bf16[1024,128]{1,0:T(8,128)(2,1)} collective-permute-done((bf16[1024,128]{1,0:T(8,128)(2,1)}, bf16[1024,128]{1,0:T(8,128)(2,1)}, u32[]{:S(2)}, u32[]{:S(2)}) %collective-permute-start.5) | collective-permute-done | bytes 262176 | tf_op jit(solution)/shard_map/ppermute | solution.py:318
  65.0 7.9 %collective-permute-start.6 = (bf16[2048,128]{1,0:T(8,128)(2,1)}, bf16[2048,128]{1,0:T(8,128)(2,1)}, u32[]{:S(2)}, u32[]{:S(2)}) collective-permute-start(bf16[2048,128]{1,0:T(8,128)(2,1)} %swap.1), channel_id=1, source_target_pairs={{0,256},{64,320},{128,384},{192,448},{256,0},{320,64},{384,128},{4... | collective-permute-start | bytes 1572872 | tf_op jit(solution)/shard_map/ppermute | solution.py:322
  73.0 3.9 %project_sent.1 = (bf16[1088,256]{1,0:T(8,128)(2,1)S(1)}, bf16[1088,256]{1,0:T(8,128)(2,1)S(1)}, bf16[1088,256]{1,0:T(8,128)(2,1)S(1)}) custom-call(bf16[64,120,128]{2,1,0:T(8,128)(2,1)S(1)} %all-to-all-done.chunks_ref, bf16[1792,128]{1,0:T(8,128)(2,1)S(1)} %collective-permute-done.1.refs_0_, bf16[1792,128]{1,0:T(8,128)(2,1)S(1)} %collective-permute-done.refs_1_, ...), custom_call_target="tpu_custom_call" | custom-call | tf_op jit(solution)/shard_map/project_sent/pallas_call | solution.py:222
  76.9 4.4 %collective-permute-start.7 = (bf16[1088,256]{1,0:T(8,128)(2,1)S(1)}, bf16[1088,256]{1,0:T(8,128)(2,1)S(1)}, u32[]{:S(2)}, u32[]{:S(2)}) collective-permute-start(bf16[1088,256]{1,0:T(8,128)(2,1)S(1)} %get-tuple-element.44), channel_id=1, source_target_pairs={{0,128},{64,192},{128,0},{192,64},{256,384},{320,448},{384,256},{4... | collective-permute-start | bytes 1671176 | tf_op jit(solution)/shard_map/ppermute | solution.py:318
  81.3 4.7 %collective-permute-start.8 = (bf16[1088,256]{1,0:T(8,128)(2,1)S(1)}, bf16[1088,256]{1,0:T(8,128)(2,1)S(1)}, u32[]{:S(2)}, u32[]{:S(2)}) collective-permute-start(bf16[1088,256]{1,0:T(8,128)(2,1)S(1)} %get-tuple-element.45), channel_id=1, source_target_pairs={{0,192},{64,0},{128,64},{192,128},{256,448},{320,256},{384,320},{4... | collective-permute-start | bytes 1671176 | tf_op jit(solution)/shard_map/ppermute | solution.py:318
  92.5 14.2 %collective-permute-done.8.refs_1_ = bf16[1088,256]{1,0:T(8,128)(2,1)S(1)} collective-permute-done((bf16[1088,256]{1,0:T(8,128)(2,1)S(1)}, bf16[1088,256]{1,0:T(8,128)(2,1)S(1)}, u32[]{:S(2)}, u32[]{:S(2)}) %collective-permute-start.8) | collective-permute-done | bytes 557088 | tf_op jit(solution)/shard_map/ppermute | solution.py:318
  109.3 4.6 %collective-permute-start.10 = (bf16[1088,128]{1,0:T(8,128)(2,1)S(1)}, bf16[1088,128]{1,0:T(8,128)(2,1)S(1)}, u32[]{:S(2)}, u32[]{:S(2)}) collective-permute-start(bf16[1088,128]{1,0:T(8,128)(2,1)S(1)} %activate.1.refs_0_), channel_id=1, source_target_pairs={{0,64},{64,128},{128,192},{192,0},{256,320},{320,384},{384,448},{4... | collective-permute-start | bytes 835592 | tf_op jit(solution)/shard_map/ppermute | solution.py:318
  113.9 3.6 %collective-permute-start.11 = (bf16[1088,128]{1,0:T(8,128)(2,1)S(1)}, bf16[1088,128]{1,0:T(8,128)(2,1)S(1)}, u32[]{:S(2)}, u32[]{:S(2)}) collective-permute-start(bf16[1088,128]{1,0:T(8,128)(2,1)S(1)} %activate.1.refs_0_), channel_id=1, source_target_pairs={{0,128},{64,192},{128,0},{192,64},{256,384},{320,448},{384,256},{4... | collective-permute-start | bytes 835592 | tf_op jit(solution)/shard_map/ppermute | solution.py:318
  117.5 2.6 %collective-permute-start.12 = (bf16[1088,128]{1,0:T(8,128)(2,1)S(1)}, bf16[1088,128]{1,0:T(8,128)(2,1)S(1)}, u32[]{:S(2)}, u32[]{:S(2)}) collective-permute-start(bf16[1088,128]{1,0:T(8,128)(2,1)S(1)} %activate.1.refs_0_), channel_id=1, source_target_pairs={{0,192},{64,0},{128,64},{192,128},{256,448},{320,256},{384,320},{4... | collective-permute-start | bytes 835592 | tf_op jit(solution)/shard_map/ppermute | solution.py:318
  120.1 5.5 %collective-permute-start.14 = (bf16[1088,128]{1,0:T(8,128)(2,1)S(1)}, bf16[1088,128]{1,0:T(8,128)(2,1)S(1)}, u32[]{:S(2)}, u32[]{:S(2)}) collective-permute-start(bf16[1088,128]{1,0:T(8,128)(2,1)S(1)} %collective-permute-done.13.refs_4_), channel_id=1, source_target_pairs={{0,64},{64,128},{128,192},{192,0},{256,320},{320,384},{384,448},{4... | collective-permute-start | bytes 835592 | tf_op jit(solution)/shard_map/ppermute | solution.py:318
  125.6 3.6 %collective-permute-start.15 = (bf16[1088,128]{1,0:T(8,128)(2,1)S(1)}, bf16[1088,128]{1,0:T(8,128)(2,1)S(1)}, u32[]{:S(2)}, u32[]{:S(2)}) collective-permute-start(bf16[1088,128]{1,0:T(8,128)(2,1)S(1)} %collective-permute-done.13.refs_4_), channel_id=1, source_target_pairs={{0,128},{64,192},{128,0},{192,64},{256,384},{320,448},{384,256},{4... | collective-permute-start | bytes 835592 | tf_op jit(solution)/shard_map/ppermute | solution.py:318
  129.3 2.6 %collective-permute-start.16 = (bf16[1088,128]{1,0:T(8,128)(2,1)S(1)}, bf16[1088,128]{1,0:T(8,128)(2,1)S(1)}, u32[]{:S(2)}, u32[]{:S(2)}) collective-permute-start(bf16[1088,128]{1,0:T(8,128)(2,1)S(1)} %collective-permute-done.13.refs_4_), channel_id=1, source_target_pairs={{0,192},{64,0},{128,64},{192,128},{256,448},{320,256},{384,320},{4... | collective-permute-start | bytes 835592 | tf_op jit(solution)/shard_map/ppermute | solution.py:318
  131.9 2.5 %collective-permute-done.15.refs_6_ = bf16[1088,128]{1,0:T(8,128)(2,1)S(1)} collective-permute-done((bf16[1088,128]{1,0:T(8,128)(2,1)S(1)}, bf16[1088,128]{1,0:T(8,128)(2,1)S(1)}, u32[]{:S(2)}, u32[]{:S(2)}) %collective-permute-start.15) | collective-permute-done | bytes 278560 | tf_op jit(solution)/shard_map/ppermute | solution.py:318
  134.4 2.5 %collective-permute-done.16.refs_7_ = bf16[1088,128]{1,0:T(8,128)(2,1)S(1)} collective-permute-done((bf16[1088,128]{1,0:T(8,128)(2,1)S(1)}, bf16[1088,128]{1,0:T(8,128)(2,1)S(1)}, u32[]{:S(2)}, u32[]{:S(2)}) %collective-permute-start.16) | collective-permute-done | bytes 278560 | tf_op jit(solution)/shard_map/ppermute | solution.py:318
  138.4 49.5 %all_to_all.10.chunks_ref = bf16[64,64,128]{2,1,0:T(8,128)(2,1)S(1)} all-to-all(bf16[64,64,128]{2,1,0:T(8,128)(2,1)S(1)} %down.1), channel_id=1, replica_groups=mesh['pipe'=8,'expert'=64] {'expert'}, dimensions={0} | all-to-all | bytes 2097152 | tf_op jit(solution)/shard_map/all_to_all | solution.py:349
  (31 shorter events, 17.2 us)
Async XLA Ops:
  3.5 69.4 %all-to-all-start = ((bf16[64,120,128]{2,1,0:T(8,128)(2,1)}), bf16[64,120,128]{2,1,0:T(8,128)(2,1)S(1)}, u32[]{:S(2)}, u32[]{:S(2)}) async-start(bf16[64,120,128]{2,1,0:T(8,128)(2,1)} %dispatch.1), calls=%async_computation | async-start | bytes 3932160 | tf_op jit(solution)/shard_map/all_to_all | solution.py:333
  21.6 15.8 %collective-permute-start.3 = (bf16[1024,128]{1,0:T(8,128)(2,1)}, bf16[1024,128]{1,0:T(8,128)(2,1)}, u32[]{:S(2)}, u32[]{:S(2)}) collective-permute-start(bf16[1024,128]{1,0:T(8,128)(2,1)} %get-tuple-element.31), channel_id=1, source_target_pairs={{0,64},{64,128},{128,192},{192,0},{256,320},{320,384},{384,448},{4... | collective-permute-start | bytes 786440 | tf_op jit(solution)/shard_map/ppermute | solution.py:318
  24.7 38.4 %collective-permute-start = (bf16[1792,128]{1,0:T(8,128)(2,1)}, bf16[1792,128]{1,0:T(8,128)(2,1)S(1)}, u32[]{:S(2)}, u32[]{:S(2)}) collective-permute-start(bf16[1792,128]{1,0:T(8,128)(2,1)} %get-tuple-element.27), channel_id=1, source_target_pairs={{0,64},{64,128},{128,192},{192,0},{256,320},{320,384},{384,448},{4... | collective-permute-start | bytes 1376264 | tf_op jit(solution)/shard_map/ppermute | solution.py:318
  27.8 35.3 %collective-permute-start.1 = (bf16[1792,128]{1,0:T(8,128)(2,1)}, bf16[1792,128]{1,0:T(8,128)(2,1)S(1)}, u32[]{:S(2)}, u32[]{:S(2)}) collective-permute-start(bf16[1792,128]{1,0:T(8,128)(2,1)} %get-tuple-element.28), channel_id=1, source_target_pairs={{0,128},{64,192},{128,0},{192,64},{256,384},{320,448},{384,256},{4... | collective-permute-start | bytes 1376264 | tf_op jit(solution)/shard_map/ppermute | solution.py:318
  31.2 31.9 %collective-permute-start.2 = (bf16[1792,128]{1,0:T(8,128)(2,1)}, bf16[1792,128]{1,0:T(8,128)(2,1)S(1)}, u32[]{:S(2)}, u32[]{:S(2)}) collective-permute-start(bf16[1792,128]{1,0:T(8,128)(2,1)} %get-tuple-element.29), channel_id=1, source_target_pairs={{0,192},{64,0},{128,64},{192,128},{256,448},{320,256},{384,320},{4... | collective-permute-start | bytes 1376264 | tf_op jit(solution)/shard_map/ppermute | solution.py:318
  35.0 23.7 %collective-permute-start.4 = (bf16[1024,128]{1,0:T(8,128)(2,1)}, bf16[1024,128]{1,0:T(8,128)(2,1)}, u32[]{:S(2)}, u32[]{:S(2)}) collective-permute-start(bf16[1024,128]{1,0:T(8,128)(2,1)} %get-tuple-element.32), channel_id=1, source_target_pairs={{0,128},{64,192},{128,0},{192,64},{256,384},{320,448},{384,256},{4... | collective-permute-start | bytes 786440 | tf_op jit(solution)/shard_map/ppermute | solution.py:318
  37.4 25.7 %collective-permute-start.5 = (bf16[1024,128]{1,0:T(8,128)(2,1)}, bf16[1024,128]{1,0:T(8,128)(2,1)}, u32[]{:S(2)}, u32[]{:S(2)}) collective-permute-start(bf16[1024,128]{1,0:T(8,128)(2,1)} %get-tuple-element.33), channel_id=1, source_target_pairs={{0,192},{64,0},{128,64},{192,128},{256,448},{320,256},{384,320},{4... | collective-permute-start | bytes 786440 | tf_op jit(solution)/shard_map/ppermute | solution.py:318
  65.0 23.0 %collective-permute-start.6 = (bf16[2048,128]{1,0:T(8,128)(2,1)}, bf16[2048,128]{1,0:T(8,128)(2,1)}, u32[]{:S(2)}, u32[]{:S(2)}) collective-permute-start(bf16[2048,128]{1,0:T(8,128)(2,1)} %swap.1), channel_id=1, source_target_pairs={{0,256},{64,320},{128,384},{192,448},{256,0},{320,64},{384,128},{4... | collective-permute-start | bytes 1572872 | tf_op jit(solution)/shard_map/ppermute | solution.py:322
  73.0 15.1 %copy-start.1 = (bf16[1024,128]{1,0:T(8,128)(2,1)S(1)}, bf16[1024,128]{1,0:T(8,128)(2,1)}, u32[]{:S(2)}) copy-start(bf16[1024,128]{1,0:T(8,128)(2,1)} %get-tuple-element.34.refs_0_) | copy-start | bytes 786436
  76.9 15.6 %collective-permute-start.7 = (bf16[1088,256]{1,0:T(8,128)(2,1)S(1)}, bf16[1088,256]{1,0:T(8,128)(2,1)S(1)}, u32[]{:S(2)}, u32[]{:S(2)}) collective-permute-start(bf16[1088,256]{1,0:T(8,128)(2,1)S(1)} %get-tuple-element.44), channel_id=1, source_target_pairs={{0,128},{64,192},{128,0},{192,64},{256,384},{320,448},{384,256},{4... | collective-permute-start | bytes 1671176 | tf_op jit(solution)/shard_map/ppermute | solution.py:318
  81.3 25.5 %collective-permute-start.8 = (bf16[1088,256]{1,0:T(8,128)(2,1)S(1)}, bf16[1088,256]{1,0:T(8,128)(2,1)S(1)}, u32[]{:S(2)}, u32[]{:S(2)}) collective-permute-start(bf16[1088,256]{1,0:T(8,128)(2,1)S(1)} %get-tuple-element.45), channel_id=1, source_target_pairs={{0,192},{64,0},{128,64},{192,128},{256,448},{320,256},{384,320},{4... | collective-permute-start | bytes 1671176 | tf_op jit(solution)/shard_map/ppermute | solution.py:318
  86.0 3.6 %copy-start = (bf16[1792,128]{1,0:T(8,128)(2,1)S(1)}, bf16[1792,128]{1,0:T(8,128)(2,1)}, u32[]{:S(2)}) copy-start(bf16[1792,128]{1,0:T(8,128)(2,1)} %get-tuple-element.40.refs_0_) | copy-start | bytes 1376260
  86.0 20.8 %collective-permute-start.9 = (bf16[1088,256]{1,0:T(8,128)(2,1)S(1)}, bf16[1088,256]{1,0:T(8,128)(2,1)S(1)}, u32[]{:S(2)}, u32[]{:S(2)}) collective-permute-start(bf16[1088,256]{1,0:T(8,128)(2,1)S(1)} %get-tuple-element.46), channel_id=1, source_target_pairs={{0,64},{64,128},{128,192},{192,0},{256,320},{320,384},{384,448},{4... | collective-permute-start | bytes 1671176 | tf_op jit(solution)/shard_map/ppermute | solution.py:318
  107.1 12.9 %collective-permute-start.13 = (bf16[1088,128]{1,0:T(8,128)(2,1)S(1)}, bf16[1088,128]{1,0:T(8,128)(2,1)S(1)}, u32[]{:S(2)}, u32[]{:S(2)}) collective-permute-start(bf16[1088,128]{1,0:T(8,128)(2,1)S(1)} %activate.1.refs_0_), channel_id=1, source_target_pairs={{0,256},{64,320},{128,384},{192,448},{256,0},{320,64},{384,128},{4... | collective-permute-start | bytes 835592 | tf_op jit(solution)/shard_map/ppermute | solution.py:322
  109.3 20.0 %collective-permute-start.10 = (bf16[1088,128]{1,0:T(8,128)(2,1)S(1)}, bf16[1088,128]{1,0:T(8,128)(2,1)S(1)}, u32[]{:S(2)}, u32[]{:S(2)}) collective-permute-start(bf16[1088,128]{1,0:T(8,128)(2,1)S(1)} %activate.1.refs_0_), channel_id=1, source_target_pairs={{0,64},{64,128},{128,192},{192,0},{256,320},{320,384},{384,448},{4... | collective-permute-start | bytes 835592 | tf_op jit(solution)/shard_map/ppermute | solution.py:318
  113.9 18.0 %collective-permute-start.11 = (bf16[1088,128]{1,0:T(8,128)(2,1)S(1)}, bf16[1088,128]{1,0:T(8,128)(2,1)S(1)}, u32[]{:S(2)}, u32[]{:S(2)}) collective-permute-start(bf16[1088,128]{1,0:T(8,128)(2,1)S(1)} %activate.1.refs_0_), channel_id=1, source_target_pairs={{0,128},{64,192},{128,0},{192,64},{256,384},{320,448},{384,256},{4... | collective-permute-start | bytes 835592 | tf_op jit(solution)/shard_map/ppermute | solution.py:318
  117.5 14.4 %collective-permute-start.12 = (bf16[1088,128]{1,0:T(8,128)(2,1)S(1)}, bf16[1088,128]{1,0:T(8,128)(2,1)S(1)}, u32[]{:S(2)}, u32[]{:S(2)}) collective-permute-start(bf16[1088,128]{1,0:T(8,128)(2,1)S(1)} %activate.1.refs_0_), channel_id=1, source_target_pairs={{0,192},{64,0},{128,64},{192,128},{256,448},{320,256},{384,320},{4... | collective-permute-start | bytes 835592 | tf_op jit(solution)/shard_map/ppermute | solution.py:318
  120.1 11.8 %collective-permute-start.14 = (bf16[1088,128]{1,0:T(8,128)(2,1)S(1)}, bf16[1088,128]{1,0:T(8,128)(2,1)S(1)}, u32[]{:S(2)}, u32[]{:S(2)}) collective-permute-start(bf16[1088,128]{1,0:T(8,128)(2,1)S(1)} %collective-permute-done.13.refs_4_), channel_id=1, source_target_pairs={{0,64},{64,128},{128,192},{192,0},{256,320},{320,384},{384,448},{4... | collective-permute-start | bytes 835592 | tf_op jit(solution)/shard_map/ppermute | solution.py:318
  125.6 8.8 %collective-permute-start.15 = (bf16[1088,128]{1,0:T(8,128)(2,1)S(1)}, bf16[1088,128]{1,0:T(8,128)(2,1)S(1)}, u32[]{:S(2)}, u32[]{:S(2)}) collective-permute-start(bf16[1088,128]{1,0:T(8,128)(2,1)S(1)} %collective-permute-done.13.refs_4_), channel_id=1, source_target_pairs={{0,128},{64,192},{128,0},{192,64},{256,384},{320,448},{384,256},{4... | collective-permute-start | bytes 835592 | tf_op jit(solution)/shard_map/ppermute | solution.py:318
  129.3 7.6 %collective-permute-start.16 = (bf16[1088,128]{1,0:T(8,128)(2,1)S(1)}, bf16[1088,128]{1,0:T(8,128)(2,1)S(1)}, u32[]{:S(2)}, u32[]{:S(2)}) collective-permute-start(bf16[1088,128]{1,0:T(8,128)(2,1)S(1)} %collective-permute-done.13.refs_4_), channel_id=1, source_target_pairs={{0,192},{64,0},{128,64},{192,128},{256,448},{320,256},{384,320},{4... | collective-permute-start | bytes 835592 | tf_op jit(solution)/shard_map/ppermute | solution.py:318
  138.4 49.5 %copy-start.2 = (s32[128,8]{0,1:T(8,128)S(1)}, s32[128,8]{0,1:T(8,128)}, u32[]{:S(2)}) copy-start(s32[128,8]{0,1:T(8,128)} %param.7) | copy-start | bytes 12292
  138.4 49.5 %copy-start.3 = (f32[128,8]{0,1:T(8,128)S(1)}, f32[128,8]{0,1:T(8,128)}, u32[]{:S(2)}) copy-start(f32[128,8]{0,1:T(8,128)} %param.8) | copy-start | bytes 12292

commit v11 on v10

--- a/solution.py
+++ b/solution.py
@@ -9,6 +9,7 @@
 F32 = jnp.float32
 LANES = 128
 X = 4
+ORDER = (1, 3, 2)
 PARTS = 4
 HOLD = 50_000_000_000
 FULL = 60 * 1024 * 1024
@@ -239,7 +240,7 @@
 def down_kernel(x_ref, weight_ref, *refs):
     hiddens, out_ref = refs[:-1], refs[-1]
     experts = out_ref.shape[0]
-    hidden = jnp.concatenate([ref[...] for ref in hiddens], axis=1)
+    hidden = jnp.concatenate([hiddens[i][...] for i in (0, 3, 2, 1, 4, 7, 6, 5)], axis=1)
     weight = weight_ref[...]
     count = experts * 16
     main = jnp.dot(hidden[:count], weight, preferred_element_type=F32)
@@ -332,19 +333,19 @@
     buffer = dispatch(x, ids, tokens, groups)
     chunks = lax.all_to_all(buffer, "expert", split_axis=0, concat_axis=0, tiled=True)
     both, downs = pack(x, w_gate, w_up, w_down)
-    both = [both[0]] + [shift(both[d], d) for d in range(1, X)]
-    downs = [downs[0]] + [shift(downs[d], d) for d in range(1, X)]
+    both = [both[0]] + [shift(both[d], d) for d in ORDER]
+    downs = [downs[0]] + [shift(downs[d], d) for d in ORDER]
     held = lax.optimization_barrier((*both, *downs))
     both, downs = held[:X], held[X:]
     other = cross(swap(z, downs))
-    parts = project(chunks, [both[d] for d in (2, 1, 3)], BF, "project_sent")
-    arrived = [shift(part, -d) for d, part in zip((2, 1, 3), parts)]
+    parts = project(chunks, both[1:], BF, "project_sent")
+    arrived = [shift(part, -d) for d, part in zip(ORDER, parts)]
     chunks, weight = lax.optimization_barrier((chunks, assemble(z, downs, other)))
     (mine,) = project(chunks, both[:1], F32, "project_own")
     hidden = activate(mine, arrived)
     swapped = cross(hidden)
-    hiddens = [hidden] + [shift(hidden, d) for d in range(1, X)]
-    hiddens += [swapped] + [shift(swapped, d) for d in range(1, X)]
+    hiddens = [hidden] + [shift(hidden, d) for d in ORDER[::-1]]
+    hiddens += [swapped] + [shift(swapped, d) for d in ORDER[::-1]]
     output = down(x, weight, hiddens, groups)
     returned = lax.all_to_all(output, "expert", split_axis=0, concat_axis=0, tiled=True)
     return combine(x, ids, scale, returned, tokens.shape[1] // (2 * X))

time: 191 us -> 186 us (0.974)
  starting transfers between devices: 77.5 us -> 73.8 us
  blocking collectives: 49.5 us -> 46.3 us
    ppermute x15, starting transfers between devices: 52.8 us -> 48.4 us  [shift(): return lax.ppermute(value, 'pipe', pairs)]
    all_to_all x1, blocking collectives: 49.5 us -> 46.3 us  [body(): lax.all_to_all(output, 'expert', split_axis=0, concat_axis=0, tiled=True)]
  transfers between devices with their start and end apart: 18 -> 18, of which waited for: 6 -> 10; matrix products, arithmetic and copies ran while one was open for 0% -> 0% of each run, Pallas kernels for 6% -> 6%
where the time goes in v11:
time: 186 us; the launch traced here: 185 us
  starting transfers between devices  73.8 us (40%)
  blocking collectives  46.3 us (25%)
  waiting for transfers between devices  45.1 us (24%)
  Pallas kernels  18.9 us (10%)
    ppermute x15, starting transfers between devices, shift(): return lax.ppermute(value, 'pipe', pairs)  48.4 us
    all_to_all x1, blocking collectives, body(): lax.all_to_all(output, 'expert', split_axis=0, concat_axis=0, tiled=True)  46.3 us
    ppermute x15, waiting for transfers between devices, shift(): return lax.ppermute(value, 'pipe', pairs)  44.8 us
    all_to_all x1, starting transfers between devices, body(): lax.all_to_all(buffer, 'expert', split_axis=0, concat_axis=0, tiled=True)  14.6 us
    ppermute x2, starting transfers between devices, cross(): lax.ppermute(value, 'pipe', [(p, (p + X) % (2 * X)) for p in range(2 * X)])  10.7 us
    pallas_call x2, Pallas kernels, project(): return call(kernel, name, shapes, specs, scratch=scratch)(chunks, *packs)  5.08 us
  transfers between devices with their start and end apart: 18, of which 10 were waited for; matrix products, arithmetic and copies ran while one was open for 0% of the time, Pallas kernels for 6%

profile of v11, /device:TPU:1, one launch (start us, length us, event | category | flops | bytes accessed | tf_op | source)
XLA Modules:
  0.0 185.0 jit_solution(10626671481800970275)
XLA Ops:
  0.0 3.5 %dispatch.1 = bf16[64,120,128]{2,1,0:T(8,128)(2,1)} custom-call(s32[1]{0:T(128)} %bitcast.x_ref, s32[8,128]{1,0:T(8,128)} %bitcast.7, bf16[128,3584]{1,0:T(8,128)(2,1)} %tok_ref.1), custom_call_target="tpu_custom_call" | custom-call | tf_op jit(solution)/shard_map/dispatch/pallas_call | solution.py:108
  3.5 14.6 %all-to-all-start = ((bf16[64,120,128]{2,1,0:T(8,128)(2,1)}), bf16[64,120,128]{2,1,0:T(8,128)(2,1)S(1)}, u32[]{:S(2)}, u32[]{:S(2)}) async-start(bf16[64,120,128]{2,1,0:T(8,128)(2,1)} %dispatch.1), calls=%async_computation | async-start | bytes 3932160 | tf_op jit(solution)/shard_map/all_to_all | solution.py:334
  18.2 3.4 %pack.1 = (bf16[1792,128]{1,0:T(8,128)(2,1)}, bf16[1792,128]{1,0:T(8,128)(2,1)}, bf16[1792,128]{1,0:T(8,128)(2,1)}, bf16[1792,128]{1,0:T(8,128)(2,1)}, bf16[1024...) custom-call(s32[1]{0:T(128)} %bitcast.x_ref, ...), custom_call_target="tpu_custom_call" | custom-call | tf_op jit(solution)/shard_map/pack/pallas_call | solution.py:145
  21.6 3.1 %collective-permute-start.3 = (bf16[1024,128]{1,0:T(8,128)(2,1)}, bf16[1024,128]{1,0:T(8,128)(2,1)}, u32[]{:S(2)}, u32[]{:S(2)}) collective-permute-start(bf16[1024,128]{1,0:T(8,128)(2,1)} %get-tuple-element.31), channel_id=1, source_target_pairs={{0,64},{64,128},{128,192},{192,0},{256,320},{320,384},{384,448},{4... | collective-permute-start | bytes 786440 | tf_op jit(solution)/shard_map/ppermute | solution.py:319
  24.7 3.1 %collective-permute-start = (bf16[1792,128]{1,0:T(8,128)(2,1)}, bf16[1792,128]{1,0:T(8,128)(2,1)S(1)}, u32[]{:S(2)}, u32[]{:S(2)}) collective-permute-start(bf16[1792,128]{1,0:T(8,128)(2,1)} %get-tuple-element.27), channel_id=1, source_target_pairs={{0,64},{64,128},{128,192},{192,0},{256,320},{320,384},{384,448},{4... | collective-permute-start | bytes 1376264 | tf_op jit(solution)/shard_map/ppermute | solution.py:319
  27.8 3.4 %collective-permute-start.1 = (bf16[1792,128]{1,0:T(8,128)(2,1)}, bf16[1792,128]{1,0:T(8,128)(2,1)S(1)}, u32[]{:S(2)}, u32[]{:S(2)}) collective-permute-start(bf16[1792,128]{1,0:T(8,128)(2,1)} %get-tuple-element.28), channel_id=1, source_target_pairs={{0,192},{64,0},{128,64},{192,128},{256,448},{320,256},{384,320},{4... | collective-permute-start | bytes 1376264 | tf_op jit(solution)/shard_map/ppermute | solution.py:319
  31.2 3.1 %collective-permute-start.2 = (bf16[1792,128]{1,0:T(8,128)(2,1)}, bf16[1792,128]{1,0:T(8,128)(2,1)S(1)}, u32[]{:S(2)}, u32[]{:S(2)}) collective-permute-start(bf16[1792,128]{1,0:T(8,128)(2,1)} %get-tuple-element.29), channel_id=1, source_target_pairs={{0,128},{64,192},{128,0},{192,64},{256,384},{320,448},{384,256},{4... | collective-permute-start | bytes 1376264 | tf_op jit(solution)/shard_map/ppermute | solution.py:319
  34.3 3.1 %collective-permute-start.4 = (bf16[1024,128]{1,0:T(8,128)(2,1)}, bf16[1024,128]{1,0:T(8,128)(2,1)}, u32[]{:S(2)}, u32[]{:S(2)}) collective-permute-start(bf16[1024,128]{1,0:T(8,128)(2,1)} %get-tuple-element.32), channel_id=1, source_target_pairs={{0,192},{64,0},{128,64},{192,128},{256,448},{320,256},{384,320},{4... | collective-permute-start | bytes 786440 | tf_op jit(solution)/shard_map/ppermute | solution.py:319
  37.4 2.5 %collective-permute-start.5 = (bf16[1024,128]{1,0:T(8,128)(2,1)}, bf16[1024,128]{1,0:T(8,128)(2,1)}, u32[]{:S(2)}, u32[]{:S(2)}) collective-permute-start(bf16[1024,128]{1,0:T(8,128)(2,1)} %get-tuple-element.33), channel_id=1, source_target_pairs={{0,128},{64,192},{128,0},{192,64},{256,384},{320,448},{384,256},{4... | collective-permute-start | bytes 786440 | tf_op jit(solution)/shard_map/ppermute | solution.py:319
  39.9 16.6 %collective-permute-done.4.refs_2_ = bf16[1024,128]{1,0:T(8,128)(2,1)} collective-permute-done((bf16[1024,128]{1,0:T(8,128)(2,1)}, bf16[1024,128]{1,0:T(8,128)(2,1)}, u32[]{:S(2)}, u32[]{:S(2)}) %collective-permute-start.4) | collective-permute-done | bytes 262176 | tf_op jit(solution)/shard_map/ppermute | solution.py:319
  60.6 7.9 %collective-permute-start.6 = (bf16[2048,128]{1,0:T(8,128)(2,1)}, bf16[2048,128]{1,0:T(8,128)(2,1)}, u32[]{:S(2)}, u32[]{:S(2)}) collective-permute-start(bf16[2048,128]{1,0:T(8,128)(2,1)} %swap.1), channel_id=1, source_target_pairs={{0,256},{64,320},{128,384},{192,448},{256,0},{320,64},{384,128},{4... | collective-permute-start | bytes 1572872 | tf_op jit(solution)/shard_map/ppermute | solution.py:323
  68.6 3.9 %project_sent.1 = (bf16[1088,256]{1,0:T(8,128)(2,1)S(1)}, bf16[1088,256]{1,0:T(8,128)(2,1)S(1)}, bf16[1088,256]{1,0:T(8,128)(2,1)S(1)}) custom-call(bf16[64,120,128]{2,1,0:T(8,128)(2,1)S(1)} %all-to-all-done.chunks_ref, bf16[1792,128]{1,0:T(8,128)(2,1)S(1)} %collective-permute-done.refs_0_, bf16[1792,128]{1,0:T(8,128)(2,1)S(1)} %collective-permute-done.1.refs_1_, ...), custom_call_target="tpu_custom_call" | custom-call | tf_op jit(solution)/shard_map/project_sent/pallas_call | solution.py:223
  72.5 7.8 %collective-permute-start.7 = (bf16[1088,256]{1,0:T(8,128)(2,1)S(1)}, bf16[1088,256]{1,0:T(8,128)(2,1)S(1)}, u32[]{:S(2)}, u32[]{:S(2)}) collective-permute-start(bf16[1088,256]{1,0:T(8,128)(2,1)S(1)} %get-tuple-element.44), channel_id=1, source_target_pairs={{0,192},{64,0},{128,64},{192,128},{256,448},{320,256},{384,320},{4... | collective-permute-start | bytes 1671176 | tf_op jit(solution)/shard_map/ppermute | solution.py:319
  82.2 3.2 %collective-permute-start.9 = (bf16[1088,256]{1,0:T(8,128)(2,1)S(1)}, bf16[1088,256]{1,0:T(8,128)(2,1)S(1)}, u32[]{:S(2)}, u32[]{:S(2)}) collective-permute-start(bf16[1088,256]{1,0:T(8,128)(2,1)S(1)} %get-tuple-element.46), channel_id=1, source_target_pairs={{0,128},{64,192},{128,0},{192,64},{256,384},{320,448},{384,256},{4... | collective-permute-start | bytes 1671176 | tf_op jit(solution)/shard_map/ppermute | solution.py:319
  88.2 2.5 %collective-permute-done.7.refs_0_ = bf16[1088,256]{1,0:T(8,128)(2,1)S(1)} collective-permute-done((bf16[1088,256]{1,0:T(8,128)(2,1)S(1)}, bf16[1088,256]{1,0:T(8,128)(2,1)S(1)}, u32[]{:S(2)}, u32[]{:S(2)}) %collective-permute-start.7) | collective-permute-done | bytes 557088 | tf_op jit(solution)/shard_map/ppermute | solution.py:319
  90.7 5.3 %collective-permute-done.8.refs_1_ = bf16[1088,256]{1,0:T(8,128)(2,1)S(1)} collective-permute-done((bf16[1088,256]{1,0:T(8,128)(2,1)S(1)}, bf16[1088,256]{1,0:T(8,128)(2,1)S(1)}, u32[]{:S(2)}, u32[]{:S(2)}) %collective-permute-start.8) | collective-permute-done | bytes 557088 | tf_op jit(solution)/shard_map/ppermute | solution.py:319
  96.0 9.6 %collective-permute-done.9.refs_2_ = bf16[1088,256]{1,0:T(8,128)(2,1)S(1)} collective-permute-done((bf16[1088,256]{1,0:T(8,128)(2,1)S(1)}, bf16[1088,256]{1,0:T(8,128)(2,1)S(1)}, u32[]{:S(2)}, u32[]{:S(2)}) %collective-permute-start.9) | collective-permute-done | bytes 557088 | tf_op jit(solution)/shard_map/ppermute | solution.py:319
  105.9 2.8 %collective-permute-start.13 = (bf16[1088,128]{1,0:T(8,128)(2,1)S(1)}, bf16[1088,128]{1,0:T(8,128)(2,1)S(1)}, u32[]{:S(2)}, u32[]{:S(2)}) collective-permute-start(bf16[1088,128]{1,0:T(8,128)(2,1)S(1)} %activate.1.refs_0_), channel_id=1, source_target_pairs={{0,256},{64,320},{128,384},{192,448},{256,0},{320,64},{384,128},{4... | collective-permute-start | bytes 835592 | tf_op jit(solution)/shard_map/ppermute | solution.py:323
  108.7 3.1 %collective-permute-start.10 = (bf16[1088,128]{1,0:T(8,128)(2,1)S(1)}, bf16[1088,128]{1,0:T(8,128)(2,1)S(1)}, u32[]{:S(2)}, u32[]{:S(2)}) collective-permute-start(bf16[1088,128]{1,0:T(8,128)(2,1)S(1)} %activate.1.refs_0_), channel_id=1, source_target_pairs={{0,128},{64,192},{128,0},{192,64},{256,384},{320,448},{384,256},{4... | collective-permute-start | bytes 835592 | tf_op jit(solution)/shard_map/ppermute | solution.py:319
  113.8 3.4 %collective-permute-start.12 = (bf16[1088,128]{1,0:T(8,128)(2,1)S(1)}, bf16[1088,128]{1,0:T(8,128)(2,1)S(1)}, u32[]{:S(2)}, u32[]{:S(2)}) collective-permute-start(bf16[1088,128]{1,0:T(8,128)(2,1)S(1)} %activate.1.refs_0_), channel_id=1, source_target_pairs={{0,64},{64,128},{128,192},{192,0},{256,320},{320,384},{384,448},{4... | collective-permute-start | bytes 835592 | tf_op jit(solution)/shard_map/ppermute | solution.py:319
  117.4 3.5 %collective-permute-start.14 = (bf16[1088,128]{1,0:T(8,128)(2,1)S(1)}, bf16[1088,128]{1,0:T(8,128)(2,1)S(1)}, u32[]{:S(2)}, u32[]{:S(2)}) collective-permute-start(bf16[1088,128]{1,0:T(8,128)(2,1)S(1)} %collective-permute-done.13.refs_4_), channel_id=1, source_target_pairs={{0,128},{64,192},{128,0},{192,64},{256,384},{320,448},{384,256},{4... | collective-permute-start | bytes 835592 | tf_op jit(solution)/shard_map/ppermute | solution.py:319
  123.4 2.8 %collective-permute-start.16 = (bf16[1088,128]{1,0:T(8,128)(2,1)S(1)}, bf16[1088,128]{1,0:T(8,128)(2,1)S(1)}, u32[]{:S(2)}, u32[]{:S(2)}) collective-permute-start(bf16[1088,128]{1,0:T(8,128)(2,1)S(1)} %collective-permute-done.13.refs_4_), channel_id=1, source_target_pairs={{0,64},{64,128},{128,192},{192,0},{256,320},{320,384},{384,448},{4... | collective-permute-start | bytes 835592 | tf_op jit(solution)/shard_map/ppermute | solution.py:319
  127.4 3.7 %collective-permute-done.14.refs_5_ = bf16[1088,128]{1,0:T(8,128)(2,1)S(1)} collective-permute-done((bf16[1088,128]{1,0:T(8,128)(2,1)S(1)}, bf16[1088,128]{1,0:T(8,128)(2,1)S(1)}, u32[]{:S(2)}, u32[]{:S(2)}) %collective-permute-start.14) | collective-permute-done | bytes 278560 | tf_op jit(solution)/shard_map/ppermute | solution.py:319
  136.4 46.3 %all_to_all.10.chunks_ref = bf16[64,64,128]{2,1,0:T(8,128)(2,1)S(1)} all-to-all(bf16[64,64,128]{2,1,0:T(8,128)(2,1)S(1)} %down.1), channel_id=1, replica_groups=mesh['pipe'=8,'expert'=64] {'expert'}, dimensions={0} | all-to-all | bytes 2097152 | tf_op jit(solution)/shard_map/all_to_all | solution.py:350
  (31 shorter events, 22.5 us)
Async XLA Ops:
  3.5 65.0 %all-to-all-start = ((bf16[64,120,128]{2,1,0:T(8,128)(2,1)}), bf16[64,120,128]{2,1,0:T(8,128)(2,1)S(1)}, u32[]{:S(2)}, u32[]{:S(2)}) async-start(bf16[64,120,128]{2,1,0:T(8,128)(2,1)} %dispatch.1), calls=%async_computation | async-start | bytes 3932160 | tf_op jit(solution)/shard_map/all_to_all | solution.py:334
  21.6 15.9 %collective-permute-start.3 = (bf16[1024,128]{1,0:T(8,128)(2,1)}, bf16[1024,128]{1,0:T(8,128)(2,1)}, u32[]{:S(2)}, u32[]{:S(2)}) collective-permute-start(bf16[1024,128]{1,0:T(8,128)(2,1)} %get-tuple-element.31), channel_id=1, source_target_pairs={{0,64},{64,128},{128,192},{192,0},{256,320},{320,384},{384,448},{4... | collective-permute-start | bytes 786440 | tf_op jit(solution)/shard_map/ppermute | solution.py:319
  24.7 34.0 %collective-permute-start = (bf16[1792,128]{1,0:T(8,128)(2,1)}, bf16[1792,128]{1,0:T(8,128)(2,1)S(1)}, u32[]{:S(2)}, u32[]{:S(2)}) collective-permute-start(bf16[1792,128]{1,0:T(8,128)(2,1)} %get-tuple-element.27), channel_id=1, source_target_pairs={{0,64},{64,128},{128,192},{192,0},{256,320},{320,384},{384,448},{4... | collective-permute-start | bytes 1376264 | tf_op jit(solution)/shard_map/ppermute | solution.py:319
  27.8 30.9 %collective-permute-start.1 = (bf16[1792,128]{1,0:T(8,128)(2,1)}, bf16[1792,128]{1,0:T(8,128)(2,1)S(1)}, u32[]{:S(2)}, u32[]{:S(2)}) collective-permute-start(bf16[1792,128]{1,0:T(8,128)(2,1)} %get-tuple-element.28), channel_id=1, source_target_pairs={{0,192},{64,0},{128,64},{192,128},{256,448},{320,256},{384,320},{4... | collective-permute-start | bytes 1376264 | tf_op jit(solution)/shard_map/ppermute | solution.py:319
  31.2 27.5 %collective-permute-start.2 = (bf16[1792,128]{1,0:T(8,128)(2,1)}, bf16[1792,128]{1,0:T(8,128)(2,1)S(1)}, u32[]{:S(2)}, u32[]{:S(2)}) collective-permute-start(bf16[1792,128]{1,0:T(8,128)(2,1)} %get-tuple-element.29), channel_id=1, source_target_pairs={{0,128},{64,192},{128,0},{192,64},{256,384},{320,448},{384,256},{4... | collective-permute-start | bytes 1376264 | tf_op jit(solution)/shard_map/ppermute | solution.py:319
  34.3 22.2 %collective-permute-start.4 = (bf16[1024,128]{1,0:T(8,128)(2,1)}, bf16[1024,128]{1,0:T(8,128)(2,1)}, u32[]{:S(2)}, u32[]{:S(2)}) collective-permute-start(bf16[1024,128]{1,0:T(8,128)(2,1)} %get-tuple-element.32), channel_id=1, source_target_pairs={{0,192},{64,0},{128,64},{192,128},{256,448},{320,256},{384,320},{4... | collective-permute-start | bytes 786440 | tf_op jit(solution)/shard_map/ppermute | solution.py:319
  37.4 21.2 %collective-permute-start.5 = (bf16[1024,128]{1,0:T(8,128)(2,1)}, bf16[1024,128]{1,0:T(8,128)(2,1)}, u32[]{:S(2)}, u32[]{:S(2)}) collective-permute-start(bf16[1024,128]{1,0:T(8,128)(2,1)} %get-tuple-element.33), channel_id=1, source_target_pairs={{0,128},{64,192},{128,0},{192,64},{256,384},{320,448},{384,256},{4... | collective-permute-start | bytes 786440 | tf_op jit(solution)/shard_map/ppermute | solution.py:319
  60.6 24.8 %collective-permute-start.6 = (bf16[2048,128]{1,0:T(8,128)(2,1)}, bf16[2048,128]{1,0:T(8,128)(2,1)}, u32[]{:S(2)}, u32[]{:S(2)}) collective-permute-start(bf16[2048,128]{1,0:T(8,128)(2,1)} %swap.1), channel_id=1, source_target_pairs={{0,256},{64,320},{128,384},{192,448},{256,0},{320,64},{384,128},{4... | collective-permute-start | bytes 1572872 | tf_op jit(solution)/shard_map/ppermute | solution.py:323
  68.6 16.9 %copy-start.1 = (bf16[1024,128]{1,0:T(8,128)(2,1)S(1)}, bf16[1024,128]{1,0:T(8,128)(2,1)}, u32[]{:S(2)}) copy-start(bf16[1024,128]{1,0:T(8,128)(2,1)} %get-tuple-element.34.refs_0_) | copy-start | bytes 786436
  72.5 18.2 %collective-permute-start.7 = (bf16[1088,256]{1,0:T(8,128)(2,1)S(1)}, bf16[1088,256]{1,0:T(8,128)(2,1)S(1)}, u32[]{:S(2)}, u32[]{:S(2)}) collective-permute-start(bf16[1088,256]{1,0:T(8,128)(2,1)S(1)} %get-tuple-element.44), channel_id=1, source_target_pairs={{0,192},{64,0},{128,64},{192,128},{256,448},{320,256},{384,320},{4... | collective-permute-start | bytes 1671176 | tf_op jit(solution)/shard_map/ppermute | solution.py:319
  80.3 15.7 %collective-permute-start.8 = (bf16[1088,256]{1,0:T(8,128)(2,1)S(1)}, bf16[1088,256]{1,0:T(8,128)(2,1)S(1)}, u32[]{:S(2)}, u32[]{:S(2)}) collective-permute-start(bf16[1088,256]{1,0:T(8,128)(2,1)S(1)} %get-tuple-element.45), channel_id=1, source_target_pairs={{0,64},{64,128},{128,192},{192,0},{256,320},{320,384},{384,448},{4... | collective-permute-start | bytes 1671176 | tf_op jit(solution)/shard_map/ppermute | solution.py:319
  82.2 4.7 %copy-start = (bf16[1792,128]{1,0:T(8,128)(2,1)S(1)}, bf16[1792,128]{1,0:T(8,128)(2,1)}, u32[]{:S(2)}) copy-start(bf16[1792,128]{1,0:T(8,128)(2,1)} %get-tuple-element.40.refs_0_) | copy-start | bytes 1376260
  82.2 23.4 %collective-permute-start.9 = (bf16[1088,256]{1,0:T(8,128)(2,1)S(1)}, bf16[1088,256]{1,0:T(8,128)(2,1)S(1)}, u32[]{:S(2)}, u32[]{:S(2)}) collective-permute-start(bf16[1088,256]{1,0:T(8,128)(2,1)S(1)} %get-tuple-element.46), channel_id=1, source_target_pairs={{0,128},{64,192},{128,0},{192,64},{256,384},{320,448},{384,256},{4... | collective-permute-start | bytes 1671176 | tf_op jit(solution)/shard_map/ppermute | solution.py:319
  105.9 11.4 %collective-permute-start.13 = (bf16[1088,128]{1,0:T(8,128)(2,1)S(1)}, bf16[1088,128]{1,0:T(8,128)(2,1)S(1)}, u32[]{:S(2)}, u32[]{:S(2)}) collective-permute-start(bf16[1088,128]{1,0:T(8,128)(2,1)S(1)} %activate.1.refs_0_), channel_id=1, source_target_pairs={{0,256},{64,320},{128,384},{192,448},{256,0},{320,64},{384,128},{4... | collective-permute-start | bytes 835592 | tf_op jit(solution)/shard_map/ppermute | solution.py:323
  108.7 14.7 %collective-permute-start.10 = (bf16[1088,128]{1,0:T(8,128)(2,1)S(1)}, bf16[1088,128]{1,0:T(8,128)(2,1)S(1)}, u32[]{:S(2)}, u32[]{:S(2)}) collective-permute-start(bf16[1088,128]{1,0:T(8,128)(2,1)S(1)} %activate.1.refs_0_), channel_id=1, source_target_pairs={{0,128},{64,192},{128,0},{192,64},{256,384},{320,448},{384,256},{4... | collective-permute-start | bytes 835592 | tf_op jit(solution)/shard_map/ppermute | solution.py:319
  111.8 14.4 %collective-permute-start.11 = (bf16[1088,128]{1,0:T(8,128)(2,1)S(1)}, bf16[1088,128]{1,0:T(8,128)(2,1)S(1)}, u32[]{:S(2)}, u32[]{:S(2)}) collective-permute-start(bf16[1088,128]{1,0:T(8,128)(2,1)S(1)} %activate.1.refs_0_), channel_id=1, source_target_pairs={{0,192},{64,0},{128,64},{192,128},{256,448},{320,256},{384,320},{4... | collective-permute-start | bytes 835592 | tf_op jit(solution)/shard_map/ppermute | solution.py:319
  113.8 13.7 %collective-permute-start.12 = (bf16[1088,128]{1,0:T(8,128)(2,1)S(1)}, bf16[1088,128]{1,0:T(8,128)(2,1)S(1)}, u32[]{:S(2)}, u32[]{:S(2)}) collective-permute-start(bf16[1088,128]{1,0:T(8,128)(2,1)S(1)} %activate.1.refs_0_), channel_id=1, source_target_pairs={{0,64},{64,128},{128,192},{192,0},{256,320},{320,384},{384,448},{4... | collective-permute-start | bytes 835592 | tf_op jit(solution)/shard_map/ppermute | solution.py:319
  117.4 13.8 %collective-permute-start.14 = (bf16[1088,128]{1,0:T(8,128)(2,1)S(1)}, bf16[1088,128]{1,0:T(8,128)(2,1)S(1)}, u32[]{:S(2)}, u32[]{:S(2)}) collective-permute-start(bf16[1088,128]{1,0:T(8,128)(2,1)S(1)} %collective-permute-done.13.refs_4_), channel_id=1, source_target_pairs={{0,128},{64,192},{128,0},{192,64},{256,384},{320,448},{384,256},{4... | collective-permute-start | bytes 835592 | tf_op jit(solution)/shard_map/ppermute | solution.py:319
  120.9 11.9 %collective-permute-start.15 = (bf16[1088,128]{1,0:T(8,128)(2,1)S(1)}, bf16[1088,128]{1,0:T(8,128)(2,1)S(1)}, u32[]{:S(2)}, u32[]{:S(2)}) collective-permute-start(bf16[1088,128]{1,0:T(8,128)(2,1)S(1)} %collective-permute-done.13.refs_4_), channel_id=1, source_target_pairs={{0,192},{64,0},{128,64},{192,128},{256,448},{320,256},{384,320},{4... | collective-permute-start | bytes 835592 | tf_op jit(solution)/shard_map/ppermute | solution.py:319
  123.4 11.5 %collective-permute-start.16 = (bf16[1088,128]{1,0:T(8,128)(2,1)S(1)}, bf16[1088,128]{1,0:T(8,128)(2,1)S(1)}, u32[]{:S(2)}, u32[]{:S(2)}) collective-permute-start(bf16[1088,128]{1,0:T(8,128)(2,1)S(1)} %collective-permute-done.13.refs_4_), channel_id=1, source_target_pairs={{0,64},{64,128},{128,192},{192,0},{256,320},{320,384},{384,448},{4... | collective-permute-start | bytes 835592 | tf_op jit(solution)/shard_map/ppermute | solution.py:319
  136.4 46.3 %copy-start.2 = (s32[128,8]{0,1:T(8,128)S(1)}, s32[128,8]{0,1:T(8,128)}, u32[]{:S(2)}) copy-start(s32[128,8]{0,1:T(8,128)} %param.7) | copy-start | bytes 12292
  136.4 46.3 %copy-start.3 = (f32[128,8]{0,1:T(8,128)S(1)}, f32[128,8]{0,1:T(8,128)}, u32[]{:S(2)}) copy-start(f32[128,8]{0,1:T(8,128)} %param.8) | copy-start | bytes 12292

commit v12 on v11

--- a/solution.py
+++ b/solution.py
@@ -200,27 +200,15 @@
     quarter = depth // 16 * LANES
 
     def kernel(chunks_ref, *refs):
-        count = len(packs)
-        sent, outs, (weight_ref, sems) = refs[:count], refs[count : 2 * count], refs[2 * count :]
-        copies = []
-        for d in range(count):
-            for half in range(2):
-                rows, cols = pl.ds(half * quarter, quarter), pl.ds(half * LANES, LANES)
-                copy = pltpu.make_async_copy(sent[d].at[rows, :], weight_ref.at[d, :, cols], sems.at[d, half])
-                copy.start()
-                copies.append(copy)
+        sent, outs = refs[: len(packs)], refs[len(packs) :]
         main, last = stacked(chunks_ref)
-        for d in range(count):
-            copies[2 * d].wait()
-            copies[2 * d + 1].wait()
-            weight = weight_ref[d]
-            outs[d][pl.ds(0, sources * 16), :] = jnp.dot(main, weight, preferred_element_type=F32).astype(dtype)
-            outs[d][pl.ds(sources * 16, sources), :] = jnp.dot(last, weight, preferred_element_type=F32).astype(dtype)
+        for pack_ref, out_ref in zip(sent, outs):
+            weight = jnp.concatenate([pack_ref[pl.ds(0, quarter), :], pack_ref[pl.ds(quarter, quarter), :]], axis=1)
+            out_ref[pl.ds(0, sources * 16), :] = jnp.dot(main, weight, preferred_element_type=F32).astype(dtype)
+            out_ref[pl.ds(sources * 16, sources), :] = jnp.dot(last, weight, preferred_element_type=F32).astype(dtype)
 
     shapes = [jax.ShapeDtypeStruct((sources * 17, 2 * LANES), dtype)] * len(packs)
-    scratch = [pltpu.VMEM((len(packs), quarter, 2 * LANES), BF), pltpu.SemaphoreType.DMA((len(packs), 2))]
-    specs = [in_vmem()] + [anywhere()] * len(packs)
-    return call(kernel, name, shapes, specs, scratch=scratch)(chunks, *packs)
+    return call(kernel, name, shapes, [in_vmem()] * (1 + len(packs)))(chunks, *packs)
 
 
 def activate_kernel(own_ref, *refs):

time: 186 us -> 184 us (0.989)
  Pallas kernels: 18.9 us -> 16.9 us
    pallas_call x2, Pallas kernels: 5.08 us -> 3.08 us  [project(): call(kernel, name, shapes, [in_vmem()] * (1 + len(packs)))(chunks, *packs)]
  transfers between devices with their start and end apart: 18 -> 18, of which waited for: 10 -> 10; matrix products, arithmetic and copies ran while one was open for 0% -> 0% of each run, Pallas kernels for 6% -> 5%
where the time goes in v12:
time: 184 us; the launch traced here: 183 us
  starting transfers between devices  73.7 us (40%)
  blocking collectives  46.3 us (25%)
  waiting for transfers between devices  45.3 us (25%)
  Pallas kernels  16.9 us (9%)
    ppermute x15, starting transfers between devices, shift(): return lax.ppermute(value, 'pipe', pairs)  48.4 us
    all_to_all x1, blocking collectives, body(): lax.all_to_all(output, 'expert', split_axis=0, concat_axis=0, tiled=True)  46.3 us
    ppermute x15, waiting for transfers between devices, shift(): return lax.ppermute(value, 'pipe', pairs)  45.1 us
    all_to_all x1, starting transfers between devices, body(): lax.all_to_all(buffer, 'expert', split_axis=0, concat_axis=0, tiled=True)  14.6 us
    ppermute x2, starting transfers between devices, cross(): lax.ppermute(value, 'pipe', [(p, (p + X) % (2 * X)) for p in range(2 * X)])  10.7 us
  transfers between devices with their start and end apart: 18, of which 10 were waited for; matrix products, arithmetic and copies ran while one was open for 0% of the time, Pallas kernels for 5%

profile of v12, /device:TPU:1, one launch (start us, length us, event | category | flops | bytes accessed | tf_op | source)
XLA Modules:
  0.0 183.3 jit_solution(17663319576183298878)
XLA Ops:
  0.0 3.5 %dispatch.1 = bf16[64,120,128]{2,1,0:T(8,128)(2,1)} custom-call(s32[1]{0:T(128)} %bitcast.x_ref, s32[8,128]{1,0:T(8,128)} %bitcast.7, bf16[128,3584]{1,0:T(8,128)(2,1)} %tok_ref.1), custom_call_target="tpu_custom_call" | custom-call | tf_op jit(solution)/shard_map/dispatch/pallas_call | solution.py:108
  3.5 14.6 %all-to-all-start = ((bf16[64,120,128]{2,1,0:T(8,128)(2,1)}), bf16[64,120,128]{2,1,0:T(8,128)(2,1)S(1)}, u32[]{:S(2)}, u32[]{:S(2)}) async-start(bf16[64,120,128]{2,1,0:T(8,128)(2,1)} %dispatch.1), calls=%async_computation | async-start | bytes 3932160 | tf_op jit(solution)/shard_map/all_to_all | solution.py:322
  18.2 3.4 %pack.1 = (bf16[1792,128]{1,0:T(8,128)(2,1)}, bf16[1792,128]{1,0:T(8,128)(2,1)}, bf16[1792,128]{1,0:T(8,128)(2,1)}, bf16[1792,128]{1,0:T(8,128)(2,1)}, bf16[1024...) custom-call(s32[1]{0:T(128)} %bitcast.x_ref, ...), custom_call_target="tpu_custom_call" | custom-call | tf_op jit(solution)/shard_map/pack/pallas_call | solution.py:145
  21.6 3.1 %collective-permute-start.3 = (bf16[1024,128]{1,0:T(8,128)(2,1)}, bf16[1024,128]{1,0:T(8,128)(2,1)}, u32[]{:S(2)}, u32[]{:S(2)}) collective-permute-start(bf16[1024,128]{1,0:T(8,128)(2,1)} %get-tuple-element.31), channel_id=1, source_target_pairs={{0,64},{64,128},{128,192},{192,0},{256,320},{320,384},{384,448},{4... | collective-permute-start | bytes 786440 | tf_op jit(solution)/shard_map/ppermute | solution.py:307
  24.7 3.1 %collective-permute-start = (bf16[1792,128]{1,0:T(8,128)(2,1)}, bf16[1792,128]{1,0:T(8,128)(2,1)S(1)}, u32[]{:S(2)}, u32[]{:S(2)}) collective-permute-start(bf16[1792,128]{1,0:T(8,128)(2,1)} %get-tuple-element.27), channel_id=1, source_target_pairs={{0,64},{64,128},{128,192},{192,0},{256,320},{320,384},{384,448},{4... | collective-permute-start | bytes 1376264 | tf_op jit(solution)/shard_map/ppermute | solution.py:307
  27.8 3.4 %collective-permute-start.1 = (bf16[1792,128]{1,0:T(8,128)(2,1)}, bf16[1792,128]{1,0:T(8,128)(2,1)S(1)}, u32[]{:S(2)}, u32[]{:S(2)}) collective-permute-start(bf16[1792,128]{1,0:T(8,128)(2,1)} %get-tuple-element.28), channel_id=1, source_target_pairs={{0,192},{64,0},{128,64},{192,128},{256,448},{320,256},{384,320},{4... | collective-permute-start | bytes 1376264 | tf_op jit(solution)/shard_map/ppermute | solution.py:307
  31.2 3.1 %collective-permute-start.2 = (bf16[1792,128]{1,0:T(8,128)(2,1)}, bf16[1792,128]{1,0:T(8,128)(2,1)S(1)}, u32[]{:S(2)}, u32[]{:S(2)}) collective-permute-start(bf16[1792,128]{1,0:T(8,128)(2,1)} %get-tuple-element.29), channel_id=1, source_target_pairs={{0,128},{64,192},{128,0},{192,64},{256,384},{320,448},{384,256},{4... | collective-permute-start | bytes 1376264 | tf_op jit(solution)/shard_map/ppermute | solution.py:307
  34.3 3.1 %collective-permute-start.4 = (bf16[1024,128]{1,0:T(8,128)(2,1)}, bf16[1024,128]{1,0:T(8,128)(2,1)}, u32[]{:S(2)}, u32[]{:S(2)}) collective-permute-start(bf16[1024,128]{1,0:T(8,128)(2,1)} %get-tuple-element.32), channel_id=1, source_target_pairs={{0,192},{64,0},{128,64},{192,128},{256,448},{320,256},{384,320},{4... | collective-permute-start | bytes 786440 | tf_op jit(solution)/shard_map/ppermute | solution.py:307
  37.4 2.5 %collective-permute-start.5 = (bf16[1024,128]{1,0:T(8,128)(2,1)}, bf16[1024,128]{1,0:T(8,128)(2,1)}, u32[]{:S(2)}, u32[]{:S(2)}) collective-permute-start(bf16[1024,128]{1,0:T(8,128)(2,1)} %get-tuple-element.33), channel_id=1, source_target_pairs={{0,128},{64,192},{128,0},{192,64},{256,384},{320,448},{384,256},{4... | collective-permute-start | bytes 786440 | tf_op jit(solution)/shard_map/ppermute | solution.py:307
  39.9 16.6 %collective-permute-done.4.refs_2_ = bf16[1024,128]{1,0:T(8,128)(2,1)} collective-permute-done((bf16[1024,128]{1,0:T(8,128)(2,1)}, bf16[1024,128]{1,0:T(8,128)(2,1)}, u32[]{:S(2)}, u32[]{:S(2)}) %collective-permute-start.4) | collective-permute-done | bytes 262176 | tf_op jit(solution)/shard_map/ppermute | solution.py:307
  60.6 7.9 %collective-permute-start.6 = (bf16[2048,128]{1,0:T(8,128)(2,1)}, bf16[2048,128]{1,0:T(8,128)(2,1)}, u32[]{:S(2)}, u32[]{:S(2)}) collective-permute-start(bf16[2048,128]{1,0:T(8,128)(2,1)} %swap.1), channel_id=1, source_target_pairs={{0,256},{64,320},{128,384},{192,448},{256,0},{320,64},{384,128},{4... | collective-permute-start | bytes 1572872 | tf_op jit(solution)/shard_map/ppermute | solution.py:311
  70.7 7.8 %collective-permute-start.7 = (bf16[1088,256]{1,0:T(8,128)(2,1)S(1)}, bf16[1088,256]{1,0:T(8,128)(2,1)S(1)}, u32[]{:S(2)}, u32[]{:S(2)}) collective-permute-start(bf16[1088,256]{1,0:T(8,128)(2,1)S(1)} %get-tuple-element.44), channel_id=1, source_target_pairs={{0,192},{64,0},{128,64},{192,128},{256,448},{320,256},{384,320},{4... | collective-permute-start | bytes 1671176 | tf_op jit(solution)/shard_map/ppermute | solution.py:307
  80.5 3.2 %collective-permute-start.9 = (bf16[1088,256]{1,0:T(8,128)(2,1)S(1)}, bf16[1088,256]{1,0:T(8,128)(2,1)S(1)}, u32[]{:S(2)}, u32[]{:S(2)}) collective-permute-start(bf16[1088,256]{1,0:T(8,128)(2,1)S(1)} %get-tuple-element.46), channel_id=1, source_target_pairs={{0,128},{64,192},{128,0},{192,64},{256,384},{320,448},{384,256},{4... | collective-permute-start | bytes 1671176 | tf_op jit(solution)/shard_map/ppermute | solution.py:307
  86.2 2.8 %collective-permute-done.7.refs_0_ = bf16[1088,256]{1,0:T(8,128)(2,1)S(1)} collective-permute-done((bf16[1088,256]{1,0:T(8,128)(2,1)S(1)}, bf16[1088,256]{1,0:T(8,128)(2,1)S(1)}, u32[]{:S(2)}, u32[]{:S(2)}) %collective-permute-start.7) | collective-permute-done | bytes 557088 | tf_op jit(solution)/shard_map/ppermute | solution.py:307
  89.0 5.3 %collective-permute-done.8.refs_1_ = bf16[1088,256]{1,0:T(8,128)(2,1)S(1)} collective-permute-done((bf16[1088,256]{1,0:T(8,128)(2,1)S(1)}, bf16[1088,256]{1,0:T(8,128)(2,1)S(1)}, u32[]{:S(2)}, u32[]{:S(2)}) %collective-permute-start.8) | collective-permute-done | bytes 557088 | tf_op jit(solution)/shard_map/ppermute | solution.py:307
  94.3 9.6 %collective-permute-done.9.refs_2_ = bf16[1088,256]{1,0:T(8,128)(2,1)S(1)} collective-permute-done((bf16[1088,256]{1,0:T(8,128)(2,1)S(1)}, bf16[1088,256]{1,0:T(8,128)(2,1)S(1)}, u32[]{:S(2)}, u32[]{:S(2)}) %collective-permute-start.9) | collective-permute-done | bytes 557088 | tf_op jit(solution)/shard_map/ppermute | solution.py:307
  104.2 2.7 %collective-permute-start.13 = (bf16[1088,128]{1,0:T(8,128)(2,1)S(1)}, bf16[1088,128]{1,0:T(8,128)(2,1)S(1)}, u32[]{:S(2)}, u32[]{:S(2)}) collective-permute-start(bf16[1088,128]{1,0:T(8,128)(2,1)S(1)} %activate.1.refs_0_), channel_id=1, source_target_pairs={{0,256},{64,320},{128,384},{192,448},{256,0},{320,64},{384,128},{4... | collective-permute-start | bytes 835592 | tf_op jit(solution)/shard_map/ppermute | solution.py:311
  107.0 3.1 %collective-permute-start.10 = (bf16[1088,128]{1,0:T(8,128)(2,1)S(1)}, bf16[1088,128]{1,0:T(8,128)(2,1)S(1)}, u32[]{:S(2)}, u32[]{:S(2)}) collective-permute-start(bf16[1088,128]{1,0:T(8,128)(2,1)S(1)} %activate.1.refs_0_), channel_id=1, source_target_pairs={{0,128},{64,192},{128,0},{192,64},{256,384},{320,448},{384,256},{4... | collective-permute-start | bytes 835592 | tf_op jit(solution)/shard_map/ppermute | solution.py:307
  112.0 3.4 %collective-permute-start.12 = (bf16[1088,128]{1,0:T(8,128)(2,1)S(1)}, bf16[1088,128]{1,0:T(8,128)(2,1)S(1)}, u32[]{:S(2)}, u32[]{:S(2)}) collective-permute-start(bf16[1088,128]{1,0:T(8,128)(2,1)S(1)} %activate.1.refs_0_), channel_id=1, source_target_pairs={{0,64},{64,128},{128,192},{192,0},{256,320},{320,384},{384,448},{4... | collective-permute-start | bytes 835592 | tf_op jit(solution)/shard_map/ppermute | solution.py:307
  115.7 3.5 %collective-permute-start.14 = (bf16[1088,128]{1,0:T(8,128)(2,1)S(1)}, bf16[1088,128]{1,0:T(8,128)(2,1)S(1)}, u32[]{:S(2)}, u32[]{:S(2)}) collective-permute-start(bf16[1088,128]{1,0:T(8,128)(2,1)S(1)} %collective-permute-done.13.refs_4_), channel_id=1, source_target_pairs={{0,128},{64,192},{128,0},{192,64},{256,384},{320,448},{384,256},{4... | collective-permute-start | bytes 835592 | tf_op jit(solution)/shard_map/ppermute | solution.py:307
  119.2 2.5 %collective-permute-start.15 = (bf16[1088,128]{1,0:T(8,128)(2,1)S(1)}, bf16[1088,128]{1,0:T(8,128)(2,1)S(1)}, u32[]{:S(2)}, u32[]{:S(2)}) collective-permute-start(bf16[1088,128]{1,0:T(8,128)(2,1)S(1)} %collective-permute-done.13.refs_4_), channel_id=1, source_target_pairs={{0,192},{64,0},{128,64},{192,128},{256,448},{320,256},{384,320},{4... | collective-permute-start | bytes 835592 | tf_op jit(solution)/shard_map/ppermute | solution.py:307
  121.6 2.8 %collective-permute-start.16 = (bf16[1088,128]{1,0:T(8,128)(2,1)S(1)}, bf16[1088,128]{1,0:T(8,128)(2,1)S(1)}, u32[]{:S(2)}, u32[]{:S(2)}) collective-permute-start(bf16[1088,128]{1,0:T(8,128)(2,1)S(1)} %collective-permute-done.13.refs_4_), channel_id=1, source_target_pairs={{0,64},{64,128},{128,192},{192,0},{256,320},{320,384},{384,448},{4... | collective-permute-start | bytes 835592 | tf_op jit(solution)/shard_map/ppermute | solution.py:307
  125.7 3.7 %collective-permute-done.14.refs_5_ = bf16[1088,128]{1,0:T(8,128)(2,1)S(1)} collective-permute-done((bf16[1088,128]{1,0:T(8,128)(2,1)S(1)}, bf16[1088,128]{1,0:T(8,128)(2,1)S(1)}, u32[]{:S(2)}, u32[]{:S(2)}) %collective-permute-start.14) | collective-permute-done | bytes 278560 | tf_op jit(solution)/shard_map/ppermute | solution.py:307
  134.7 46.3 %all_to_all.10.chunks_ref = bf16[64,64,128]{2,1,0:T(8,128)(2,1)S(1)} all-to-all(bf16[64,64,128]{2,1,0:T(8,128)(2,1)S(1)} %down.1), channel_id=1, replica_groups=mesh['pipe'=8,'expert'=64] {'expert'}, dimensions={0} | all-to-all | bytes 2097152 | tf_op jit(solution)/shard_map/all_to_all | solution.py:338
  (31 shorter events, 21.9 us)
Async XLA Ops:
  3.5 65.0 %all-to-all-start = ((bf16[64,120,128]{2,1,0:T(8,128)(2,1)}), bf16[64,120,128]{2,1,0:T(8,128)(2,1)S(1)}, u32[]{:S(2)}, u32[]{:S(2)}) async-start(bf16[64,120,128]{2,1,0:T(8,128)(2,1)} %dispatch.1), calls=%async_computation | async-start | bytes 3932160 | tf_op jit(solution)/shard_map/all_to_all | solution.py:322
  21.6 15.9 %collective-permute-start.3 = (bf16[1024,128]{1,0:T(8,128)(2,1)}, bf16[1024,128]{1,0:T(8,128)(2,1)}, u32[]{:S(2)}, u32[]{:S(2)}) collective-permute-start(bf16[1024,128]{1,0:T(8,128)(2,1)} %get-tuple-element.31), channel_id=1, source_target_pairs={{0,64},{64,128},{128,192},{192,0},{256,320},{320,384},{384,448},{4... | collective-permute-start | bytes 786440 | tf_op jit(solution)/shard_map/ppermute | solution.py:307
  24.7 34.0 %collective-permute-start = (bf16[1792,128]{1,0:T(8,128)(2,1)}, bf16[1792,128]{1,0:T(8,128)(2,1)S(1)}, u32[]{:S(2)}, u32[]{:S(2)}) collective-permute-start(bf16[1792,128]{1,0:T(8,128)(2,1)} %get-tuple-element.27), channel_id=1, source_target_pairs={{0,64},{64,128},{128,192},{192,0},{256,320},{320,384},{384,448},{4... | collective-permute-start | bytes 1376264 | tf_op jit(solution)/shard_map/ppermute | solution.py:307
  27.8 30.9 %collective-permute-start.1 = (bf16[1792,128]{1,0:T(8,128)(2,1)}, bf16[1792,128]{1,0:T(8,128)(2,1)S(1)}, u32[]{:S(2)}, u32[]{:S(2)}) collective-permute-start(bf16[1792,128]{1,0:T(8,128)(2,1)} %get-tuple-element.28), channel_id=1, source_target_pairs={{0,192},{64,0},{128,64},{192,128},{256,448},{320,256},{384,320},{4... | collective-permute-start | bytes 1376264 | tf_op jit(solution)/shard_map/ppermute | solution.py:307
  31.2 27.5 %collective-permute-start.2 = (bf16[1792,128]{1,0:T(8,128)(2,1)}, bf16[1792,128]{1,0:T(8,128)(2,1)S(1)}, u32[]{:S(2)}, u32[]{:S(2)}) collective-permute-start(bf16[1792,128]{1,0:T(8,128)(2,1)} %get-tuple-element.29), channel_id=1, source_target_pairs={{0,128},{64,192},{128,0},{192,64},{256,384},{320,448},{384,256},{4... | collective-permute-start | bytes 1376264 | tf_op jit(solution)/shard_map/ppermute | solution.py:307
  34.3 22.2 %collective-permute-start.4 = (bf16[1024,128]{1,0:T(8,128)(2,1)}, bf16[1024,128]{1,0:T(8,128)(2,1)}, u32[]{:S(2)}, u32[]{:S(2)}) collective-permute-start(bf16[1024,128]{1,0:T(8,128)(2,1)} %get-tuple-element.32), channel_id=1, source_target_pairs={{0,192},{64,0},{128,64},{192,128},{256,448},{320,256},{384,320},{4... | collective-permute-start | bytes 786440 | tf_op jit(solution)/shard_map/ppermute | solution.py:307
  37.4 21.2 %collective-permute-start.5 = (bf16[1024,128]{1,0:T(8,128)(2,1)}, bf16[1024,128]{1,0:T(8,128)(2,1)}, u32[]{:S(2)}, u32[]{:S(2)}) collective-permute-start(bf16[1024,128]{1,0:T(8,128)(2,1)} %get-tuple-element.33), channel_id=1, source_target_pairs={{0,128},{64,192},{128,0},{192,64},{256,384},{320,448},{384,256},{4... | collective-permute-start | bytes 786440 | tf_op jit(solution)/shard_map/ppermute | solution.py:307
  60.6 23.1 %collective-permute-start.6 = (bf16[2048,128]{1,0:T(8,128)(2,1)}, bf16[2048,128]{1,0:T(8,128)(2,1)}, u32[]{:S(2)}, u32[]{:S(2)}) collective-permute-start(bf16[2048,128]{1,0:T(8,128)(2,1)} %swap.1), channel_id=1, source_target_pairs={{0,256},{64,320},{128,384},{192,448},{256,0},{320,64},{384,128},{4... | collective-permute-start | bytes 1572872 | tf_op jit(solution)/shard_map/ppermute | solution.py:311
  68.6 15.2 %copy-start.1 = (bf16[1024,128]{1,0:T(8,128)(2,1)S(1)}, bf16[1024,128]{1,0:T(8,128)(2,1)}, u32[]{:S(2)}) copy-start(bf16[1024,128]{1,0:T(8,128)(2,1)} %get-tuple-element.34.refs_0_) | copy-start | bytes 786436
  70.7 18.2 %collective-permute-start.7 = (bf16[1088,256]{1,0:T(8,128)(2,1)S(1)}, bf16[1088,256]{1,0:T(8,128)(2,1)S(1)}, u32[]{:S(2)}, u32[]{:S(2)}) collective-permute-start(bf16[1088,256]{1,0:T(8,128)(2,1)S(1)} %get-tuple-element.44), channel_id=1, source_target_pairs={{0,192},{64,0},{128,64},{192,128},{256,448},{320,256},{384,320},{4... | collective-permute-start | bytes 1671176 | tf_op jit(solution)/shard_map/ppermute | solution.py:307
  78.6 15.7 %collective-permute-start.8 = (bf16[1088,256]{1,0:T(8,128)(2,1)S(1)}, bf16[1088,256]{1,0:T(8,128)(2,1)S(1)}, u32[]{:S(2)}, u32[]{:S(2)}) collective-permute-start(bf16[1088,256]{1,0:T(8,128)(2,1)S(1)} %get-tuple-element.45), channel_id=1, source_target_pairs={{0,64},{64,128},{128,192},{192,0},{256,320},{320,384},{384,448},{4... | collective-permute-start | bytes 1671176 | tf_op jit(solution)/shard_map/ppermute | solution.py:307
  80.5 4.7 %copy-start = (bf16[1792,128]{1,0:T(8,128)(2,1)S(1)}, bf16[1792,128]{1,0:T(8,128)(2,1)}, u32[]{:S(2)}) copy-start(bf16[1792,128]{1,0:T(8,128)(2,1)} %get-tuple-element.40.refs_0_) | copy-start | bytes 1376260
  80.5 23.4 %collective-permute-start.9 = (bf16[1088,256]{1,0:T(8,128)(2,1)S(1)}, bf16[1088,256]{1,0:T(8,128)(2,1)S(1)}, u32[]{:S(2)}, u32[]{:S(2)}) collective-permute-start(bf16[1088,256]{1,0:T(8,128)(2,1)S(1)} %get-tuple-element.46), channel_id=1, source_target_pairs={{0,128},{64,192},{128,0},{192,64},{256,384},{320,448},{384,256},{4... | collective-permute-start | bytes 1671176 | tf_op jit(solution)/shard_map/ppermute | solution.py:307
  104.2 11.4 %collective-permute-start.13 = (bf16[1088,128]{1,0:T(8,128)(2,1)S(1)}, bf16[1088,128]{1,0:T(8,128)(2,1)S(1)}, u32[]{:S(2)}, u32[]{:S(2)}) collective-permute-start(bf16[1088,128]{1,0:T(8,128)(2,1)S(1)} %activate.1.refs_0_), channel_id=1, source_target_pairs={{0,256},{64,320},{128,384},{192,448},{256,0},{320,64},{384,128},{4... | collective-permute-start | bytes 835592 | tf_op jit(solution)/shard_map/ppermute | solution.py:311
  107.0 14.7 %collective-permute-start.10 = (bf16[1088,128]{1,0:T(8,128)(2,1)S(1)}, bf16[1088,128]{1,0:T(8,128)(2,1)S(1)}, u32[]{:S(2)}, u32[]{:S(2)}) collective-permute-start(bf16[1088,128]{1,0:T(8,128)(2,1)S(1)} %activate.1.refs_0_), channel_id=1, source_target_pairs={{0,128},{64,192},{128,0},{192,64},{256,384},{320,448},{384,256},{4... | collective-permute-start | bytes 835592 | tf_op jit(solution)/shard_map/ppermute | solution.py:307
  110.1 14.4 %collective-permute-start.11 = (bf16[1088,128]{1,0:T(8,128)(2,1)S(1)}, bf16[1088,128]{1,0:T(8,128)(2,1)S(1)}, u32[]{:S(2)}, u32[]{:S(2)}) collective-permute-start(bf16[1088,128]{1,0:T(8,128)(2,1)S(1)} %activate.1.refs_0_), channel_id=1, source_target_pairs={{0,192},{64,0},{128,64},{192,128},{256,448},{320,256},{384,320},{4... | collective-permute-start | bytes 835592 | tf_op jit(solution)/shard_map/ppermute | solution.py:307
  112.0 13.7 %collective-permute-start.12 = (bf16[1088,128]{1,0:T(8,128)(2,1)S(1)}, bf16[1088,128]{1,0:T(8,128)(2,1)S(1)}, u32[]{:S(2)}, u32[]{:S(2)}) collective-permute-start(bf16[1088,128]{1,0:T(8,128)(2,1)S(1)} %activate.1.refs_0_), channel_id=1, source_target_pairs={{0,64},{64,128},{128,192},{192,0},{256,320},{320,384},{384,448},{4... | collective-permute-start | bytes 835592 | tf_op jit(solution)/shard_map/ppermute | solution.py:307
  115.7 13.8 %collective-permute-start.14 = (bf16[1088,128]{1,0:T(8,128)(2,1)S(1)}, bf16[1088,128]{1,0:T(8,128)(2,1)S(1)}, u32[]{:S(2)}, u32[]{:S(2)}) collective-permute-start(bf16[1088,128]{1,0:T(8,128)(2,1)S(1)} %collective-permute-done.13.refs_4_), channel_id=1, source_target_pairs={{0,128},{64,192},{128,0},{192,64},{256,384},{320,448},{384,256},{4... | collective-permute-start | bytes 835592 | tf_op jit(solution)/shard_map/ppermute | solution.py:307
  119.2 11.9 %collective-permute-start.15 = (bf16[1088,128]{1,0:T(8,128)(2,1)S(1)}, bf16[1088,128]{1,0:T(8,128)(2,1)S(1)}, u32[]{:S(2)}, u32[]{:S(2)}) collective-permute-start(bf16[1088,128]{1,0:T(8,128)(2,1)S(1)} %collective-permute-done.13.refs_4_), channel_id=1, source_target_pairs={{0,192},{64,0},{128,64},{192,128},{256,448},{320,256},{384,320},{4... | collective-permute-start | bytes 835592 | tf_op jit(solution)/shard_map/ppermute | solution.py:307
  121.6 11.5 %collective-permute-start.16 = (bf16[1088,128]{1,0:T(8,128)(2,1)S(1)}, bf16[1088,128]{1,0:T(8,128)(2,1)S(1)}, u32[]{:S(2)}, u32[]{:S(2)}) collective-permute-start(bf16[1088,128]{1,0:T(8,128)(2,1)S(1)} %collective-permute-done.13.refs_4_), channel_id=1, source_target_pairs={{0,64},{64,128},{128,192},{192,0},{256,320},{320,384},{384,448},{4... | collective-permute-start | bytes 835592 | tf_op jit(solution)/shard_map/ppermute | solution.py:307
  134.6 46.3 %copy-start.2 = (s32[128,8]{0,1:T(8,128)S(1)}, s32[128,8]{0,1:T(8,128)}, u32[]{:S(2)}) copy-start(s32[128,8]{0,1:T(8,128)} %param.7) | copy-start | bytes 12292
  134.7 46.3 %copy-start.3 = (f32[128,8]{0,1:T(8,128)S(1)}, f32[128,8]{0,1:T(8,128)}, u32[]{:S(2)}) copy-start(f32[128,8]{0,1:T(8,128)} %param.8) | copy-start | bytes 12292

commit v13 on v12

--- a/solution.py
+++ b/solution.py
@@ -323,8 +323,8 @@
     both, downs = pack(x, w_gate, w_up, w_down)
     both = [both[0]] + [shift(both[d], d) for d in ORDER]
     downs = [downs[0]] + [shift(downs[d], d) for d in ORDER]
-    held = lax.optimization_barrier((*both, *downs))
-    both, downs = held[:X], held[X:]
+    held = lax.optimization_barrier((both[0], both[2], both[1], both[3], *downs))
+    both, downs = (held[0], held[2], held[1], held[3]), held[X:]
     other = cross(swap(z, downs))
     parts = project(chunks, both[1:], BF, "project_sent")
     arrived = [shift(part, -d) for d, part in zip(ORDER, parts)]

time: 184 us -> 182 us (0.989)
  blocking collectives: 46.3 us -> 38.4 us
  waiting for transfers between devices: 45.3 us -> 48.7 us
  starting transfers between devices: 73.7 us -> 76.1 us
    all_to_all x1, blocking collectives: 46.3 us -> 38.4 us  [body(): lax.all_to_all(output, 'expert', split_axis=0, concat_axis=0, tiled=True)]
    ppermute x2, starting transfers between devices: 10.7 us -> 16.1 us  [cross(): lax.ppermute(value, 'pipe', [(p, (p + X) % (2 * X)) for p in range(2 * X)])]
    ppermute x2, waiting for transfers between devices: 0.27 us -> 3.6 us  [cross(): lax.ppermute(value, 'pipe', [(p, (p + X) % (2 * X)) for p in range(2 * X)])]
    ppermute x15, starting transfers between devices: 48.4 us -> 45.4 us  [shift(): return lax.ppermute(value, 'pipe', pairs)]
  transfers between devices with their start and end apart: 18 -> 18, of which waited for: 10 -> 9; matrix products, arithmetic and copies ran while one was open for 0% -> 0% of each run, Pallas kernels for 5% -> 5%
where the time goes in v13:
time: 182 us; the launch traced here: 181 us
  starting transfers between devices  76.1 us (42%)
  waiting for transfers between devices  48.7 us (27%)
  blocking collectives  38.4 us (21%)
  Pallas kernels  16.9 us (9%)
    ppermute x15, starting transfers between devices, shift(): return lax.ppermute(value, 'pipe', pairs)  45.4 us
    ppermute x15, waiting for transfers between devices, shift(): return lax.ppermute(value, 'pipe', pairs)  45.1 us
    all_to_all x1, blocking collectives, body(): lax.all_to_all(output, 'expert', split_axis=0, concat_axis=0, tiled=True)  38.4 us
    ppermute x2, starting transfers between devices, cross(): lax.ppermute(value, 'pipe', [(p, (p + X) % (2 * X)) for p in range(2 * X)])  16.1 us
    all_to_all x1, starting transfers between devices, body(): lax.all_to_all(buffer, 'expert', split_axis=0, concat_axis=0, tiled=True)  14.6 us
  transfers between devices with their start and end apart: 18, of which 9 were waited for; matrix products, arithmetic and copies ran while one was open for 0% of the time, Pallas kernels for 5%

profile of v13, /device:TPU:1, one launch (start us, length us, event | category | flops | bytes accessed | tf_op | source)
XLA Modules:
  0.0 181.1 jit_solution(8213845391622647904)
XLA Ops:
  0.0 3.5 %dispatch.1 = bf16[64,120,128]{2,1,0:T(8,128)(2,1)} custom-call(s32[1]{0:T(128)} %bitcast.x_ref, s32[8,128]{1,0:T(8,128)} %bitcast.7, bf16[128,3584]{1,0:T(8,128)(2,1)} %tok_ref.1), custom_call_target="tpu_custom_call" | custom-call | tf_op jit(solution)/shard_map/dispatch/pallas_call | solution.py:108
  3.5 14.6 %all-to-all-start = ((bf16[64,120,128]{2,1,0:T(8,128)(2,1)}), bf16[64,120,128]{2,1,0:T(8,128)(2,1)S(1)}, u32[]{:S(2)}, u32[]{:S(2)}) async-start(bf16[64,120,128]{2,1,0:T(8,128)(2,1)} %dispatch.1), calls=%async_computation | async-start | bytes 3932160 | tf_op jit(solution)/shard_map/all_to_all | solution.py:322
  18.2 3.4 %pack.1 = (bf16[1792,128]{1,0:T(8,128)(2,1)}, bf16[1792,128]{1,0:T(8,128)(2,1)}, bf16[1792,128]{1,0:T(8,128)(2,1)}, bf16[1792,128]{1,0:T(8,128)(2,1)}, bf16[1024...) custom-call(s32[1]{0:T(128)} %bitcast.x_ref, ...), custom_call_target="tpu_custom_call" | custom-call | tf_op jit(solution)/shard_map/pack/pallas_call | solution.py:145
  21.6 3.1 %collective-permute-start.3 = (bf16[1024,128]{1,0:T(8,128)(2,1)}, bf16[1024,128]{1,0:T(8,128)(2,1)}, u32[]{:S(2)}, u32[]{:S(2)}) collective-permute-start(bf16[1024,128]{1,0:T(8,128)(2,1)} %get-tuple-element.31), channel_id=1, source_target_pairs={{0,64},{64,128},{128,192},{192,0},{256,320},{320,384},{384,448},{4... | collective-permute-start | bytes 786440 | tf_op jit(solution)/shard_map/ppermute | solution.py:307
  24.7 3.4 %collective-permute-start = (bf16[1792,128]{1,0:T(8,128)(2,1)}, bf16[1792,128]{1,0:T(8,128)(2,1)S(1)}, u32[]{:S(2)}, u32[]{:S(2)}) collective-permute-start(bf16[1792,128]{1,0:T(8,128)(2,1)} %get-tuple-element.27), channel_id=1, source_target_pairs={{0,192},{64,0},{128,64},{192,128},{256,448},{320,256},{384,320},{4... | collective-permute-start | bytes 1376264 | tf_op jit(solution)/shard_map/ppermute | solution.py:307
  30.0 4.3 %collective-permute-start.2 = (bf16[1792,128]{1,0:T(8,128)(2,1)}, bf16[1792,128]{1,0:T(8,128)(2,1)S(1)}, u32[]{:S(2)}, u32[]{:S(2)}) collective-permute-start(bf16[1792,128]{1,0:T(8,128)(2,1)} %get-tuple-element.29), channel_id=1, source_target_pairs={{0,128},{64,192},{128,0},{192,64},{256,384},{320,448},{384,256},{4... | collective-permute-start | bytes 1376264 | tf_op jit(solution)/shard_map/ppermute | solution.py:307
  34.3 3.1 %collective-permute-start.4 = (bf16[1024,128]{1,0:T(8,128)(2,1)}, bf16[1024,128]{1,0:T(8,128)(2,1)}, u32[]{:S(2)}, u32[]{:S(2)}) collective-permute-start(bf16[1024,128]{1,0:T(8,128)(2,1)} %get-tuple-element.32), channel_id=1, source_target_pairs={{0,192},{64,0},{128,64},{192,128},{256,448},{320,256},{384,320},{4... | collective-permute-start | bytes 786440 | tf_op jit(solution)/shard_map/ppermute | solution.py:307
  37.4 3.3 %collective-permute-start.5 = (bf16[1024,128]{1,0:T(8,128)(2,1)}, bf16[1024,128]{1,0:T(8,128)(2,1)}, u32[]{:S(2)}, u32[]{:S(2)}) collective-permute-start(bf16[1024,128]{1,0:T(8,128)(2,1)} %get-tuple-element.33), channel_id=1, source_target_pairs={{0,128},{64,192},{128,0},{192,64},{256,384},{320,448},{384,256},{4... | collective-permute-start | bytes 786440 | tf_op jit(solution)/shard_map/ppermute | solution.py:307
  40.8 12.9 %collective-permute-done.4.refs_2_ = bf16[1024,128]{1,0:T(8,128)(2,1)} collective-permute-done((bf16[1024,128]{1,0:T(8,128)(2,1)}, bf16[1024,128]{1,0:T(8,128)(2,1)}, u32[]{:S(2)}, u32[]{:S(2)}) %collective-permute-start.4) | collective-permute-done | bytes 262176 | tf_op jit(solution)/shard_map/ppermute | solution.py:307
  53.7 4.6 %collective-permute-done.5.refs_3_ = bf16[1024,128]{1,0:T(8,128)(2,1)} collective-permute-done((bf16[1024,128]{1,0:T(8,128)(2,1)}, bf16[1024,128]{1,0:T(8,128)(2,1)}, u32[]{:S(2)}, u32[]{:S(2)}) %collective-permute-start.5) | collective-permute-done | bytes 262176 | tf_op jit(solution)/shard_map/ppermute | solution.py:307
  60.3 7.9 %collective-permute-start.6 = (bf16[2048,128]{1,0:T(8,128)(2,1)}, bf16[2048,128]{1,0:T(8,128)(2,1)}, u32[]{:S(2)}, u32[]{:S(2)}) collective-permute-start(bf16[2048,128]{1,0:T(8,128)(2,1)} %swap.1), channel_id=1, source_target_pairs={{0,256},{64,320},{128,384},{192,448},{256,0},{320,64},{384,128},{4... | collective-permute-start | bytes 1572872 | tf_op jit(solution)/shard_map/ppermute | solution.py:311
  70.4 5.3 %collective-permute-start.7 = (bf16[1088,256]{1,0:T(8,128)(2,1)S(1)}, bf16[1088,256]{1,0:T(8,128)(2,1)S(1)}, u32[]{:S(2)}, u32[]{:S(2)}) collective-permute-start(bf16[1088,256]{1,0:T(8,128)(2,1)S(1)} %get-tuple-element.44), channel_id=1, source_target_pairs={{0,192},{64,0},{128,64},{192,128},{256,448},{320,256},{384,320},{4... | collective-permute-start | bytes 1671176 | tf_op jit(solution)/shard_map/ppermute | solution.py:307
  77.7 3.2 %collective-permute-start.9 = (bf16[1088,256]{1,0:T(8,128)(2,1)S(1)}, bf16[1088,256]{1,0:T(8,128)(2,1)S(1)}, u32[]{:S(2)}, u32[]{:S(2)}) collective-permute-start(bf16[1088,256]{1,0:T(8,128)(2,1)S(1)} %get-tuple-element.46), channel_id=1, source_target_pairs={{0,128},{64,192},{128,0},{192,64},{256,384},{320,448},{384,256},{4... | collective-permute-start | bytes 1671176 | tf_op jit(solution)/shard_map/ppermute | solution.py:307
  83.4 2.8 %collective-permute-done.7.refs_0_ = bf16[1088,256]{1,0:T(8,128)(2,1)S(1)} collective-permute-done((bf16[1088,256]{1,0:T(8,128)(2,1)S(1)}, bf16[1088,256]{1,0:T(8,128)(2,1)S(1)}, u32[]{:S(2)}, u32[]{:S(2)}) %collective-permute-start.7) | collective-permute-done | bytes 557088 | tf_op jit(solution)/shard_map/ppermute | solution.py:307
  86.2 5.6 %collective-permute-done.8.refs_1_ = bf16[1088,256]{1,0:T(8,128)(2,1)S(1)} collective-permute-done((bf16[1088,256]{1,0:T(8,128)(2,1)S(1)}, bf16[1088,256]{1,0:T(8,128)(2,1)S(1)}, u32[]{:S(2)}, u32[]{:S(2)}) %collective-permute-start.8) | collective-permute-done | bytes 557088 | tf_op jit(solution)/shard_map/ppermute | solution.py:307
  91.7 9.6 %collective-permute-done.9.refs_2_ = bf16[1088,256]{1,0:T(8,128)(2,1)S(1)} collective-permute-done((bf16[1088,256]{1,0:T(8,128)(2,1)S(1)}, bf16[1088,256]{1,0:T(8,128)(2,1)S(1)}, u32[]{:S(2)}, u32[]{:S(2)}) %collective-permute-start.9) | collective-permute-done | bytes 557088 | tf_op jit(solution)/shard_map/ppermute | solution.py:307
  101.8 8.2 %collective-permute-start.13 = (bf16[1088,128]{1,0:T(8,128)(2,1)S(1)}, bf16[1088,128]{1,0:T(8,128)(2,1)S(1)}, u32[]{:S(2)}, u32[]{:S(2)}) collective-permute-start(bf16[1088,128]{1,0:T(8,128)(2,1)S(1)} %activate.1.refs_0_), channel_id=1, source_target_pairs={{0,256},{64,320},{128,384},{192,448},{256,0},{320,64},{384,128},{4... | collective-permute-start | bytes 835592 | tf_op jit(solution)/shard_map/ppermute | solution.py:311
  114.3 3.4 %collective-permute-start.12 = (bf16[1088,128]{1,0:T(8,128)(2,1)S(1)}, bf16[1088,128]{1,0:T(8,128)(2,1)S(1)}, u32[]{:S(2)}, u32[]{:S(2)}) collective-permute-start(bf16[1088,128]{1,0:T(8,128)(2,1)S(1)} %activate.1.refs_0_), channel_id=1, source_target_pairs={{0,64},{64,128},{128,192},{192,0},{256,320},{320,384},{384,448},{4... | collective-permute-start | bytes 835592 | tf_op jit(solution)/shard_map/ppermute | solution.py:307
  117.7 3.6 %collective-permute-done.13.refs_4_ = bf16[1088,128]{1,0:T(8,128)(2,1)S(1)} collective-permute-done((bf16[1088,128]{1,0:T(8,128)(2,1)S(1)}, bf16[1088,128]{1,0:T(8,128)(2,1)S(1)}, u32[]{:S(2)}, u32[]{:S(2)}) %collective-permute-start.13) | collective-permute-done | bytes 278560 | tf_op jit(solution)/shard_map/ppermute | solution.py:311
  121.3 2.7 %collective-permute-start.14 = (bf16[1088,128]{1,0:T(8,128)(2,1)S(1)}, bf16[1088,128]{1,0:T(8,128)(2,1)S(1)}, u32[]{:S(2)}, u32[]{:S(2)}) collective-permute-start(bf16[1088,128]{1,0:T(8,128)(2,1)S(1)} %collective-permute-done.13.refs_4_), channel_id=1, source_target_pairs={{0,128},{64,192},{128,0},{192,64},{256,384},{320,448},{384,256},{4... | collective-permute-start | bytes 835592 | tf_op jit(solution)/shard_map/ppermute | solution.py:307
  126.0 3.4 %collective-permute-start.16 = (bf16[1088,128]{1,0:T(8,128)(2,1)S(1)}, bf16[1088,128]{1,0:T(8,128)(2,1)S(1)}, u32[]{:S(2)}, u32[]{:S(2)}) collective-permute-start(bf16[1088,128]{1,0:T(8,128)(2,1)S(1)} %collective-permute-done.13.refs_4_), channel_id=1, source_target_pairs={{0,64},{64,128},{128,192},{192,0},{256,320},{320,384},{384,448},{4... | collective-permute-start | bytes 835592 | tf_op jit(solution)/shard_map/ppermute | solution.py:307
  131.7 3.1 %collective-permute-done.15.refs_6_ = bf16[1088,128]{1,0:T(8,128)(2,1)S(1)} collective-permute-done((bf16[1088,128]{1,0:T(8,128)(2,1)S(1)}, bf16[1088,128]{1,0:T(8,128)(2,1)S(1)}, u32[]{:S(2)}, u32[]{:S(2)}) %collective-permute-start.15) | collective-permute-done | bytes 278560 | tf_op jit(solution)/shard_map/ppermute | solution.py:307
  134.8 4.0 %collective-permute-done.16.refs_7_ = bf16[1088,128]{1,0:T(8,128)(2,1)S(1)} collective-permute-done((bf16[1088,128]{1,0:T(8,128)(2,1)S(1)}, bf16[1088,128]{1,0:T(8,128)(2,1)S(1)}, u32[]{:S(2)}, u32[]{:S(2)}) %collective-permute-start.16) | collective-permute-done | bytes 278560 | tf_op jit(solution)/shard_map/ppermute | solution.py:307
  140.4 38.4 %all_to_all.10.chunks_ref = bf16[64,64,128]{2,1,0:T(8,128)(2,1)S(1)} all-to-all(bf16[64,64,128]{2,1,0:T(8,128)(2,1)S(1)} %down.1), channel_id=1, replica_groups=mesh['pipe'=8,'expert'=64] {'expert'}, dimensions={0} | all-to-all | bytes 2097152 | tf_op jit(solution)/shard_map/all_to_all | solution.py:338
  (31 shorter events, 23.2 us)
Async XLA Ops:
  3.5 64.7 %all-to-all-start = ((bf16[64,120,128]{2,1,0:T(8,128)(2,1)}), bf16[64,120,128]{2,1,0:T(8,128)(2,1)S(1)}, u32[]{:S(2)}, u32[]{:S(2)}) async-start(bf16[64,120,128]{2,1,0:T(8,128)(2,1)} %dispatch.1), calls=%async_computation | async-start | bytes 3932160 | tf_op jit(solution)/shard_map/all_to_all | solution.py:322
  21.6 15.9 %collective-permute-start.3 = (bf16[1024,128]{1,0:T(8,128)(2,1)}, bf16[1024,128]{1,0:T(8,128)(2,1)}, u32[]{:S(2)}, u32[]{:S(2)}) collective-permute-start(bf16[1024,128]{1,0:T(8,128)(2,1)} %get-tuple-element.31), channel_id=1, source_target_pairs={{0,64},{64,128},{128,192},{192,0},{256,320},{320,384},{384,448},{4... | collective-permute-start | bytes 786440 | tf_op jit(solution)/shard_map/ppermute | solution.py:307
  24.7 33.7 %collective-permute-start = (bf16[1792,128]{1,0:T(8,128)(2,1)}, bf16[1792,128]{1,0:T(8,128)(2,1)S(1)}, u32[]{:S(2)}, u32[]{:S(2)}) collective-permute-start(bf16[1792,128]{1,0:T(8,128)(2,1)} %get-tuple-element.27), channel_id=1, source_target_pairs={{0,192},{64,0},{128,64},{192,128},{256,448},{320,256},{384,320},{4... | collective-permute-start | bytes 1376264 | tf_op jit(solution)/shard_map/ppermute | solution.py:307
  28.1 30.3 %collective-permute-start.1 = (bf16[1792,128]{1,0:T(8,128)(2,1)}, bf16[1792,128]{1,0:T(8,128)(2,1)S(1)}, u32[]{:S(2)}, u32[]{:S(2)}) collective-permute-start(bf16[1792,128]{1,0:T(8,128)(2,1)} %get-tuple-element.28), channel_id=1, source_target_pairs={{0,64},{64,128},{128,192},{192,0},{256,320},{320,384},{384,448},{4... | collective-permute-start | bytes 1376264 | tf_op jit(solution)/shard_map/ppermute | solution.py:307
  30.0 28.4 %collective-permute-start.2 = (bf16[1792,128]{1,0:T(8,128)(2,1)}, bf16[1792,128]{1,0:T(8,128)(2,1)S(1)}, u32[]{:S(2)}, u32[]{:S(2)}) collective-permute-start(bf16[1792,128]{1,0:T(8,128)(2,1)} %get-tuple-element.29), channel_id=1, source_target_pairs={{0,128},{64,192},{128,0},{192,64},{256,384},{320,448},{384,256},{4... | collective-permute-start | bytes 1376264 | tf_op jit(solution)/shard_map/ppermute | solution.py:307
  34.3 19.4 %collective-permute-start.4 = (bf16[1024,128]{1,0:T(8,128)(2,1)}, bf16[1024,128]{1,0:T(8,128)(2,1)}, u32[]{:S(2)}, u32[]{:S(2)}) collective-permute-start(bf16[1024,128]{1,0:T(8,128)(2,1)} %get-tuple-element.32), channel_id=1, source_target_pairs={{0,192},{64,0},{128,64},{192,128},{256,448},{320,256},{384,320},{4... | collective-permute-start | bytes 786440 | tf_op jit(solution)/shard_map/ppermute | solution.py:307
  37.4 20.9 %collective-permute-start.5 = (bf16[1024,128]{1,0:T(8,128)(2,1)}, bf16[1024,128]{1,0:T(8,128)(2,1)}, u32[]{:S(2)}, u32[]{:S(2)}) collective-permute-start(bf16[1024,128]{1,0:T(8,128)(2,1)} %get-tuple-element.33), channel_id=1, source_target_pairs={{0,128},{64,192},{128,0},{192,64},{256,384},{320,448},{384,256},{4... | collective-permute-start | bytes 786440 | tf_op jit(solution)/shard_map/ppermute | solution.py:307
  60.3 20.6 %collective-permute-start.6 = (bf16[2048,128]{1,0:T(8,128)(2,1)}, bf16[2048,128]{1,0:T(8,128)(2,1)}, u32[]{:S(2)}, u32[]{:S(2)}) collective-permute-start(bf16[2048,128]{1,0:T(8,128)(2,1)} %swap.1), channel_id=1, source_target_pairs={{0,256},{64,320},{128,384},{192,448},{256,0},{320,64},{384,128},{4... | collective-permute-start | bytes 1572872 | tf_op jit(solution)/shard_map/ppermute | solution.py:311
  68.3 12.7 %copy-start.1 = (bf16[1024,128]{1,0:T(8,128)(2,1)S(1)}, bf16[1024,128]{1,0:T(8,128)(2,1)}, u32[]{:S(2)}) copy-start(bf16[1024,128]{1,0:T(8,128)(2,1)} %get-tuple-element.34.refs_0_) | copy-start | bytes 786436
  70.4 15.8 %collective-permute-start.7 = (bf16[1088,256]{1,0:T(8,128)(2,1)S(1)}, bf16[1088,256]{1,0:T(8,128)(2,1)S(1)}, u32[]{:S(2)}, u32[]{:S(2)}) collective-permute-start(bf16[1088,256]{1,0:T(8,128)(2,1)S(1)} %get-tuple-element.44), channel_id=1, source_target_pairs={{0,192},{64,0},{128,64},{192,128},{256,448},{320,256},{384,320},{4... | collective-permute-start | bytes 1671176 | tf_op jit(solution)/shard_map/ppermute | solution.py:307
  75.7 16.0 %collective-permute-start.8 = (bf16[1088,256]{1,0:T(8,128)(2,1)S(1)}, bf16[1088,256]{1,0:T(8,128)(2,1)S(1)}, u32[]{:S(2)}, u32[]{:S(2)}) collective-permute-start(bf16[1088,256]{1,0:T(8,128)(2,1)S(1)} %get-tuple-element.45), channel_id=1, source_target_pairs={{0,64},{64,128},{128,192},{192,0},{256,320},{320,384},{384,448},{4... | collective-permute-start | bytes 1671176 | tf_op jit(solution)/shard_map/ppermute | solution.py:307
  77.7 4.7 %copy-start = (bf16[1792,128]{1,0:T(8,128)(2,1)S(1)}, bf16[1792,128]{1,0:T(8,128)(2,1)}, u32[]{:S(2)}) copy-start(bf16[1792,128]{1,0:T(8,128)(2,1)} %get-tuple-element.40.refs_0_) | copy-start | bytes 1376260
  77.7 23.7 %collective-permute-start.9 = (bf16[1088,256]{1,0:T(8,128)(2,1)S(1)}, bf16[1088,256]{1,0:T(8,128)(2,1)S(1)}, u32[]{:S(2)}, u32[]{:S(2)}) collective-permute-start(bf16[1088,256]{1,0:T(8,128)(2,1)S(1)} %get-tuple-element.46), channel_id=1, source_target_pairs={{0,128},{64,192},{128,0},{192,64},{256,384},{320,448},{384,256},{4... | collective-permute-start | bytes 1671176 | tf_op jit(solution)/shard_map/ppermute | solution.py:307
  101.8 19.5 %collective-permute-start.13 = (bf16[1088,128]{1,0:T(8,128)(2,1)S(1)}, bf16[1088,128]{1,0:T(8,128)(2,1)S(1)}, u32[]{:S(2)}, u32[]{:S(2)}) collective-permute-start(bf16[1088,128]{1,0:T(8,128)(2,1)S(1)} %activate.1.refs_0_), channel_id=1, source_target_pairs={{0,256},{64,320},{128,384},{192,448},{256,0},{320,64},{384,128},{4... | collective-permute-start | bytes 835592 | tf_op jit(solution)/shard_map/ppermute | solution.py:311
  110.0 16.0 %collective-permute-start.10 = (bf16[1088,128]{1,0:T(8,128)(2,1)S(1)}, bf16[1088,128]{1,0:T(8,128)(2,1)S(1)}, u32[]{:S(2)}, u32[]{:S(2)}) collective-permute-start(bf16[1088,128]{1,0:T(8,128)(2,1)S(1)} %activate.1.refs_0_), channel_id=1, source_target_pairs={{0,128},{64,192},{128,0},{192,64},{256,384},{320,448},{384,256},{4... | collective-permute-start | bytes 835592 | tf_op jit(solution)/shard_map/ppermute | solution.py:307
  112.4 16.9 %collective-permute-start.11 = (bf16[1088,128]{1,0:T(8,128)(2,1)S(1)}, bf16[1088,128]{1,0:T(8,128)(2,1)S(1)}, u32[]{:S(2)}, u32[]{:S(2)}) collective-permute-start(bf16[1088,128]{1,0:T(8,128)(2,1)S(1)} %activate.1.refs_0_), channel_id=1, source_target_pairs={{0,192},{64,0},{128,64},{192,128},{256,448},{320,256},{384,320},{4... | collective-permute-start | bytes 835592 | tf_op jit(solution)/shard_map/ppermute | solution.py:307
  114.3 15.0 %collective-permute-start.12 = (bf16[1088,128]{1,0:T(8,128)(2,1)S(1)}, bf16[1088,128]{1,0:T(8,128)(2,1)S(1)}, u32[]{:S(2)}, u32[]{:S(2)}) collective-permute-start(bf16[1088,128]{1,0:T(8,128)(2,1)S(1)} %activate.1.refs_0_), channel_id=1, source_target_pairs={{0,64},{64,128},{128,192},{192,0},{256,320},{320,384},{384,448},{4... | collective-permute-start | bytes 835592 | tf_op jit(solution)/shard_map/ppermute | solution.py:307
  121.3 10.4 %collective-permute-start.14 = (bf16[1088,128]{1,0:T(8,128)(2,1)S(1)}, bf16[1088,128]{1,0:T(8,128)(2,1)S(1)}, u32[]{:S(2)}, u32[]{:S(2)}) collective-permute-start(bf16[1088,128]{1,0:T(8,128)(2,1)S(1)} %collective-permute-done.13.refs_4_), channel_id=1, source_target_pairs={{0,128},{64,192},{128,0},{192,64},{256,384},{320,448},{384,256},{4... | collective-permute-start | bytes 835592 | tf_op jit(solution)/shard_map/ppermute | solution.py:307
  124.0 10.8 %collective-permute-start.15 = (bf16[1088,128]{1,0:T(8,128)(2,1)S(1)}, bf16[1088,128]{1,0:T(8,128)(2,1)S(1)}, u32[]{:S(2)}, u32[]{:S(2)}) collective-permute-start(bf16[1088,128]{1,0:T(8,128)(2,1)S(1)} %collective-permute-done.13.refs_4_), channel_id=1, source_target_pairs={{0,192},{64,0},{128,64},{192,128},{256,448},{320,256},{384,320},{4... | collective-permute-start | bytes 835592 | tf_op jit(solution)/shard_map/ppermute | solution.py:307
  126.0 12.9 %collective-permute-start.16 = (bf16[1088,128]{1,0:T(8,128)(2,1)S(1)}, bf16[1088,128]{1,0:T(8,128)(2,1)S(1)}, u32[]{:S(2)}, u32[]{:S(2)}) collective-permute-start(bf16[1088,128]{1,0:T(8,128)(2,1)S(1)} %collective-permute-done.13.refs_4_), channel_id=1, source_target_pairs={{0,64},{64,128},{128,192},{192,0},{256,320},{320,384},{384,448},{4... | collective-permute-start | bytes 835592 | tf_op jit(solution)/shard_map/ppermute | solution.py:307
  140.4 38.4 %copy-start.2 = (s32[128,8]{0,1:T(8,128)S(1)}, s32[128,8]{0,1:T(8,128)}, u32[]{:S(2)}) copy-start(s32[128,8]{0,1:T(8,128)} %param.7) | copy-start | bytes 12292
  140.4 38.4 %copy-start.3 = (f32[128,8]{0,1:T(8,128)S(1)}, f32[128,8]{0,1:T(8,128)}, u32[]{:S(2)}) copy-start(f32[128,8]{0,1:T(8,128)} %param.8) | copy-start | bytes 12292

commit v14 on v13

--- a/solution.py
+++ b/solution.py
@@ -326,8 +326,8 @@
     held = lax.optimization_barrier((both[0], both[2], both[1], both[3], *downs))
     both, downs = (held[0], held[2], held[1], held[3]), held[X:]
     other = cross(swap(z, downs))
-    parts = project(chunks, both[1:], BF, "project_sent")
-    arrived = [shift(part, -d) for d, part in zip(ORDER, parts)]
+    parts = project(chunks, [both[i] for i in (2, 1, 3)], BF, "project_sent")
+    arrived = [shift(part, -d) for d, part in zip((3, 1, 2), parts)]
     chunks, weight = lax.optimization_barrier((chunks, assemble(z, downs, other)))
     (mine,) = project(chunks, both[:1], F32, "project_own")
     hidden = activate(mine, arrived)

time: 182 us -> 183 us (level)
  waiting for transfers between devices: 48.7 us -> 41.7 us
  starting transfers between devices: 76.1 us -> 80.3 us
  blocking collectives: 38.4 us -> 42 us
    ppermute x15, starting transfers between devices: 45.4 us -> 50.7 us  [shift(): return lax.ppermute(value, 'pipe', pairs)]
    ppermute x15, waiting for transfers between devices: 45.1 us -> 40.8 us  [shift(): return lax.ppermute(value, 'pipe', pairs)]
    all_to_all x1, blocking collectives: 38.4 us -> 42 us  [body(): lax.all_to_all(output, 'expert', split_axis=0, concat_axis=0, tiled=True)]
    ppermute x2, waiting for transfers between devices: 3.6 us -> 0.95 us  [cross(): lax.ppermute(value, 'pipe', [(p, (p + X) % (2 * X)) for p in range(2 * X)])]
  transfers between devices with their start and end apart: 18 -> 18, of which waited for: 9 -> 8; matrix products, arithmetic and copies ran while one was open for 0% -> 0% of each run, Pallas kernels for 5% -> 5%
where the time goes in v14:
time: 183 us; the launch traced here: 182 us
  starting transfers between devices  80.3 us (44%)
  blocking collectives  42 us (23%)
  waiting for transfers between devices  41.7 us (23%)
  Pallas kernels  16.9 us (9%)
    ppermute x15, starting transfers between devices, shift(): return lax.ppermute(value, 'pipe', pairs)  50.7 us
    all_to_all x1, blocking collectives, body(): lax.all_to_all(output, 'expert', split_axis=0, concat_axis=0, tiled=True)  42 us
    ppermute x15, waiting for transfers between devices, shift(): return lax.ppermute(value, 'pipe', pairs)  40.8 us
    ppermute x2, starting transfers between devices, cross(): lax.ppermute(value, 'pipe', [(p, (p + X) % (2 * X)) for p in range(2 * X)])  15 us
    all_to_all x1, starting transfers between devices, body(): lax.all_to_all(buffer, 'expert', split_axis=0, concat_axis=0, tiled=True)  14.6 us
  transfers between devices with their start and end apart: 18, of which 8 were waited for; matrix products, arithmetic and copies ran while one was open for 0% of the time, Pallas kernels for 5%

profile of v14, /device:TPU:1, one launch (start us, length us, event | category | flops | bytes accessed | tf_op | source)
XLA Modules:
  0.0 182.0 jit_solution(10598284520623742801)
XLA Ops:
  0.0 3.5 %dispatch.1 = bf16[64,120,128]{2,1,0:T(8,128)(2,1)} custom-call(s32[1]{0:T(128)} %bitcast.x_ref, s32[8,128]{1,0:T(8,128)} %bitcast.7, bf16[128,3584]{1,0:T(8,128)(2,1)} %tok_ref.1), custom_call_target="tpu_custom_call" | custom-call | tf_op jit(solution)/shard_map/dispatch/pallas_call | solution.py:108
  3.5 14.6 %all-to-all-start = ((bf16[64,120,128]{2,1,0:T(8,128)(2,1)}), bf16[64,120,128]{2,1,0:T(8,128)(2,1)S(1)}, u32[]{:S(2)}, u32[]{:S(2)}) async-start(bf16[64,120,128]{2,1,0:T(8,128)(2,1)} %dispatch.1), calls=%async_computation | async-start | bytes 3932160 | tf_op jit(solution)/shard_map/all_to_all | solution.py:322
  18.2 3.4 %pack.1 = (bf16[1792,128]{1,0:T(8,128)(2,1)}, bf16[1792,128]{1,0:T(8,128)(2,1)}, bf16[1792,128]{1,0:T(8,128)(2,1)}, bf16[1792,128]{1,0:T(8,128)(2,1)}, bf16[1024...) custom-call(s32[1]{0:T(128)} %bitcast.x_ref, ...), custom_call_target="tpu_custom_call" | custom-call | tf_op jit(solution)/shard_map/pack/pallas_call | solution.py:145
  21.6 3.1 %collective-permute-start.3 = (bf16[1024,128]{1,0:T(8,128)(2,1)}, bf16[1024,128]{1,0:T(8,128)(2,1)}, u32[]{:S(2)}, u32[]{:S(2)}) collective-permute-start(bf16[1024,128]{1,0:T(8,128)(2,1)} %get-tuple-element.31), channel_id=1, source_target_pairs={{0,64},{64,128},{128,192},{192,0},{256,320},{320,384},{384,448},{4... | collective-permute-start | bytes 786440 | tf_op jit(solution)/shard_map/ppermute | solution.py:307
  24.7 3.4 %collective-permute-start = (bf16[1792,128]{1,0:T(8,128)(2,1)}, bf16[1792,128]{1,0:T(8,128)(2,1)S(1)}, u32[]{:S(2)}, u32[]{:S(2)}) collective-permute-start(bf16[1792,128]{1,0:T(8,128)(2,1)} %get-tuple-element.27), channel_id=1, source_target_pairs={{0,192},{64,0},{128,64},{192,128},{256,448},{320,256},{384,320},{4... | collective-permute-start | bytes 1376264 | tf_op jit(solution)/shard_map/ppermute | solution.py:307
  30.0 4.3 %collective-permute-start.2 = (bf16[1792,128]{1,0:T(8,128)(2,1)}, bf16[1792,128]{1,0:T(8,128)(2,1)S(1)}, u32[]{:S(2)}, u32[]{:S(2)}) collective-permute-start(bf16[1792,128]{1,0:T(8,128)(2,1)} %get-tuple-element.29), channel_id=1, source_target_pairs={{0,128},{64,192},{128,0},{192,64},{256,384},{320,448},{384,256},{4... | collective-permute-start | bytes 1376264 | tf_op jit(solution)/shard_map/ppermute | solution.py:307
  34.3 3.1 %collective-permute-start.4 = (bf16[1024,128]{1,0:T(8,128)(2,1)}, bf16[1024,128]{1,0:T(8,128)(2,1)}, u32[]{:S(2)}, u32[]{:S(2)}) collective-permute-start(bf16[1024,128]{1,0:T(8,128)(2,1)} %get-tuple-element.32), channel_id=1, source_target_pairs={{0,192},{64,0},{128,64},{192,128},{256,448},{320,256},{384,320},{4... | collective-permute-start | bytes 786440 | tf_op jit(solution)/shard_map/ppermute | solution.py:307
  37.4 3.3 %collective-permute-start.5 = (bf16[1024,128]{1,0:T(8,128)(2,1)}, bf16[1024,128]{1,0:T(8,128)(2,1)}, u32[]{:S(2)}, u32[]{:S(2)}) collective-permute-start(bf16[1024,128]{1,0:T(8,128)(2,1)} %get-tuple-element.33), channel_id=1, source_target_pairs={{0,128},{64,192},{128,0},{192,64},{256,384},{320,448},{384,256},{4... | collective-permute-start | bytes 786440 | tf_op jit(solution)/shard_map/ppermute | solution.py:307
  40.8 12.9 %collective-permute-done.4.refs_2_ = bf16[1024,128]{1,0:T(8,128)(2,1)} collective-permute-done((bf16[1024,128]{1,0:T(8,128)(2,1)}, bf16[1024,128]{1,0:T(8,128)(2,1)}, u32[]{:S(2)}, u32[]{:S(2)}) %collective-permute-start.4) | collective-permute-done | bytes 262176 | tf_op jit(solution)/shard_map/ppermute | solution.py:307
  53.7 4.6 %collective-permute-done.5.refs_3_ = bf16[1024,128]{1,0:T(8,128)(2,1)} collective-permute-done((bf16[1024,128]{1,0:T(8,128)(2,1)}, bf16[1024,128]{1,0:T(8,128)(2,1)}, u32[]{:S(2)}, u32[]{:S(2)}) %collective-permute-start.5) | collective-permute-done | bytes 262176 | tf_op jit(solution)/shard_map/ppermute | solution.py:307
  60.3 7.9 %collective-permute-start.6 = (bf16[2048,128]{1,0:T(8,128)(2,1)}, bf16[2048,128]{1,0:T(8,128)(2,1)}, u32[]{:S(2)}, u32[]{:S(2)}) collective-permute-start(bf16[2048,128]{1,0:T(8,128)(2,1)} %swap.1), channel_id=1, source_target_pairs={{0,256},{64,320},{128,384},{192,448},{256,0},{320,64},{384,128},{4... | collective-permute-start | bytes 1572872 | tf_op jit(solution)/shard_map/ppermute | solution.py:311
  70.4 4.7 %collective-permute-start.7 = (bf16[1088,256]{1,0:T(8,128)(2,1)S(1)}, bf16[1088,256]{1,0:T(8,128)(2,1)S(1)}, u32[]{:S(2)}, u32[]{:S(2)}) collective-permute-start(bf16[1088,256]{1,0:T(8,128)(2,1)S(1)} %get-tuple-element.44), channel_id=1, source_target_pairs={{0,64},{64,128},{128,192},{192,0},{256,320},{320,384},{384,448},{4... | collective-permute-start | bytes 1671176 | tf_op jit(solution)/shard_map/ppermute | solution.py:307
  75.2 2.5 %collective-permute-start.8 = (bf16[1088,256]{1,0:T(8,128)(2,1)S(1)}, bf16[1088,256]{1,0:T(8,128)(2,1)S(1)}, u32[]{:S(2)}, u32[]{:S(2)}) collective-permute-start(bf16[1088,256]{1,0:T(8,128)(2,1)S(1)} %get-tuple-element.45), channel_id=1, source_target_pairs={{0,192},{64,0},{128,64},{192,128},{256,448},{320,256},{384,320},{4... | collective-permute-start | bytes 1671176 | tf_op jit(solution)/shard_map/ppermute | solution.py:307
  77.7 3.2 %collective-permute-start.9 = (bf16[1088,256]{1,0:T(8,128)(2,1)S(1)}, bf16[1088,256]{1,0:T(8,128)(2,1)S(1)}, u32[]{:S(2)}, u32[]{:S(2)}) collective-permute-start(bf16[1088,256]{1,0:T(8,128)(2,1)S(1)} %get-tuple-element.46), channel_id=1, source_target_pairs={{0,128},{64,192},{128,0},{192,64},{256,384},{320,448},{384,256},{4... | collective-permute-start | bytes 1671176 | tf_op jit(solution)/shard_map/ppermute | solution.py:307
  83.4 3.2 %collective-permute-done.7.refs_0_ = bf16[1088,256]{1,0:T(8,128)(2,1)S(1)} collective-permute-done((bf16[1088,256]{1,0:T(8,128)(2,1)S(1)}, bf16[1088,256]{1,0:T(8,128)(2,1)S(1)}, u32[]{:S(2)}, u32[]{:S(2)}) %collective-permute-start.7) | collective-permute-done | bytes 557088 | tf_op jit(solution)/shard_map/ppermute | solution.py:307
  86.6 2.4 %collective-permute-done.8.refs_1_ = bf16[1088,256]{1,0:T(8,128)(2,1)S(1)} collective-permute-done((bf16[1088,256]{1,0:T(8,128)(2,1)S(1)}, bf16[1088,256]{1,0:T(8,128)(2,1)S(1)}, u32[]{:S(2)}, u32[]{:S(2)}) %collective-permute-start.8) | collective-permute-done | bytes 557088 | tf_op jit(solution)/shard_map/ppermute | solution.py:307
  89.0 10.4 %collective-permute-done.9.refs_2_ = bf16[1088,256]{1,0:T(8,128)(2,1)S(1)} collective-permute-done((bf16[1088,256]{1,0:T(8,128)(2,1)S(1)}, bf16[1088,256]{1,0:T(8,128)(2,1)S(1)}, u32[]{:S(2)}, u32[]{:S(2)}) %collective-permute-start.9) | collective-permute-done | bytes 557088 | tf_op jit(solution)/shard_map/ppermute | solution.py:307
  99.8 7.0 %collective-permute-start.13 = (bf16[1088,128]{1,0:T(8,128)(2,1)S(1)}, bf16[1088,128]{1,0:T(8,128)(2,1)S(1)}, u32[]{:S(2)}, u32[]{:S(2)}) collective-permute-start(bf16[1088,128]{1,0:T(8,128)(2,1)S(1)} %activate.1.refs_0_), channel_id=1, source_target_pairs={{0,256},{64,320},{128,384},{192,448},{256,0},{320,64},{384,128},{4... | collective-permute-start | bytes 835592 | tf_op jit(solution)/shard_map/ppermute | solution.py:311
  106.8 2.2 %collective-permute-start.10 = (bf16[1088,128]{1,0:T(8,128)(2,1)S(1)}, bf16[1088,128]{1,0:T(8,128)(2,1)S(1)}, u32[]{:S(2)}, u32[]{:S(2)}) collective-permute-start(bf16[1088,128]{1,0:T(8,128)(2,1)S(1)} %activate.1.refs_0_), channel_id=1, source_target_pairs={{0,128},{64,192},{128,0},{192,64},{256,384},{320,448},{384,256},{4... | collective-permute-start | bytes 835592 | tf_op jit(solution)/shard_map/ppermute | solution.py:307
  109.0 6.6 %collective-permute-start.11 = (bf16[1088,128]{1,0:T(8,128)(2,1)S(1)}, bf16[1088,128]{1,0:T(8,128)(2,1)S(1)}, u32[]{:S(2)}, u32[]{:S(2)}) collective-permute-start(bf16[1088,128]{1,0:T(8,128)(2,1)S(1)} %activate.1.refs_0_), channel_id=1, source_target_pairs={{0,192},{64,0},{128,64},{192,128},{256,448},{320,256},{384,320},{4... | collective-permute-start | bytes 835592 | tf_op jit(solution)/shard_map/ppermute | solution.py:307
  118.4 3.4 %collective-permute-start.14 = (bf16[1088,128]{1,0:T(8,128)(2,1)S(1)}, bf16[1088,128]{1,0:T(8,128)(2,1)S(1)}, u32[]{:S(2)}, u32[]{:S(2)}) collective-permute-start(bf16[1088,128]{1,0:T(8,128)(2,1)S(1)} %collective-permute-done.13.refs_4_), channel_id=1, source_target_pairs={{0,128},{64,192},{128,0},{192,64},{256,384},{320,448},{384,256},{4... | collective-permute-start | bytes 835592 | tf_op jit(solution)/shard_map/ppermute | solution.py:307
  121.8 5.0 %collective-permute-start.15 = (bf16[1088,128]{1,0:T(8,128)(2,1)S(1)}, bf16[1088,128]{1,0:T(8,128)(2,1)S(1)}, u32[]{:S(2)}, u32[]{:S(2)}) collective-permute-start(bf16[1088,128]{1,0:T(8,128)(2,1)S(1)} %collective-permute-done.13.refs_4_), channel_id=1, source_target_pairs={{0,192},{64,0},{128,64},{192,128},{256,448},{320,256},{384,320},{4... | collective-permute-start | bytes 835592 | tf_op jit(solution)/shard_map/ppermute | solution.py:307
  130.4 5.6 %collective-permute-done.15.refs_6_ = bf16[1088,128]{1,0:T(8,128)(2,1)S(1)} collective-permute-done((bf16[1088,128]{1,0:T(8,128)(2,1)S(1)}, bf16[1088,128]{1,0:T(8,128)(2,1)S(1)}, u32[]{:S(2)}, u32[]{:S(2)}) %collective-permute-start.15) | collective-permute-done | bytes 278560 | tf_op jit(solution)/shard_map/ppermute | solution.py:307
  137.6 42.0 %all_to_all.10.chunks_ref = bf16[64,64,128]{2,1,0:T(8,128)(2,1)S(1)} all-to-all(bf16[64,64,128]{2,1,0:T(8,128)(2,1)S(1)} %down.1), channel_id=1, replica_groups=mesh['pipe'=8,'expert'=64] {'expert'}, dimensions={0} | all-to-all | bytes 2097152 | tf_op jit(solution)/shard_map/all_to_all | solution.py:338
  (31 shorter events, 19.1 us)
Async XLA Ops:
  3.5 64.7 %all-to-all-start = ((bf16[64,120,128]{2,1,0:T(8,128)(2,1)}), bf16[64,120,128]{2,1,0:T(8,128)(2,1)S(1)}, u32[]{:S(2)}, u32[]{:S(2)}) async-start(bf16[64,120,128]{2,1,0:T(8,128)(2,1)} %dispatch.1), calls=%async_computation | async-start | bytes 3932160 | tf_op jit(solution)/shard_map/all_to_all | solution.py:322
  21.6 15.9 %collective-permute-start.3 = (bf16[1024,128]{1,0:T(8,128)(2,1)}, bf16[1024,128]{1,0:T(8,128)(2,1)}, u32[]{:S(2)}, u32[]{:S(2)}) collective-permute-start(bf16[1024,128]{1,0:T(8,128)(2,1)} %get-tuple-element.31), channel_id=1, source_target_pairs={{0,64},{64,128},{128,192},{192,0},{256,320},{320,384},{384,448},{4... | collective-permute-start | bytes 786440 | tf_op jit(solution)/shard_map/ppermute | solution.py:307
  24.7 33.7 %collective-permute-start = (bf16[1792,128]{1,0:T(8,128)(2,1)}, bf16[1792,128]{1,0:T(8,128)(2,1)S(1)}, u32[]{:S(2)}, u32[]{:S(2)}) collective-permute-start(bf16[1792,128]{1,0:T(8,128)(2,1)} %get-tuple-element.27), channel_id=1, source_target_pairs={{0,192},{64,0},{128,64},{192,128},{256,448},{320,256},{384,320},{4... | collective-permute-start | bytes 1376264 | tf_op jit(solution)/shard_map/ppermute | solution.py:307
  28.1 30.3 %collective-permute-start.1 = (bf16[1792,128]{1,0:T(8,128)(2,1)}, bf16[1792,128]{1,0:T(8,128)(2,1)S(1)}, u32[]{:S(2)}, u32[]{:S(2)}) collective-permute-start(bf16[1792,128]{1,0:T(8,128)(2,1)} %get-tuple-element.28), channel_id=1, source_target_pairs={{0,64},{64,128},{128,192},{192,0},{256,320},{320,384},{384,448},{4... | collective-permute-start | bytes 1376264 | tf_op jit(solution)/shard_map/ppermute | solution.py:307
  30.0 28.4 %collective-permute-start.2 = (bf16[1792,128]{1,0:T(8,128)(2,1)}, bf16[1792,128]{1,0:T(8,128)(2,1)S(1)}, u32[]{:S(2)}, u32[]{:S(2)}) collective-permute-start(bf16[1792,128]{1,0:T(8,128)(2,1)} %get-tuple-element.29), channel_id=1, source_target_pairs={{0,128},{64,192},{128,0},{192,64},{256,384},{320,448},{384,256},{4... | collective-permute-start | bytes 1376264 | tf_op jit(solution)/shard_map/ppermute | solution.py:307
  34.3 19.4 %collective-permute-start.4 = (bf16[1024,128]{1,0:T(8,128)(2,1)}, bf16[1024,128]{1,0:T(8,128)(2,1)}, u32[]{:S(2)}, u32[]{:S(2)}) collective-permute-start(bf16[1024,128]{1,0:T(8,128)(2,1)} %get-tuple-element.32), channel_id=1, source_target_pairs={{0,192},{64,0},{128,64},{192,128},{256,448},{320,256},{384,320},{4... | collective-permute-start | bytes 786440 | tf_op jit(solution)/shard_map/ppermute | solution.py:307
  37.4 20.9 %collective-permute-start.5 = (bf16[1024,128]{1,0:T(8,128)(2,1)}, bf16[1024,128]{1,0:T(8,128)(2,1)}, u32[]{:S(2)}, u32[]{:S(2)}) collective-permute-start(bf16[1024,128]{1,0:T(8,128)(2,1)} %get-tuple-element.33), channel_id=1, source_target_pairs={{0,128},{64,192},{128,0},{192,64},{256,384},{320,448},{384,256},{4... | collective-permute-start | bytes 786440 | tf_op jit(solution)/shard_map/ppermute | solution.py:307
  60.3 20.6 %collective-permute-start.6 = (bf16[2048,128]{1,0:T(8,128)(2,1)}, bf16[2048,128]{1,0:T(8,128)(2,1)}, u32[]{:S(2)}, u32[]{:S(2)}) collective-permute-start(bf16[2048,128]{1,0:T(8,128)(2,1)} %swap.1), channel_id=1, source_target_pairs={{0,256},{64,320},{128,384},{192,448},{256,0},{320,64},{384,128},{4... | collective-permute-start | bytes 1572872 | tf_op jit(solution)/shard_map/ppermute | solution.py:311
  68.3 12.7 %copy-start.1 = (bf16[1024,128]{1,0:T(8,128)(2,1)S(1)}, bf16[1024,128]{1,0:T(8,128)(2,1)}, u32[]{:S(2)}) copy-start(bf16[1024,128]{1,0:T(8,128)(2,1)} %get-tuple-element.34.refs_0_) | copy-start | bytes 786436
  70.4 16.1 %collective-permute-start.7 = (bf16[1088,256]{1,0:T(8,128)(2,1)S(1)}, bf16[1088,256]{1,0:T(8,128)(2,1)S(1)}, u32[]{:S(2)}, u32[]{:S(2)}) collective-permute-start(bf16[1088,256]{1,0:T(8,128)(2,1)S(1)} %get-tuple-element.44), channel_id=1, source_target_pairs={{0,64},{64,128},{128,192},{192,0},{256,320},{320,384},{384,448},{4... | collective-permute-start | bytes 1671176 | tf_op jit(solution)/shard_map/ppermute | solution.py:307
  75.2 13.8 %collective-permute-start.8 = (bf16[1088,256]{1,0:T(8,128)(2,1)S(1)}, bf16[1088,256]{1,0:T(8,128)(2,1)S(1)}, u32[]{:S(2)}, u32[]{:S(2)}) collective-permute-start(bf16[1088,256]{1,0:T(8,128)(2,1)S(1)} %get-tuple-element.45), channel_id=1, source_target_pairs={{0,192},{64,0},{128,64},{192,128},{256,448},{320,256},{384,320},{4... | collective-permute-start | bytes 1671176 | tf_op jit(solution)/shard_map/ppermute | solution.py:307
  77.7 4.7 %copy-start = (bf16[1792,128]{1,0:T(8,128)(2,1)S(1)}, bf16[1792,128]{1,0:T(8,128)(2,1)}, u32[]{:S(2)}) copy-start(bf16[1792,128]{1,0:T(8,128)(2,1)} %get-tuple-element.40.refs_0_) | copy-start | bytes 1376260
  77.7 21.7 %collective-permute-start.9 = (bf16[1088,256]{1,0:T(8,128)(2,1)S(1)}, bf16[1088,256]{1,0:T(8,128)(2,1)S(1)}, u32[]{:S(2)}, u32[]{:S(2)}) collective-permute-start(bf16[1088,256]{1,0:T(8,128)(2,1)S(1)} %get-tuple-element.46), channel_id=1, source_target_pairs={{0,128},{64,192},{128,0},{192,64},{256,384},{320,448},{384,256},{4... | collective-permute-start | bytes 1671176 | tf_op jit(solution)/shard_map/ppermute | solution.py:307
  99.8 18.7 %collective-permute-start.13 = (bf16[1088,128]{1,0:T(8,128)(2,1)S(1)}, bf16[1088,128]{1,0:T(8,128)(2,1)S(1)}, u32[]{:S(2)}, u32[]{:S(2)}) collective-permute-start(bf16[1088,128]{1,0:T(8,128)(2,1)S(1)} %activate.1.refs_0_), channel_id=1, source_target_pairs={{0,256},{64,320},{128,384},{192,448},{256,0},{320,64},{384,128},{4... | collective-permute-start | bytes 835592 | tf_op jit(solution)/shard_map/ppermute | solution.py:311
  106.8 20.0 %collective-permute-start.10 = (bf16[1088,128]{1,0:T(8,128)(2,1)S(1)}, bf16[1088,128]{1,0:T(8,128)(2,1)S(1)}, u32[]{:S(2)}, u32[]{:S(2)}) collective-permute-start(bf16[1088,128]{1,0:T(8,128)(2,1)S(1)} %activate.1.refs_0_), channel_id=1, source_target_pairs={{0,128},{64,192},{128,0},{192,64},{256,384},{320,448},{384,256},{4... | collective-permute-start | bytes 835592 | tf_op jit(solution)/shard_map/ppermute | solution.py:307
  109.0 19.9 %collective-permute-start.11 = (bf16[1088,128]{1,0:T(8,128)(2,1)S(1)}, bf16[1088,128]{1,0:T(8,128)(2,1)S(1)}, u32[]{:S(2)}, u32[]{:S(2)}) collective-permute-start(bf16[1088,128]{1,0:T(8,128)(2,1)S(1)} %activate.1.refs_0_), channel_id=1, source_target_pairs={{0,192},{64,0},{128,64},{192,128},{256,448},{320,256},{384,320},{4... | collective-permute-start | bytes 835592 | tf_op jit(solution)/shard_map/ppermute | solution.py:307
  115.5 13.3 %collective-permute-start.12 = (bf16[1088,128]{1,0:T(8,128)(2,1)S(1)}, bf16[1088,128]{1,0:T(8,128)(2,1)S(1)}, u32[]{:S(2)}, u32[]{:S(2)}) collective-permute-start(bf16[1088,128]{1,0:T(8,128)(2,1)S(1)} %activate.1.refs_0_), channel_id=1, source_target_pairs={{0,64},{64,128},{128,192},{192,0},{256,320},{320,384},{384,448},{4... | collective-permute-start | bytes 835592 | tf_op jit(solution)/shard_map/ppermute | solution.py:307
  118.4 12.0 %collective-permute-start.14 = (bf16[1088,128]{1,0:T(8,128)(2,1)S(1)}, bf16[1088,128]{1,0:T(8,128)(2,1)S(1)}, u32[]{:S(2)}, u32[]{:S(2)}) collective-permute-start(bf16[1088,128]{1,0:T(8,128)(2,1)S(1)} %collective-permute-done.13.refs_4_), channel_id=1, source_target_pairs={{0,128},{64,192},{128,0},{192,64},{256,384},{320,448},{384,256},{4... | collective-permute-start | bytes 835592 | tf_op jit(solution)/shard_map/ppermute | solution.py:307
  121.8 14.3 %collective-permute-start.15 = (bf16[1088,128]{1,0:T(8,128)(2,1)S(1)}, bf16[1088,128]{1,0:T(8,128)(2,1)S(1)}, u32[]{:S(2)}, u32[]{:S(2)}) collective-permute-start(bf16[1088,128]{1,0:T(8,128)(2,1)S(1)} %collective-permute-done.13.refs_4_), channel_id=1, source_target_pairs={{0,192},{64,0},{128,64},{192,128},{256,448},{320,256},{384,320},{4... | collective-permute-start | bytes 835592 | tf_op jit(solution)/shard_map/ppermute | solution.py:307
  126.8 9.3 %collective-permute-start.16 = (bf16[1088,128]{1,0:T(8,128)(2,1)S(1)}, bf16[1088,128]{1,0:T(8,128)(2,1)S(1)}, u32[]{:S(2)}, u32[]{:S(2)}) collective-permute-start(bf16[1088,128]{1,0:T(8,128)(2,1)S(1)} %collective-permute-done.13.refs_4_), channel_id=1, source_target_pairs={{0,64},{64,128},{128,192},{192,0},{256,320},{320,384},{384,448},{4... | collective-permute-start | bytes 835592 | tf_op jit(solution)/shard_map/ppermute | solution.py:307
  137.6 42.1 %copy-start.2 = (s32[128,8]{0,1:T(8,128)S(1)}, s32[128,8]{0,1:T(8,128)}, u32[]{:S(2)}) copy-start(s32[128,8]{0,1:T(8,128)} %param.7) | copy-start | bytes 12292
  137.6 42.1 %copy-start.3 = (f32[128,8]{0,1:T(8,128)S(1)}, f32[128,8]{0,1:T(8,128)}, u32[]{:S(2)}) copy-start(f32[128,8]{0,1:T(8,128)} %param.8) | copy-start | bytes 12292
